TPU v7x, 32 devices: a whole 2x2x4 slice. The times are simulated.
32 devices in a mesh: blk: 8 (over z, core), narrow: 4 (over y, x).
Axes of the slice: x: 2, y: 2, z: 4, core: 2. Of those that a mesh axis runs over, the one named last changes fastest.
Arguments:
- student_img: bfloat16 [4096, 1152], P(('blk', 'narrow')), may hold values from -6 to 6
- student_txt: bfloat16 [4096, 1152], P(('blk', 'narrow')), may hold values from -6 to 6
- teacher_img: bfloat16 [4096, 1536], P(('blk', 'narrow')), may hold values from -6 to 6
- teacher_txt: bfloat16 [4096, 1536], P(('blk', 'narrow')), may hold values from -6 to 6
Outputs:
- image_grad: float32 [4096, 1152], P(('blk', 'narrow'))
- text_grad: float32 [4096, 1152], P(('blk', 'narrow'))
All inputs are finite; a program needn't handle non-finite values.
Results may differ from a plain program's by a relative error of at most 0.0097.
Values may be sent and summed in bfloat16 or wider, within the bound.
No kernel may reach another device: no remote copies, remote signals or barrier semaphores. Data moves between devices by JAX's collectives and lax.ppermute only.
A program may use at most 128 MiB of HBM per device.

v0:
```python
import jax
import jax.numpy as jnp
from jax import lax
from jax.sharding import PartitionSpec as P

epsilon = 1e-06
logit_scale = 100.0
logit_bias = -4.0


def shifted(x, axis, by):
    count = lax.axis_size(axis)
    return lax.ppermute(x, axis, [(i, (i + by) % count) for i in range(count)])


def unit_rows(raw_rows):
    raw_float = raw_rows.astype(jnp.float32)
    radius = jnp.sqrt(jnp.sum(raw_float * raw_float, axis=1, keepdims=True) + epsilon)
    return (raw_float / radius, radius)


def unit_back(grad_unit, unit_float, radius):
    along_unit = jnp.sum(unit_float * grad_unit, axis=1, keepdims=True)
    return (grad_unit - unit_float * along_unit) / radius


def body(student_img, student_txt, teacher_img, teacher_txt):
    block_count = lax.axis_size("blk")
    block_index = lax.axis_index("blk")
    group_index = lax.axis_index("narrow")
    own_rows = student_txt.shape[0]
    embed_width = student_txt.shape[1]
    image_block, teacher_block = (
        lax.all_gather(student_img, "narrow", axis=0, tiled=True),
        lax.all_gather(teacher_img, "narrow", axis=0, tiled=True),
    )
    block_rows = image_block.shape[0]
    img_float, img_radius = unit_rows(image_block)
    img_unit = img_float.astype(jnp.bfloat16)
    t_img_unit = unit_rows(teacher_block)[0].astype(jnp.bfloat16)
    txt_float, txt_radius = unit_rows(student_txt)
    txt_unit = txt_float.astype(jnp.bfloat16)
    t_txt_unit = unit_rows(teacher_txt)[0].astype(jnp.bfloat16)
    teacher_tile = (
        logit_scale
        * jnp.einsum(
            "rd,cd->rc",
            t_img_unit,
            lax.all_gather(t_txt_unit, "blk", axis=0, tiled=True),
            preferred_element_type=jnp.float32,
        )
        + logit_bias
    )
    row_ids = lax.broadcasted_iota(jnp.int32, (block_rows, own_rows), 0)
    col_ids = lax.broadcasted_iota(jnp.int32, (block_rows, own_rows), 1) + group_index * own_rows
    same_slot = row_ids == col_ids
    pair_start = jnp.zeros((block_rows, own_rows * block_count), jnp.bfloat16)

    def advance(cycle_step, cycle_state):
        text_cur, teach_cur, grad_acc, img_acc, pair_store = cycle_state
        source = (block_index - cycle_step) % block_count
        teacher_logit = lax.dynamic_slice_in_dim(teacher_tile, source * own_rows, own_rows, 1)
        student_logit = (
            logit_scale
            * jnp.einsum("rd,cd->rc", img_unit, text_cur, preferred_element_type=jnp.float32)
            + logit_bias
        )
        positive = jnp.where(same_slot & (source == block_index), 1.0, 0.0).astype(jnp.float32)
        pair_grad = (
            2.0 * jax.nn.sigmoid(student_logit) - jax.nn.sigmoid(teacher_logit) - positive
        ).astype(jnp.bfloat16)
        img_acc = img_acc + jnp.dot(pair_grad, text_cur, preferred_element_type=jnp.float32)
        pair_store = lax.dynamic_update_slice_in_dim(pair_store, pair_grad, source * own_rows, 1)
        text_cur = shifted(text_cur, "blk", 1)
        return (text_cur, teach_cur, grad_acc, img_acc, pair_store)

    start_state = (
        txt_unit,
        t_txt_unit,
        jnp.zeros((own_rows, embed_width), jnp.float32),
        jnp.zeros((block_rows, embed_width), jnp.float32),
        pair_start,
    )
    final_state = lax.fori_loop(0, block_count, advance, start_state)
    grad_acc = final_state[2]
    img_acc = final_state[3]
    pair_store = final_state[4]
    img_grad_unit = lax.psum_scatter(
        logit_scale * img_acc, "narrow", scatter_dimension=0, tiled=True
    )
    own_float = lax.dynamic_slice_in_dim(img_float, group_index * own_rows, own_rows, 0)
    own_radius = lax.dynamic_slice_in_dim(img_radius, group_index * own_rows, own_rows, 0)
    image_grad = unit_back(img_grad_unit, own_float, own_radius)
    txt_grad_unit = lax.psum_scatter(
        logit_scale
        * jnp.einsum("rc,rd->cd", pair_store, img_unit, preferred_element_type=jnp.float32),
        "blk",
        scatter_dimension=0,
        tiled=True,
    )
    text_grad = unit_back(txt_grad_unit, txt_float, txt_radius)
    return (image_grad, text_grad)


def solution(mesh):
    in_specs = (
        P(("blk", "narrow"), None),
        P(("blk", "narrow"), None),
        P(("blk", "narrow"), None),
        P(("blk", "narrow"), None),
    )
    out_specs = (P(("blk", "narrow"), None), P(("blk", "narrow"), None))
    return jax.shard_map(body, mesh=mesh, in_specs=in_specs, out_specs=out_specs, check_vma=False)
```

profile of v0, /device:TPU:0, one launch (start us, length us, event | category | flops | bytes accessed | tf_op | source)
XLA Modules:
  0.0 289.0 jit_solution(9864913803693960785)
XLA Ops:
  9.9 1.9 fusion.18
  12.2 28.1 %all-gather.4.cloned.1.call-done = bf16[512,1152]{1,0:T(8,128)(2,1)} async-done(((bf16[128,1152]{1,0:T(8,128)(2,1)}), bf16[512,1152]{1,0:T(8,128)(2,1)}) %all-gather.4.cloned.1.call-update) | async-done | bytes 1179664 | tf_op jit(solution)/shard_map/all_gather | solution.py:34
  40.3 1.6 fusion.14
  41.9 3.4 %convert_divide_fusion.1 = (f32[512,1152]{1,0:T(8,128)}, bf16[512,1152]{1,0:T(8,128)(2,1)}) fusion(bf16[512,1152]{1,0:T(8,128)(2,1)} %all-gather.4.cloned.1.call-done, f32[512]{0:T(512)S(1)} %add_sqrt_fusion.1), kind=kLoop, calls=%fused_computation.20 | loop fusion | flops 1769472 | bytes 4720640 | tf_op jit(solution)/shard_map/div | solution.py:19
  45.3 27.8 %all-gather.6.cloned.1.call-done = bf16[512,1536]{1,0:T(8,128)(2,1)} async-done(((bf16[128,1536]{1,0:T(8,128)(2,1)}), bf16[512,1536]{1,0:T(8,128)(2,1)}) %all-gather.6.cloned.1.call-update) | async-done | bytes 1572880 | tf_op jit(solution)/shard_map/all_gather | solution.py:35
  73.2 1.8 fusion.12
  75.0 38.7 %all-gather.8.cloned.1.call-done = bf16[1024,1536]{1,0:T(8,128)(2,1)} async-done(((bf16[128,1536]{1,0:T(8,128)(2,1)}), bf16[1024,1536]{1,0:T(8,128)(2,1)}) %all-gather.8.cloned.1.call-update) | async-done | bytes 3145744 | tf_op jit(solution)/shard_map/all_gather | solution.py:49
  113.7 5.6 %multiply_add_fusion = f32[512,1024]{1,0:T(8,128)} fusion(bf16[1024,1536]{1,0:T(8,128)(2,1)} %all-gather.8.cloned.1.call-done, bf16[512,1536]{1,0:T(8,128)(2,1)} %all-gather.6.cloned.1.call-done, f32[512]{0:T(512)S(1)} %add_sqrt_fusion), kind=kOutput, calls=%fused_computation.23 | convolution fusion | flops 1614020608 | bytes 6817792 | tf_op jit(solution)/shard_map/rd,cd->rc/dot_general | solution.py:46
  120.4 64.2 %while.20 = (s32[]{:T(128)}, bf16[128,1152]{1,0:T(8,128)(2,1)S(1)}, f32[512,1152]{1,0:T(8,128)S(1)}, bf16[512,1024]{1,0:T(8,128)(2,1)}, bf16[512,1152]{1,0:T(8,1...) while((s32[]{:T(128)}, bf16[128,1152]{1,0:T(8,128)(2,1)S(1)}, ...), condition=%wide.region_5.6_spmd.clone, body=%wide.region_4.5_spmd.clone.sunk | while | flops 304152576 | bytes 8913772 | solution.py:84
  120.7 2.5 constant_dynamic-update-slice_fusion.2
  124.0 4.5 %collective-permute-done = bf16[128,1152]{1,0:T(8,128)(2,1)S(1)} collective-permute-done((bf16[128,1152]{1,0:T(8,128)(2,1)S(1)}, bf16[128,1152]{1,0:T(8,128)(2,1)S(1)}, u32[]{:S(2)}, u32[]{:S(2)}) %collective-permute-start) | collective-permute-done | bytes 294944 | tf_op jit(solution)/shard_map/while/body/eval_jaxpr/ppermute | solution.py:13
  128.6 2.5 constant_dynamic-update-slice_fusion.2
  131.8 4.6 %collective-permute-done = bf16[128,1152]{1,0:T(8,128)(2,1)S(1)} collective-permute-done((bf16[128,1152]{1,0:T(8,128)(2,1)S(1)}, bf16[128,1152]{1,0:T(8,128)(2,1)S(1)}, u32[]{:S(2)}, u32[]{:S(2)}) %collective-permute-start) | collective-permute-done | bytes 294944 | tf_op jit(solution)/shard_map/while/body/eval_jaxpr/ppermute | solution.py:13
  136.6 2.5 constant_dynamic-update-slice_fusion.2
  139.9 4.6 %collective-permute-done = bf16[128,1152]{1,0:T(8,128)(2,1)S(1)} collective-permute-done((bf16[128,1152]{1,0:T(8,128)(2,1)S(1)}, bf16[128,1152]{1,0:T(8,128)(2,1)S(1)}, u32[]{:S(2)}, u32[]{:S(2)}) %collective-permute-start) | collective-permute-done | bytes 294944 | tf_op jit(solution)/shard_map/while/body/eval_jaxpr/ppermute | solution.py:13
  144.6 2.5 constant_dynamic-update-slice_fusion.2
  147.9 4.6 %collective-permute-done = bf16[128,1152]{1,0:T(8,128)(2,1)S(1)} collective-permute-done((bf16[128,1152]{1,0:T(8,128)(2,1)S(1)}, bf16[128,1152]{1,0:T(8,128)(2,1)S(1)}, u32[]{:S(2)}, u32[]{:S(2)}) %collective-permute-start) | collective-permute-done | bytes 294944 | tf_op jit(solution)/shard_map/while/body/eval_jaxpr/ppermute | solution.py:13
  152.6 2.5 constant_dynamic-update-slice_fusion.2
  155.9 4.6 %collective-permute-done = bf16[128,1152]{1,0:T(8,128)(2,1)S(1)} collective-permute-done((bf16[128,1152]{1,0:T(8,128)(2,1)S(1)}, bf16[128,1152]{1,0:T(8,128)(2,1)S(1)}, u32[]{:S(2)}, u32[]{:S(2)}) %collective-permute-start) | collective-permute-done | bytes 294944 | tf_op jit(solution)/shard_map/while/body/eval_jaxpr/ppermute | solution.py:13
  160.7 2.5 constant_dynamic-update-slice_fusion.2
  163.9 4.7 %collective-permute-done = bf16[128,1152]{1,0:T(8,128)(2,1)S(1)} collective-permute-done((bf16[128,1152]{1,0:T(8,128)(2,1)S(1)}, bf16[128,1152]{1,0:T(8,128)(2,1)S(1)}, u32[]{:S(2)}, u32[]{:S(2)}) %collective-permute-start) | collective-permute-done | bytes 294944 | tf_op jit(solution)/shard_map/while/body/eval_jaxpr/ppermute | solution.py:13
  168.7 2.5 constant_dynamic-update-slice_fusion.2
  172.0 4.6 %collective-permute-done = bf16[128,1152]{1,0:T(8,128)(2,1)S(1)} collective-permute-done((bf16[128,1152]{1,0:T(8,128)(2,1)S(1)}, bf16[128,1152]{1,0:T(8,128)(2,1)S(1)}, u32[]{:S(2)}, u32[]{:S(2)}) %collective-permute-start) | collective-permute-done | bytes 294944 | tf_op jit(solution)/shard_map/while/body/eval_jaxpr/ppermute | solution.py:13
  176.7 2.6 constant_dynamic-update-slice_fusion.2
  180.0 4.6 %collective-permute-done = bf16[128,1152]{1,0:T(8,128)(2,1)S(1)} collective-permute-done((bf16[128,1152]{1,0:T(8,128)(2,1)S(1)}, bf16[128,1152]{1,0:T(8,128)(2,1)S(1)}, u32[]{:S(2)}, u32[]{:S(2)}) %collective-permute-start) | collective-permute-done | bytes 294944 | tf_op jit(solution)/shard_map/while/body/eval_jaxpr/ppermute | solution.py:13
  184.6 1.6 broadcast_multiply_fusion
  187.8 3.7 %convolution_multiply_fusion.1 = f32[1024,1152]{1,0:T(8,128)} fusion(bf16[512,1024]{1,0:T(8,128)(2,1)S(1)} %copy-done.3, bf16[512,1152]{1,0:T(8,128)(2,1)S(1)} %copy-done.2), kind=kOutput, calls=%fused_computation.15 | convolution fusion | flops 1209139200 | bytes 6946816 | tf_op jit(solution)/shard_map/rc,rd->cd/dot_general | solution.py:96
  191.6 30.3 %reduce-scatter.3.cloned.1.call-done = f32[128,1152]{1,0:T(8,128)} async-done(((f32[512,1152]{1,0:T(8,128)}), f32[128,1152]{1,0:T(8,128)}) %reduce-scatter.3.cloned.1.call-update) | async-done | bytes 589840 | tf_op jit(solution)/shard_map/reduce_scatter | solution.py:88
  223.2 2.0 subtract_divide_fusion.1
  225.2 53.9 %reduce-scatter.5.cloned.1.call-done = f32[128,1152]{1,0:T(8,128)} async-done(((f32[1024,1152]{1,0:T(8,128)}), f32[128,1152]{1,0:T(8,128)}) %reduce-scatter.5.cloned.1.call-update) | async-done | bytes 589840 | tf_op jit(solution)/shard_map/reduce_scatter | solution.py:94
  279.1 1.3 multiply_reduce_fusion
  280.4 2.1 subtract_divide_fusion
  (54 shorter events, 13.6 us)
Async XLA Ops:
  7.2 4.7 %copy-start.1 = (bf16[128,1152]{1,0:T(8,128)(2,1)S(1)}, bf16[128,1152]{1,0:T(8,128)(2,1)}, u32[]{:S(2)}) copy-start(bf16[128,1152]{1,0:T(8,128)(2,1)} %param.7) | copy-start | bytes 884740
  7.2 33.1 %all-gather.4.cloned.1.call-start = ((), (), s32[]{:S(2)}) async-start(), calls=%async_computation.2 | async-start | bytes 1474560 | tf_op jit(solution)/shard_map/all_gather | solution.py:34
  7.9 65.2 %all-gather.6.cloned.1.call-start = ((), (), s32[]{:S(2)}) async-start(), calls=%async_computation.3 | async-start | bytes 1966080 | tf_op jit(solution)/shard_map/all_gather | solution.py:35
  8.7 105.0 %all-gather.8.cloned.1.call-start = ((), (), s32[]{:S(2)}) async-start(), calls=%async_computation.4 | async-start | bytes 3538944 | tf_op jit(solution)/shard_map/all_gather | solution.py:49
  11.8 210.2 %reduce-scatter.3.cloned.1.call-start = ((), (), s32[]{:S(2)}) async-start(), calls=%async_computation.5 | async-start | bytes 2949120 | tf_op jit(solution)/shard_map/reduce_scatter | solution.py:88
  120.4 8.0 %collective-permute-start = (bf16[128,1152]{1,0:T(8,128)(2,1)S(1)}, bf16[128,1152]{1,0:T(8,128)(2,1)S(1)}, u32[]{:S(2)}, u32[]{:S(2)}) collective-permute-start(bf16[128,1152]{1,0:T(8,128)(2,1)S(1)} %copy.12), channel_id=1, source_target_pairs={{0,4},{4,8},{8,12},{12,16},{16,20},{20,24},{24,28},{28,0},{1,5},{5... | collective-permute-start | bytes 884744 | tf_op jit(solution)/shard_map/while/body/eval_jaxpr/ppermute | solution.py:13
  128.5 8.0 %collective-permute-start = (bf16[128,1152]{1,0:T(8,128)(2,1)S(1)}, bf16[128,1152]{1,0:T(8,128)(2,1)S(1)}, u32[]{:S(2)}, u32[]{:S(2)}) collective-permute-start(bf16[128,1152]{1,0:T(8,128)(2,1)S(1)} %copy.12), channel_id=1, source_target_pairs={{0,4},{4,8},{8,12},{12,16},{16,20},{20,24},{24,28},{28,0},{1,5},{5... | collective-permute-start | bytes 884744 | tf_op jit(solution)/shard_map/while/body/eval_jaxpr/ppermute | solution.py:13
  136.5 8.0 %collective-permute-start = (bf16[128,1152]{1,0:T(8,128)(2,1)S(1)}, bf16[128,1152]{1,0:T(8,128)(2,1)S(1)}, u32[]{:S(2)}, u32[]{:S(2)}) collective-permute-start(bf16[128,1152]{1,0:T(8,128)(2,1)S(1)} %copy.12), channel_id=1, source_target_pairs={{0,4},{4,8},{8,12},{12,16},{16,20},{20,24},{24,28},{28,0},{1,5},{5... | collective-permute-start | bytes 884744 | tf_op jit(solution)/shard_map/while/body/eval_jaxpr/ppermute | solution.py:13
  144.5 8.0 %collective-permute-start = (bf16[128,1152]{1,0:T(8,128)(2,1)S(1)}, bf16[128,1152]{1,0:T(8,128)(2,1)S(1)}, u32[]{:S(2)}, u32[]{:S(2)}) collective-permute-start(bf16[128,1152]{1,0:T(8,128)(2,1)S(1)} %copy.12), channel_id=1, source_target_pairs={{0,4},{4,8},{8,12},{12,16},{16,20},{20,24},{24,28},{28,0},{1,5},{5... | collective-permute-start | bytes 884744 | tf_op jit(solution)/shard_map/while/body/eval_jaxpr/ppermute | solution.py:13
  152.5 8.0 %collective-permute-start = (bf16[128,1152]{1,0:T(8,128)(2,1)S(1)}, bf16[128,1152]{1,0:T(8,128)(2,1)S(1)}, u32[]{:S(2)}, u32[]{:S(2)}) collective-permute-start(bf16[128,1152]{1,0:T(8,128)(2,1)S(1)} %copy.12), channel_id=1, source_target_pairs={{0,4},{4,8},{8,12},{12,16},{16,20},{20,24},{24,28},{28,0},{1,5},{5... | collective-permute-start | bytes 884744 | tf_op jit(solution)/shard_map/while/body/eval_jaxpr/ppermute | solution.py:13
  160.6 8.0 %collective-permute-start = (bf16[128,1152]{1,0:T(8,128)(2,1)S(1)}, bf16[128,1152]{1,0:T(8,128)(2,1)S(1)}, u32[]{:S(2)}, u32[]{:S(2)}) collective-permute-start(bf16[128,1152]{1,0:T(8,128)(2,1)S(1)} %copy.12), channel_id=1, source_target_pairs={{0,4},{4,8},{8,12},{12,16},{16,20},{20,24},{24,28},{28,0},{1,5},{5... | collective-permute-start | bytes 884744 | tf_op jit(solution)/shard_map/while/body/eval_jaxpr/ppermute | solution.py:13
  168.6 8.0 %collective-permute-start = (bf16[128,1152]{1,0:T(8,128)(2,1)S(1)}, bf16[128,1152]{1,0:T(8,128)(2,1)S(1)}, u32[]{:S(2)}, u32[]{:S(2)}) collective-permute-start(bf16[128,1152]{1,0:T(8,128)(2,1)S(1)} %copy.12), channel_id=1, source_target_pairs={{0,4},{4,8},{8,12},{12,16},{16,20},{20,24},{24,28},{28,0},{1,5},{5... | collective-permute-start | bytes 884744 | tf_op jit(solution)/shard_map/while/body/eval_jaxpr/ppermute | solution.py:13
  176.6 8.0 %collective-permute-start = (bf16[128,1152]{1,0:T(8,128)(2,1)S(1)}, bf16[128,1152]{1,0:T(8,128)(2,1)S(1)}, u32[]{:S(2)}, u32[]{:S(2)}) collective-permute-start(bf16[128,1152]{1,0:T(8,128)(2,1)S(1)} %copy.12), channel_id=1, source_target_pairs={{0,4},{4,8},{8,12},{12,16},{16,20},{20,24},{24,28},{28,0},{1,5},{5... | collective-permute-start | bytes 884744 | tf_op jit(solution)/shard_map/while/body/eval_jaxpr/ppermute | solution.py:13
  186.2 1.3 copy-start.2
  186.2 1.6 copy-start.3
  186.3 92.8 %reduce-scatter.5.cloned.1.call-start = ((), (), s32[]{:S(2)}) async-start(), calls=%async_computation.6 | async-start | bytes 5308416 | tf_op jit(solution)/shard_map/reduce_scatter | solution.py:94
  191.5 30.4 %copy-start = (f32[512,1152]{1,0:T(8,128)S(1)}, f32[512,1152]{1,0:T(8,128)}, u32[]{:S(2)}) copy-start(f32[512,1152]{1,0:T(8,128)} %get-tuple-element.252) | copy-start | bytes 7077892
Sparse Core Ops, SparseCore 0:
  9.8 30.4 all-gather.3
  42.1 30.9 all-gather.5
  75.4 38.2 all-gather.7
  186.4 35.5 reduce-scatter.2
  224.1 54.9 reduce-scatter.4
where the time goes:
time: 290 us; the launch traced here: 289 us
  waiting for transfers between devices  217 us (75%)
  matrix products  35.3 us (12%)
  other arithmetic  18.4 us (6%)
  between operations  13.8 us (5%)
    reduce_scatter x1, waiting for transfers between devices, body(): lax.psum_scatter(logit_scale * jnp.einsum('rc,rd->cd', pair_store, img_un...  53.9 us
    all_gather x1, waiting for transfers between devices, body(): lax.all_gather(t_txt_unit, 'blk', axis=0, tiled=True)  38.7 us
    ppermute x8, waiting for transfers between devices, shifted(): return lax.ppermute(x, axis, [(i, (i + by) % count) for i in range(count)])  36.9 us
    reduce_scatter x1, waiting for transfers between devices, body(): lax.psum_scatter(logit_scale * img_acc, 'narrow', scatter_dimension=0, ti...  30.3 us
    all_gather x1, waiting for transfers between devices, body(): lax.all_gather(student_img, 'narrow', axis=0, tiled=True)  28.1 us
    all_gather x1, waiting for transfers between devices, body(): lax.all_gather(teacher_img, 'narrow', axis=0, tiled=True)  27.8 us
    dot_general x8, matrix products, advance(): jnp.einsum('rd,cd->rc', img_unit, text_cur, preferred_element_type=jnp.fl...  20.3 us
  transfers between devices with their start and end apart: 13, of which 13 were waited for; matrix products, arithmetic and copies ran while one was open for 15% of the time, Pallas kernels for 0%

commit v1 on v0

v1 whole, which is shorter than its diff:
```python
import functools
import jax
import jax.numpy as jnp
from jax import lax
from jax.experimental import pallas as pl
from jax.experimental.pallas import tpu as pltpu
from jax.sharding import PartitionSpec as P

epsilon = 1e-06
logit_scale = 100.0
logit_bias = -4.0

AXES = ("blk", "narrow")
ANY = pl.BlockSpec(memory_space=pl.ANY)
VMEM = pl.BlockSpec(memory_space=pltpu.VMEM)
f32 = jnp.float32
bf16 = jnp.bfloat16


def split_two(size):
    fast = int(size**0.5)
    while size % fast:
        fast -= 1
    return max(fast, size // fast), min(fast, size // fast)


class Plan:
    def __init__(self, mesh):
        blk, narrow = mesh.shape["blk"], mesh.shape["narrow"]
        core = 2 if blk % 2 == 0 else 1
        far, near = split_two(blk // core)
        large, small = split_two(narrow)
        self.digits = {"far": far, "near": near, "core": core, "row": small, "col": large}
        self.order = ["far", "near", "core", "row", "col"]

    def __getitem__(self, name):
        return self.digits[name]

    def place(self, index):
        out = {}
        for name in reversed(self.order):
            out[name] = index % self.digits[name]
            index //= self.digits[name]
        return out

    def index(self, place):
        out = 0
        for name in self.order:
            out = out * self.digits[name] + place[name]
        return out

    def send(self, x, name, by):
        total = 1
        for size in self.digits.values():
            total *= size
        pairs = []
        for src in range(total):
            place = self.place(src)
            place[name] = (place[name] + by) % self.digits[name]
            pairs.append((src, self.index(place)))
        return lax.ppermute(x, AXES, pairs)


def params(limit=56):
    return pltpu.CompilerParams(vmem_limit_bytes=limit * 2**20)


def tile_rows(rows, most):
    step = most
    while rows % step:
        step //= 2
    return step


def unit_kernel(count, *refs):
    for x_ref, out_ref in zip(refs[:count], refs[count:]):
        rows = x_ref.shape[0]
        step = tile_rows(rows, 32)

        def one(i, carry, x_ref=x_ref, out_ref=out_ref, step=step):
            at = pl.ds(pl.multiple_of(i * step, step), step)
            x = x_ref[at, :].astype(f32)
            scale = 1.0 / jnp.sqrt(jnp.sum(x * x, axis=1, keepdims=True) + epsilon)
            out_ref[at, :] = (x * scale).astype(bf16)
            return carry

        lax.fori_loop(0, rows // step, one, 0)


def unit_rows(*arrays):
    return pl.pallas_call(
        functools.partial(unit_kernel, len(arrays)),
        out_shape=[jax.ShapeDtypeStruct(a.shape, bf16) for a in arrays],
        in_specs=[VMEM] * len(arrays),
        out_specs=[VMEM] * len(arrays),
        compiler_params=params(16),
        cost_estimate=pl.CostEstimate(
            flops=4 * sum(a.size for a in arrays),
            bytes_accessed=4 * sum(a.size for a in arrays),
            transcendentals=0,
        ),
        name="unit_rows",
    )(*arrays)


def load_all(refs, targets, sems):
    copies = []
    for k, (ref, target) in enumerate(zip(refs, targets)):
        copies.append(pltpu.make_async_copy(ref, target, sems.at[k]))
        copies[-1].start()
    return copies


def teacher_kernel(images, texts, *refs):
    img_refs, txt_refs = refs[:images], refs[images : images + texts]
    p_ref, img, txt, sems = refs[images + texts :]
    rows = img_refs[0].shape[0]
    copies = load_all(
        img_refs + txt_refs,
        [img.at[pl.ds(k * rows, rows), :] for k in range(images)]
        + [txt.at[pl.ds(k * rows, rows), :] for k in range(texts)],
        sems,
    )
    for copy in copies:
        copy.wait()
    step = tile_rows(texts * rows, 256)

    def one(j, carry):
        at = pl.ds(pl.multiple_of(j * step, step), step)
        dots = lax.dot_general(img[...], txt[at, :], (((1,), (1,)), ((), ())), preferred_element_type=f32)
        p_ref[:, at] = jax.nn.sigmoid(logit_scale * dots + logit_bias)
        return carry

    lax.fori_loop(0, texts * rows // step, one, 0)
    own = lax.broadcasted_iota(jnp.int32, (rows, rows), 0) == lax.broadcasted_iota(jnp.int32, (rows, rows), 1)
    p_ref[:rows, :rows] = p_ref[:rows, :rows] + jnp.where(own, 1.0, 0.0).astype(f32)


def teacher_targets(img_blocks, txt_blocks):
    images, texts = len(img_blocks), len(txt_blocks)
    rows, width = img_blocks[0].shape
    return pl.pallas_call(
        functools.partial(teacher_kernel, images, texts),
        out_shape=jax.ShapeDtypeStruct((images * rows, texts * rows), f32),
        in_specs=[ANY] * (images + texts),
        out_specs=VMEM,
        scratch_shapes=[
            pltpu.VMEM((images * rows, width), bf16),
            pltpu.VMEM((texts * rows, width), bf16),
            pltpu.SemaphoreType.DMA((images + texts,)),
        ],
        compiler_params=params(),
        cost_estimate=pl.CostEstimate(
            flops=2 * images * texts * rows * rows * width,
            bytes_accessed=2 * (images + texts) * rows * width + 4 * images * texts * rows * rows,
            transcendentals=images * texts * rows * rows,
        ),
        name="teacher_targets",
    )(*img_blocks, *txt_blocks)


def pair_kernel(images, texts, img_out, txt_out, *refs):
    img_refs, txt_refs = refs[:images], refs[images : images + texts]
    p_ref, pair_ref = refs[images + texts : images + texts + 2]
    rest = refs[images + texts + 2 :]
    img_grads, rest = rest[: len(img_out)], rest[len(img_out) :]
    txt_grads, rest = rest[: len(txt_out)], rest[len(txt_out) :]
    img, txt, sems = rest
    rows = img_refs[0].shape[0]
    copies = load_all(
        img_refs + txt_refs,
        [img.at[pl.ds(k * rows, rows), :] for k in range(images)]
        + [txt.at[pl.ds(k * rows, rows), :] for k in range(texts)],
        sems,
    )
    for copy in copies:
        copy.wait()
    step = tile_rows(texts * rows, 256)

    def one(j, carry):
        at = pl.ds(pl.multiple_of(j * step, step), step)
        dots = lax.dot_general(img[...], txt[at, :], (((1,), (1,)), ((), ())), preferred_element_type=f32)
        pair_ref[:, at] = (2.0 * jax.nn.sigmoid(logit_scale * dots + logit_bias) - p_ref[:, at]).astype(bf16)
        return carry

    lax.fori_loop(0, texts * rows // step, one, 0)
    write_grads(rows, pair_ref, img, txt, img_out, img_grads, txt_out, txt_grads)


def write_grads(rows, pair_ref, img, txt, img_out, img_grads, txt_out, txt_grads):
    for spans, grads, other, axis in ((img_out, img_grads, txt, 1), (txt_out, txt_grads, img, 0)):
        for (first, count), grad in zip(spans, grads):
            size = count * rows
            step = tile_rows(size, 256)
            for k in range(0, size, step):
                at = slice(first * rows + k, first * rows + k + step)
                pair = pair_ref[at, :] if axis == 1 else pair_ref[:, at]
                part = lax.dot_general(pair, other[...], (((axis,), (0,)), ((), ())), preferred_element_type=f32)
                grad[k : k + step, :] = part.astype(grad.dtype)


def grad_shapes(rows, width, spans, dtype):
    return [jax.ShapeDtypeStruct((count * rows, width), dtype) for _, count in spans]


def pair_and_sent(img_blocks, txt_blocks, targets, img_out, txt_out):
    images, texts = len(img_blocks), len(txt_blocks)
    rows, width = img_blocks[0].shape
    shapes = [jax.ShapeDtypeStruct((images * rows, texts * rows), bf16)]
    shapes += grad_shapes(rows, width, img_out, bf16) + grad_shapes(rows, width, txt_out, bf16)
    return pl.pallas_call(
        functools.partial(pair_kernel, images, texts, img_out, txt_out),
        out_shape=shapes,
        in_specs=[ANY] * (images + texts) + [VMEM],
        out_specs=[VMEM] * len(shapes),
        scratch_shapes=[
            pltpu.VMEM((images * rows, width), bf16),
            pltpu.VMEM((texts * rows, width), bf16),
            pltpu.SemaphoreType.DMA((images + texts,)),
        ],
        compiler_params=params(),
        cost_estimate=pl.CostEstimate(
            flops=4 * images * texts * rows * rows * width,
            bytes_accessed=2 * (images + texts) * rows * width + 8 * images * texts * rows * rows,
            transcendentals=images * texts * rows * rows,
        ),
        name="pair_and_sent",
    )(*img_blocks, *txt_blocks, targets)


def kept_kernel(images, texts, img_out, txt_out, *refs):
    img_refs, txt_refs = refs[:images], refs[images : images + texts]
    pair_ref = refs[images + texts]
    rest = refs[images + texts + 1 :]
    img_grads, rest = rest[: len(img_out)], rest[len(img_out) :]
    txt_grads, rest = rest[: len(txt_out)], rest[len(txt_out) :]
    img, txt, sems = rest
    rows = img_refs[0].shape[0]
    copies = load_all(
        img_refs + txt_refs,
        [img.at[pl.ds(k * rows, rows), :] for k in range(images)]
        + [txt.at[pl.ds(k * rows, rows), :] for k in range(texts)],
        sems,
    )
    for copy in copies:
        copy.wait()
    write_grads(rows, pair_ref, img, txt, img_out, img_grads, txt_out, txt_grads)


def kept(img_blocks, txt_blocks, pair, img_out, txt_out):
    images, texts = len(img_blocks), len(txt_blocks)
    rows, width = img_blocks[0].shape
    shapes = grad_shapes(rows, width, img_out, f32) + grad_shapes(rows, width, txt_out, f32)
    return pl.pallas_call(
        functools.partial(kept_kernel, images, texts, img_out, txt_out),
        out_shape=shapes,
        in_specs=[ANY] * (images + texts) + [VMEM],
        out_specs=[VMEM] * len(shapes),
        scratch_shapes=[
            pltpu.VMEM((images * rows, width), bf16),
            pltpu.VMEM((texts * rows, width), bf16),
            pltpu.SemaphoreType.DMA((images + texts,)),
        ],
        compiler_params=params(),
        cost_estimate=pl.CostEstimate(
            flops=2 * images * texts * rows * rows * width,
            bytes_accessed=2 * (images + texts) * rows * width + 8 * images * texts * rows * rows,
            transcendentals=0,
        ),
        name="kept",
    )(*img_blocks, *txt_blocks, pair)


def final_kernel(parts, *refs):
    x_ref, part_refs, out_ref = refs[0], refs[1 : 1 + parts], refs[1 + parts]
    rows = x_ref.shape[0]
    step = tile_rows(rows, 16)

    def one(i, carry):
        at = pl.ds(pl.multiple_of(i * step, step), step)
        x = x_ref[at, :].astype(f32)
        inverse = 1.0 / jnp.sqrt(jnp.sum(x * x, axis=1, keepdims=True) + epsilon)
        unit = x * inverse
        grad = part_refs[0][at, :].astype(f32)
        for part in part_refs[1:]:
            grad = grad + part[at, :].astype(f32)
        grad = logit_scale * grad
        along = jnp.sum(unit * grad, axis=1, keepdims=True)
        out_ref[at, :] = (grad - unit * along) * inverse
        return carry

    lax.fori_loop(0, rows // step, one, 0)


def final(x, parts):
    return pl.pallas_call(
        functools.partial(final_kernel, len(parts)),
        out_shape=jax.ShapeDtypeStruct(x.shape, f32),
        in_specs=[VMEM] * (1 + len(parts)),
        out_specs=VMEM,
        compiler_params=params(16),
        cost_estimate=pl.CostEstimate(flops=10 * x.size, bytes_accessed=12 * x.size, transcendentals=0),
        name="final",
    )(x, *parts)


def gather(plan, block, first, second):
    blocks = {(0, 0): block}
    for a in range(1, plan[first]):
        blocks[0, a] = plan.send(block, first, a)
    for b in range(1, plan[second]):
        for a in range(plan[first]):
            blocks[b, a] = plan.send(blocks[0, a], second, b)
    return blocks


def body(plan, student_img, student_txt, teacher_img, teacher_txt):
    rows, width = student_img.shape
    far, near, core, row, col = (plan[k] for k in plan.order)
    t_img, t_txt = unit_rows(teacher_img, teacher_txt)
    s_img, s_txt = unit_rows(student_img, student_txt)

    def spread(img, txt):
        img_blocks = gather(plan, img, "near", "col")
        txt_blocks = gather(plan, txt, "far", "row")
        imgs = [img_blocks[b, a] for b in range(col) for a in range(near)]
        txts = [txt_blocks[b, a] for b in range(row) for a in range(far)]
        for c in range(1, core):
            txts = txts + [plan.send(txt_blocks[b, a], "core", c) for b in range(row) for a in range(far)]
        return imgs, txts

    t_imgs, t_txts = spread(t_img, t_txt)
    s_imgs, s_txts = spread(s_img, s_txt)
    targets = teacher_targets(t_imgs, t_txts)

    own_img, own_txt = near, row * far
    img_out = tuple((b * near + a, 1) for b in range(1, col) for a in range(near))
    txt_out = tuple((c * own_txt + b * far, far) for c in range(1, core) for b in range(row))
    out = pair_and_sent(s_imgs, s_txts, targets, img_out, txt_out)
    pair = out[0]
    img_sent = {(1 + k // near, k % near): v for k, v in enumerate(out[1 : 1 + len(img_out)])}
    txt_sent = {(1 + k // row, k % row): v for k, v in enumerate(out[1 + len(img_out) :])}

    txt_in = {key: plan.send(v, "core", -key[0]) for key, v in txt_sent.items()}
    img_in = {key: plan.send(v, "col", -key[0]) for key, v in img_sent.items()}

    stay = kept(s_imgs, s_txts, pair, tuple((a, 1) for a in range(near)), tuple((k, 1) for k in range(own_txt)))
    img_part = {a: stay[a] for a in range(near)}
    txt_part = {(b, a): stay[near + b * far + a] for b in range(row) for a in range(far)}

    def img_sum(a):
        total = img_part[a]
        for b in range(1, col):
            total = total + img_in[b, a].astype(f32)
        return total

    img_last = [plan.send(img_sum(a).astype(bf16), "near", -a) for a in range(1, near)]
    image_grad = final(student_img, [img_part[0]] + [img_in[b, 0] for b in range(1, col)] + img_last)

    for c in range(1, core):
        for b in range(row):
            for a in range(far):
                txt_part[b, a] = txt_part[b, a] + txt_in[c, b][a * rows : (a + 1) * rows].astype(f32)
    row_in = {
        (b, a): plan.send(txt_part[b, a].astype(bf16), "row", -b) for b in range(1, row) for a in range(far)
    }

    def txt_sum(a):
        total = txt_part[0, a]
        for b in range(1, row):
            total = total + row_in[b, a].astype(f32)
        return total

    txt_last = [plan.send(txt_sum(a).astype(bf16), "far", -a) for a in range(1, far)]
    text_grad = final(student_txt, [txt_part[0, 0]] + [row_in[b, 0] for b in range(1, row)] + txt_last)
    return image_grad, text_grad


def solution(mesh):
    spec = P(AXES, None)
    return jax.shard_map(
        functools.partial(body, Plan(mesh)), mesh=mesh, in_specs=(spec,) * 4, out_specs=(spec,) * 2, check_vma=False
    )
```

time: 290 us -> 127 us (0.44)
  waiting for transfers between devices: 217 us -> 66.5 us
  matrix products: 35.3 us -> 0 us
  Pallas kernels: 0 us -> 26.9 us
  starting transfers between devices: 0.89 us -> 24.3 us
  other arithmetic: 18.4 us -> 1.65 us
  between operations: 13.8 us -> 1.09 us
  local copies, waits for them, and re-layouts: 2.89 us -> 6.02 us
    all_gather x3 -> x0, waiting for transfers between devices: 94.7 us -> none  [the longest x1 38.7 us: body(): lax.all_gather(t_txt_unit, 'blk', axis=0, tiled=True)]
    reduce_scatter x2 -> x0, waiting for transfers between devices: 84.2 us -> none  [the longest x1 53.9 us: body(): lax.psum_scatter(logit_scale * jnp.einsum('rc,rd->cd', pair_store, img_un...]
    dot_general x18 -> x0, matrix products: 35.3 us -> none  [the longest x8 20.3 us: advance(): jnp.einsum('rd,cd->rc', img_unit, text_cur, preferred_element_type=jnp.fl...]
    ppermute x8 -> x28, waiting for transfers between devices: 36.9 us -> 66.5 us  [send(): return lax.ppermute(x, AXES, pairs)]
    pallas_call x0 -> x7, Pallas kernels: none -> 26.9 us  [the longest x1 8.19 us: pair_and_sent(): pl.pallas_call(functools.partial(pair_kernel, images, texts, img_out, txt...]
    ppermute x8 -> x28, starting transfers between devices: 0.69 us -> 24.3 us  [send(): return lax.ppermute(x, AXES, pairs)]
    div x3 -> x0, other arithmetic: 7.51 us -> none  [the longest x2 4.1 us: unit_back(): return (grad_unit - unit_float * along_unit) / radius]
    reduce_sum x6 -> x0, other arithmetic: 7.16 us -> none  [the longest x4 4.66 us: unit_rows(): jnp.sum(raw_float * raw_float, axis=1, keepdims=True) + epsilon]
  transfers between devices with their start and end apart: 13 -> 28, of which waited for: 13 -> 9; matrix products, arithmetic and copies ran while one was open for 15% -> 1% of each run, Pallas kernels for 0% -> 12%
where the time goes in v1:
time: 127 us; the launch traced here: 126 us
  waiting for transfers between devices  66.5 us (52%)
  Pallas kernels  26.9 us (21%)
  starting transfers between devices  24.3 us (19%)
  local copies, waits for them, and re-layouts  6.02 us (5%)
  other arithmetic  1.65 us (1%)
    ppermute x28, waiting for transfers between devices, send(): return lax.ppermute(x, AXES, pairs)  66.5 us
    ppermute x28, starting transfers between devices, send(): return lax.ppermute(x, AXES, pairs)  24.3 us
    pallas_call x1, Pallas kernels, pair_and_sent(): pl.pallas_call(functools.partial(pair_kernel, images, texts, img_out, txt...  8.19 us
    pallas_call x1, Pallas kernels, teacher_targets(): pl.pallas_call(functools.partial(teacher_kernel, images, texts), out_shap...  6.23 us
    unnamed x68, local copies, waits for them, and re-layouts  6.02 us
    pallas_call x1, Pallas kernels, kept(): pl.pallas_call(functools.partial(kept_kernel, images, texts, img_out, txt...  5.78 us
    pallas_call x2, Pallas kernels, final(): pl.pallas_call(functools.partial(final_kernel, len(parts)), out_shape=jax...  4.8 us
  transfers between devices with their start and end apart: 28, of which 9 were waited for; matrix products, arithmetic and copies ran while one was open for 1% of the time, Pallas kernels for 12%

profile of v1, /device:TPU:0, one launch (start us, length us, event | category | flops | bytes accessed | tf_op | source)
XLA Modules:
  0.0 126.4 jit_solution(7352567852304709741)
XLA Ops:
  0.6 1.0 copy-done.5
  1.6 1.0 copy-done.6
  2.6 1.0 unit_rows.3
  3.6 4.1 %collective-permute-start.13 = (bf16[128,1536]{1,0:T(8,128)(2,1)S(1)}, bf16[128,1536]{1,0:T(8,128)(2,1)S(1)}, u32[]{:S(2)}, u32[]{:S(2)}) collective-permute-start(bf16[128,1536]{1,0:T(8,128)(2,1)S(1)} %get-tuple-element.20.refs_4_), channel_id=1, source_target_pairs={{0,16},{1,17},{2,18},{3,19},{4,20},{5,21},{6,22},{7,23},{8,24},{9,... | collective-permute-start | bytes 1179656 | tf_op jit(solution)/shard_map/ppermute | solution.py:61
  7.7 1.0 copy-done
  8.7 1.0 copy-done.2
  9.6 0.9 unit_rows.2
  10.9 1.6 %collective-permute-start.4 = (bf16[128,1152]{1,0:T(8,128)(2,1)S(1)}, bf16[128,1152]{1,0:T(8,128)(2,1)S(1)}, u32[]{:S(2)}, u32[]{:S(2)}) collective-permute-start(bf16[128,1152]{1,0:T(8,128)(2,1)S(1)} %get-tuple-element.18.refs_4_), channel_id=1, source_target_pairs={{0,2},{1,3},{2,0},{3,1},{4,6},{5,7},{6,4},{7,5},{8,10},{9,11},{10,... | collective-permute-start | bytes 884744 | tf_op jit(solution)/shard_map/ppermute | solution.py:61
  12.5 1.6 %collective-permute-start = (bf16[128,1152]{1,0:T(8,128)(2,1)S(1)}, bf16[128,1152]{1,0:T(8,128)(2,1)S(1)}, u32[]{:S(2)}, u32[]{:S(2)}) collective-permute-start(bf16[128,1152]{1,0:T(8,128)(2,1)S(1)} %get-tuple-element.17.refs_0_), channel_id=1, source_target_pairs={{0,8},{1,9},{2,10},{3,11},{4,12},{5,13},{6,14},{7,15},{8,0},{9,1},... | collective-permute-start | bytes 884744 | tf_op jit(solution)/shard_map/ppermute | solution.py:61
  14.1 23.8 %collective-permute-done.3.refs_5_ = bf16[128,1152]{1,0:T(8,128)(2,1)S(1)} collective-permute-done((bf16[128,1152]{1,0:T(8,128)(2,1)S(1)}, bf16[128,1152]{1,0:T(8,128)(2,1)S(1)}, u32[]{:S(2)}, u32[]{:S(2)}) %collective-permute-start.3) | collective-permute-done | bytes 294944 | tf_op jit(solution)/shard_map/ppermute | solution.py:61
  37.9 1.6 %collective-permute-start.14 = (bf16[128,1536]{1,0:T(8,128)(2,1)S(1)}, bf16[128,1536]{1,0:T(8,128)(2,1)S(1)}, u32[]{:S(2)}, u32[]{:S(2)}) collective-permute-start(bf16[128,1536]{1,0:T(8,128)(2,1)S(1)} %get-tuple-element.20.refs_4_), channel_id=1, source_target_pairs={{0,2},{1,3},{2,0},{3,1},{4,6},{5,7},{6,4},{7,5},{8,10},{9,11},{10,... | collective-permute-start | bytes 1179656 | tf_op jit(solution)/shard_map/ppermute | solution.py:61
  40.8 1.5 %collective-permute-start.11 = (bf16[128,1536]{1,0:T(8,128)(2,1)S(1)}, bf16[128,1536]{1,0:T(8,128)(2,1)S(1)}, u32[]{:S(2)}, u32[]{:S(2)}) collective-permute-start(bf16[128,1536]{1,0:T(8,128)(2,1)S(1)} %get-tuple-element.19.refs_0_), channel_id=1, source_target_pairs={{0,1},{1,0},{2,3},{3,2},{4,5},{5,4},{6,7},{7,6},{8,9},{9,8},{10,11... | collective-permute-start | bytes 1179656 | tf_op jit(solution)/shard_map/ppermute | solution.py:61
  42.3 7.7 %collective-permute-done.14.refs_6_ = bf16[128,1536]{1,0:T(8,128)(2,1)S(1)} collective-permute-done((bf16[128,1536]{1,0:T(8,128)(2,1)S(1)}, bf16[128,1536]{1,0:T(8,128)(2,1)S(1)}, u32[]{:S(2)}, u32[]{:S(2)}) %collective-permute-start.14) | collective-permute-done | bytes 393248 | tf_op jit(solution)/shard_map/ppermute | solution.py:61
  50.5 1.5 %collective-permute-start.12 = (bf16[128,1536]{1,0:T(8,128)(2,1)S(1)}, bf16[128,1536]{1,0:T(8,128)(2,1)S(1)}, u32[]{:S(2)}, u32[]{:S(2)}) collective-permute-start(bf16[128,1536]{1,0:T(8,128)(2,1)S(1)} %collective-permute-done.10.refs_1_), channel_id=1, source_target_pairs={{0,1},{1,0},{2,3},{3,2},{4,5},{5,4},{6,7},{7,6},{8,9},{9,8},{10,11... | collective-permute-start | bytes 1179656 | tf_op jit(solution)/shard_map/ppermute | solution.py:61
  52.0 4.6 %collective-permute-done.15.refs_7_ = bf16[128,1536]{1,0:T(8,128)(2,1)S(1)} collective-permute-done((bf16[128,1536]{1,0:T(8,128)(2,1)S(1)}, bf16[128,1536]{1,0:T(8,128)(2,1)S(1)}, u32[]{:S(2)}, u32[]{:S(2)}) %collective-permute-start.15) | collective-permute-done | bytes 393248 | tf_op jit(solution)/shard_map/ppermute | solution.py:61
  56.7 1.3 %collective-permute-start.5 = (bf16[128,1152]{1,0:T(8,128)(2,1)S(1)}, bf16[128,1152]{1,0:T(8,128)(2,1)S(1)}, u32[]{:S(2)}, u32[]{:S(2)}) collective-permute-start(bf16[128,1152]{1,0:T(8,128)(2,1)S(1)} %collective-permute-done.3.refs_5_), channel_id=1, source_target_pairs={{0,2},{1,3},{2,0},{3,1},{4,6},{5,7},{6,4},{7,5},{8,10},{9,11},{10,... | collective-permute-start | bytes 884744 | tf_op jit(solution)/shard_map/ppermute | solution.py:61
  58.0 8.1 %collective-permute-done.5.refs_7_ = bf16[128,1152]{1,0:T(8,128)(2,1)S(1)} collective-permute-done((bf16[128,1152]{1,0:T(8,128)(2,1)S(1)}, bf16[128,1152]{1,0:T(8,128)(2,1)S(1)}, u32[]{:S(2)}, u32[]{:S(2)}) %collective-permute-start.5) | collective-permute-done | bytes 294944 | tf_op jit(solution)/shard_map/ppermute | solution.py:61
  66.1 1.2 collective-permute-start.1
  67.9 0.8 collective-permute-start.2
  69.4 6.2 %teacher_targets.1.refs_12_ = f32[512,1024]{1,0:T(8,128)} custom-call(bf16[128,1536]{1,0:T(8,128)(2,1)} %copy-done.7, bf16[128,1536]{1,0:T(8,128)(2,1)} %copy-done.16, bf16[128,1536]{1,0:T(8,128)(2,1)} %copy-done.19, bf16[128,1536]{1,0:T(8,128)(2,1)} %copy-done.22, bf16[128,1536]{1,0:T(8,128)(2,1)} %copy-done.8, bf16[128,1536]{1,0:T(8,128)(2,1)} %copy-done.14, ...), custom_call_target="tpu_custom_call" | custom-call | flops 1610612736 | bytes 6815744 | tf_op jit(solution)/shard_map/teacher_targets/pallas_call | solution.py:142
  76.0 5.0 %collective-permute-done.2.refs_3_ = bf16[128,1152]{1,0:T(8,128)(2,1)S(1)} collective-permute-done((bf16[128,1152]{1,0:T(8,128)(2,1)S(1)}, bf16[128,1152]{1,0:T(8,128)(2,1)S(1)}, u32[]{:S(2)}, u32[]{:S(2)}) %collective-permute-start.2) | collective-permute-done | bytes 294944 | tf_op jit(solution)/shard_map/ppermute | solution.py:61
  82.4 8.2 %pair_and_sent.1 = (bf16[512,1024]{1,0:T(8,128)(2,1)}, bf16[128,1152]{1,0:T(8,128)(2,1)}, bf16[128,1152]{1,0:T(8,128)(2,1)}, bf16[256,1152]{1,0:T(8,128)(2,1)}, bf16[256,1152]{1,0:T(8,128)(2,1)}) custom-call(bf16[128,1152]{1,0:T(8,128)(2,1)} %copy-done.9, bf16[128,1152]{1,0:T(8,128)(2,1)} %copy-done.26, bf16[128,1152]{1,0:T(8,128)(2,1)} %copy-done.29, ...), custom_call_target="tpu_custom_call" | custom-call | flops 2415919104 | bytes 7733248 | tf_op jit(solution)/shard_map/pair_and_sent/pallas_call | solution.py:211
  91.2 1.2 collective-permute-start.21
  93.2 5.8 %kept.1 = (f32[128,1152]{1,0:T(8,128)}, f32[128,1152]{1,0:T(8,128)}, f32[128,1152]{1,0:T(8,128)}, f32[128,1152]{1,0:T(8,128)}, f32[128,1152]{1,0:T(8,128)}, /*index=5*/f32[128,1152]{1,0:T(8,128)}) custom-call(bf16[128,1152]{1,0:T(8,128)(2,1)} %copy-done.9, bf16[128,1152]{1,0:T(8,128)(2,1)} %copy-done.26, bf16[128,1152]{1,0:T(8,128)(2,1)} %copy-done.29, ...), custom_call_target="tpu_custom_call" | custom-call | flops 1207959552 | bytes 7733248 | tf_op jit(solution)/shard_map/kept/pallas_call | solution.py:254
  99.0 1.5 %add_convert_fusion.1 = (bf16[128,1152]{1,0:T(8,128)(2,1)S(1)}, bf16[128,1152]{1,0:T(8,128)(2,1)S(1)}) fusion(f32[128,1152]{1,0:T(8,128)} %get-tuple-element.31, bf16[256,1152]{1,0:T(8,128)(2,1)S(1)} %collective-permute-done.24, f32[128,1152]{1,0:T(8,128)} %get-tuple-element.28), kind=kLoop, calls=%fused_computation.1 | loop fusion | flops 884736 | bytes 2359296 | tf_op jit(solution)/shard_map/convert_element_type | solution.py:365
  100.5 1.4 %collective-permute-start.26 = (bf16[128,1152]{1,0:T(8,128)(2,1)S(1)}, bf16[128,1152]{1,0:T(8,128)(2,1)S(1)}, u32[]{:S(2)}, u32[]{:S(2)}) collective-permute-start(bf16[128,1152]{1,0:T(8,128)(2,1)S(1)} %get-tuple-element.34), channel_id=1, source_target_pairs={{0,2},{1,3},{2,0},{3,1},{4,6},{5,7},{6,4},{7,5},{8,10},{9,11},{10,... | collective-permute-start | bytes 884744 | tf_op jit(solution)/shard_map/ppermute | solution.py:61
  101.9 1.8 %collective-permute-start.22 = (bf16[128,1152]{1,0:T(8,128)(2,1)S(1)}, bf16[128,1152]{1,0:T(8,128)(2,1)S(1)}, u32[]{:S(2)}, u32[]{:S(2)}) collective-permute-start(bf16[128,1152]{1,0:T(8,128)(2,1)S(1)} %add_convert_fusion.3), channel_id=1, source_target_pairs={{0,8},{1,9},{2,10},{3,11},{4,12},{5,13},{6,14},{7,15},{8,0},{9,1},... | collective-permute-start | bytes 884744 | tf_op jit(solution)/shard_map/ppermute | solution.py:61
  104.4 6.2 %collective-permute-done.26 = bf16[128,1152]{1,0:T(8,128)(2,1)S(1)} collective-permute-done((bf16[128,1152]{1,0:T(8,128)(2,1)S(1)}, bf16[128,1152]{1,0:T(8,128)(2,1)S(1)}, u32[]{:S(2)}, u32[]{:S(2)}) %collective-permute-start.26) | collective-permute-done | bytes 294944 | tf_op jit(solution)/shard_map/ppermute | solution.py:61
  110.8 2.4 %final.2 = f32[128,1152]{1,0:T(8,128)} custom-call(bf16[128,1152]{1,0:T(8,128)(2,1)S(1)} %copy-done.1, f32[128,1152]{1,0:T(8,128)S(1)} %copy-done.4, bf16[128,1152]{1,0:T(8,128)(2,1)S(1)} %collective-permute-done.20.refs_2_, bf16[128,1152]{1,0:T(8,128)(2,1)S(1)} %collective-permute-done.22.refs_3_), custom_call_target="tpu_custom_call" | custom-call | flops 1474560 | bytes 1769472 | tf_op jit(solution)/shard_map/final/pallas_call | solution.py:296
  113.2 2.1 %collective-permute-done.25.refs_2_ = bf16[128,1152]{1,0:T(8,128)(2,1)S(1)} collective-permute-done((bf16[128,1152]{1,0:T(8,128)(2,1)S(1)}, bf16[128,1152]{1,0:T(8,128)(2,1)S(1)}, u32[]{:S(2)}, u32[]{:S(2)}) %collective-permute-start.25) | collective-permute-done | bytes 294944 | tf_op jit(solution)/shard_map/ppermute | solution.py:61
  115.3 8.6 %collective-permute-done.27.refs_3_ = bf16[128,1152]{1,0:T(8,128)(2,1)S(1)} collective-permute-done((bf16[128,1152]{1,0:T(8,128)(2,1)S(1)}, bf16[128,1152]{1,0:T(8,128)(2,1)S(1)}, u32[]{:S(2)}, u32[]{:S(2)}) %collective-permute-start.27) | collective-permute-done | bytes 294944 | tf_op jit(solution)/shard_map/ppermute | solution.py:61
  124.0 2.4 %final.3 = f32[128,1152]{1,0:T(8,128)} custom-call(bf16[128,1152]{1,0:T(8,128)(2,1)S(1)} %copy-done.3, f32[128,1152]{1,0:T(8,128)S(1)} %get-tuple-element.33.refs_1_, bf16[128,1152]{1,0:T(8,128)(2,1)S(1)} %collective-permute-done.25.refs_2_, bf16[128,1152]{1,0:T(8,128)(2,1)S(1)} %collective-permute-done.27.refs_3_), custom_call_target="tpu_custom_call" | custom-call | flops 1474560 | bytes 1769472 | tf_op jit(solution)/shard_map/final/pallas_call | solution.py:296
  (102 shorter events, 7.3 us)
Async XLA Ops:
  3.6 65.1 %copy-start.7 = (bf16[128,1536]{1,0:T(8,128)(2,1)}, bf16[128,1536]{1,0:T(8,128)(2,1)S(1)}, u32[]{:S(2)}) copy-start(bf16[128,1536]{1,0:T(8,128)(2,1)S(1)} %get-tuple-element.19.refs_0_) | copy-start | bytes 1179652
  3.6 65.1 %copy-start.8 = (bf16[128,1536]{1,0:T(8,128)(2,1)}, bf16[128,1536]{1,0:T(8,128)(2,1)S(1)}, u32[]{:S(2)}) copy-start(bf16[128,1536]{1,0:T(8,128)(2,1)S(1)} %get-tuple-element.20.refs_4_) | copy-start | bytes 1179652
  3.6 36.5 %collective-permute-start.13 = (bf16[128,1536]{1,0:T(8,128)(2,1)S(1)}, bf16[128,1536]{1,0:T(8,128)(2,1)S(1)}, u32[]{:S(2)}, u32[]{:S(2)}) collective-permute-start(bf16[128,1536]{1,0:T(8,128)(2,1)S(1)} %get-tuple-element.20.refs_4_), channel_id=1, source_target_pairs={{0,16},{1,17},{2,18},{3,19},{4,20},{5,21},{6,22},{7,23},{8,24},{9,... | collective-permute-start | bytes 1179656 | tf_op jit(solution)/shard_map/ppermute | solution.py:61
  10.6 65.1 %copy-start.9 = (bf16[128,1152]{1,0:T(8,128)(2,1)}, bf16[128,1152]{1,0:T(8,128)(2,1)S(1)}, u32[]{:S(2)}) copy-start(bf16[128,1152]{1,0:T(8,128)(2,1)S(1)} %get-tuple-element.17.refs_0_) | copy-start | bytes 884740
  10.6 65.1 %copy-start.10 = (bf16[128,1152]{1,0:T(8,128)(2,1)}, bf16[128,1152]{1,0:T(8,128)(2,1)S(1)}, u32[]{:S(2)}) copy-start(bf16[128,1152]{1,0:T(8,128)(2,1)S(1)} %get-tuple-element.18.refs_4_) | copy-start | bytes 884740
  10.6 27.3 %collective-permute-start.3 = (bf16[128,1152]{1,0:T(8,128)(2,1)S(1)}, bf16[128,1152]{1,0:T(8,128)(2,1)S(1)}, u32[]{:S(2)}, u32[]{:S(2)}) collective-permute-start(bf16[128,1152]{1,0:T(8,128)(2,1)S(1)} %get-tuple-element.18.refs_4_), channel_id=1, source_target_pairs={{0,16},{1,17},{2,18},{3,19},{4,20},{5,21},{6,22},{7,23},{8,24},{9,... | collective-permute-start | bytes 884744 | tf_op jit(solution)/shard_map/ppermute | solution.py:61
  10.9 28.6 %collective-permute-start.4 = (bf16[128,1152]{1,0:T(8,128)(2,1)S(1)}, bf16[128,1152]{1,0:T(8,128)(2,1)S(1)}, u32[]{:S(2)}, u32[]{:S(2)}) collective-permute-start(bf16[128,1152]{1,0:T(8,128)(2,1)S(1)} %get-tuple-element.18.refs_4_), channel_id=1, source_target_pairs={{0,2},{1,3},{2,0},{3,1},{4,6},{5,7},{6,4},{7,5},{8,10},{9,11},{10,... | collective-permute-start | bytes 884744 | tf_op jit(solution)/shard_map/ppermute | solution.py:61
  12.5 27.6 %collective-permute-start = (bf16[128,1152]{1,0:T(8,128)(2,1)S(1)}, bf16[128,1152]{1,0:T(8,128)(2,1)S(1)}, u32[]{:S(2)}, u32[]{:S(2)}) collective-permute-start(bf16[128,1152]{1,0:T(8,128)(2,1)S(1)} %get-tuple-element.17.refs_0_), channel_id=1, source_target_pairs={{0,8},{1,9},{2,10},{3,11},{4,12},{5,13},{6,14},{7,15},{8,0},{9,1},... | collective-permute-start | bytes 884744 | tf_op jit(solution)/shard_map/ppermute | solution.py:61
  14.1 26.7 %collective-permute-start.6 = (bf16[128,1152]{1,0:T(8,128)(2,1)S(1)}, bf16[128,1152]{1,0:T(8,128)(2,1)S(1)}, u32[]{:S(2)}, u32[]{:S(2)}) collective-permute-start(bf16[128,1152]{1,0:T(8,128)(2,1)S(1)} %get-tuple-element.18.refs_4_), channel_id=1, source_target_pairs={{0,4},{1,5},{2,6},{3,7},{4,0},{5,1},{6,2},{7,3},{8,12},{9,13},{10,... | collective-permute-start | bytes 884744 | tf_op jit(solution)/shard_map/ppermute | solution.py:61
  37.9 12.1 %collective-permute-start.14 = (bf16[128,1536]{1,0:T(8,128)(2,1)S(1)}, bf16[128,1536]{1,0:T(8,128)(2,1)S(1)}, u32[]{:S(2)}, u32[]{:S(2)}) collective-permute-start(bf16[128,1536]{1,0:T(8,128)(2,1)S(1)} %get-tuple-element.20.refs_4_), channel_id=1, source_target_pairs={{0,2},{1,3},{2,0},{3,1},{4,6},{5,7},{6,4},{7,5},{8,10},{9,11},{10,... | collective-permute-start | bytes 1179656 | tf_op jit(solution)/shard_map/ppermute | solution.py:61
  39.5 10.5 %collective-permute-start.10 = (bf16[128,1536]{1,0:T(8,128)(2,1)S(1)}, bf16[128,1536]{1,0:T(8,128)(2,1)S(1)}, u32[]{:S(2)}, u32[]{:S(2)}) collective-permute-start(bf16[128,1536]{1,0:T(8,128)(2,1)S(1)} %get-tuple-element.19.refs_0_), channel_id=1, source_target_pairs={{0,8},{1,9},{2,10},{3,11},{4,12},{5,13},{6,14},{7,15},{8,0},{9,1},... | collective-permute-start | bytes 1179656 | tf_op jit(solution)/shard_map/ppermute | solution.py:61
  40.2 10.3 %collective-permute-start.16 = (bf16[128,1536]{1,0:T(8,128)(2,1)S(1)}, bf16[128,1536]{1,0:T(8,128)(2,1)S(1)}, u32[]{:S(2)}, u32[]{:S(2)}) collective-permute-start(bf16[128,1536]{1,0:T(8,128)(2,1)S(1)} %get-tuple-element.20.refs_4_), channel_id=1, source_target_pairs={{0,4},{1,5},{2,6},{3,7},{4,0},{5,1},{6,2},{7,3},{8,12},{9,13},{10,... | collective-permute-start | bytes 1179656 | tf_op jit(solution)/shard_map/ppermute | solution.py:61
  40.2 16.4 %collective-permute-start.15 = (bf16[128,1536]{1,0:T(8,128)(2,1)S(1)}, bf16[128,1536]{1,0:T(8,128)(2,1)S(1)}, u32[]{:S(2)}, u32[]{:S(2)}) collective-permute-start(bf16[128,1536]{1,0:T(8,128)(2,1)S(1)} %collective-permute-done.13.refs_5_), channel_id=1, source_target_pairs={{0,2},{1,3},{2,0},{3,1},{4,6},{5,7},{6,4},{7,5},{8,10},{9,11},{10,... | collective-permute-start | bytes 1179656 | tf_op jit(solution)/shard_map/ppermute | solution.py:61
  40.8 15.9 %collective-permute-start.11 = (bf16[128,1536]{1,0:T(8,128)(2,1)S(1)}, bf16[128,1536]{1,0:T(8,128)(2,1)S(1)}, u32[]{:S(2)}, u32[]{:S(2)}) collective-permute-start(bf16[128,1536]{1,0:T(8,128)(2,1)S(1)} %get-tuple-element.19.refs_0_), channel_id=1, source_target_pairs={{0,1},{1,0},{2,3},{3,2},{4,5},{5,4},{6,7},{7,6},{8,9},{9,8},{10,11... | collective-permute-start | bytes 1179656 | tf_op jit(solution)/shard_map/ppermute | solution.py:61
  50.0 17.4 %collective-permute-start.17 = (bf16[128,1536]{1,0:T(8,128)(2,1)S(1)}, bf16[128,1536]{1,0:T(8,128)(2,1)S(1)}, u32[]{:S(2)}, u32[]{:S(2)}) collective-permute-start(bf16[128,1536]{1,0:T(8,128)(2,1)S(1)} %collective-permute-done.13.refs_5_), channel_id=1, source_target_pairs={{0,4},{1,5},{2,6},{3,7},{4,0},{5,1},{6,2},{7,3},{8,12},{9,13},{10,... | collective-permute-start | bytes 1179656 | tf_op jit(solution)/shard_map/ppermute | solution.py:61
  50.0 17.4 %collective-permute-start.18 = (bf16[128,1536]{1,0:T(8,128)(2,1)S(1)}, bf16[128,1536]{1,0:T(8,128)(2,1)S(1)}, u32[]{:S(2)}, u32[]{:S(2)}) collective-permute-start(bf16[128,1536]{1,0:T(8,128)(2,1)S(1)} %collective-permute-done.14.refs_6_), channel_id=1, source_target_pairs={{0,4},{1,5},{2,6},{3,7},{4,0},{5,1},{6,2},{7,3},{8,12},{9,13},{10,... | collective-permute-start | bytes 1179656 | tf_op jit(solution)/shard_map/ppermute | solution.py:61
  50.5 17.4 %collective-permute-start.12 = (bf16[128,1536]{1,0:T(8,128)(2,1)S(1)}, bf16[128,1536]{1,0:T(8,128)(2,1)S(1)}, u32[]{:S(2)}, u32[]{:S(2)}) collective-permute-start(bf16[128,1536]{1,0:T(8,128)(2,1)S(1)} %collective-permute-done.10.refs_1_), channel_id=1, source_target_pairs={{0,1},{1,0},{2,3},{3,2},{4,5},{5,4},{6,7},{7,6},{8,9},{9,8},{10,11... | collective-permute-start | bytes 1179656 | tf_op jit(solution)/shard_map/ppermute | solution.py:61
  56.6 12.0 %collective-permute-start.19 = (bf16[128,1536]{1,0:T(8,128)(2,1)S(1)}, bf16[128,1536]{1,0:T(8,128)(2,1)S(1)}, u32[]{:S(2)}, u32[]{:S(2)}) collective-permute-start(bf16[128,1536]{1,0:T(8,128)(2,1)S(1)} %collective-permute-done.15.refs_7_), channel_id=1, source_target_pairs={{0,4},{1,5},{2,6},{3,7},{4,0},{5,1},{6,2},{7,3},{8,12},{9,13},{10,... | collective-permute-start | bytes 1179656 | tf_op jit(solution)/shard_map/ppermute | solution.py:61
  56.7 9.4 %collective-permute-start.5 = (bf16[128,1152]{1,0:T(8,128)(2,1)S(1)}, bf16[128,1152]{1,0:T(8,128)(2,1)S(1)}, u32[]{:S(2)}, u32[]{:S(2)}) collective-permute-start(bf16[128,1152]{1,0:T(8,128)(2,1)S(1)} %collective-permute-done.3.refs_5_), channel_id=1, source_target_pairs={{0,2},{1,3},{2,0},{3,1},{4,6},{5,7},{6,4},{7,5},{8,10},{9,11},{10,... | collective-permute-start | bytes 884744 | tf_op jit(solution)/shard_map/ppermute | solution.py:61
  66.1 9.9 %collective-permute-start.1 = (bf16[128,1152]{1,0:T(8,128)(2,1)S(1)}, bf16[128,1152]{1,0:T(8,128)(2,1)S(1)}, u32[]{:S(2)}, u32[]{:S(2)}) collective-permute-start(bf16[128,1152]{1,0:T(8,128)(2,1)S(1)} %get-tuple-element.17.refs_0_), channel_id=1, source_target_pairs={{0,1},{1,0},{2,3},{3,2},{4,5},{5,4},{6,7},{7,6},{8,9},{9,8},{10,11... | collective-permute-start | bytes 884744 | tf_op jit(solution)/shard_map/ppermute | solution.py:61
  67.3 8.7 %collective-permute-start.7 = (bf16[128,1152]{1,0:T(8,128)(2,1)S(1)}, bf16[128,1152]{1,0:T(8,128)(2,1)S(1)}, u32[]{:S(2)}, u32[]{:S(2)}) collective-permute-start(bf16[128,1152]{1,0:T(8,128)(2,1)S(1)} %collective-permute-done.3.refs_5_), channel_id=1, source_target_pairs={{0,4},{1,5},{2,6},{3,7},{4,0},{5,1},{6,2},{7,3},{8,12},{9,13},{10,... | collective-permute-start | bytes 884744 | tf_op jit(solution)/shard_map/ppermute | solution.py:61
  67.4 8.7 %collective-permute-start.8 = (bf16[128,1152]{1,0:T(8,128)(2,1)S(1)}, bf16[128,1152]{1,0:T(8,128)(2,1)S(1)}, u32[]{:S(2)}, u32[]{:S(2)}) collective-permute-start(bf16[128,1152]{1,0:T(8,128)(2,1)S(1)} %collective-permute-done.4.refs_6_), channel_id=1, source_target_pairs={{0,4},{1,5},{2,6},{3,7},{4,0},{5,1},{6,2},{7,3},{8,12},{9,13},{10,... | collective-permute-start | bytes 884744 | tf_op jit(solution)/shard_map/ppermute | solution.py:61
  67.9 13.1 %collective-permute-start.2 = (bf16[128,1152]{1,0:T(8,128)(2,1)S(1)}, bf16[128,1152]{1,0:T(8,128)(2,1)S(1)}, u32[]{:S(2)}, u32[]{:S(2)}) collective-permute-start(bf16[128,1152]{1,0:T(8,128)(2,1)S(1)} %collective-permute-done.refs_1_), channel_id=1, source_target_pairs={{0,1},{1,0},{2,3},{3,2},{4,5},{5,4},{6,7},{7,6},{8,9},{9,8},{10,11... | collective-permute-start | bytes 884744 | tf_op jit(solution)/shard_map/ppermute | solution.py:61
  68.6 12.3 %collective-permute-start.9 = (bf16[128,1152]{1,0:T(8,128)(2,1)S(1)}, bf16[128,1152]{1,0:T(8,128)(2,1)S(1)}, u32[]{:S(2)}, u32[]{:S(2)}) collective-permute-start(bf16[128,1152]{1,0:T(8,128)(2,1)S(1)} %collective-permute-done.5.refs_7_), channel_id=1, source_target_pairs={{0,4},{1,5},{2,6},{3,7},{4,0},{5,1},{6,2},{7,3},{8,12},{9,13},{10,... | collective-permute-start | bytes 884744 | tf_op jit(solution)/shard_map/ppermute | solution.py:61
  90.6 8.4 %collective-permute-start.24 = (bf16[256,1152]{1,0:T(8,128)(2,1)}, bf16[256,1152]{1,0:T(8,128)(2,1)S(1)}, u32[]{:S(2)}, u32[]{:S(2)}) collective-permute-start(bf16[256,1152]{1,0:T(8,128)(2,1)} %get-tuple-element.29), channel_id=1, source_target_pairs={{0,4},{1,5},{2,6},{3,7},{4,0},{5,1},{6,2},{7,3},{8,12},{9,13},{10,... | collective-permute-start | bytes 1769480 | tf_op jit(solution)/shard_map/ppermute | solution.py:61
  90.7 13.7 %collective-permute-start.23 = (bf16[256,1152]{1,0:T(8,128)(2,1)}, bf16[256,1152]{1,0:T(8,128)(2,1)S(1)}, u32[]{:S(2)}, u32[]{:S(2)}) collective-permute-start(bf16[256,1152]{1,0:T(8,128)(2,1)} %get-tuple-element.27), channel_id=1, source_target_pairs={{0,4},{1,5},{2,6},{3,7},{4,0},{5,1},{6,2},{7,3},{8,12},{9,13},{10,... | collective-permute-start | bytes 1769480 | tf_op jit(solution)/shard_map/ppermute | solution.py:61
  91.2 10.7 %collective-permute-start.21 = (bf16[128,1152]{1,0:T(8,128)(2,1)}, bf16[128,1152]{1,0:T(8,128)(2,1)S(1)}, u32[]{:S(2)}, u32[]{:S(2)}) collective-permute-start(bf16[128,1152]{1,0:T(8,128)(2,1)} %get-tuple-element.25), channel_id=1, source_target_pairs={{0,1},{1,0},{2,3},{3,2},{4,5},{5,4},{6,7},{7,6},{8,9},{9,8},{10,11... | collective-permute-start | bytes 884744 | tf_op jit(solution)/shard_map/ppermute | solution.py:61
  92.4 18.3 %collective-permute-start.20 = (bf16[128,1152]{1,0:T(8,128)(2,1)}, bf16[128,1152]{1,0:T(8,128)(2,1)S(1)}, u32[]{:S(2)}, u32[]{:S(2)}) collective-permute-start(bf16[128,1152]{1,0:T(8,128)(2,1)} %get-tuple-element.23), channel_id=1, source_target_pairs={{0,1},{1,0},{2,3},{3,2},{4,5},{5,4},{6,7},{7,6},{8,9},{9,8},{10,11... | collective-permute-start | bytes 884744 | tf_op jit(solution)/shard_map/ppermute | solution.py:61
  100.5 10.0 %collective-permute-start.26 = (bf16[128,1152]{1,0:T(8,128)(2,1)S(1)}, bf16[128,1152]{1,0:T(8,128)(2,1)S(1)}, u32[]{:S(2)}, u32[]{:S(2)}) collective-permute-start(bf16[128,1152]{1,0:T(8,128)(2,1)S(1)} %get-tuple-element.34), channel_id=1, source_target_pairs={{0,2},{1,3},{2,0},{3,1},{4,6},{5,7},{6,4},{7,5},{8,10},{9,11},{10,... | collective-permute-start | bytes 884744 | tf_op jit(solution)/shard_map/ppermute | solution.py:61
  101.9 8.8 %collective-permute-start.22 = (bf16[128,1152]{1,0:T(8,128)(2,1)S(1)}, bf16[128,1152]{1,0:T(8,128)(2,1)S(1)}, u32[]{:S(2)}, u32[]{:S(2)}) collective-permute-start(bf16[128,1152]{1,0:T(8,128)(2,1)S(1)} %add_convert_fusion.3), channel_id=1, source_target_pairs={{0,8},{1,9},{2,10},{3,11},{4,12},{5,13},{6,14},{7,15},{8,0},{9,1},... | collective-permute-start | bytes 884744 | tf_op jit(solution)/shard_map/ppermute | solution.py:61
  103.7 11.6 %collective-permute-start.25 = (bf16[128,1152]{1,0:T(8,128)(2,1)S(1)}, bf16[128,1152]{1,0:T(8,128)(2,1)S(1)}, u32[]{:S(2)}, u32[]{:S(2)}) collective-permute-start(bf16[128,1152]{1,0:T(8,128)(2,1)S(1)} %get-tuple-element.35), channel_id=1, source_target_pairs={{0,2},{1,3},{2,0},{3,1},{4,6},{5,7},{6,4},{7,5},{8,10},{9,11},{10,... | collective-permute-start | bytes 884744 | tf_op jit(solution)/shard_map/ppermute | solution.py:61
  110.7 13.3 %collective-permute-start.27 = (bf16[128,1152]{1,0:T(8,128)(2,1)S(1)}, bf16[128,1152]{1,0:T(8,128)(2,1)S(1)}, u32[]{:S(2)}, u32[]{:S(2)}) collective-permute-start(bf16[128,1152]{1,0:T(8,128)(2,1)S(1)} %get-tuple-element.32), channel_id=1, source_target_pairs={{0,16},{1,17},{2,18},{3,19},{4,20},{5,21},{6,22},{7,23},{8,24},{9,... | collective-permute-start | bytes 884744 | tf_op jit(solution)/shard_map/ppermute | solution.py:61
  (30 other events, 373.8 us)

commit v2 on v1

v2 whole, which is shorter than its diff:
```python
import functools
import math
import jax
import jax.numpy as jnp
from jax import lax
from jax.experimental import pallas as pl
from jax.experimental.pallas import tpu as pltpu
from jax.sharding import PartitionSpec as P

epsilon = 1e-06
logit_scale = 100.0
logit_bias = -4.0

AXES = ("blk", "narrow")
ANY = pl.BlockSpec(memory_space=pl.ANY)
VMEM = pl.BlockSpec(memory_space=pltpu.VMEM)
f32 = jnp.float32
bf16 = jnp.bfloat16


def split_two(size):
    fast = int(size**0.5)
    while size % fast:
        fast -= 1
    return max(fast, size // fast), min(fast, size // fast)


class Plan:
    def __init__(self, mesh):
        blk, narrow = mesh.shape["blk"], mesh.shape["narrow"]
        core = 2 if blk % 2 == 0 else 1
        far, near = split_two(blk // core)
        large, small = split_two(narrow)
        self.digits = {"far": far, "near": near, "core": core, "row": small, "col": large}
        self.order = ["far", "near", "core", "row", "col"]

    def __getitem__(self, name):
        return self.digits[name]

    def place(self, index):
        out = {}
        for name in reversed(self.order):
            out[name] = index % self.digits[name]
            index //= self.digits[name]
        return out

    def index(self, place):
        out = 0
        for name in self.order:
            out = out * self.digits[name] + place[name]
        return out

    def send(self, x, name, by):
        total = 1
        for size in self.digits.values():
            total *= size
        pairs = []
        for src in range(total):
            place = self.place(src)
            place[name] = (place[name] + by) % self.digits[name]
            pairs.append((src, self.index(place)))
        return lax.ppermute(x, AXES, pairs)


def params(*held):
    total = sum(math.prod(shape) * size for shape, size in held)
    return pltpu.CompilerParams(vmem_limit_bytes=int(total) + 8 * 2**20)


def tile_rows(rows, most):
    step = most
    while rows % step:
        step //= 2
    return step


def load_all(refs, targets, sems, columns=None):
    copies = []
    for k, (ref, target) in enumerate(zip(refs, targets)):
        if columns is not None and ref.shape[1] != target.shape[1]:
            ref = ref.at[:, pl.ds(columns, target.shape[1])]
        copies.append(pltpu.make_async_copy(ref, target, sems.at[k]))
        copies[-1].start()
    return copies


def unit_kernel(count, *refs):
    x_refs, out_refs, both_refs = refs[:count], refs[count : 2 * count], refs[2 * count : 2 * count + count // 2]
    held, sems = refs[2 * count + count // 2 : -1], refs[-1]
    copies = load_all(x_refs, held, sems)
    for k, (copy, x_ref, out_ref) in enumerate(zip(copies, held, out_refs)):
        copy.wait()
        x = x_ref[...].astype(f32)
        scale = 1.0 / jnp.sqrt(jnp.sum(x * x, axis=1, keepdims=True) + epsilon)
        unit = (x * scale).astype(bf16)
        out_ref[...] = unit
        both, width = both_refs[k % (count // 2)], x.shape[1]
        if k < count // 2:
            both[:, :width] = unit
        else:
            both[:, both.shape[1] - width :] = unit


def unit_rows(*arrays):
    half = len(arrays) // 2
    both = [(a.shape[0], a.shape[1] + b.shape[1]) for a, b in zip(arrays[:half], arrays[half:])]
    return pl.pallas_call(
        functools.partial(unit_kernel, len(arrays)),
        out_shape=[jax.ShapeDtypeStruct(a.shape, bf16) for a in arrays]
        + [jax.ShapeDtypeStruct(shape, bf16) for shape in both],
        in_specs=[ANY] * len(arrays),
        out_specs=[VMEM] * (len(arrays) + half),
        scratch_shapes=[pltpu.VMEM(a.shape, bf16) for a in arrays]
        + [pltpu.SemaphoreType.DMA((len(arrays),))],
        compiler_params=params(*[(a.shape, 10) for a in arrays]),
        cost_estimate=pl.CostEstimate(
            flops=4 * sum(a.size for a in arrays),
            bytes_accessed=6 * sum(a.size for a in arrays),
            transcendentals=0,
        ),
        name="unit_rows",
    )(*arrays)


def teacher_kernel(images, texts, *refs):
    img_refs, txt_refs = refs[:images], refs[images : images + texts]
    p_ref, img, txt, sems = refs[images + texts :]
    rows = img_refs[0].shape[0]
    copies = load_all(
        img_refs + txt_refs,
        [img.at[pl.ds(k * rows, rows), :] for k in range(images)]
        + [txt.at[pl.ds(k * rows, rows), :] for k in range(texts)],
        sems,
        0,
    )
    for copy in copies:
        copy.wait()
    step = tile_rows(texts * rows, 256)

    def one(j, carry):
        at = pl.ds(pl.multiple_of(j * step, step), step)
        dots = lax.dot_general(img[...], txt[at, :], (((1,), (1,)), ((), ())), preferred_element_type=f32)
        p_ref[:, at] = jax.nn.sigmoid(logit_scale * dots + logit_bias)
        return carry

    lax.fori_loop(0, texts * rows // step, one, 0)
    own = lax.broadcasted_iota(jnp.int32, (rows, rows), 0) == lax.broadcasted_iota(jnp.int32, (rows, rows), 1)
    p_ref[:rows, :rows] = p_ref[:rows, :rows] + jnp.where(own, 1.0, 0.0).astype(f32)


def teacher_targets(img_blocks, txt_blocks):
    images, texts = len(img_blocks), len(txt_blocks)
    rows, width = img_blocks[0].shape
    return pl.pallas_call(
        functools.partial(teacher_kernel, images, texts),
        out_shape=jax.ShapeDtypeStruct((images * rows, texts * rows), f32),
        in_specs=[ANY] * (images + texts),
        out_specs=VMEM,
        scratch_shapes=[
            pltpu.VMEM((images * rows, width), bf16),
            pltpu.VMEM((texts * rows, width), bf16),
            pltpu.SemaphoreType.DMA((images + texts,)),
        ],
        compiler_params=params(((images + texts, rows, width), 2), ((images, rows, texts, rows), 4)),
        cost_estimate=pl.CostEstimate(
            flops=2 * images * texts * rows * rows * width,
            bytes_accessed=2 * (images + texts) * rows * width + 4 * images * texts * rows * rows,
            transcendentals=images * texts * rows * rows,
        ),
        name="teacher_targets",
    )(*img_blocks, *txt_blocks)


def write_grads(rows, pair, other, axis, first, grads):
    size = sum(g.shape[0] for g in grads)
    at = slice(first * rows, first * rows + size)
    part = pair[at, :] if axis == 1 else pair[:, at]
    part = lax.dot_general(part, other[...], (((axis,), (0,)), ((), ())), preferred_element_type=f32)
    done = 0
    for grad in grads:
        grad[...] = part[done : done + grad.shape[0], :].astype(grad.dtype)
        done += grad.shape[0]


def pair_kernel(images, texts, skip, img_first, txt_first, img_count, *refs):
    img_refs, txt_refs = refs[:images], refs[images : images + texts]
    p_ref, pair_ref, img, txt = refs[images + texts : images + texts + 4]
    grads, sems = refs[images + texts + 4 : -1], refs[-1]
    rows = img_refs[0].shape[0]
    copies = load_all(
        img_refs + txt_refs,
        [img.at[pl.ds(k * rows, rows), :] for k in range(images)]
        + [txt.at[pl.ds(k * rows, rows), :] for k in range(texts)],
        sems,
        skip,
    )
    for copy in copies[:images]:
        copy.wait()
    step = tile_rows(texts * rows, 256)
    for j in range(texts * rows // step):
        for copy in copies[images + j * step // rows : images + (j + 1) * step // rows]:
            copy.wait()
        at = slice(j * step, (j + 1) * step)
        dots = lax.dot_general(img[...], txt[at, :], (((1,), (1,)), ((), ())), preferred_element_type=f32)
        pair_ref[:, at] = (2.0 * jax.nn.sigmoid(logit_scale * dots + logit_bias) - p_ref[:, at]).astype(bf16)
    if img_count:
        write_grads(rows, pair_ref, txt, 1, img_first, grads[:img_count])
    if len(grads) > img_count:
        write_grads(rows, pair_ref, img, 0, txt_first, grads[img_count:])


def pair_and_sent(img_blocks, txt_blocks, skip, targets, img_first, img_out, txt_first, txt_out):
    images, texts = len(img_blocks), len(txt_blocks)
    rows, width = img_blocks[0].shape
    shapes = [jax.ShapeDtypeStruct((images * rows, texts * rows), bf16)]
    shapes += [jax.ShapeDtypeStruct((n * rows, width), bf16) for n in (images, texts) + img_out + txt_out]
    return pl.pallas_call(
        functools.partial(pair_kernel, images, texts, skip, img_first, txt_first, len(img_out)),
        out_shape=shapes,
        in_specs=[ANY] * (images + texts) + [VMEM],
        out_specs=[VMEM] * len(shapes),
        scratch_shapes=[pltpu.SemaphoreType.DMA((images + texts,))],
        compiler_params=params(
            ((images * rows, texts * rows), 6),
            ((images + texts, rows, width), 2),
            ((sum(img_out) + sum(txt_out), rows, width), 6),
        ),
        cost_estimate=pl.CostEstimate(
            flops=4 * images * texts * rows * rows * width,
            bytes_accessed=2 * (images + texts) * rows * width + 8 * images * texts * rows * rows,
            transcendentals=images * texts * rows * rows,
        ),
        name="pair_and_sent",
    )(*img_blocks, *txt_blocks, targets)


def grads_kernel(rows, img_first, img_count, txt_first, pair_ref, img, txt, *grads):
    if len(grads) > img_count:
        write_grads(rows, pair_ref, img, 0, txt_first, grads[img_count:])
    if img_count:
        write_grads(rows, pair_ref, txt, 1, img_first, grads[:img_count])


def some_grads(pair, img, txt, rows, img_first, img_out, txt_first, txt_out, dtype, name):
    width = img.shape[1]
    shapes = [jax.ShapeDtypeStruct((n * rows, width), dtype) for n in img_out + txt_out]
    out = pl.pallas_call(
        functools.partial(grads_kernel, rows, img_first, len(img_out), txt_first),
        out_shape=shapes,
        in_specs=[VMEM] * 3,
        out_specs=[VMEM] * len(shapes),
        compiler_params=params(
            (pair.shape, 2), (img.shape, 2), (txt.shape, 2), ((sum(img_out) + sum(txt_out), rows, width), 8)
        ),
        cost_estimate=pl.CostEstimate(
            flops=2 * pair.size * width,
            bytes_accessed=2 * (pair.size + img.size + txt.size) + 4 * len(shapes) * rows * width,
            transcendentals=0,
        ),
        name=name,
    )(pair, img, txt)
    return out[: len(img_out)], out[len(img_out) :]


def final_kernel(parts, *refs):
    x_ref, part_refs, out_ref = refs[0], refs[1 : 1 + parts], refs[1 + parts]
    x = x_ref[...].astype(f32)
    inverse = 1.0 / jnp.sqrt(jnp.sum(x * x, axis=1, keepdims=True) + epsilon)
    unit = x * inverse
    grad = part_refs[0][...].astype(f32)
    for part in part_refs[1:]:
        grad = grad + part[...].astype(f32)
    grad = logit_scale * grad
    along = jnp.sum(unit * grad, axis=1, keepdims=True)
    out_ref[...] = (grad - unit * along) * inverse


def final(x, parts):
    return pl.pallas_call(
        functools.partial(final_kernel, len(parts)),
        out_shape=jax.ShapeDtypeStruct(x.shape, f32),
        in_specs=[VMEM] * (1 + len(parts)),
        out_specs=VMEM,
        compiler_params=params((x.shape, 4 * (4 + len(parts)))),
        cost_estimate=pl.CostEstimate(flops=10 * x.size, bytes_accessed=12 * x.size, transcendentals=0),
        name="final",
    )(x, *parts)


def after(x, *others):
    others = [v for other in others for v in (other.values() if isinstance(other, dict) else [other])]
    return lax.optimization_barrier((x, *others))[0] if others else x


def body(plan, student_img, student_txt, teacher_img, teacher_txt):
    rows, width = student_img.shape
    far, near, core, row, col = (plan[k] for k in plan.order)

    def spread(x, name, *before):
        return {a: plan.send(after(x, *before), name, a) for a in range(1, plan[name])}

    def onward(blocks, name, *before):
        return {
            (b, a): plan.send(after(x, *before), name, b) for b in range(1, plan[name]) for a, x in blocks.items()
        }

    t_img, t_txt, s_img, s_txt, b_img, b_txt = unit_rows(teacher_img, teacher_txt, student_img, student_txt)
    t_far = spread(t_img, "far")
    t_near = spread(t_txt, "near")
    b_col = spread(b_img, "col")
    b_row = spread(b_txt, "row")
    b_core = spread(b_txt, "core")
    first = [t_far, t_near, b_col, b_row, b_core]
    s_far = spread(s_img, "far", *first)
    s_near = spread(s_txt, "near", *first)
    t_far_col = onward(t_far, "col", *first)
    t_near_row = onward(t_near, "row", *first)
    b_row_core = onward(b_row, "core", *first)
    second = [s_far, s_near, t_far_col, t_near_row, b_row_core]
    s_far_col = onward(s_far, "col", *second)
    s_near_row = onward(s_near, "row", *second)
    s_near_core = onward(s_near, "core", *second)
    t_near_core = onward(t_near, "core", *second)
    t_both_core = onward(t_near_row, "core", t_near_core)
    s_both_core = onward(s_near_row, "core", s_near_core)

    def images(own, by_far, by_col, by_both):
        blocks = {(0, 0): own, **by_both}
        blocks.update({(0, a): x for a, x in by_far.items()})
        blocks.update({(b, 0): x for b, x in by_col.items()})
        return [blocks[b, a] for b in range(col) for a in range(far)]

    def texts(own, by_near, by_row, by_both, by_core, by_core_near, by_core_row, by_core_both):
        blocks = {(0, 0, 0): own}
        blocks.update({(0, 0, a): x for a, x in by_near.items()})
        blocks.update({(0, b, 0): x for b, x in by_row.items()})
        blocks.update({(0, *key): x for key, x in by_both.items()})
        blocks.update({(c, 0, 0): x for c, x in by_core.items()})
        blocks.update({(c, 0, a): x for (c, a), x in by_core_near.items()})
        blocks.update({(c, b, 0): x for (c, b), x in by_core_row.items()})
        blocks.update({(c, *key): x for (c, key), x in by_core_both.items()})
        return [blocks[c, b, a] for c in range(core) for b in range(row) for a in range(near)]

    targets = teacher_targets(
        images(t_img, t_far, b_col, t_far_col),
        texts(t_txt, t_near, b_row, t_near_row, b_core, t_near_core, b_row_core, t_both_core),
    )
    s_imgs = images(s_img, s_far, b_col, s_far_col)
    s_txts = texts(s_txt, s_near, b_row, s_near_row, b_core, s_near_core, b_row_core, s_both_core)

    own_txt = row * near
    img_out = (1,) * (far * (col - 1))
    txt_out = (near,) * (row * (core - 1))
    skip = teacher_img.shape[1]
    out = pair_and_sent(s_imgs, s_txts, skip, targets, far, img_out, own_txt, txt_out)
    pair, img_pack, txt_pack = out[:3]
    out = out[3:]
    img_sent = {(1 + k // far, k % far): v for k, v in enumerate(out[: len(img_out)])}
    txt_sent = {(1 + k // row, k % row): v for k, v in enumerate(out[len(img_out) :])}
    img_part, txt_part = some_grads(pair, img_pack, txt_pack, rows, 0, (1,) * far, 0, (1,) * own_txt, f32, "kept")
    txt_part = {divmod(k, near): v for k, v in enumerate(txt_part)}

    img_in = {key: plan.send(v, "col", -key[0]) for key, v in img_sent.items() if key[1]}
    ahead = list(img_in.values())
    img_in.update({key: plan.send(after(v, *ahead), "col", -key[0]) for key, v in img_sent.items() if not key[1]})
    txt_in = {key: plan.send(v, "core", -key[0]) for key, v in txt_sent.items()}

    def img_sum(a):
        total = img_part[a]
        for b in range(1, col):
            total = total + img_in[b, a].astype(f32)
        return total

    img_last = [plan.send(img_sum(a).astype(bf16), "far", -a) for a in range(1, far)]
    image_grad = final(student_img, [img_part[0]] + [img_in[b, 0] for b in range(1, col)] + img_last)

    for c in range(1, core):
        for b in range(row):
            for a in range(near):
                txt_part[b, a] = txt_part[b, a] + txt_in[c, b][a * rows : (a + 1) * rows].astype(f32)
    row_in = {}
    for a in reversed(range(near)):
        ahead = list(row_in.values())
        for b in range(1, row):
            row_in[b, a] = plan.send(after(txt_part[b, a].astype(bf16), *ahead), "row", -b)

    def txt_sum(a):
        total = txt_part[0, a]
        for b in range(1, row):
            total = total + row_in[b, a].astype(f32)
        return total

    txt_last = [plan.send(txt_sum(a).astype(bf16), "near", -a) for a in range(1, near)]
    text_grad = final(student_txt, [txt_part[0, 0]] + [row_in[b, 0] for b in range(1, row)] + txt_last)
    return image_grad, text_grad


def solution(mesh):
    spec = P(AXES, None)
    return jax.shard_map(
        functools.partial(body, Plan(mesh)), mesh=mesh, in_specs=(spec,) * 4, out_specs=(spec,) * 2, check_vma=False
    )
```

time: 127 us -> 103 us (0.81)
  Pallas kernels: 26.9 us -> 14.7 us
  waiting for transfers between devices: 66.5 us -> 56.8 us
  local copies, waits for them, and re-layouts: 6.02 us -> 3.92 us
  starting transfers between devices: 24.3 us -> 26.1 us
  other arithmetic: 1.65 us -> 0.28 us
    ppermute x28 -> x24, waiting for transfers between devices: 66.5 us -> 56.8 us  [send(): return lax.ppermute(x, AXES, pairs)]
    pallas_call x2, Pallas kernels: 14 us -> 6.99 us  [the longest x1 5.44 us: pair_and_sent(): pl.pallas_call(functools.partial(pair_kernel, images, texts, skip, img_fi...]
    pallas_call x2, Pallas kernels: 4.8 us -> 2.31 us  [final(): pl.pallas_call(functools.partial(final_kernel, len(parts)), out_shape=jax...]
    unnamed x68 -> x12, local copies, waits for them, and re-layouts: 6.02 us -> 3.92 us
    pallas_call x1, Pallas kernels: 6.23 us -> 4.2 us  [teacher_targets(): pl.pallas_call(functools.partial(teacher_kernel, images, texts), out_shap...]
    ppermute x28 -> x24, starting transfers between devices: 24.3 us -> 26.1 us  [send(): return lax.ppermute(x, AXES, pairs)]
    convert_element_type x1, other arithmetic: 1.47 us -> 0.1 us  [body(): txt_part[b, a].astype(bf16)]
  transfers between devices with their start and end apart: 28 -> 24, of which waited for: 9 -> 8; matrix products, arithmetic and copies ran while one was open for 1% -> 0% of each run, Pallas kernels for 12% -> 7%
where the time goes in v2:
time: 103 us
  waiting for transfers between devices  56.8 us (55%)
  starting transfers between devices  26.1 us (25%)
  Pallas kernels  14.7 us (14%)
  local copies, waits for them, and re-layouts  3.92 us (4%)
    ppermute x24, waiting for transfers between devices, send(): return lax.ppermute(x, AXES, pairs)  56.8 us
    ppermute x24, starting transfers between devices, send(): return lax.ppermute(x, AXES, pairs)  26.1 us
    pallas_call x1, Pallas kernels, pair_and_sent(): pl.pallas_call(functools.partial(pair_kernel, images, texts, skip, img_fi...  5.44 us
    pallas_call x1, Pallas kernels, teacher_targets(): pl.pallas_call(functools.partial(teacher_kernel, images, texts), out_shap...  4.2 us
    unnamed x12, local copies, waits for them, and re-layouts  3.92 us
    pallas_call x2, Pallas kernels, final(): pl.pallas_call(functools.partial(final_kernel, len(parts)), out_shape=jax...  2.31 us
  transfers between devices with their start and end apart: 24, of which 8 were waited for; matrix products, arithmetic and copies ran while one was open for 0% of the time, Pallas kernels for 7%

profile of v2, /device:TPU:0, one launch (start us, length us, event | category | flops | bytes accessed | tf_op | source)
XLA Modules:
  0.0 102.6 jit_solution(11549398465730467805)
XLA Ops:
  0.6 1.0 copy-done
  1.6 1.0 copy-done.2
  2.6 1.0 copy-done.4
  3.6 1.0 copy-done.5
  4.5 1.2 %unit_rows.1 = (bf16[128,1536]{1,0:T(8,128)(2,1)S(1)}, bf16[128,1536]{1,0:T(8,128)(2,1)S(1)}, bf16[128,1152]{1,0:T(8,128)(2,1)S(1)}, bf16[128,1152]{1,0:T(8,128)...) custom-call(bf16[128,1536]{1,0:T(8,128)(2,1)S(1)} %copy-done.4, bf16[128,1536]{1,0:T(8,128)(2,1)S(1)} %copy-done.5, ...), custom_call_target="tpu_custom_call" | custom-call | flops 2752512 | bytes 4128768 | tf_op jit(solution)/shard_map/unit_rows/pallas_call | solution.py:107
  5.8 3.0 %collective-permute-start.2 = (bf16[128,2688]{1,0:T(8,128)(2,1)S(1)}, bf16[128,2688]{1,0:T(8,128)(2,1)S(1)}, u32[]{:S(2)}, u32[]{:S(2)}) collective-permute-start(bf16[128,2688]{1,0:T(8,128)(2,1)S(1)} %get-tuple-element.36), channel_id=1, source_target_pairs={{0,1},{1,0},{2,3},{3,2},{4,5},{5,4},{6,7},{7,6},{8,9},{9,8},{10,11... | collective-permute-start | bytes 2064392 | tf_op jit(solution)/shard_map/ppermute | solution.py:62
  8.8 1.5 %collective-permute-start.3 = (bf16[128,2688]{1,0:T(8,128)(2,1)S(1)}, bf16[128,2688]{1,0:T(8,128)(2,1)S(1)}, u32[]{:S(2)}, u32[]{:S(2)}) collective-permute-start(bf16[128,2688]{1,0:T(8,128)(2,1)S(1)} %get-tuple-element.37), channel_id=1, source_target_pairs={{0,2},{1,3},{2,0},{3,1},{4,6},{5,7},{6,4},{7,5},{8,10},{9,11},{10,... | collective-permute-start | bytes 2064392 | tf_op jit(solution)/shard_map/ppermute | solution.py:62
  10.3 2.6 %collective-permute-start = (bf16[128,1536]{1,0:T(8,128)(2,1)S(1)}, bf16[128,1536]{1,0:T(8,128)(2,1)S(1)}, u32[]{:S(2)}, u32[]{:S(2)}) collective-permute-start(bf16[128,1536]{1,0:T(8,128)(2,1)S(1)} %get-tuple-element.34.refs_0_), channel_id=1, source_target_pairs={{0,16},{1,17},{2,18},{3,19},{4,20},{5,21},{6,22},{7,23},{8,24},{9,... | collective-permute-start | bytes 1179656 | tf_op jit(solution)/shard_map/ppermute | solution.py:62
  12.9 1.6 %collective-permute-start.1 = (bf16[128,1536]{1,0:T(8,128)(2,1)S(1)}, bf16[128,1536]{1,0:T(8,128)(2,1)S(1)}, u32[]{:S(2)}, u32[]{:S(2)}) collective-permute-start(bf16[128,1536]{1,0:T(8,128)(2,1)S(1)} %get-tuple-element.35.refs_4_), channel_id=1, source_target_pairs={{0,8},{1,9},{2,10},{3,11},{4,12},{5,13},{6,14},{7,15},{8,0},{9,1},... | collective-permute-start | bytes 1179656 | tf_op jit(solution)/shard_map/ppermute | solution.py:62
  14.5 16.5 %collective-permute-done.refs_1_ = bf16[128,1536]{1,0:T(8,128)(2,1)S(1)} collective-permute-done((bf16[128,1536]{1,0:T(8,128)(2,1)S(1)}, bf16[128,1536]{1,0:T(8,128)(2,1)S(1)}, u32[]{:S(2)}, u32[]{:S(2)}) %collective-permute-start) | collective-permute-done | bytes 393248 | tf_op jit(solution)/shard_map/ppermute | solution.py:62
  31.3 0.6 collective-permute-start.7
  32.3 1.4 %collective-permute-start.5 = (bf16[128,1152]{1,0:T(8,128)(2,1)S(1)}, bf16[128,1152]{1,0:T(8,128)(2,1)S(1)}, u32[]{:S(2)}, u32[]{:S(2)}) collective-permute-start(bf16[128,1152]{1,0:T(8,128)(2,1)S(1)} %get-tuple-element.38.refs_0_), channel_id=1, source_target_pairs={{0,16},{1,17},{2,18},{3,19},{4,20},{5,21},{6,22},{7,23},{8,24},{9,... | collective-permute-start | bytes 884744 | tf_op jit(solution)/shard_map/ppermute | solution.py:62
  33.7 2.4 %collective-permute-start.6 = (bf16[128,1152]{1,0:T(8,128)(2,1)S(1)}, bf16[128,1152]{1,0:T(8,128)(2,1)S(1)}, u32[]{:S(2)}, u32[]{:S(2)}) collective-permute-start(bf16[128,1152]{1,0:T(8,128)(2,1)S(1)} %get-tuple-element.40.refs_4_), channel_id=1, source_target_pairs={{0,8},{1,9},{2,10},{3,11},{4,12},{5,13},{6,14},{7,15},{8,0},{9,1},... | collective-permute-start | bytes 884744 | tf_op jit(solution)/shard_map/ppermute | solution.py:62
  36.2 12.2 %collective-permute-done.5.refs_1_ = bf16[128,1152]{1,0:T(8,128)(2,1)S(1)} collective-permute-done((bf16[128,1152]{1,0:T(8,128)(2,1)S(1)}, bf16[128,1152]{1,0:T(8,128)(2,1)S(1)}, u32[]{:S(2)}, u32[]{:S(2)}) %collective-permute-start.5) | collective-permute-done | bytes 294944 | tf_op jit(solution)/shard_map/ppermute | solution.py:62
  49.0 1.6 %collective-permute-start.11 = (bf16[128,1152]{1,0:T(8,128)(2,1)S(1)}, bf16[128,1152]{1,0:T(8,128)(2,1)S(1)}, u32[]{:S(2)}, u32[]{:S(2)}) collective-permute-start(bf16[128,1152]{1,0:T(8,128)(2,1)S(1)} %collective-permute-done.6.refs_5_), channel_id=1, source_target_pairs={{0,2},{1,3},{2,0},{3,1},{4,6},{5,7},{6,4},{7,5},{8,10},{9,11},{10,... | collective-permute-start | bytes 884744 | tf_op jit(solution)/shard_map/ppermute | solution.py:62
  50.5 1.5 %collective-permute-start.10 = (bf16[128,1152]{1,0:T(8,128)(2,1)S(1)}, bf16[128,1152]{1,0:T(8,128)(2,1)S(1)}, u32[]{:S(2)}, u32[]{:S(2)}) collective-permute-start(bf16[128,1152]{1,0:T(8,128)(2,1)S(1)} %collective-permute-done.5.refs_1_), channel_id=1, source_target_pairs={{0,1},{1,0},{2,3},{3,2},{4,5},{5,4},{6,7},{7,6},{8,9},{9,8},{10,11... | collective-permute-start | bytes 884744 | tf_op jit(solution)/shard_map/ppermute | solution.py:62
  52.0 5.9 %collective-permute-done.11.refs_7_ = bf16[128,1152]{1,0:T(8,128)(2,1)S(1)} collective-permute-done((bf16[128,1152]{1,0:T(8,128)(2,1)S(1)}, bf16[128,1152]{1,0:T(8,128)(2,1)S(1)}, u32[]{:S(2)}, u32[]{:S(2)}) %collective-permute-start.11) | collective-permute-done | bytes 294944 | tf_op jit(solution)/shard_map/ppermute | solution.py:62
  58.0 4.2 %teacher_targets.1.refs_12_ = f32[512,1024]{1,0:T(8,128)S(1)} custom-call(bf16[128,1536]{1,0:T(8,128)(2,1)S(1)} %get-tuple-element.34.refs_0_, bf16[128,1536]{1,0:T(8,128)(2,1)S(1)} %collective-permute-done.refs_1_, bf16[128,2688]{1,0:T(8,128)(2,1)S(1)} %collective-permute-done.2.refs_2_, bf16[128,1536]{1,0:T(8,128)(2,1)S(1)} %collective-permute-done.7.refs_3_, ...), custom_call_target="tpu_custom_call" | custom-call | flops 1610612736 | bytes 6815744 | tf_op jit(solution)/shard_map/teacher_targets/pallas_call | solution.py:154
  62.2 5.4 %pair_and_sent.1 = (bf16[512,1024]{1,0:T(8,128)(2,1)S(1)}, bf16[512,1152]{1,0:T(8,128)(2,1)S(1)}, bf16[1024,1152]{1,0:T(8,128)(2,1)S(1)}, bf16[128,1152]{1,0:T(8...) custom-call(bf16[128,1152]{1,0:T(8,128)(2,1)S(1)} %get-tuple-element.38., ...), custom_call_target="tpu_custom_call" | custom-call | flops 2415919104 | bytes 7733248 | tf_op jit(solution)/shard_map/pair_and_sent/pallas_call | solution.py:217
  67.6 0.6 collective-permute-start.20
  68.2 1.6 %collective-permute-start.16 = (bf16[128,1152]{1,0:T(8,128)(2,1)S(1)}, bf16[128,1152]{1,0:T(8,128)(2,1)S(1)}, u32[]{:S(2)}, u32[]{:S(2)}) collective-permute-start(bf16[128,1152]{1,0:T(8,128)(2,1)S(1)} %get-tuple-element.54), channel_id=1, source_target_pairs={{0,1},{1,0},{2,3},{3,2},{4,5},{5,4},{6,7},{7,6},{8,9},{9,8},{10,11... | collective-permute-start | bytes 884744 | tf_op jit(solution)/shard_map/ppermute | solution.py:62
  69.8 1.6 %kept.1 = (f32[128,1152]{1,0:T(8,128)S(1)}, f32[128,1152]{1,0:T(8,128)S(1)}, f32[128,1152]{1,0:T(8,128)S(1)}, f32[128,1152]{1,0:T(8,128)S(1)}, f32[128,1152]{1,0:T(8,128)S(1)}, /*index=5*/f32[128,1152]{1,0:T(8,128)S(1)}) custom-call(bf16[512,1024]{1,0:T(8,128)(2,1)S(1)} %get-tuple-element.49.pair_ref, bf16[512,1152]{1,0:T(8,128)(2,1)S(1)} %get-tuple-element.50.img, ...), custom_call_target="tpu_custom_call" | custom-call | flops 1207959552 | bytes 8126464 | tf_op jit(solution)/shard_map/kept/pallas_call | solution.py:247
  71.3 5.9 %collective-permute-done.16 = bf16[128,1152]{1,0:T(8,128)(2,1)S(1)} collective-permute-done((bf16[128,1152]{1,0:T(8,128)(2,1)S(1)}, bf16[128,1152]{1,0:T(8,128)(2,1)S(1)}, u32[]{:S(2)}, u32[]{:S(2)}) %collective-permute-start.16) | collective-permute-done | bytes 294944 | tf_op jit(solution)/shard_map/ppermute | solution.py:62
  77.2 1.6 %collective-permute-start.17 = (bf16[128,1152]{1,0:T(8,128)(2,1)S(1)}, bf16[128,1152]{1,0:T(8,128)(2,1)S(1)}, u32[]{:S(2)}, u32[]{:S(2)}) collective-permute-start(bf16[128,1152]{1,0:T(8,128)(2,1)S(1)} %get-tuple-element.55), channel_id=1, source_target_pairs={{0,1},{1,0},{2,3},{3,2},{4,5},{5,4},{6,7},{7,6},{8,9},{9,8},{10,11... | collective-permute-start | bytes 884744 | tf_op jit(solution)/shard_map/ppermute | solution.py:62
  78.9 1.6 %collective-permute-start.21 = (bf16[128,1152]{1,0:T(8,128)(2,1)S(1)}, bf16[128,1152]{1,0:T(8,128)(2,1)S(1)}, u32[]{:S(2)}, u32[]{:S(2)}) collective-permute-start(bf16[128,1152]{1,0:T(8,128)(2,1)S(1)} %get-tuple-element.66), channel_id=1, source_target_pairs={{0,2},{1,3},{2,0},{3,1},{4,6},{5,7},{6,4},{7,5},{8,10},{9,11},{10,... | collective-permute-start | bytes 884744 | tf_op jit(solution)/shard_map/ppermute | solution.py:62
  80.5 1.5 %collective-permute-start.18 = (bf16[128,1152]{1,0:T(8,128)(2,1)S(1)}, bf16[128,1152]{1,0:T(8,128)(2,1)S(1)}, u32[]{:S(2)}, u32[]{:S(2)}) collective-permute-start(bf16[128,1152]{1,0:T(8,128)(2,1)S(1)} %add_convert_fusion.3), channel_id=1, source_target_pairs={{0,16},{1,17},{2,18},{3,19},{4,20},{5,21},{6,22},{7,23},{8,24},{9,... | collective-permute-start | bytes 884744 | tf_op jit(solution)/shard_map/ppermute | solution.py:62
  82.0 4.8 %collective-permute-done.21 = bf16[128,1152]{1,0:T(8,128)(2,1)S(1)} collective-permute-done((bf16[128,1152]{1,0:T(8,128)(2,1)S(1)}, bf16[128,1152]{1,0:T(8,128)(2,1)S(1)}, u32[]{:S(2)}, u32[]{:S(2)}) %collective-permute-start.21) | collective-permute-done | bytes 294944 | tf_op jit(solution)/shard_map/ppermute | solution.py:62
  86.8 1.5 %collective-permute-start.22 = (bf16[128,1152]{1,0:T(8,128)(2,1)S(1)}, bf16[128,1152]{1,0:T(8,128)(2,1)S(1)}, u32[]{:S(2)}, u32[]{:S(2)}) collective-permute-start(bf16[128,1152]{1,0:T(8,128)(2,1)S(1)} %get-tuple-element.62), channel_id=1, source_target_pairs={{0,2},{1,3},{2,0},{3,1},{4,6},{5,7},{6,4},{7,5},{8,10},{9,11},{10,... | collective-permute-start | bytes 884744 | tf_op jit(solution)/shard_map/ppermute | solution.py:62
  89.0 6.5 %collective-permute-done.18.refs_3_ = bf16[128,1152]{1,0:T(8,128)(2,1)S(1)} collective-permute-done((bf16[128,1152]{1,0:T(8,128)(2,1)S(1)}, bf16[128,1152]{1,0:T(8,128)(2,1)S(1)}, u32[]{:S(2)}, u32[]{:S(2)}) %collective-permute-start.18) | collective-permute-done | bytes 294944 | tf_op jit(solution)/shard_map/ppermute | solution.py:62
  95.4 1.2 %final.2 = f32[128,1152]{1,0:T(8,128)} custom-call(bf16[128,1152]{1,0:T(8,128)(2,1)S(1)} %copy-done.1, f32[128,1152]{1,0:T(8,128)S(1)} %get-tuple-element.52.refs_1_, bf16[128,1152]{1,0:T(8,128)(2,1)S(1)} %collective-permute-done.17.refs_2_, bf16[128,1152]{1,0:T(8,128)(2,1)S(1)} %collective-permute-done.18.refs_3_), custom_call_target="tpu_custom_call" | custom-call | flops 1474560 | bytes 1769472 | tf_op jit(solution)/shard_map/final/pallas_call | solution.py:279
  96.6 4.8 %collective-permute-done.23.refs_3_ = bf16[128,1152]{1,0:T(8,128)(2,1)S(1)} collective-permute-done((bf16[128,1152]{1,0:T(8,128)(2,1)S(1)}, bf16[128,1152]{1,0:T(8,128)(2,1)S(1)}, u32[]{:S(2)}, u32[]{:S(2)}) %collective-permute-start.23) | collective-permute-done | bytes 294944 | tf_op jit(solution)/shard_map/ppermute | solution.py:62
  101.4 1.2 %final.3 = f32[128,1152]{1,0:T(8,128)} custom-call(bf16[128,1152]{1,0:T(8,128)(2,1)S(1)} %copy-done.3, f32[128,1152]{1,0:T(8,128)S(1)} %get-tuple-element.65.refs_1_, bf16[128,1152]{1,0:T(8,128)(2,1)S(1)} %collective-permute-done.22.refs_2_, bf16[128,1152]{1,0:T(8,128)(2,1)S(1)} %collective-permute-done.23.refs_3_), custom_call_target="tpu_custom_call" | custom-call | flops 1474560 | bytes 1769472 | tf_op jit(solution)/shard_map/final/pallas_call | solution.py:279
  (37 shorter events, 2.2 us)
Async XLA Ops:
  0.6 1.0 copy-start
  1.6 1.0 copy-start.2
  2.6 1.0 copy-start.4
  3.6 1.0 copy-start.5
  5.8 25.4 %collective-permute-start.2 = (bf16[128,2688]{1,0:T(8,128)(2,1)S(1)}, bf16[128,2688]{1,0:T(8,128)(2,1)S(1)}, u32[]{:S(2)}, u32[]{:S(2)}) collective-permute-start(bf16[128,2688]{1,0:T(8,128)(2,1)S(1)} %get-tuple-element.36), channel_id=1, source_target_pairs={{0,1},{1,0},{2,3},{3,2},{4,5},{5,4},{6,7},{7,6},{8,9},{9,8},{10,11... | collective-permute-start | bytes 2064392 | tf_op jit(solution)/shard_map/ppermute | solution.py:62
  8.8 22.4 %collective-permute-start.4 = (bf16[128,2688]{1,0:T(8,128)(2,1)S(1)}, bf16[128,2688]{1,0:T(8,128)(2,1)S(1)}, u32[]{:S(2)}, u32[]{:S(2)}) collective-permute-start(bf16[128,2688]{1,0:T(8,128)(2,1)S(1)} %get-tuple-element.37), channel_id=1, source_target_pairs={{0,4},{1,5},{2,6},{3,7},{4,0},{5,1},{6,2},{7,3},{8,12},{9,13},{10,... | collective-permute-start | bytes 2064392 | tf_op jit(solution)/shard_map/ppermute | solution.py:62
  8.8 22.4 %collective-permute-start.3 = (bf16[128,2688]{1,0:T(8,128)(2,1)S(1)}, bf16[128,2688]{1,0:T(8,128)(2,1)S(1)}, u32[]{:S(2)}, u32[]{:S(2)}) collective-permute-start(bf16[128,2688]{1,0:T(8,128)(2,1)S(1)} %get-tuple-element.37), channel_id=1, source_target_pairs={{0,2},{1,3},{2,0},{3,1},{4,6},{5,7},{6,4},{7,5},{8,10},{9,11},{10,... | collective-permute-start | bytes 2064392 | tf_op jit(solution)/shard_map/ppermute | solution.py:62
  10.3 20.7 %collective-permute-start = (bf16[128,1536]{1,0:T(8,128)(2,1)S(1)}, bf16[128,1536]{1,0:T(8,128)(2,1)S(1)}, u32[]{:S(2)}, u32[]{:S(2)}) collective-permute-start(bf16[128,1536]{1,0:T(8,128)(2,1)S(1)} %get-tuple-element.34.refs_0_), channel_id=1, source_target_pairs={{0,16},{1,17},{2,18},{3,19},{4,20},{5,21},{6,22},{7,23},{8,24},{9,... | collective-permute-start | bytes 1179656 | tf_op jit(solution)/shard_map/ppermute | solution.py:62
  12.9 18.3 %collective-permute-start.1 = (bf16[128,1536]{1,0:T(8,128)(2,1)S(1)}, bf16[128,1536]{1,0:T(8,128)(2,1)S(1)}, u32[]{:S(2)}, u32[]{:S(2)}) collective-permute-start(bf16[128,1536]{1,0:T(8,128)(2,1)S(1)} %get-tuple-element.35.refs_4_), channel_id=1, source_target_pairs={{0,8},{1,9},{2,10},{3,11},{4,12},{5,13},{6,14},{7,15},{8,0},{9,1},... | collective-permute-start | bytes 1179656 | tf_op jit(solution)/shard_map/ppermute | solution.py:62
  31.2 17.2 %collective-permute-start.9 = (bf16[128,2688]{1,0:T(8,128)(2,1)S(1)}, bf16[128,2688]{1,0:T(8,128)(2,1)S(1)}, u32[]{:S(2)}, u32[]{:S(2)}) collective-permute-start(bf16[128,2688]{1,0:T(8,128)(2,1)S(1)} %collective-permute-done.3.refs_6_), channel_id=1, source_target_pairs={{0,4},{1,5},{2,6},{3,7},{4,0},{5,1},{6,2},{7,3},{8,12},{9,13},{10,... | collective-permute-start | bytes 2064392 | tf_op jit(solution)/shard_map/ppermute | solution.py:62
  31.3 17.1 %collective-permute-start.7 = (bf16[128,1536]{1,0:T(8,128)(2,1)S(1)}, bf16[128,1536]{1,0:T(8,128)(2,1)S(1)}, u32[]{:S(2)}, u32[]{:S(2)}) collective-permute-start(bf16[128,1536]{1,0:T(8,128)(2,1)S(1)} %collective-permute-done.refs_1_), channel_id=1, source_target_pairs={{0,1},{1,0},{2,3},{3,2},{4,5},{5,4},{6,7},{7,6},{8,9},{9,8},{10,11... | collective-permute-start | bytes 1179656 | tf_op jit(solution)/shard_map/ppermute | solution.py:62
  31.9 16.5 %collective-permute-start.8 = (bf16[128,1536]{1,0:T(8,128)(2,1)S(1)}, bf16[128,1536]{1,0:T(8,128)(2,1)S(1)}, u32[]{:S(2)}, u32[]{:S(2)}) collective-permute-start(bf16[128,1536]{1,0:T(8,128)(2,1)S(1)} %collective-permute-done.1.refs_5_), channel_id=1, source_target_pairs={{0,2},{1,3},{2,0},{3,1},{4,6},{5,7},{6,4},{7,5},{8,10},{9,11},{10,... | collective-permute-start | bytes 1179656 | tf_op jit(solution)/shard_map/ppermute | solution.py:62
  32.3 16.0 %collective-permute-start.5 = (bf16[128,1152]{1,0:T(8,128)(2,1)S(1)}, bf16[128,1152]{1,0:T(8,128)(2,1)S(1)}, u32[]{:S(2)}, u32[]{:S(2)}) collective-permute-start(bf16[128,1152]{1,0:T(8,128)(2,1)S(1)} %get-tuple-element.38.refs_0_), channel_id=1, source_target_pairs={{0,16},{1,17},{2,18},{3,19},{4,20},{5,21},{6,22},{7,23},{8,24},{9,... | collective-permute-start | bytes 884744 | tf_op jit(solution)/shard_map/ppermute | solution.py:62
  33.7 14.6 %collective-permute-start.6 = (bf16[128,1152]{1,0:T(8,128)(2,1)S(1)}, bf16[128,1152]{1,0:T(8,128)(2,1)S(1)}, u32[]{:S(2)}, u32[]{:S(2)}) collective-permute-start(bf16[128,1152]{1,0:T(8,128)(2,1)S(1)} %get-tuple-element.40.refs_4_), channel_id=1, source_target_pairs={{0,8},{1,9},{2,10},{3,11},{4,12},{5,13},{6,14},{7,15},{8,0},{9,1},... | collective-permute-start | bytes 884744 | tf_op jit(solution)/shard_map/ppermute | solution.py:62
  48.4 2.2 %collective-permute-start.14 = (bf16[128,1536]{1,0:T(8,128)(2,1)S(1)}, bf16[128,1536]{1,0:T(8,128)(2,1)S(1)}, u32[]{:S(2)}, u32[]{:S(2)}) collective-permute-start(bf16[128,1536]{1,0:T(8,128)(2,1)S(1)} %collective-permute-done.1.refs_5_), channel_id=1, source_target_pairs={{0,4},{1,5},{2,6},{3,7},{4,0},{5,1},{6,2},{7,3},{8,12},{9,13},{10,... | collective-permute-start | bytes 1179656 | tf_op jit(solution)/shard_map/ppermute | solution.py:62
  48.5 3.6 %collective-permute-start.12 = (bf16[128,1152]{1,0:T(8,128)(2,1)S(1)}, bf16[128,1152]{1,0:T(8,128)(2,1)S(1)}, u32[]{:S(2)}, u32[]{:S(2)}) collective-permute-start(bf16[128,1152]{1,0:T(8,128)(2,1)S(1)} %collective-permute-done.6.refs_5_), channel_id=1, source_target_pairs={{0,4},{1,5},{2,6},{3,7},{4,0},{5,1},{6,2},{7,3},{8,12},{9,13},{10,... | collective-permute-start | bytes 884744 | tf_op jit(solution)/shard_map/ppermute | solution.py:62
  49.0 9.0 %collective-permute-start.11 = (bf16[128,1152]{1,0:T(8,128)(2,1)S(1)}, bf16[128,1152]{1,0:T(8,128)(2,1)S(1)}, u32[]{:S(2)}, u32[]{:S(2)}) collective-permute-start(bf16[128,1152]{1,0:T(8,128)(2,1)S(1)} %collective-permute-done.6.refs_5_), channel_id=1, source_target_pairs={{0,2},{1,3},{2,0},{3,1},{4,6},{5,7},{6,4},{7,5},{8,10},{9,11},{10,... | collective-permute-start | bytes 884744 | tf_op jit(solution)/shard_map/ppermute | solution.py:62
  50.5 7.4 %collective-permute-start.15 = (bf16[128,1536]{1,0:T(8,128)(2,1)S(1)}, bf16[128,1536]{1,0:T(8,128)(2,1)S(1)}, u32[]{:S(2)}, u32[]{:S(2)}) collective-permute-start(bf16[128,1536]{1,0:T(8,128)(2,1)S(1)} %collective-permute-done.8.refs_7_), channel_id=1, source_target_pairs={{0,4},{1,5},{2,6},{3,7},{4,0},{5,1},{6,2},{7,3},{8,12},{9,13},{10,... | collective-permute-start | bytes 1179656 | tf_op jit(solution)/shard_map/ppermute | solution.py:62
  50.5 11.6 %collective-permute-start.10 = (bf16[128,1152]{1,0:T(8,128)(2,1)S(1)}, bf16[128,1152]{1,0:T(8,128)(2,1)S(1)}, u32[]{:S(2)}, u32[]{:S(2)}) collective-permute-start(bf16[128,1152]{1,0:T(8,128)(2,1)S(1)} %collective-permute-done.5.refs_1_), channel_id=1, source_target_pairs={{0,1},{1,0},{2,3},{3,2},{4,5},{5,4},{6,7},{7,6},{8,9},{9,8},{10,11... | collective-permute-start | bytes 884744 | tf_op jit(solution)/shard_map/ppermute | solution.py:62
  57.9 4.2 %collective-permute-start.13 = (bf16[128,1152]{1,0:T(8,128)(2,1)S(1)}, bf16[128,1152]{1,0:T(8,128)(2,1)S(1)}, u32[]{:S(2)}, u32[]{:S(2)}) collective-permute-start(bf16[128,1152]{1,0:T(8,128)(2,1)S(1)} %collective-permute-done.11.refs_7_), channel_id=1, source_target_pairs={{0,4},{1,5},{2,6},{3,7},{4,0},{5,1},{6,2},{7,3},{8,12},{9,13},{10,... | collective-permute-start | bytes 884744 | tf_op jit(solution)/shard_map/ppermute | solution.py:62
  67.6 11.1 %collective-permute-start.20 = (bf16[256,1152]{1,0:T(8,128)(2,1)S(1)}, bf16[256,1152]{1,0:T(8,128)(2,1)S(1)}, u32[]{:S(2)}, u32[]{:S(2)}) collective-permute-start(bf16[256,1152]{1,0:T(8,128)(2,1)S(1)} %get-tuple-element.60), channel_id=1, source_target_pairs={{0,4},{1,5},{2,6},{3,7},{4,0},{5,1},{6,2},{7,3},{8,12},{9,13},{10,... | collective-permute-start | bytes 1769480 | tf_op jit(solution)/shard_map/ppermute | solution.py:62
  68.2 9.0 %collective-permute-start.16 = (bf16[128,1152]{1,0:T(8,128)(2,1)S(1)}, bf16[128,1152]{1,0:T(8,128)(2,1)S(1)}, u32[]{:S(2)}, u32[]{:S(2)}) collective-permute-start(bf16[128,1152]{1,0:T(8,128)(2,1)S(1)} %get-tuple-element.54), channel_id=1, source_target_pairs={{0,1},{1,0},{2,3},{3,2},{4,5},{5,4},{6,7},{7,6},{8,9},{9,8},{10,11... | collective-permute-start | bytes 884744 | tf_op jit(solution)/shard_map/ppermute | solution.py:62
  69.8 18.6 %collective-permute-start.19 = (bf16[256,1152]{1,0:T(8,128)(2,1)S(1)}, bf16[256,1152]{1,0:T(8,128)(2,1)S(1)}, u32[]{:S(2)}, u32[]{:S(2)}) collective-permute-start(bf16[256,1152]{1,0:T(8,128)(2,1)S(1)} %get-tuple-element.58), channel_id=1, source_target_pairs={{0,4},{1,5},{2,6},{3,7},{4,0},{5,1},{6,2},{7,3},{8,12},{9,13},{10,... | collective-permute-start | bytes 1769480 | tf_op jit(solution)/shard_map/ppermute | solution.py:62
  77.2 11.8 %collective-permute-start.17 = (bf16[128,1152]{1,0:T(8,128)(2,1)S(1)}, bf16[128,1152]{1,0:T(8,128)(2,1)S(1)}, u32[]{:S(2)}, u32[]{:S(2)}) collective-permute-start(bf16[128,1152]{1,0:T(8,128)(2,1)S(1)} %get-tuple-element.55), channel_id=1, source_target_pairs={{0,1},{1,0},{2,3},{3,2},{4,5},{5,4},{6,7},{7,6},{8,9},{9,8},{10,11... | collective-permute-start | bytes 884744 | tf_op jit(solution)/shard_map/ppermute | solution.py:62
  78.9 16.6 %copy-start.1 = (bf16[128,1152]{1,0:T(8,128)(2,1)S(1)}, bf16[128,1152]{1,0:T(8,128)(2,1)}, u32[]{:S(2)}) copy-start(bf16[128,1152]{1,0:T(8,128)(2,1)} %refs_0_.4) | copy-start | bytes 884740
  78.9 7.9 %collective-permute-start.21 = (bf16[128,1152]{1,0:T(8,128)(2,1)S(1)}, bf16[128,1152]{1,0:T(8,128)(2,1)S(1)}, u32[]{:S(2)}, u32[]{:S(2)}) collective-permute-start(bf16[128,1152]{1,0:T(8,128)(2,1)S(1)} %get-tuple-element.66), channel_id=1, source_target_pairs={{0,2},{1,3},{2,0},{3,1},{4,6},{5,7},{6,4},{7,5},{8,10},{9,11},{10,... | collective-permute-start | bytes 884744 | tf_op jit(solution)/shard_map/ppermute | solution.py:62
  80.5 14.9 %collective-permute-start.18 = (bf16[128,1152]{1,0:T(8,128)(2,1)S(1)}, bf16[128,1152]{1,0:T(8,128)(2,1)S(1)}, u32[]{:S(2)}, u32[]{:S(2)}) collective-permute-start(bf16[128,1152]{1,0:T(8,128)(2,1)S(1)} %add_convert_fusion.3), channel_id=1, source_target_pairs={{0,16},{1,17},{2,18},{3,19},{4,20},{5,21},{6,22},{7,23},{8,24},{9,... | collective-permute-start | bytes 884744 | tf_op jit(solution)/shard_map/ppermute | solution.py:62
  86.8 9.8 %collective-permute-start.22 = (bf16[128,1152]{1,0:T(8,128)(2,1)S(1)}, bf16[128,1152]{1,0:T(8,128)(2,1)S(1)}, u32[]{:S(2)}, u32[]{:S(2)}) collective-permute-start(bf16[128,1152]{1,0:T(8,128)(2,1)S(1)} %get-tuple-element.62), channel_id=1, source_target_pairs={{0,2},{1,3},{2,0},{3,1},{4,6},{5,7},{6,4},{7,5},{8,10},{9,11},{10,... | collective-permute-start | bytes 884744 | tf_op jit(solution)/shard_map/ppermute | solution.py:62
  88.3 13.1 %copy-start.3 = (bf16[128,1152]{1,0:T(8,128)(2,1)S(1)}, bf16[128,1152]{1,0:T(8,128)(2,1)}, u32[]{:S(2)}) copy-start(bf16[128,1152]{1,0:T(8,128)(2,1)} %refs_0_.5) | copy-start | bytes 884740
  88.5 13.0 %collective-permute-start.23 = (bf16[128,1152]{1,0:T(8,128)(2,1)S(1)}, bf16[128,1152]{1,0:T(8,128)(2,1)S(1)}, u32[]{:S(2)}, u32[]{:S(2)}) collective-permute-start(bf16[128,1152]{1,0:T(8,128)(2,1)S(1)} %get-tuple-element.64), channel_id=1, source_target_pairs={{0,8},{1,9},{2,10},{3,11},{4,12},{5,13},{6,14},{7,15},{8,0},{9,1},... | collective-permute-start | bytes 884744 | tf_op jit(solution)/shard_map/ppermute | solution.py:62

commit v3 on v2

--- a/solution.py
+++ b/solution.py
@@ -108,7 +108,7 @@
         functools.partial(unit_kernel, len(arrays)),
         out_shape=[jax.ShapeDtypeStruct(a.shape, bf16) for a in arrays]
         + [jax.ShapeDtypeStruct(shape, bf16) for shape in both],
-        in_specs=[ANY] * len(arrays),
+        in_specs=[pl.BlockSpec(memory_space=pltpu.HBM)] * len(arrays),
         out_specs=[VMEM] * (len(arrays) + half),
         scratch_shapes=[pltpu.VMEM(a.shape, bf16) for a in arrays]
         + [pltpu.SemaphoreType.DMA((len(arrays),))],
@@ -322,7 +322,6 @@
     s_near_core = onward(s_near, "core", *second)
     t_near_core = onward(t_near, "core", *second)
     t_both_core = onward(t_near_row, "core", t_near_core)
-    s_both_core = onward(s_near_row, "core", s_near_core)
 
     def images(own, by_far, by_col, by_both):
         blocks = {(0, 0): own, **by_both}
@@ -345,6 +344,7 @@
         images(t_img, t_far, b_col, t_far_col),
         texts(t_txt, t_near, b_row, t_near_row, b_core, t_near_core, b_row_core, t_both_core),
     )
+    s_both_core = onward(s_near_row, "core", s_near_core, targets)
     s_imgs = images(s_img, s_far, b_col, s_far_col)
     s_txts = texts(s_txt, s_near, b_row, s_near_row, b_core, s_near_core, b_row_core, s_both_core)
 
@@ -361,9 +361,21 @@
     txt_part = {divmod(k, near): v for k, v in enumerate(txt_part)}
 
     img_in = {key: plan.send(v, "col", -key[0]) for key, v in img_sent.items() if key[1]}
-    ahead = list(img_in.values())
-    img_in.update({key: plan.send(after(v, *ahead), "col", -key[0]) for key, v in img_sent.items() if not key[1]})
     txt_in = {key: plan.send(v, "core", -key[0]) for key, v in txt_sent.items()}
+
+    for c in range(1, core):
+        for b in range(row):
+            for a in range(near):
+                txt_part[b, a] = txt_part[b, a] + txt_in[c, b][a * rows : (a + 1) * rows].astype(f32)
+    row_in = {}
+    for b in range(1, row):
+        for a in range(1, near):
+            row_in[b, a] = plan.send(txt_part[b, a].astype(bf16), "row", -b)
+    ahead = list(row_in.values())
+    for b in range(1, row):
+        row_in[b, 0] = plan.send(after(txt_part[b, 0].astype(bf16), *ahead), "row", -b)
+    for b in range(1, col):
+        img_in[b, 0] = plan.send(after(img_sent[b, 0], *ahead), "col", -b)
 
     def img_sum(a):
         total = img_part[a]
@@ -374,16 +386,6 @@
     img_last = [plan.send(img_sum(a).astype(bf16), "far", -a) for a in range(1, far)]
     image_grad = final(student_img, [img_part[0]] + [img_in[b, 0] for b in range(1, col)] + img_last)
 
-    for c in range(1, core):
-        for b in range(row):
-            for a in range(near):
-                txt_part[b, a] = txt_part[b, a] + txt_in[c, b][a * rows : (a + 1) * rows].astype(f32)
-    row_in = {}
-    for a in reversed(range(near)):
-        ahead = list(row_in.values())
-        for b in range(1, row):
-            row_in[b, a] = plan.send(after(txt_part[b, a].astype(bf16), *ahead), "row", -b)
-
     def txt_sum(a):
         total = txt_part[0, a]
         for b in range(1, row):

time: 103 us -> 97.6 us (0.948)
  waiting for transfers between devices: 56.8 us -> 52.4 us
    ppermute x24, waiting for transfers between devices: 56.8 us -> 52.4 us  [send(): return lax.ppermute(x, AXES, pairs)]
  transfers between devices with their start and end apart: 24 -> 24, of which waited for: 8 -> 11; matrix products, arithmetic and copies ran while one was open for 0% -> 0% of each run, Pallas kernels for 7% -> 7%
where the time goes in v3:
time: 97.6 us; the launch traced here: 97.3 us
  waiting for transfers between devices  52.4 us (54%)
  starting transfers between devices  25.3 us (26%)
  Pallas kernels  14.7 us (15%)
  local copies, waits for them, and re-layouts  3.92 us (4%)
    ppermute x24, waiting for transfers between devices, send(): return lax.ppermute(x, AXES, pairs)  52.4 us
    ppermute x24, starting transfers between devices, send(): return lax.ppermute(x, AXES, pairs)  25.3 us
    pallas_call x1, Pallas kernels, pair_and_sent(): pl.pallas_call(functools.partial(pair_kernel, images, texts, skip, img_fi...  5.42 us
    pallas_call x1, Pallas kernels, teacher_targets(): pl.pallas_call(functools.partial(teacher_kernel, images, texts), out_shap...  4.2 us
    unnamed x12, local copies, waits for them, and re-layouts  3.92 us
    pallas_call x2, Pallas kernels, final(): pl.pallas_call(functools.partial(final_kernel, len(parts)), out_shape=jax...  2.31 us
  transfers between devices with their start and end apart: 24, of which 11 were waited for; matrix products, arithmetic and copies ran while one was open for 0% of the time, Pallas kernels for 7%

profile of v3, /device:TPU:0, one launch (start us, length us, event | category | flops | bytes accessed | tf_op | source)
XLA Modules:
  0.0 97.3 jit_solution(16210080439260642893)
XLA Ops:
  0.6 1.0 copy-done
  1.6 1.0 copy-done.2
  2.6 1.0 %copy-done.4 = bf16[128,1536]{1,0:T(8,128)(2,1)S(1)} copy-done((bf16[128,1536]{1,0:T(8,128)(2,1)S(1)}, bf16[128,1536]{1,0:T(8,128)(2,1)}, u32[]{:S(2)}) %copy-start.4) | copy-done | bytes 393240
  3.6 1.0 %copy-done.5 = bf16[128,1536]{1,0:T(8,128)(2,1)S(1)} copy-done((bf16[128,1536]{1,0:T(8,128)(2,1)S(1)}, bf16[128,1536]{1,0:T(8,128)(2,1)}, u32[]{:S(2)}) %copy-start.5) | copy-done | bytes 393240
  4.5 1.2 %unit_rows.1 = (bf16[128,1536]{1,0:T(8,128)(2,1)S(1)}, bf16[128,1536]{1,0:T(8,128)(2,1)S(1)}, bf16[128,1152]{1,0:T(8,128)(2,1)S(1)}, bf16[128,1152]{1,0:T(8,128)...) custom-call(bf16[128,1536]{1,0:T(8,128)(2,1)S(1)} %copy-done.4, bf16[128,1536]{1,0:T(8,128)(2,1)S(1)} %copy-done.5, ...), custom_call_target="tpu_custom_call" | custom-call | flops 2752512 | bytes 4128768 | tf_op jit(solution)/shard_map/unit_rows/pallas_call | solution.py:107
  5.8 3.0 %collective-permute-start.2 = (bf16[128,2688]{1,0:T(8,128)(2,1)S(1)}, bf16[128,2688]{1,0:T(8,128)(2,1)S(1)}, u32[]{:S(2)}, u32[]{:S(2)}) collective-permute-start(bf16[128,2688]{1,0:T(8,128)(2,1)S(1)} %get-tuple-element.36), channel_id=1, source_target_pairs={{0,1},{1,0},{2,3},{3,2},{4,5},{5,4},{6,7},{7,6},{8,9},{9,8},{10,11... | collective-permute-start | bytes 2064392 | tf_op jit(solution)/shard_map/ppermute | solution.py:62
  8.8 1.5 %collective-permute-start.3 = (bf16[128,2688]{1,0:T(8,128)(2,1)S(1)}, bf16[128,2688]{1,0:T(8,128)(2,1)S(1)}, u32[]{:S(2)}, u32[]{:S(2)}) collective-permute-start(bf16[128,2688]{1,0:T(8,128)(2,1)S(1)} %get-tuple-element.37), channel_id=1, source_target_pairs={{0,2},{1,3},{2,0},{3,1},{4,6},{5,7},{6,4},{7,5},{8,10},{9,11},{10,... | collective-permute-start | bytes 2064392 | tf_op jit(solution)/shard_map/ppermute | solution.py:62
  10.3 2.6 %collective-permute-start = (bf16[128,1536]{1,0:T(8,128)(2,1)S(1)}, bf16[128,1536]{1,0:T(8,128)(2,1)S(1)}, u32[]{:S(2)}, u32[]{:S(2)}) collective-permute-start(bf16[128,1536]{1,0:T(8,128)(2,1)S(1)} %get-tuple-element.34.refs_0_), channel_id=1, source_target_pairs={{0,16},{1,17},{2,18},{3,19},{4,20},{5,21},{6,22},{7,23},{8,24},{9,... | collective-permute-start | bytes 1179656 | tf_op jit(solution)/shard_map/ppermute | solution.py:62
  12.9 1.6 %collective-permute-start.1 = (bf16[128,1536]{1,0:T(8,128)(2,1)S(1)}, bf16[128,1536]{1,0:T(8,128)(2,1)S(1)}, u32[]{:S(2)}, u32[]{:S(2)}) collective-permute-start(bf16[128,1536]{1,0:T(8,128)(2,1)S(1)} %get-tuple-element.35.refs_4_), channel_id=1, source_target_pairs={{0,8},{1,9},{2,10},{3,11},{4,12},{5,13},{6,14},{7,15},{8,0},{9,1},... | collective-permute-start | bytes 1179656 | tf_op jit(solution)/shard_map/ppermute | solution.py:62
  14.5 16.5 %collective-permute-done.refs_1_ = bf16[128,1536]{1,0:T(8,128)(2,1)S(1)} collective-permute-done((bf16[128,1536]{1,0:T(8,128)(2,1)S(1)}, bf16[128,1536]{1,0:T(8,128)(2,1)S(1)}, u32[]{:S(2)}, u32[]{:S(2)}) %collective-permute-start) | collective-permute-done | bytes 393248 | tf_op jit(solution)/shard_map/ppermute | solution.py:62
  32.3 1.4 %collective-permute-start.5 = (bf16[128,1152]{1,0:T(8,128)(2,1)S(1)}, bf16[128,1152]{1,0:T(8,128)(2,1)S(1)}, u32[]{:S(2)}, u32[]{:S(2)}) collective-permute-start(bf16[128,1152]{1,0:T(8,128)(2,1)S(1)} %get-tuple-element.38.refs_0_), channel_id=1, source_target_pairs={{0,16},{1,17},{2,18},{3,19},{4,20},{5,21},{6,22},{7,23},{8,24},{9,... | collective-permute-start | bytes 884744 | tf_op jit(solution)/shard_map/ppermute | solution.py:62
  33.7 2.4 %collective-permute-start.6 = (bf16[128,1152]{1,0:T(8,128)(2,1)S(1)}, bf16[128,1152]{1,0:T(8,128)(2,1)S(1)}, u32[]{:S(2)}, u32[]{:S(2)}) collective-permute-start(bf16[128,1152]{1,0:T(8,128)(2,1)S(1)} %get-tuple-element.40.refs_4_), channel_id=1, source_target_pairs={{0,8},{1,9},{2,10},{3,11},{4,12},{5,13},{6,14},{7,15},{8,0},{9,1},... | collective-permute-start | bytes 884744 | tf_op jit(solution)/shard_map/ppermute | solution.py:62
  36.2 12.2 %collective-permute-done.5.refs_1_ = bf16[128,1152]{1,0:T(8,128)(2,1)S(1)} collective-permute-done((bf16[128,1152]{1,0:T(8,128)(2,1)S(1)}, bf16[128,1152]{1,0:T(8,128)(2,1)S(1)}, u32[]{:S(2)}, u32[]{:S(2)}) %collective-permute-start.5) | collective-permute-done | bytes 294944 | tf_op jit(solution)/shard_map/ppermute | solution.py:62
  48.5 1.7 %collective-permute-done.13.refs_9_ = bf16[128,1536]{1,0:T(8,128)(2,1)S(1)} collective-permute-done((bf16[128,1536]{1,0:T(8,128)(2,1)S(1)}, bf16[128,1536]{1,0:T(8,128)(2,1)S(1)}, u32[]{:S(2)}, u32[]{:S(2)}) %collective-permute-start.13) | collective-permute-done | bytes 393248 | tf_op jit(solution)/shard_map/ppermute | solution.py:62
  50.7 1.6 %collective-permute-start.11 = (bf16[128,1152]{1,0:T(8,128)(2,1)S(1)}, bf16[128,1152]{1,0:T(8,128)(2,1)S(1)}, u32[]{:S(2)}, u32[]{:S(2)}) collective-permute-start(bf16[128,1152]{1,0:T(8,128)(2,1)S(1)} %collective-permute-done.6.refs_5_), channel_id=1, source_target_pairs={{0,2},{1,3},{2,0},{3,1},{4,6},{5,7},{6,4},{7,5},{8,10},{9,11},{10,... | collective-permute-start | bytes 884744 | tf_op jit(solution)/shard_map/ppermute | solution.py:62
  52.3 1.5 %collective-permute-start.10 = (bf16[128,1152]{1,0:T(8,128)(2,1)S(1)}, bf16[128,1152]{1,0:T(8,128)(2,1)S(1)}, u32[]{:S(2)}, u32[]{:S(2)}) collective-permute-start(bf16[128,1152]{1,0:T(8,128)(2,1)S(1)} %collective-permute-done.5.refs_1_), channel_id=1, source_target_pairs={{0,1},{1,0},{2,3},{3,2},{4,5},{5,4},{6,7},{7,6},{8,9},{9,8},{10,11... | collective-permute-start | bytes 884744 | tf_op jit(solution)/shard_map/ppermute | solution.py:62
  53.7 4.2 %teacher_targets.1.refs_12_ = f32[512,1024]{1,0:T(8,128)S(1)} custom-call(bf16[128,1536]{1,0:T(8,128)(2,1)S(1)} %get-tuple-element.34.refs_0_, bf16[128,1536]{1,0:T(8,128)(2,1)S(1)} %collective-permute-done.refs_1_, bf16[128,2688]{1,0:T(8,128)(2,1)S(1)} %collective-permute-done.2.refs_2_, bf16[128,1536]{1,0:T(8,128)(2,1)S(1)} %collective-permute-done.7.refs_3_, ...), custom_call_target="tpu_custom_call" | custom-call | flops 1610612736 | bytes 6815744 | tf_op jit(solution)/shard_map/teacher_targets/pallas_call | solution.py:154
  58.0 1.8 %collective-permute-done.11.refs_7_ = bf16[128,1152]{1,0:T(8,128)(2,1)S(1)} collective-permute-done((bf16[128,1152]{1,0:T(8,128)(2,1)S(1)}, bf16[128,1152]{1,0:T(8,128)(2,1)S(1)}, u32[]{:S(2)}, u32[]{:S(2)}) %collective-permute-start.11) | collective-permute-done | bytes 294944 | tf_op jit(solution)/shard_map/ppermute | solution.py:62
  59.7 1.3 %collective-permute-done.10.refs_3_ = bf16[128,1152]{1,0:T(8,128)(2,1)S(1)} collective-permute-done((bf16[128,1152]{1,0:T(8,128)(2,1)S(1)}, bf16[128,1152]{1,0:T(8,128)(2,1)S(1)}, u32[]{:S(2)}, u32[]{:S(2)}) %collective-permute-start.10) | collective-permute-done | bytes 294944 | tf_op jit(solution)/shard_map/ppermute | solution.py:62
  61.3 5.4 %pair_and_sent.1 = (bf16[512,1024]{1,0:T(8,128)(2,1)S(1)}, bf16[512,1152]{1,0:T(8,128)(2,1)S(1)}, bf16[1024,1152]{1,0:T(8,128)(2,1)S(1)}, bf16[128,1152]{1,0:T(8...) custom-call(bf16[128,1152]{1,0:T(8,128)(2,1)S(1)} %get-tuple-element.38., ...), custom_call_target="tpu_custom_call" | custom-call | flops 2415919104 | bytes 7733248 | tf_op jit(solution)/shard_map/pair_and_sent/pallas_call | solution.py:217
  66.9 1.6 %collective-permute-start.19 = (bf16[128,1152]{1,0:T(8,128)(2,1)S(1)}, bf16[128,1152]{1,0:T(8,128)(2,1)S(1)}, u32[]{:S(2)}, u32[]{:S(2)}) collective-permute-start(bf16[128,1152]{1,0:T(8,128)(2,1)S(1)} %get-tuple-element.58), channel_id=1, source_target_pairs={{0,1},{1,0},{2,3},{3,2},{4,5},{5,4},{6,7},{7,6},{8,9},{9,8},{10,11... | collective-permute-start | bytes 884744 | tf_op jit(solution)/shard_map/ppermute | solution.py:62
  68.6 1.6 %kept.1 = (f32[128,1152]{1,0:T(8,128)S(1)}, f32[128,1152]{1,0:T(8,128)S(1)}, f32[128,1152]{1,0:T(8,128)S(1)}, f32[128,1152]{1,0:T(8,128)S(1)}, f32[128,1152]{1,0:T(8,128)S(1)}, /*index=5*/f32[128,1152]{1,0:T(8,128)S(1)}) custom-call(bf16[512,1024]{1,0:T(8,128)(2,1)S(1)} %get-tuple-element.49.pair_ref, bf16[512,1152]{1,0:T(8,128)(2,1)S(1)} %get-tuple-element.50.img, ...), custom_call_target="tpu_custom_call" | custom-call | flops 1207959552 | bytes 8126464 | tf_op jit(solution)/shard_map/kept/pallas_call | solution.py:247
  70.3 1.6 %collective-permute-start.17 = (bf16[128,1152]{1,0:T(8,128)(2,1)S(1)}, bf16[128,1152]{1,0:T(8,128)(2,1)S(1)}, u32[]{:S(2)}, u32[]{:S(2)}) collective-permute-start(bf16[128,1152]{1,0:T(8,128)(2,1)S(1)} %get-tuple-element.67), channel_id=1, source_target_pairs={{0,2},{1,3},{2,0},{3,1},{4,6},{5,7},{6,4},{7,5},{8,10},{9,11},{10,... | collective-permute-start | bytes 884744 | tf_op jit(solution)/shard_map/ppermute | solution.py:62
  71.9 4.4 %collective-permute-done.19 = bf16[128,1152]{1,0:T(8,128)(2,1)S(1)} collective-permute-done((bf16[128,1152]{1,0:T(8,128)(2,1)S(1)}, bf16[128,1152]{1,0:T(8,128)(2,1)S(1)}, u32[]{:S(2)}, u32[]{:S(2)}) %collective-permute-start.19) | collective-permute-done | bytes 294944 | tf_op jit(solution)/shard_map/ppermute | solution.py:62
  76.3 1.6 %collective-permute-start.20 = (bf16[128,1152]{1,0:T(8,128)(2,1)S(1)}, bf16[128,1152]{1,0:T(8,128)(2,1)S(1)}, u32[]{:S(2)}, u32[]{:S(2)}) collective-permute-start(bf16[128,1152]{1,0:T(8,128)(2,1)S(1)} %add_convert_fusion.2), channel_id=1, source_target_pairs={{0,16},{1,17},{2,18},{3,19},{4,20},{5,21},{6,22},{7,23},{8,24},{9,... | collective-permute-start | bytes 884744 | tf_op jit(solution)/shard_map/ppermute | solution.py:62
  77.9 1.8 %collective-permute-done.17 = bf16[128,1152]{1,0:T(8,128)(2,1)S(1)} collective-permute-done((bf16[128,1152]{1,0:T(8,128)(2,1)S(1)}, bf16[128,1152]{1,0:T(8,128)(2,1)S(1)}, u32[]{:S(2)}, u32[]{:S(2)}) %collective-permute-start.17) | collective-permute-done | bytes 294944 | tf_op jit(solution)/shard_map/ppermute | solution.py:62
  80.2 1.6 %collective-permute-start.22 = (bf16[128,1152]{1,0:T(8,128)(2,1)S(1)}, bf16[128,1152]{1,0:T(8,128)(2,1)S(1)}, u32[]{:S(2)}, u32[]{:S(2)}) collective-permute-start(bf16[128,1152]{1,0:T(8,128)(2,1)S(1)} %get-tuple-element.62), channel_id=1, source_target_pairs={{0,2},{1,3},{2,0},{3,1},{4,6},{5,7},{6,4},{7,5},{8,10},{9,11},{10,... | collective-permute-start | bytes 884744 | tf_op jit(solution)/shard_map/ppermute | solution.py:62
  81.9 0.9 collective-permute-start.23
  82.8 9.3 %collective-permute-done.20.refs_3_ = bf16[128,1152]{1,0:T(8,128)(2,1)S(1)} collective-permute-done((bf16[128,1152]{1,0:T(8,128)(2,1)S(1)}, bf16[128,1152]{1,0:T(8,128)(2,1)S(1)}, u32[]{:S(2)}, u32[]{:S(2)}) %collective-permute-start.20) | collective-permute-done | bytes 294944 | tf_op jit(solution)/shard_map/ppermute | solution.py:62
  92.2 1.2 %final.2 = f32[128,1152]{1,0:T(8,128)} custom-call(bf16[128,1152]{1,0:T(8,128)(2,1)S(1)} %copy-done.1, f32[128,1152]{1,0:T(8,128)S(1)} %get-tuple-element.52.refs_1_, bf16[128,1152]{1,0:T(8,128)(2,1)S(1)} %collective-permute-done.18.refs_2_, bf16[128,1152]{1,0:T(8,128)(2,1)S(1)} %collective-permute-done.20.refs_3_), custom_call_target="tpu_custom_call" | custom-call | flops 1474560 | bytes 1769472 | tf_op jit(solution)/shard_map/final/pallas_call | solution.py:279
  93.3 2.9 %collective-permute-done.23.refs_3_ = bf16[128,1152]{1,0:T(8,128)(2,1)S(1)} collective-permute-done((bf16[128,1152]{1,0:T(8,128)(2,1)S(1)}, bf16[128,1152]{1,0:T(8,128)(2,1)S(1)}, u32[]{:S(2)}, u32[]{:S(2)}) %collective-permute-start.23) | collective-permute-done | bytes 294944 | tf_op jit(solution)/shard_map/ppermute | solution.py:62
  96.2 1.2 %final.3 = f32[128,1152]{1,0:T(8,128)} custom-call(bf16[128,1152]{1,0:T(8,128)(2,1)S(1)} %copy-done.3, f32[128,1152]{1,0:T(8,128)S(1)} %get-tuple-element.65.refs_1_, bf16[128,1152]{1,0:T(8,128)(2,1)S(1)} %collective-permute-done.22.refs_2_, bf16[128,1152]{1,0:T(8,128)(2,1)S(1)} %collective-permute-done.23.refs_3_), custom_call_target="tpu_custom_call" | custom-call | flops 1474560 | bytes 1769472 | tf_op jit(solution)/shard_map/final/pallas_call | solution.py:279
  (37 shorter events, 3.3 us)
Async XLA Ops:
  0.6 1.0 copy-start
  1.6 1.0 copy-start.2
  2.6 1.0 %copy-start.4 = (bf16[128,1536]{1,0:T(8,128)(2,1)S(1)}, bf16[128,1536]{1,0:T(8,128)(2,1)}, u32[]{:S(2)}) copy-start(bf16[128,1536]{1,0:T(8,128)(2,1)} %refs_0_.3) | copy-start | bytes 1179652
  3.6 1.0 %copy-start.5 = (bf16[128,1536]{1,0:T(8,128)(2,1)S(1)}, bf16[128,1536]{1,0:T(8,128)(2,1)}, u32[]{:S(2)}) copy-start(bf16[128,1536]{1,0:T(8,128)(2,1)} %refs_1_.1) | copy-start | bytes 1179652
  5.8 25.4 %collective-permute-start.2 = (bf16[128,2688]{1,0:T(8,128)(2,1)S(1)}, bf16[128,2688]{1,0:T(8,128)(2,1)S(1)}, u32[]{:S(2)}, u32[]{:S(2)}) collective-permute-start(bf16[128,2688]{1,0:T(8,128)(2,1)S(1)} %get-tuple-element.36), channel_id=1, source_target_pairs={{0,1},{1,0},{2,3},{3,2},{4,5},{5,4},{6,7},{7,6},{8,9},{9,8},{10,11... | collective-permute-start | bytes 2064392 | tf_op jit(solution)/shard_map/ppermute | solution.py:62
  8.8 22.4 %collective-permute-start.4 = (bf16[128,2688]{1,0:T(8,128)(2,1)S(1)}, bf16[128,2688]{1,0:T(8,128)(2,1)S(1)}, u32[]{:S(2)}, u32[]{:S(2)}) collective-permute-start(bf16[128,2688]{1,0:T(8,128)(2,1)S(1)} %get-tuple-element.37), channel_id=1, source_target_pairs={{0,4},{1,5},{2,6},{3,7},{4,0},{5,1},{6,2},{7,3},{8,12},{9,13},{10,... | collective-permute-start | bytes 2064392 | tf_op jit(solution)/shard_map/ppermute | solution.py:62
  8.8 22.4 %collective-permute-start.3 = (bf16[128,2688]{1,0:T(8,128)(2,1)S(1)}, bf16[128,2688]{1,0:T(8,128)(2,1)S(1)}, u32[]{:S(2)}, u32[]{:S(2)}) collective-permute-start(bf16[128,2688]{1,0:T(8,128)(2,1)S(1)} %get-tuple-element.37), channel_id=1, source_target_pairs={{0,2},{1,3},{2,0},{3,1},{4,6},{5,7},{6,4},{7,5},{8,10},{9,11},{10,... | collective-permute-start | bytes 2064392 | tf_op jit(solution)/shard_map/ppermute | solution.py:62
  10.3 20.7 %collective-permute-start = (bf16[128,1536]{1,0:T(8,128)(2,1)S(1)}, bf16[128,1536]{1,0:T(8,128)(2,1)S(1)}, u32[]{:S(2)}, u32[]{:S(2)}) collective-permute-start(bf16[128,1536]{1,0:T(8,128)(2,1)S(1)} %get-tuple-element.34.refs_0_), channel_id=1, source_target_pairs={{0,16},{1,17},{2,18},{3,19},{4,20},{5,21},{6,22},{7,23},{8,24},{9,... | collective-permute-start | bytes 1179656 | tf_op jit(solution)/shard_map/ppermute | solution.py:62
  12.9 18.3 %collective-permute-start.1 = (bf16[128,1536]{1,0:T(8,128)(2,1)S(1)}, bf16[128,1536]{1,0:T(8,128)(2,1)S(1)}, u32[]{:S(2)}, u32[]{:S(2)}) collective-permute-start(bf16[128,1536]{1,0:T(8,128)(2,1)S(1)} %get-tuple-element.35.refs_4_), channel_id=1, source_target_pairs={{0,8},{1,9},{2,10},{3,11},{4,12},{5,13},{6,14},{7,15},{8,0},{9,1},... | collective-permute-start | bytes 1179656 | tf_op jit(solution)/shard_map/ppermute | solution.py:62
  31.2 17.2 %collective-permute-start.9 = (bf16[128,2688]{1,0:T(8,128)(2,1)S(1)}, bf16[128,2688]{1,0:T(8,128)(2,1)S(1)}, u32[]{:S(2)}, u32[]{:S(2)}) collective-permute-start(bf16[128,2688]{1,0:T(8,128)(2,1)S(1)} %collective-permute-done.3.refs_6_), channel_id=1, source_target_pairs={{0,4},{1,5},{2,6},{3,7},{4,0},{5,1},{6,2},{7,3},{8,12},{9,13},{10,... | collective-permute-start | bytes 2064392 | tf_op jit(solution)/shard_map/ppermute | solution.py:62
  31.3 17.1 %collective-permute-start.7 = (bf16[128,1536]{1,0:T(8,128)(2,1)S(1)}, bf16[128,1536]{1,0:T(8,128)(2,1)S(1)}, u32[]{:S(2)}, u32[]{:S(2)}) collective-permute-start(bf16[128,1536]{1,0:T(8,128)(2,1)S(1)} %collective-permute-done.refs_1_), channel_id=1, source_target_pairs={{0,1},{1,0},{2,3},{3,2},{4,5},{5,4},{6,7},{7,6},{8,9},{9,8},{10,11... | collective-permute-start | bytes 1179656 | tf_op jit(solution)/shard_map/ppermute | solution.py:62
  31.9 16.5 %collective-permute-start.8 = (bf16[128,1536]{1,0:T(8,128)(2,1)S(1)}, bf16[128,1536]{1,0:T(8,128)(2,1)S(1)}, u32[]{:S(2)}, u32[]{:S(2)}) collective-permute-start(bf16[128,1536]{1,0:T(8,128)(2,1)S(1)} %collective-permute-done.1.refs_5_), channel_id=1, source_target_pairs={{0,2},{1,3},{2,0},{3,1},{4,6},{5,7},{6,4},{7,5},{8,10},{9,11},{10,... | collective-permute-start | bytes 1179656 | tf_op jit(solution)/shard_map/ppermute | solution.py:62
  32.3 16.0 %collective-permute-start.5 = (bf16[128,1152]{1,0:T(8,128)(2,1)S(1)}, bf16[128,1152]{1,0:T(8,128)(2,1)S(1)}, u32[]{:S(2)}, u32[]{:S(2)}) collective-permute-start(bf16[128,1152]{1,0:T(8,128)(2,1)S(1)} %get-tuple-element.38.refs_0_), channel_id=1, source_target_pairs={{0,16},{1,17},{2,18},{3,19},{4,20},{5,21},{6,22},{7,23},{8,24},{9,... | collective-permute-start | bytes 884744 | tf_op jit(solution)/shard_map/ppermute | solution.py:62
  33.7 14.6 %collective-permute-start.6 = (bf16[128,1152]{1,0:T(8,128)(2,1)S(1)}, bf16[128,1152]{1,0:T(8,128)(2,1)S(1)}, u32[]{:S(2)}, u32[]{:S(2)}) collective-permute-start(bf16[128,1152]{1,0:T(8,128)(2,1)S(1)} %get-tuple-element.40.refs_4_), channel_id=1, source_target_pairs={{0,8},{1,9},{2,10},{3,11},{4,12},{5,13},{6,14},{7,15},{8,0},{9,1},... | collective-permute-start | bytes 884744 | tf_op jit(solution)/shard_map/ppermute | solution.py:62
  48.4 1.8 %collective-permute-start.13 = (bf16[128,1536]{1,0:T(8,128)(2,1)S(1)}, bf16[128,1536]{1,0:T(8,128)(2,1)S(1)}, u32[]{:S(2)}, u32[]{:S(2)}) collective-permute-start(bf16[128,1536]{1,0:T(8,128)(2,1)S(1)} %collective-permute-done.1.refs_5_), channel_id=1, source_target_pairs={{0,4},{1,5},{2,6},{3,7},{4,0},{5,1},{6,2},{7,3},{8,12},{9,13},{10,... | collective-permute-start | bytes 1179656 | tf_op jit(solution)/shard_map/ppermute | solution.py:62
  50.2 3.6 %collective-permute-start.14 = (bf16[128,1536]{1,0:T(8,128)(2,1)S(1)}, bf16[128,1536]{1,0:T(8,128)(2,1)S(1)}, u32[]{:S(2)}, u32[]{:S(2)}) collective-permute-start(bf16[128,1536]{1,0:T(8,128)(2,1)S(1)} %collective-permute-done.8.refs_7_), channel_id=1, source_target_pairs={{0,4},{1,5},{2,6},{3,7},{4,0},{5,1},{6,2},{7,3},{8,12},{9,13},{10,... | collective-permute-start | bytes 1179656 | tf_op jit(solution)/shard_map/ppermute | solution.py:62
  50.3 7.7 %collective-permute-start.12 = (bf16[128,1152]{1,0:T(8,128)(2,1)S(1)}, bf16[128,1152]{1,0:T(8,128)(2,1)S(1)}, u32[]{:S(2)}, u32[]{:S(2)}) collective-permute-start(bf16[128,1152]{1,0:T(8,128)(2,1)S(1)} %collective-permute-done.6.refs_5_), channel_id=1, source_target_pairs={{0,4},{1,5},{2,6},{3,7},{4,0},{5,1},{6,2},{7,3},{8,12},{9,13},{10,... | collective-permute-start | bytes 884744 | tf_op jit(solution)/shard_map/ppermute | solution.py:62
  50.7 9.1 %collective-permute-start.11 = (bf16[128,1152]{1,0:T(8,128)(2,1)S(1)}, bf16[128,1152]{1,0:T(8,128)(2,1)S(1)}, u32[]{:S(2)}, u32[]{:S(2)}) collective-permute-start(bf16[128,1152]{1,0:T(8,128)(2,1)S(1)} %collective-permute-done.6.refs_5_), channel_id=1, source_target_pairs={{0,2},{1,3},{2,0},{3,1},{4,6},{5,7},{6,4},{7,5},{8,10},{9,11},{10,... | collective-permute-start | bytes 884744 | tf_op jit(solution)/shard_map/ppermute | solution.py:62
  52.3 8.8 %collective-permute-start.10 = (bf16[128,1152]{1,0:T(8,128)(2,1)S(1)}, bf16[128,1152]{1,0:T(8,128)(2,1)S(1)}, u32[]{:S(2)}, u32[]{:S(2)}) collective-permute-start(bf16[128,1152]{1,0:T(8,128)(2,1)S(1)} %collective-permute-done.5.refs_1_), channel_id=1, source_target_pairs={{0,1},{1,0},{2,3},{3,2},{4,5},{5,4},{6,7},{7,6},{8,9},{9,8},{10,11... | collective-permute-start | bytes 884744 | tf_op jit(solution)/shard_map/ppermute | solution.py:62
  59.7 1.6 %collective-permute-start.15 = (bf16[128,1152]{1,0:T(8,128)(2,1)S(1)}, bf16[128,1152]{1,0:T(8,128)(2,1)S(1)}, u32[]{:S(2)}, u32[]{:S(2)}) collective-permute-start(bf16[128,1152]{1,0:T(8,128)(2,1)S(1)} %collective-permute-done.11.refs_7_), channel_id=1, source_target_pairs={{0,4},{1,5},{2,6},{3,7},{4,0},{5,1},{6,2},{7,3},{8,12},{9,13},{10,... | collective-permute-start | bytes 884744 | tf_op jit(solution)/shard_map/ppermute | solution.py:62
  66.7 3.4 %collective-permute-start.16 = (bf16[256,1152]{1,0:T(8,128)(2,1)S(1)}, bf16[256,1152]{1,0:T(8,128)(2,1)S(1)}, u32[]{:S(2)}, u32[]{:S(2)}) collective-permute-start(bf16[256,1152]{1,0:T(8,128)(2,1)S(1)} %get-tuple-element.55), channel_id=1, source_target_pairs={{0,4},{1,5},{2,6},{3,7},{4,0},{5,1},{6,2},{7,3},{8,12},{9,13},{10,... | collective-permute-start | bytes 1769480 | tf_op jit(solution)/shard_map/ppermute | solution.py:62
  66.9 9.3 %collective-permute-start.19 = (bf16[128,1152]{1,0:T(8,128)(2,1)S(1)}, bf16[128,1152]{1,0:T(8,128)(2,1)S(1)}, u32[]{:S(2)}, u32[]{:S(2)}) collective-permute-start(bf16[128,1152]{1,0:T(8,128)(2,1)S(1)} %get-tuple-element.58), channel_id=1, source_target_pairs={{0,1},{1,0},{2,3},{3,2},{4,5},{5,4},{6,7},{7,6},{8,9},{9,8},{10,11... | collective-permute-start | bytes 884744 | tf_op jit(solution)/shard_map/ppermute | solution.py:62
  68.5 13.3 %collective-permute-start.21 = (bf16[256,1152]{1,0:T(8,128)(2,1)S(1)}, bf16[256,1152]{1,0:T(8,128)(2,1)S(1)}, u32[]{:S(2)}, u32[]{:S(2)}) collective-permute-start(bf16[256,1152]{1,0:T(8,128)(2,1)S(1)} %get-tuple-element.60), channel_id=1, source_target_pairs={{0,4},{1,5},{2,6},{3,7},{4,0},{5,1},{6,2},{7,3},{8,12},{9,13},{10,... | collective-permute-start | bytes 1769480 | tf_op jit(solution)/shard_map/ppermute | solution.py:62
  70.3 21.9 %copy-start.1 = (bf16[128,1152]{1,0:T(8,128)(2,1)S(1)}, bf16[128,1152]{1,0:T(8,128)(2,1)}, u32[]{:S(2)}) copy-start(bf16[128,1152]{1,0:T(8,128)(2,1)} %refs_0_.4) | copy-start | bytes 884740
  70.3 9.4 %collective-permute-start.17 = (bf16[128,1152]{1,0:T(8,128)(2,1)S(1)}, bf16[128,1152]{1,0:T(8,128)(2,1)S(1)}, u32[]{:S(2)}, u32[]{:S(2)}) collective-permute-start(bf16[128,1152]{1,0:T(8,128)(2,1)S(1)} %get-tuple-element.67), channel_id=1, source_target_pairs={{0,2},{1,3},{2,0},{3,1},{4,6},{5,7},{6,4},{7,5},{8,10},{9,11},{10,... | collective-permute-start | bytes 884744 | tf_op jit(solution)/shard_map/ppermute | solution.py:62
  76.3 15.9 %collective-permute-start.20 = (bf16[128,1152]{1,0:T(8,128)(2,1)S(1)}, bf16[128,1152]{1,0:T(8,128)(2,1)S(1)}, u32[]{:S(2)}, u32[]{:S(2)}) collective-permute-start(bf16[128,1152]{1,0:T(8,128)(2,1)S(1)} %add_convert_fusion.2), channel_id=1, source_target_pairs={{0,16},{1,17},{2,18},{3,19},{4,20},{5,21},{6,22},{7,23},{8,24},{9,... | collective-permute-start | bytes 884744 | tf_op jit(solution)/shard_map/ppermute | solution.py:62
  79.7 12.5 %collective-permute-start.18 = (bf16[128,1152]{1,0:T(8,128)(2,1)S(1)}, bf16[128,1152]{1,0:T(8,128)(2,1)S(1)}, u32[]{:S(2)}, u32[]{:S(2)}) collective-permute-start(bf16[128,1152]{1,0:T(8,128)(2,1)S(1)} %get-tuple-element.56), channel_id=1, source_target_pairs={{0,1},{1,0},{2,3},{3,2},{4,5},{5,4},{6,7},{7,6},{8,9},{9,8},{10,11... | collective-permute-start | bytes 884744 | tf_op jit(solution)/shard_map/ppermute | solution.py:62
  80.2 13.1 %collective-permute-start.22 = (bf16[128,1152]{1,0:T(8,128)(2,1)S(1)}, bf16[128,1152]{1,0:T(8,128)(2,1)S(1)}, u32[]{:S(2)}, u32[]{:S(2)}) collective-permute-start(bf16[128,1152]{1,0:T(8,128)(2,1)S(1)} %get-tuple-element.62), channel_id=1, source_target_pairs={{0,2},{1,3},{2,0},{3,1},{4,6},{5,7},{6,4},{7,5},{8,10},{9,11},{10,... | collective-permute-start | bytes 884744 | tf_op jit(solution)/shard_map/ppermute | solution.py:62
  81.8 14.4 %copy-start.3 = (bf16[128,1152]{1,0:T(8,128)(2,1)S(1)}, bf16[128,1152]{1,0:T(8,128)(2,1)}, u32[]{:S(2)}) copy-start(bf16[128,1152]{1,0:T(8,128)(2,1)} %refs_0_.5) | copy-start | bytes 884740
  81.9 14.3 %collective-permute-start.23 = (bf16[128,1152]{1,0:T(8,128)(2,1)S(1)}, bf16[128,1152]{1,0:T(8,128)(2,1)S(1)}, u32[]{:S(2)}, u32[]{:S(2)}) collective-permute-start(bf16[128,1152]{1,0:T(8,128)(2,1)S(1)} %get-tuple-element.64), channel_id=1, source_target_pairs={{0,8},{1,9},{2,10},{3,11},{4,12},{5,13},{6,14},{7,15},{8,0},{9,1},... | collective-permute-start | bytes 884744 | tf_op jit(solution)/shard_map/ppermute | solution.py:62

commit v4 on v3

--- a/solution.py
+++ b/solution.py
@@ -108,11 +108,11 @@
         functools.partial(unit_kernel, len(arrays)),
         out_shape=[jax.ShapeDtypeStruct(a.shape, bf16) for a in arrays]
         + [jax.ShapeDtypeStruct(shape, bf16) for shape in both],
-        in_specs=[pl.BlockSpec(memory_space=pltpu.HBM)] * len(arrays),
+        in_specs=[ANY] * len(arrays),
         out_specs=[VMEM] * (len(arrays) + half),
         scratch_shapes=[pltpu.VMEM(a.shape, bf16) for a in arrays]
         + [pltpu.SemaphoreType.DMA((len(arrays),))],
-        compiler_params=params(*[(a.shape, 10) for a in arrays]),
+        compiler_params=pltpu.CompilerParams(vmem_limit_bytes=60 * 2**20),
         cost_estimate=pl.CostEstimate(
             flops=4 * sum(a.size for a in arrays),
             bytes_accessed=6 * sum(a.size for a in arrays),
@@ -287,6 +287,21 @@
     )(x, *parts)
 
 
+def token_kernel(*refs):
+    refs[-1][...] = jnp.zeros_like(refs[-1])
+
+
+def token(*arrays, flops):
+    return pl.pallas_call(
+        token_kernel,
+        out_shape=jax.ShapeDtypeStruct((8, 128), f32),
+        in_specs=[ANY] * len(arrays),
+        out_specs=VMEM,
+        cost_estimate=pl.CostEstimate(flops=flops, bytes_accessed=0, transcendentals=0),
+        name="token",
+    )(*arrays)
+
+
 def after(x, *others):
     others = [v for other in others for v in (other.values() if isinstance(other, dict) else [other])]
     return lax.optimization_barrier((x, *others))[0] if others else x
@@ -310,18 +325,18 @@
     b_col = spread(b_img, "col")
     b_row = spread(b_txt, "row")
     b_core = spread(b_txt, "core")
-    first = [t_far, t_near, b_col, b_row, b_core]
+    first = [token(*t_far.values(), *t_near.values(), flops=10000000000), b_col, b_row, b_core]
     s_far = spread(s_img, "far", *first)
     s_near = spread(s_txt, "near", *first)
     t_far_col = onward(t_far, "col", *first)
     t_near_row = onward(t_near, "row", *first)
     b_row_core = onward(b_row, "core", *first)
-    second = [s_far, s_near, t_far_col, t_near_row, b_row_core]
+    second = [token(*s_far.values(), *s_near.values(), flops=10000000000), t_far_col, t_near_row, b_row_core]
     s_far_col = onward(s_far, "col", *second)
     s_near_row = onward(s_near, "row", *second)
     s_near_core = onward(s_near, "core", *second)
     t_near_core = onward(t_near, "core", *second)
-    t_both_core = onward(t_near_row, "core", t_near_core)
+    t_both_core = onward(t_near_row, "core", *second)
 
     def images(own, by_far, by_col, by_both):
         blocks = {(0, 0): own, **by_both}

time: 97.6 us -> 91.3 us (0.935)
  starting transfers between devices: 25.3 us -> 19.8 us
  local copies, waits for them, and re-layouts: 3.92 us -> 2.01 us
  Pallas kernels: 14.7 us -> 16.6 us
    ppermute x24, starting transfers between devices: 25.3 us -> 19.8 us  [send(): return lax.ppermute(x, AXES, pairs)]
    unnamed x12, local copies, waits for them, and re-layouts: 3.92 us -> 2.01 us
    pallas_call x1, Pallas kernels: 1.24 us -> 3.13 us  [unit_rows(): pl.pallas_call(functools.partial(unit_kernel, len(arrays)), out_shape=[ja...]
  transfers between devices with their start and end apart: 24 -> 24, of which waited for: 11 -> 11; matrix products, arithmetic and copies ran while one was open for 0% -> 0% of each run, Pallas kernels for 7% -> 8%
where the time goes in v4:
time: 91.3 us; the launch traced here: 91.1 us
  waiting for transfers between devices  51.6 us (57%)
  starting transfers between devices  19.8 us (22%)
  Pallas kernels  16.6 us (18%)
  local copies, waits for them, and re-layouts  2.01 us (2%)
    ppermute x24, waiting for transfers between devices, send(): return lax.ppermute(x, AXES, pairs)  51.6 us
    ppermute x24, starting transfers between devices, send(): return lax.ppermute(x, AXES, pairs)  19.8 us
    pallas_call x1, Pallas kernels, pair_and_sent(): pl.pallas_call(functools.partial(pair_kernel, images, texts, skip, img_fi...  5.42 us
    pallas_call x1, Pallas kernels, teacher_targets(): pl.pallas_call(functools.partial(teacher_kernel, images, texts), out_shap...  4.19 us
    pallas_call x1, Pallas kernels, unit_rows(): pl.pallas_call(functools.partial(unit_kernel, len(arrays)), out_shape=[ja...  3.13 us
    pallas_call x2, Pallas kernels, final(): pl.pallas_call(functools.partial(final_kernel, len(parts)), out_shape=jax...  2.31 us
    unnamed x12, local copies, waits for them, and re-layouts  2.01 us
  transfers between devices with their start and end apart: 24, of which 11 were waited for; matrix products, arithmetic and copies ran while one was open for 0% of the time, Pallas kernels for 8%

profile of v4, /device:TPU:0, one launch (start us, length us, event | category | flops | bytes accessed | tf_op | source)
XLA Modules:
  0.0 91.1 jit_solution(15151915989714161628)
XLA Ops:
  0.6 3.1 %unit_rows.1 = (bf16[128,1536]{1,0:T(8,128)(2,1)}, bf16[128,1536]{1,0:T(8,128)(2,1)}, bf16[128,1152]{1,0:T(8,128)(2,1)}, bf16[128,1152]{1,0:T(8,128)(2,1)}, bf16...) custom-call(bf16[128,1536]{1,0:T(8,128)(2,1)} %refs_0_.3, bf16[128,1536]{1,0:T(8,128)(2,1)} %refs_1_.1, ...), custom_call_target="tpu_custom_call" | custom-call | flops 2752512 | bytes 4128768 | tf_op jit(solution)/shard_map/unit_rows/pallas_call | solution.py:107
  3.8 4.1 %collective-permute-start = (bf16[128,1536]{1,0:T(8,128)(2,1)}, bf16[128,1536]{1,0:T(8,128)(2,1)S(1)}, u32[]{:S(2)}, u32[]{:S(2)}) collective-permute-start(bf16[128,1536]{1,0:T(8,128)(2,1)} %get-tuple-element.34.refs_0_), channel_id=1, source_target_pairs={{0,16},{1,17},{2,18},{3,19},{4,20},{5,21},{6,22},{7,23},{8,24},{9,... | collective-permute-start | bytes 1179656 | tf_op jit(solution)/shard_map/ppermute | solution.py:62
  7.9 1.6 %collective-permute-start.1 = (bf16[128,1536]{1,0:T(8,128)(2,1)}, bf16[128,1536]{1,0:T(8,128)(2,1)S(1)}, u32[]{:S(2)}, u32[]{:S(2)}) collective-permute-start(bf16[128,1536]{1,0:T(8,128)(2,1)} %get-tuple-element.35.refs_4_), channel_id=1, source_target_pairs={{0,8},{1,9},{2,10},{3,11},{4,12},{5,13},{6,14},{7,15},{8,0},{9,1},... | collective-permute-start | bytes 1179656 | tf_op jit(solution)/shard_map/ppermute | solution.py:62
  9.5 1.5 %collective-permute-start.3 = (bf16[128,2688]{1,0:T(8,128)(2,1)}, bf16[128,2688]{1,0:T(8,128)(2,1)S(1)}, u32[]{:S(2)}, u32[]{:S(2)}) collective-permute-start(bf16[128,2688]{1,0:T(8,128)(2,1)} %get-tuple-element.37), channel_id=1, source_target_pairs={{0,2},{1,3},{2,0},{3,1},{4,6},{5,7},{6,4},{7,5},{8,10},{9,11},{10,... | collective-permute-start | bytes 2064392 | tf_op jit(solution)/shard_map/ppermute | solution.py:62
  11.0 1.5 %collective-permute-start.2 = (bf16[128,2688]{1,0:T(8,128)(2,1)}, bf16[128,2688]{1,0:T(8,128)(2,1)S(1)}, u32[]{:S(2)}, u32[]{:S(2)}) collective-permute-start(bf16[128,2688]{1,0:T(8,128)(2,1)} %get-tuple-element.36), channel_id=1, source_target_pairs={{0,1},{1,0},{2,3},{3,2},{4,5},{5,4},{6,7},{7,6},{8,9},{9,8},{10,11... | collective-permute-start | bytes 2064392 | tf_op jit(solution)/shard_map/ppermute | solution.py:62
  12.5 13.3 %collective-permute-done.refs_1_ = bf16[128,1536]{1,0:T(8,128)(2,1)S(1)} collective-permute-done((bf16[128,1536]{1,0:T(8,128)(2,1)}, bf16[128,1536]{1,0:T(8,128)(2,1)S(1)}, u32[]{:S(2)}, u32[]{:S(2)}) %collective-permute-start) | collective-permute-done | bytes 393248 | tf_op jit(solution)/shard_map/ppermute | solution.py:62
  25.9 2.8 %collective-permute-done.2.refs_2_ = bf16[128,2688]{1,0:T(8,128)(2,1)S(1)} collective-permute-done((bf16[128,2688]{1,0:T(8,128)(2,1)}, bf16[128,2688]{1,0:T(8,128)(2,1)S(1)}, u32[]{:S(2)}, u32[]{:S(2)}) %collective-permute-start.2) | collective-permute-done | bytes 688160 | tf_op jit(solution)/shard_map/ppermute | solution.py:62
  29.1 0.7 collective-permute-start.6
  29.8 1.5 %collective-permute-start.7 = (bf16[128,1536]{1,0:T(8,128)(2,1)S(1)}, bf16[128,1536]{1,0:T(8,128)(2,1)S(1)}, u32[]{:S(2)}, u32[]{:S(2)}) collective-permute-start(bf16[128,1536]{1,0:T(8,128)(2,1)S(1)} %collective-permute-done.refs_1_), channel_id=1, source_target_pairs={{0,1},{1,0},{2,3},{3,2},{4,5},{5,4},{6,7},{7,6},{8,9},{9,8},{10,11... | collective-permute-start | bytes 1179656 | tf_op jit(solution)/shard_map/ppermute | solution.py:62
  31.3 1.5 %collective-permute-start.8 = (bf16[128,1536]{1,0:T(8,128)(2,1)S(1)}, bf16[128,1536]{1,0:T(8,128)(2,1)S(1)}, u32[]{:S(2)}, u32[]{:S(2)}) collective-permute-start(bf16[128,1536]{1,0:T(8,128)(2,1)S(1)} %collective-permute-done.1.refs_5_), channel_id=1, source_target_pairs={{0,2},{1,3},{2,0},{3,1},{4,6},{5,7},{6,4},{7,5},{8,10},{9,11},{10,... | collective-permute-start | bytes 1179656 | tf_op jit(solution)/shard_map/ppermute | solution.py:62
  32.8 11.6 %collective-permute-done.5.refs_1_ = bf16[128,1152]{1,0:T(8,128)(2,1)S(1)} collective-permute-done((bf16[128,1152]{1,0:T(8,128)(2,1)}, bf16[128,1152]{1,0:T(8,128)(2,1)S(1)}, u32[]{:S(2)}, u32[]{:S(2)}) %collective-permute-start.5) | collective-permute-done | bytes 294944 | tf_op jit(solution)/shard_map/ppermute | solution.py:62
  44.5 0.5 collective-permute-start.14
  45.1 0.6 collective-permute-start.11
  45.7 1.5 %collective-permute-start.10 = (bf16[128,1152]{1,0:T(8,128)(2,1)S(1)}, bf16[128,1152]{1,0:T(8,128)(2,1)S(1)}, u32[]{:S(2)}, u32[]{:S(2)}) collective-permute-start(bf16[128,1152]{1,0:T(8,128)(2,1)S(1)} %collective-permute-done.5.refs_1_), channel_id=1, source_target_pairs={{0,1},{1,0},{2,3},{3,2},{4,5},{5,4},{6,7},{7,6},{8,9},{9,8},{10,11... | collective-permute-start | bytes 884744 | tf_op jit(solution)/shard_map/ppermute | solution.py:62
  47.2 1.0 %copy-done.2 = bf16[128,1536]{1,0:T(8,128)(2,1)S(1)} copy-done((bf16[128,1536]{1,0:T(8,128)(2,1)S(1)}, bf16[128,1536]{1,0:T(8,128)(2,1)}, u32[]{:S(2)}) %copy-start.2) | copy-done | bytes 393240
  48.2 1.0 %copy-done.3 = bf16[128,1536]{1,0:T(8,128)(2,1)S(1)} copy-done((bf16[128,1536]{1,0:T(8,128)(2,1)S(1)}, bf16[128,1536]{1,0:T(8,128)(2,1)}, u32[]{:S(2)}) %copy-start.3) | copy-done | bytes 393240
  49.2 4.2 %teacher_targets.1.refs_12_ = f32[512,1024]{1,0:T(8,128)S(1)} custom-call(bf16[128,1536]{1,0:T(8,128)(2,1)S(1)} %copy-done.2, bf16[128,1536]{1,0:T(8,128)(2,1)S(1)} %collective-permute-done.refs_1_, bf16[128,2688]{1,0:T(8,128)(2,1)S(1)} %collective-permute-done.2.refs_2_, bf16[128,1536]{1,0:T(8,128)(2,1)S(1)} %collective-permute-done.7.refs_3_, ...), custom_call_target="tpu_custom_call" | custom-call | flops 1610612736 | bytes 6815744 | tf_op jit(solution)/shard_map/teacher_targets/pallas_call | solution.py:154
  53.4 1.1 %collective-permute-done.11.refs_7_ = bf16[128,1152]{1,0:T(8,128)(2,1)S(1)} collective-permute-done((bf16[128,1152]{1,0:T(8,128)(2,1)S(1)}, bf16[128,1152]{1,0:T(8,128)(2,1)S(1)}, u32[]{:S(2)}, u32[]{:S(2)}) %collective-permute-start.11) | collective-permute-done | bytes 294944 | tf_op jit(solution)/shard_map/ppermute | solution.py:62
  54.7 1.3 %collective-permute-done.15.refs_11_ = bf16[128,1152]{1,0:T(8,128)(2,1)S(1)} collective-permute-done((bf16[128,1152]{1,0:T(8,128)(2,1)S(1)}, bf16[128,1152]{1,0:T(8,128)(2,1)S(1)}, u32[]{:S(2)}, u32[]{:S(2)}) %collective-permute-start.15) | collective-permute-done | bytes 294944 | tf_op jit(solution)/shard_map/ppermute | solution.py:62
  56.0 5.4 %pair_and_sent.1 = (bf16[512,1024]{1,0:T(8,128)(2,1)S(1)}, bf16[512,1152]{1,0:T(8,128)(2,1)S(1)}, bf16[1024,1152]{1,0:T(8,128)(2,1)S(1)}, bf16[128,1152]{1,0:T(8...) custom-call(bf16[128,1152]{1,0:T(8,128)(2,1)S(1)} %copy-done.4, ...), custom_call_target="tpu_custom_call" | custom-call | flops 2415919104 | bytes 7733248 | tf_op jit(solution)/shard_map/pair_and_sent/pallas_call | solution.py:217
  61.7 1.5 %collective-permute-start.19 = (bf16[128,1152]{1,0:T(8,128)(2,1)S(1)}, bf16[128,1152]{1,0:T(8,128)(2,1)S(1)}, u32[]{:S(2)}, u32[]{:S(2)}) collective-permute-start(bf16[128,1152]{1,0:T(8,128)(2,1)S(1)} %get-tuple-element.58), channel_id=1, source_target_pairs={{0,1},{1,0},{2,3},{3,2},{4,5},{5,4},{6,7},{7,6},{8,9},{9,8},{10,11... | collective-permute-start | bytes 884744 | tf_op jit(solution)/shard_map/ppermute | solution.py:62
  63.2 1.6 %kept.1 = (f32[128,1152]{1,0:T(8,128)S(1)}, f32[128,1152]{1,0:T(8,128)S(1)}, f32[128,1152]{1,0:T(8,128)S(1)}, f32[128,1152]{1,0:T(8,128)S(1)}, f32[128,1152]{1,0:T(8,128)S(1)}, /*index=5*/f32[128,1152]{1,0:T(8,128)S(1)}) custom-call(bf16[512,1024]{1,0:T(8,128)(2,1)S(1)} %get-tuple-element.49.pair_ref, bf16[512,1152]{1,0:T(8,128)(2,1)S(1)} %get-tuple-element.50.img, ...), custom_call_target="tpu_custom_call" | custom-call | flops 1207959552 | bytes 8126464 | tf_op jit(solution)/shard_map/kept/pallas_call | solution.py:247
  64.9 0.7 collective-permute-start.17
  65.6 5.3 %collective-permute-done.19 = bf16[128,1152]{1,0:T(8,128)(2,1)S(1)} collective-permute-done((bf16[128,1152]{1,0:T(8,128)(2,1)S(1)}, bf16[128,1152]{1,0:T(8,128)(2,1)S(1)}, u32[]{:S(2)}, u32[]{:S(2)}) %collective-permute-start.19) | collective-permute-done | bytes 294944 | tf_op jit(solution)/shard_map/ppermute | solution.py:62
  71.0 0.7 collective-permute-start.20
  71.7 2.7 %collective-permute-done.17 = bf16[128,1152]{1,0:T(8,128)(2,1)S(1)} collective-permute-done((bf16[128,1152]{1,0:T(8,128)(2,1)S(1)}, bf16[128,1152]{1,0:T(8,128)(2,1)S(1)}, u32[]{:S(2)}, u32[]{:S(2)}) %collective-permute-start.17) | collective-permute-done | bytes 294944 | tf_op jit(solution)/shard_map/ppermute | solution.py:62
  74.4 0.5 collective-permute-start.18
  74.9 0.6 collective-permute-start.22
  75.7 10.2 %collective-permute-done.20.refs_3_ = bf16[128,1152]{1,0:T(8,128)(2,1)S(1)} collective-permute-done((bf16[128,1152]{1,0:T(8,128)(2,1)S(1)}, bf16[128,1152]{1,0:T(8,128)(2,1)S(1)}, u32[]{:S(2)}, u32[]{:S(2)}) %collective-permute-start.20) | collective-permute-done | bytes 294944 | tf_op jit(solution)/shard_map/ppermute | solution.py:62
  85.9 1.2 %final.2 = f32[128,1152]{1,0:T(8,128)} custom-call(bf16[128,1152]{1,0:T(8,128)(2,1)S(1)} %copy-done, f32[128,1152]{1,0:T(8,128)S(1)} %get-tuple-element.52.refs_1_, bf16[128,1152]{1,0:T(8,128)(2,1)S(1)} %collective-permute-done.18.refs_2_, bf16[128,1152]{1,0:T(8,128)(2,1)S(1)} %collective-permute-done.20.refs_3_), custom_call_target="tpu_custom_call" | custom-call | flops 1474560 | bytes 1769472 | tf_op jit(solution)/shard_map/final/pallas_call | solution.py:279
  87.0 2.9 %collective-permute-done.23.refs_3_ = bf16[128,1152]{1,0:T(8,128)(2,1)S(1)} collective-permute-done((bf16[128,1152]{1,0:T(8,128)(2,1)S(1)}, bf16[128,1152]{1,0:T(8,128)(2,1)S(1)}, u32[]{:S(2)}, u32[]{:S(2)}) %collective-permute-start.23) | collective-permute-done | bytes 294944 | tf_op jit(solution)/shard_map/ppermute | solution.py:62
  89.9 1.2 %final.3 = f32[128,1152]{1,0:T(8,128)} custom-call(bf16[128,1152]{1,0:T(8,128)(2,1)S(1)} %copy-done.1, f32[128,1152]{1,0:T(8,128)S(1)} %get-tuple-element.65.refs_1_, bf16[128,1152]{1,0:T(8,128)(2,1)S(1)} %collective-permute-done.22.refs_2_, bf16[128,1152]{1,0:T(8,128)(2,1)S(1)} %collective-permute-done.23.refs_3_), custom_call_target="tpu_custom_call" | custom-call | flops 1474560 | bytes 1769472 | tf_op jit(solution)/shard_map/final/pallas_call | solution.py:279
  (37 shorter events, 1.7 us)
Async XLA Ops:
  3.8 22.0 %collective-permute-start = (bf16[128,1536]{1,0:T(8,128)(2,1)}, bf16[128,1536]{1,0:T(8,128)(2,1)S(1)}, u32[]{:S(2)}, u32[]{:S(2)}) collective-permute-start(bf16[128,1536]{1,0:T(8,128)(2,1)} %get-tuple-element.34.refs_0_), channel_id=1, source_target_pairs={{0,16},{1,17},{2,18},{3,19},{4,20},{5,21},{6,22},{7,23},{8,24},{9,... | collective-permute-start | bytes 1179656 | tf_op jit(solution)/shard_map/ppermute | solution.py:62
  7.9 18.0 %collective-permute-start.1 = (bf16[128,1536]{1,0:T(8,128)(2,1)}, bf16[128,1536]{1,0:T(8,128)(2,1)S(1)}, u32[]{:S(2)}, u32[]{:S(2)}) collective-permute-start(bf16[128,1536]{1,0:T(8,128)(2,1)} %get-tuple-element.35.refs_4_), channel_id=1, source_target_pairs={{0,8},{1,9},{2,10},{3,11},{4,12},{5,13},{6,14},{7,15},{8,0},{9,1},... | collective-permute-start | bytes 1179656 | tf_op jit(solution)/shard_map/ppermute | solution.py:62
  9.5 19.3 %collective-permute-start.4 = (bf16[128,2688]{1,0:T(8,128)(2,1)}, bf16[128,2688]{1,0:T(8,128)(2,1)S(1)}, u32[]{:S(2)}, u32[]{:S(2)}) collective-permute-start(bf16[128,2688]{1,0:T(8,128)(2,1)} %get-tuple-element.37), channel_id=1, source_target_pairs={{0,4},{1,5},{2,6},{3,7},{4,0},{5,1},{6,2},{7,3},{8,12},{9,13},{10,... | collective-permute-start | bytes 2064392 | tf_op jit(solution)/shard_map/ppermute | solution.py:62
  9.5 19.3 %collective-permute-start.3 = (bf16[128,2688]{1,0:T(8,128)(2,1)}, bf16[128,2688]{1,0:T(8,128)(2,1)S(1)}, u32[]{:S(2)}, u32[]{:S(2)}) collective-permute-start(bf16[128,2688]{1,0:T(8,128)(2,1)} %get-tuple-element.37), channel_id=1, source_target_pairs={{0,2},{1,3},{2,0},{3,1},{4,6},{5,7},{6,4},{7,5},{8,10},{9,11},{10,... | collective-permute-start | bytes 2064392 | tf_op jit(solution)/shard_map/ppermute | solution.py:62
  11.0 17.8 %collective-permute-start.2 = (bf16[128,2688]{1,0:T(8,128)(2,1)}, bf16[128,2688]{1,0:T(8,128)(2,1)S(1)}, u32[]{:S(2)}, u32[]{:S(2)}) collective-permute-start(bf16[128,2688]{1,0:T(8,128)(2,1)} %get-tuple-element.36), channel_id=1, source_target_pairs={{0,1},{1,0},{2,3},{3,2},{4,5},{5,4},{6,7},{7,6},{8,9},{9,8},{10,11... | collective-permute-start | bytes 2064392 | tf_op jit(solution)/shard_map/ppermute | solution.py:62
  28.8 15.6 %collective-permute-start.5 = (bf16[128,1152]{1,0:T(8,128)(2,1)}, bf16[128,1152]{1,0:T(8,128)(2,1)S(1)}, u32[]{:S(2)}, u32[]{:S(2)}) collective-permute-start(bf16[128,1152]{1,0:T(8,128)(2,1)} %get-tuple-element.38.refs_0_), channel_id=1, source_target_pairs={{0,16},{1,17},{2,18},{3,19},{4,20},{5,21},{6,22},{7,23},{8,24},{9,... | collective-permute-start | bytes 884744 | tf_op jit(solution)/shard_map/ppermute | solution.py:62
  29.1 15.3 %collective-permute-start.6 = (bf16[128,1152]{1,0:T(8,128)(2,1)}, bf16[128,1152]{1,0:T(8,128)(2,1)S(1)}, u32[]{:S(2)}, u32[]{:S(2)}) collective-permute-start(bf16[128,1152]{1,0:T(8,128)(2,1)} %get-tuple-element.40.refs_4_), channel_id=1, source_target_pairs={{0,8},{1,9},{2,10},{3,11},{4,12},{5,13},{6,14},{7,15},{8,0},{9,1},... | collective-permute-start | bytes 884744 | tf_op jit(solution)/shard_map/ppermute | solution.py:62
  29.8 14.6 %collective-permute-start.7 = (bf16[128,1536]{1,0:T(8,128)(2,1)S(1)}, bf16[128,1536]{1,0:T(8,128)(2,1)S(1)}, u32[]{:S(2)}, u32[]{:S(2)}) collective-permute-start(bf16[128,1536]{1,0:T(8,128)(2,1)S(1)} %collective-permute-done.refs_1_), channel_id=1, source_target_pairs={{0,1},{1,0},{2,3},{3,2},{4,5},{5,4},{6,7},{7,6},{8,9},{9,8},{10,11... | collective-permute-start | bytes 1179656 | tf_op jit(solution)/shard_map/ppermute | solution.py:62
  31.3 13.1 %collective-permute-start.8 = (bf16[128,1536]{1,0:T(8,128)(2,1)S(1)}, bf16[128,1536]{1,0:T(8,128)(2,1)S(1)}, u32[]{:S(2)}, u32[]{:S(2)}) collective-permute-start(bf16[128,1536]{1,0:T(8,128)(2,1)S(1)} %collective-permute-done.1.refs_5_), channel_id=1, source_target_pairs={{0,2},{1,3},{2,0},{3,1},{4,6},{5,7},{6,4},{7,5},{8,10},{9,11},{10,... | collective-permute-start | bytes 1179656 | tf_op jit(solution)/shard_map/ppermute | solution.py:62
  32.8 11.6 %collective-permute-start.9 = (bf16[128,2688]{1,0:T(8,128)(2,1)S(1)}, bf16[128,2688]{1,0:T(8,128)(2,1)S(1)}, u32[]{:S(2)}, u32[]{:S(2)}) collective-permute-start(bf16[128,2688]{1,0:T(8,128)(2,1)S(1)} %collective-permute-done.3.refs_6_), channel_id=1, source_target_pairs={{0,4},{1,5},{2,6},{3,7},{4,0},{5,1},{6,2},{7,3},{8,12},{9,13},{10,... | collective-permute-start | bytes 2064392 | tf_op jit(solution)/shard_map/ppermute | solution.py:62
  44.4 2.7 %collective-permute-start.13 = (bf16[128,1536]{1,0:T(8,128)(2,1)S(1)}, bf16[128,1536]{1,0:T(8,128)(2,1)S(1)}, u32[]{:S(2)}, u32[]{:S(2)}) collective-permute-start(bf16[128,1536]{1,0:T(8,128)(2,1)S(1)} %collective-permute-done.1.refs_5_), channel_id=1, source_target_pairs={{0,4},{1,5},{2,6},{3,7},{4,0},{5,1},{6,2},{7,3},{8,12},{9,13},{10,... | collective-permute-start | bytes 1179656 | tf_op jit(solution)/shard_map/ppermute | solution.py:62
  44.5 2.7 %collective-permute-start.14 = (bf16[128,1536]{1,0:T(8,128)(2,1)S(1)}, bf16[128,1536]{1,0:T(8,128)(2,1)S(1)}, u32[]{:S(2)}, u32[]{:S(2)}) collective-permute-start(bf16[128,1536]{1,0:T(8,128)(2,1)S(1)} %collective-permute-done.8.refs_7_), channel_id=1, source_target_pairs={{0,4},{1,5},{2,6},{3,7},{4,0},{5,1},{6,2},{7,3},{8,12},{9,13},{10,... | collective-permute-start | bytes 1179656 | tf_op jit(solution)/shard_map/ppermute | solution.py:62
  45.0 8.4 %collective-permute-start.12 = (bf16[128,1152]{1,0:T(8,128)(2,1)S(1)}, bf16[128,1152]{1,0:T(8,128)(2,1)S(1)}, u32[]{:S(2)}, u32[]{:S(2)}) collective-permute-start(bf16[128,1152]{1,0:T(8,128)(2,1)S(1)} %collective-permute-done.6.refs_5_), channel_id=1, source_target_pairs={{0,4},{1,5},{2,6},{3,7},{4,0},{5,1},{6,2},{7,3},{8,12},{9,13},{10,... | collective-permute-start | bytes 884744 | tf_op jit(solution)/shard_map/ppermute | solution.py:62
  45.1 9.4 %collective-permute-start.11 = (bf16[128,1152]{1,0:T(8,128)(2,1)S(1)}, bf16[128,1152]{1,0:T(8,128)(2,1)S(1)}, u32[]{:S(2)}, u32[]{:S(2)}) collective-permute-start(bf16[128,1152]{1,0:T(8,128)(2,1)S(1)} %collective-permute-done.6.refs_5_), channel_id=1, source_target_pairs={{0,2},{1,3},{2,0},{3,1},{4,6},{5,7},{6,4},{7,5},{8,10},{9,11},{10,... | collective-permute-start | bytes 884744 | tf_op jit(solution)/shard_map/ppermute | solution.py:62
  45.7 9.1 %collective-permute-start.10 = (bf16[128,1152]{1,0:T(8,128)(2,1)S(1)}, bf16[128,1152]{1,0:T(8,128)(2,1)S(1)}, u32[]{:S(2)}, u32[]{:S(2)}) collective-permute-start(bf16[128,1152]{1,0:T(8,128)(2,1)S(1)} %collective-permute-done.5.refs_1_), channel_id=1, source_target_pairs={{0,1},{1,0},{2,3},{3,2},{4,5},{5,4},{6,7},{7,6},{8,9},{9,8},{10,11... | collective-permute-start | bytes 884744 | tf_op jit(solution)/shard_map/ppermute | solution.py:62
  47.2 1.0 %copy-start.2 = (bf16[128,1536]{1,0:T(8,128)(2,1)S(1)}, bf16[128,1536]{1,0:T(8,128)(2,1)}, u32[]{:S(2)}) copy-start(bf16[128,1536]{1,0:T(8,128)(2,1)} %get-tuple-element.34.refs_0_) | copy-start | bytes 1179652
  48.2 1.0 %copy-start.3 = (bf16[128,1536]{1,0:T(8,128)(2,1)S(1)}, bf16[128,1536]{1,0:T(8,128)(2,1)}, u32[]{:S(2)}) copy-start(bf16[128,1536]{1,0:T(8,128)(2,1)} %get-tuple-element.35.refs_4_) | copy-start | bytes 1179652
  49.2 6.9 %copy-start.4 = (bf16[128,1152]{1,0:T(8,128)(2,1)S(1)}, bf16[128,1152]{1,0:T(8,128)(2,1)}, u32[]{:S(2)}) copy-start(bf16[128,1152]{1,0:T(8,128)(2,1)} %get-tuple-element.38.refs_0_) | copy-start | bytes 884740
  49.2 6.9 %copy-start.5 = (bf16[128,1152]{1,0:T(8,128)(2,1)S(1)}, bf16[128,1152]{1,0:T(8,128)(2,1)}, u32[]{:S(2)}) copy-start(bf16[128,1152]{1,0:T(8,128)(2,1)} %get-tuple-element.40.refs_4_) | copy-start | bytes 884740
  54.4 1.6 %collective-permute-start.15 = (bf16[128,1152]{1,0:T(8,128)(2,1)S(1)}, bf16[128,1152]{1,0:T(8,128)(2,1)S(1)}, u32[]{:S(2)}, u32[]{:S(2)}) collective-permute-start(bf16[128,1152]{1,0:T(8,128)(2,1)S(1)} %collective-permute-done.11.refs_7_), channel_id=1, source_target_pairs={{0,4},{1,5},{2,6},{3,7},{4,0},{5,1},{6,2},{7,3},{8,12},{9,13},{10,... | collective-permute-start | bytes 884744 | tf_op jit(solution)/shard_map/ppermute | solution.py:62
  61.5 3.4 %collective-permute-start.16 = (bf16[256,1152]{1,0:T(8,128)(2,1)S(1)}, bf16[256,1152]{1,0:T(8,128)(2,1)S(1)}, u32[]{:S(2)}, u32[]{:S(2)}) collective-permute-start(bf16[256,1152]{1,0:T(8,128)(2,1)S(1)} %get-tuple-element.55), channel_id=1, source_target_pairs={{0,4},{1,5},{2,6},{3,7},{4,0},{5,1},{6,2},{7,3},{8,12},{9,13},{10,... | collective-permute-start | bytes 1769480 | tf_op jit(solution)/shard_map/ppermute | solution.py:62
  61.7 9.3 %collective-permute-start.19 = (bf16[128,1152]{1,0:T(8,128)(2,1)S(1)}, bf16[128,1152]{1,0:T(8,128)(2,1)S(1)}, u32[]{:S(2)}, u32[]{:S(2)}) collective-permute-start(bf16[128,1152]{1,0:T(8,128)(2,1)S(1)} %get-tuple-element.58), channel_id=1, source_target_pairs={{0,1},{1,0},{2,3},{3,2},{4,5},{5,4},{6,7},{7,6},{8,9},{9,8},{10,11... | collective-permute-start | bytes 884744 | tf_op jit(solution)/shard_map/ppermute | solution.py:62
  63.2 12.3 %collective-permute-start.21 = (bf16[256,1152]{1,0:T(8,128)(2,1)S(1)}, bf16[256,1152]{1,0:T(8,128)(2,1)S(1)}, u32[]{:S(2)}, u32[]{:S(2)}) collective-permute-start(bf16[256,1152]{1,0:T(8,128)(2,1)S(1)} %get-tuple-element.60), channel_id=1, source_target_pairs={{0,4},{1,5},{2,6},{3,7},{4,0},{5,1},{6,2},{7,3},{8,12},{9,13},{10,... | collective-permute-start | bytes 1769480 | tf_op jit(solution)/shard_map/ppermute | solution.py:62
  64.9 21.0 %copy-start = (bf16[128,1152]{1,0:T(8,128)(2,1)S(1)}, bf16[128,1152]{1,0:T(8,128)(2,1)}, u32[]{:S(2)}) copy-start(bf16[128,1152]{1,0:T(8,128)(2,1)} %refs_0_.4) | copy-start | bytes 884740
  64.9 9.4 %collective-permute-start.17 = (bf16[128,1152]{1,0:T(8,128)(2,1)S(1)}, bf16[128,1152]{1,0:T(8,128)(2,1)S(1)}, u32[]{:S(2)}, u32[]{:S(2)}) collective-permute-start(bf16[128,1152]{1,0:T(8,128)(2,1)S(1)} %get-tuple-element.67), channel_id=1, source_target_pairs={{0,2},{1,3},{2,0},{3,1},{4,6},{5,7},{6,4},{7,5},{8,10},{9,11},{10,... | collective-permute-start | bytes 884744 | tf_op jit(solution)/shard_map/ppermute | solution.py:62
  71.0 14.9 %collective-permute-start.20 = (bf16[128,1152]{1,0:T(8,128)(2,1)S(1)}, bf16[128,1152]{1,0:T(8,128)(2,1)S(1)}, u32[]{:S(2)}, u32[]{:S(2)}) collective-permute-start(bf16[128,1152]{1,0:T(8,128)(2,1)S(1)} %add_convert_fusion.2), channel_id=1, source_target_pairs={{0,16},{1,17},{2,18},{3,19},{4,20},{5,21},{6,22},{7,23},{8,24},{9,... | collective-permute-start | bytes 884744 | tf_op jit(solution)/shard_map/ppermute | solution.py:62
  74.4 11.5 %collective-permute-start.18 = (bf16[128,1152]{1,0:T(8,128)(2,1)S(1)}, bf16[128,1152]{1,0:T(8,128)(2,1)S(1)}, u32[]{:S(2)}, u32[]{:S(2)}) collective-permute-start(bf16[128,1152]{1,0:T(8,128)(2,1)S(1)} %get-tuple-element.56), channel_id=1, source_target_pairs={{0,1},{1,0},{2,3},{3,2},{4,5},{5,4},{6,7},{7,6},{8,9},{9,8},{10,11... | collective-permute-start | bytes 884744 | tf_op jit(solution)/shard_map/ppermute | solution.py:62
  74.9 12.1 %collective-permute-start.22 = (bf16[128,1152]{1,0:T(8,128)(2,1)S(1)}, bf16[128,1152]{1,0:T(8,128)(2,1)S(1)}, u32[]{:S(2)}, u32[]{:S(2)}) collective-permute-start(bf16[128,1152]{1,0:T(8,128)(2,1)S(1)} %get-tuple-element.62), channel_id=1, source_target_pairs={{0,2},{1,3},{2,0},{3,1},{4,6},{5,7},{6,4},{7,5},{8,10},{9,11},{10,... | collective-permute-start | bytes 884744 | tf_op jit(solution)/shard_map/ppermute | solution.py:62
  75.5 14.4 %copy-start.1 = (bf16[128,1152]{1,0:T(8,128)(2,1)S(1)}, bf16[128,1152]{1,0:T(8,128)(2,1)}, u32[]{:S(2)}) copy-start(bf16[128,1152]{1,0:T(8,128)(2,1)} %refs_0_.5) | copy-start | bytes 884740
  75.6 14.3 %collective-permute-start.23 = (bf16[128,1152]{1,0:T(8,128)(2,1)S(1)}, bf16[128,1152]{1,0:T(8,128)(2,1)S(1)}, u32[]{:S(2)}, u32[]{:S(2)}) collective-permute-start(bf16[128,1152]{1,0:T(8,128)(2,1)S(1)} %get-tuple-element.64), channel_id=1, source_target_pairs={{0,8},{1,9},{2,10},{3,11},{4,12},{5,13},{6,14},{7,15},{8,0},{9,1},... | collective-permute-start | bytes 884744 | tf_op jit(solution)/shard_map/ppermute | solution.py:62

commit v5 on v4

--- a/solution.py
+++ b/solution.py
@@ -213,7 +213,7 @@
     images, texts = len(img_blocks), len(txt_blocks)
     rows, width = img_blocks[0].shape
     shapes = [jax.ShapeDtypeStruct((images * rows, texts * rows), bf16)]
-    shapes += [jax.ShapeDtypeStruct((n * rows, width), bf16) for n in (images, texts) + img_out + txt_out]
+    shapes += [jax.ShapeDtypeStruct((n, width), bf16) for n in (images * rows, texts * rows) + img_out + txt_out]
     return pl.pallas_call(
         functools.partial(pair_kernel, images, texts, skip, img_first, txt_first, len(img_out)),
         out_shape=shapes,
@@ -223,7 +223,7 @@
         compiler_params=params(
             ((images * rows, texts * rows), 6),
             ((images + texts, rows, width), 2),
-            ((sum(img_out) + sum(txt_out), rows, width), 6),
+            ((sum(img_out) + sum(txt_out), width), 6),
         ),
         cost_estimate=pl.CostEstimate(
             flops=4 * images * texts * rows * rows * width,
@@ -262,29 +262,40 @@
     return out[: len(img_out)], out[len(img_out) :]
 
 
-def final_kernel(parts, *refs):
-    x_ref, part_refs, out_ref = refs[0], refs[1 : 1 + parts], refs[1 + parts]
-    x = x_ref[...].astype(f32)
-    inverse = 1.0 / jnp.sqrt(jnp.sum(x * x, axis=1, keepdims=True) + epsilon)
-    unit = x * inverse
-    grad = part_refs[0][...].astype(f32)
-    for part in part_refs[1:]:
-        grad = grad + part[...].astype(f32)
-    grad = logit_scale * grad
-    along = jnp.sum(unit * grad, axis=1, keepdims=True)
-    out_ref[...] = (grad - unit * along) * inverse
+def final_kernel(counts, *refs):
+    x_ref, out_ref = refs[0], refs[-1]
+    pieces, at = [], 1
+    for count in counts:
+        pieces.append(refs[at : at + count])
+        at += count
+    most = max(counts)
+    step = x_ref.shape[0] // most
+    for k in range(most):
+        rows = slice(k * step, (k + 1) * step)
+        x = x_ref[rows, :].astype(f32)
+        inverse = 1.0 / jnp.sqrt(jnp.sum(x * x, axis=1, keepdims=True) + epsilon)
+        unit = x * inverse
+        grad = None
+        for part in pieces:
+            term = (part[0][rows, :] if len(part) == 1 else part[k][...]).astype(f32)
+            grad = term if grad is None else grad + term
+        grad = logit_scale * grad
+        along = jnp.sum(unit * grad, axis=1, keepdims=True)
+        out_ref[rows, :] = (grad - unit * along) * inverse
 
 
 def final(x, parts):
+    counts = tuple(len(part) for part in parts)
+    operands = [x] + [v for part in parts for v in part]
     return pl.pallas_call(
-        functools.partial(final_kernel, len(parts)),
+        functools.partial(final_kernel, counts),
         out_shape=jax.ShapeDtypeStruct(x.shape, f32),
-        in_specs=[VMEM] * (1 + len(parts)),
+        in_specs=[VMEM] * len(operands),
         out_specs=VMEM,
         compiler_params=params((x.shape, 4 * (4 + len(parts)))),
         cost_estimate=pl.CostEstimate(flops=10 * x.size, bytes_accessed=12 * x.size, transcendentals=0),
         name="final",
-    )(x, *parts)
+    )(*operands)
 
 
 def token_kernel(*refs):
@@ -325,9 +336,10 @@
     b_col = spread(b_img, "col")
     b_row = spread(b_txt, "row")
     b_core = spread(b_txt, "core")
-    first = [token(*t_far.values(), *t_near.values(), flops=10000000000), b_col, b_row, b_core]
-    s_far = spread(s_img, "far", *first)
-    s_near = spread(s_txt, "near", *first)
+    first = [b_col, b_row, b_core]
+    teacher_z = token(*t_far.values(), *t_near.values(), flops=10000000000)
+    s_far = spread(s_img, "far", teacher_z)
+    s_near = spread(s_txt, "near", teacher_z)
     t_far_col = onward(t_far, "col", *first)
     t_near_row = onward(t_near, "row", *first)
     b_row_core = onward(b_row, "core", *first)
@@ -364,51 +376,68 @@
     s_txts = texts(s_txt, s_near, b_row, s_near_row, b_core, s_near_core, b_row_core, s_both_core)
 
     own_txt = row * near
-    img_out = (1,) * (far * (col - 1))
-    txt_out = (near,) * (row * (core - 1))
+    pieces = 1 if rows % (16 * 1) == 0 else 1
+    cut = rows // pieces
+
+    def piece(x, i):
+        return x[i * cut : (i + 1) * cut]
+
+    onward_keys = [(b, a) for b in range(1, col) for a in range(1, far)]
+    last_keys = [(b, 0) for b in range(1, col)]
+    img_out = tuple(n for b in range(1, col) for a in range(far) for n in ((cut,) * pieces if a else (rows,)))
+    txt_out = (near * rows,) * (row * (core - 1))
     skip = teacher_img.shape[1]
     out = pair_and_sent(s_imgs, s_txts, skip, targets, far, img_out, own_txt, txt_out)
     pair, img_pack, txt_pack = out[:3]
-    out = out[3:]
-    img_sent = {(1 + k // far, k % far): v for k, v in enumerate(out[: len(img_out)])}
-    txt_sent = {(1 + k // row, k % row): v for k, v in enumerate(out[len(img_out) :])}
+    img_list, txt_list = list(out[3 : 3 + len(img_out)]), out[3 + len(img_out) :]
+    img_sent = {}
+    for b in range(1, col):
+        for a in range(far):
+            img_sent[b, a] = [img_list.pop(0) for _ in range(pieces if a else 1)]
+    txt_sent = {(1 + k // row, k % row): v for k, v in enumerate(txt_list)}
     img_part, txt_part = some_grads(pair, img_pack, txt_pack, rows, 0, (1,) * far, 0, (1,) * own_txt, f32, "kept")
     txt_part = {divmod(k, near): v for k, v in enumerate(txt_part)}
 
-    img_in = {key: plan.send(v, "col", -key[0]) for key, v in img_sent.items() if key[1]}
+    img_in = {key: [plan.send(v, "col", -key[0]) for v in img_sent[key]] for key in onward_keys}
     txt_in = {key: plan.send(v, "core", -key[0]) for key, v in txt_sent.items()}
 
     for c in range(1, core):
         for b in range(row):
             for a in range(near):
                 txt_part[b, a] = txt_part[b, a] + txt_in[c, b][a * rows : (a + 1) * rows].astype(f32)
-    row_in = {}
+    row_in = {
+        (b, a): [plan.send(piece(txt_part[b, a], i).astype(bf16), "row", -b) for i in range(pieces)]
+        for b in range(1, row)
+        for a in range(1, near)
+    }
+
+    def summed(own, arrived, i):
+        total = piece(own, i)
+        for v in arrived:
+            total = total + v[i].astype(f32)
+        return total.astype(bf16)
+
+    txt_ready = [
+        [summed(txt_part[0, a], [row_in[b, a] for b in range(1, row)], i) for i in range(pieces)]
+        for a in range(1, near)
+    ]
+    txt_last = [[plan.send(v, "near", -a) for v in part] for a, part in zip(range(1, near), txt_ready)]
+    img_last = [
+        [
+            plan.send(summed(img_part[a], [img_in[b, a] for b in range(1, col)], i), "far", -a)
+            for i in range(pieces)
+        ]
+        for a in range(1, far)
+    ]
+    col_ahead = list(txt_in.values())
+    row_ahead = [v for key in onward_keys for v in img_in[key]]
+    for key in last_keys:
+        img_in[key] = [plan.send(after(img_sent[key][0], *col_ahead), "col", -key[0])]
     for b in range(1, row):
-        for a in range(1, near):
-            row_in[b, a] = plan.send(txt_part[b, a].astype(bf16), "row", -b)
-    ahead = list(row_in.values())
-    for b in range(1, row):
-        row_in[b, 0] = plan.send(after(txt_part[b, 0].astype(bf16), *ahead), "row", -b)
-    for b in range(1, col):
-        img_in[b, 0] = plan.send(after(img_sent[b, 0], *ahead), "col", -b)
-
-    def img_sum(a):
-        total = img_part[a]
-        for b in range(1, col):
-            total = total + img_in[b, a].astype(f32)
-        return total
-
-    img_last = [plan.send(img_sum(a).astype(bf16), "far", -a) for a in range(1, far)]
-    image_grad = final(student_img, [img_part[0]] + [img_in[b, 0] for b in range(1, col)] + img_last)
-
-    def txt_sum(a):
-        total = txt_part[0, a]
-        for b in range(1, row):
-            total = total + row_in[b, a].astype(f32)
-        return total
-
-    txt_last = [plan.send(txt_sum(a).astype(bf16), "near", -a) for a in range(1, near)]
-    text_grad = final(student_txt, [txt_part[0, 0]] + [row_in[b, 0] for b in range(1, row)] + txt_last)
+        row_in[b, 0] = [plan.send(after(txt_part[b, 0].astype(bf16), *row_ahead), "row", -b)]
+    img_own, txt_own = img_part[0], txt_part[0, 0]
+    image_grad = final(student_img, [[img_own]] + [img_in[b, 0] for b in range(1, col)] + img_last)
+    text_grad = final(student_txt, [[txt_own]] + [row_in[b, 0] for b in range(1, row)] + txt_last)
     return image_grad, text_grad
 
 

time: 91.3 us -> 88.1 us (0.965)
  waiting for transfers between devices: 51.6 us -> 39.3 us
  starting transfers between devices: 19.8 us -> 29 us
    ppermute x24, waiting for transfers between devices: 51.6 us -> 39.3 us  [send(): return lax.ppermute(x, AXES, pairs)]
    ppermute x24, starting transfers between devices: 19.8 us -> 29 us  [send(): return lax.ppermute(x, AXES, pairs)]
  transfers between devices with their start and end apart: 24 -> 24, of which waited for: 11 -> 10; matrix products, arithmetic and copies ran while one was open for 0% -> 0% of each run, Pallas kernels for 8% -> 8%
where the time goes in v5:
time: 88.1 us; the launch traced here: 87.9 us
  waiting for transfers between devices  39.3 us (45%)
  starting transfers between devices  29 us (33%)
  Pallas kernels  16.6 us (19%)
  local copies, waits for them, and re-layouts  2.01 us (2%)
    ppermute x24, waiting for transfers between devices, send(): return lax.ppermute(x, AXES, pairs)  39.3 us
    ppermute x24, starting transfers between devices, send(): return lax.ppermute(x, AXES, pairs)  29 us
    pallas_call x1, Pallas kernels, pair_and_sent(): pl.pallas_call(functools.partial(pair_kernel, images, texts, skip, img_fi...  5.42 us
    pallas_call x1, Pallas kernels, teacher_targets(): pl.pallas_call(functools.partial(teacher_kernel, images, texts), out_shap...  4.19 us
    pallas_call x1, Pallas kernels, unit_rows(): pl.pallas_call(functools.partial(unit_kernel, len(arrays)), out_shape=[ja...  3.13 us
    pallas_call x2, Pallas kernels, final(): pl.pallas_call(functools.partial(final_kernel, counts), out_shape=jax.Sha...  2.31 us
    unnamed x12, local copies, waits for them, and re-layouts  2.01 us
  transfers between devices with their start and end apart: 24, of which 10 were waited for; matrix products, arithmetic and copies ran while one was open for 0% of the time, Pallas kernels for 8%

profile of v5, /device:TPU:0, one launch (start us, length us, event | category | flops | bytes accessed | tf_op | source)
XLA Modules:
  0.0 87.9 jit_solution(13193715990515623697)
XLA Ops:
  0.6 3.1 %unit_rows.1 = (bf16[128,1536]{1,0:T(8,128)(2,1)}, bf16[128,1536]{1,0:T(8,128)(2,1)}, bf16[128,1152]{1,0:T(8,128)(2,1)}, bf16[128,1152]{1,0:T(8,128)(2,1)}, bf16...) custom-call(bf16[128,1536]{1,0:T(8,128)(2,1)} %refs_0_.3, bf16[128,1536]{1,0:T(8,128)(2,1)} %refs_1_.1, ...), custom_call_target="tpu_custom_call" | custom-call | flops 2752512 | bytes 4128768 | tf_op jit(solution)/shard_map/unit_rows/pallas_call | solution.py:107
  3.8 4.1 %collective-permute-start = (bf16[128,1536]{1,0:T(8,128)(2,1)}, bf16[128,1536]{1,0:T(8,128)(2,1)S(1)}, u32[]{:S(2)}, u32[]{:S(2)}) collective-permute-start(bf16[128,1536]{1,0:T(8,128)(2,1)} %get-tuple-element.34.refs_0_), channel_id=1, source_target_pairs={{0,16},{1,17},{2,18},{3,19},{4,20},{5,21},{6,22},{7,23},{8,24},{9,... | collective-permute-start | bytes 1179656 | tf_op jit(solution)/shard_map/ppermute | solution.py:62
  7.9 1.6 %collective-permute-start.1 = (bf16[128,1536]{1,0:T(8,128)(2,1)}, bf16[128,1536]{1,0:T(8,128)(2,1)S(1)}, u32[]{:S(2)}, u32[]{:S(2)}) collective-permute-start(bf16[128,1536]{1,0:T(8,128)(2,1)} %get-tuple-element.35.refs_4_), channel_id=1, source_target_pairs={{0,8},{1,9},{2,10},{3,11},{4,12},{5,13},{6,14},{7,15},{8,0},{9,1},... | collective-permute-start | bytes 1179656 | tf_op jit(solution)/shard_map/ppermute | solution.py:62
  9.5 1.5 %collective-permute-start.5 = (bf16[128,2688]{1,0:T(8,128)(2,1)}, bf16[128,2688]{1,0:T(8,128)(2,1)S(1)}, u32[]{:S(2)}, u32[]{:S(2)}) collective-permute-start(bf16[128,2688]{1,0:T(8,128)(2,1)} %get-tuple-element.40), channel_id=1, source_target_pairs={{0,2},{1,3},{2,0},{3,1},{4,6},{5,7},{6,4},{7,5},{8,10},{9,11},{10,... | collective-permute-start | bytes 2064392 | tf_op jit(solution)/shard_map/ppermute | solution.py:62
  11.0 1.5 %collective-permute-start.3 = (bf16[128,2688]{1,0:T(8,128)(2,1)}, bf16[128,2688]{1,0:T(8,128)(2,1)S(1)}, u32[]{:S(2)}, u32[]{:S(2)}) collective-permute-start(bf16[128,2688]{1,0:T(8,128)(2,1)} %get-tuple-element.37), channel_id=1, source_target_pairs={{0,1},{1,0},{2,3},{3,2},{4,5},{5,4},{6,7},{7,6},{8,9},{9,8},{10,11... | collective-permute-start | bytes 2064392 | tf_op jit(solution)/shard_map/ppermute | solution.py:62
  12.5 13.3 %collective-permute-done.refs_1_ = bf16[128,1536]{1,0:T(8,128)(2,1)S(1)} collective-permute-done((bf16[128,1536]{1,0:T(8,128)(2,1)}, bf16[128,1536]{1,0:T(8,128)(2,1)S(1)}, u32[]{:S(2)}, u32[]{:S(2)}) %collective-permute-start) | collective-permute-done | bytes 393248 | tf_op jit(solution)/shard_map/ppermute | solution.py:62
  25.9 1.4 %collective-permute-start.2 = (bf16[128,1152]{1,0:T(8,128)(2,1)}, bf16[128,1152]{1,0:T(8,128)(2,1)S(1)}, u32[]{:S(2)}, u32[]{:S(2)}) collective-permute-start(bf16[128,1152]{1,0:T(8,128)(2,1)} %get-tuple-element.36.refs_0_), channel_id=1, source_target_pairs={{0,16},{1,17},{2,18},{3,19},{4,20},{5,21},{6,22},{7,23},{8,24},{9,... | collective-permute-start | bytes 884744 | tf_op jit(solution)/shard_map/ppermute | solution.py:62
  27.3 2.4 %collective-permute-start.4 = (bf16[128,1152]{1,0:T(8,128)(2,1)}, bf16[128,1152]{1,0:T(8,128)(2,1)S(1)}, u32[]{:S(2)}, u32[]{:S(2)}) collective-permute-start(bf16[128,1152]{1,0:T(8,128)(2,1)} %get-tuple-element.39.refs_4_), channel_id=1, source_target_pairs={{0,8},{1,9},{2,10},{3,11},{4,12},{5,13},{6,14},{7,15},{8,0},{9,1},... | collective-permute-start | bytes 884744 | tf_op jit(solution)/shard_map/ppermute | solution.py:62
  29.7 1.6 %collective-permute-start.7 = (bf16[128,1536]{1,0:T(8,128)(2,1)S(1)}, bf16[128,1536]{1,0:T(8,128)(2,1)S(1)}, u32[]{:S(2)}, u32[]{:S(2)}) collective-permute-start(bf16[128,1536]{1,0:T(8,128)(2,1)S(1)} %collective-permute-done.refs_1_), channel_id=1, source_target_pairs={{0,1},{1,0},{2,3},{3,2},{4,5},{5,4},{6,7},{7,6},{8,9},{9,8},{10,11... | collective-permute-start | bytes 1179656 | tf_op jit(solution)/shard_map/ppermute | solution.py:62
  31.3 1.5 %collective-permute-start.8 = (bf16[128,1536]{1,0:T(8,128)(2,1)S(1)}, bf16[128,1536]{1,0:T(8,128)(2,1)S(1)}, u32[]{:S(2)}, u32[]{:S(2)}) collective-permute-start(bf16[128,1536]{1,0:T(8,128)(2,1)S(1)} %collective-permute-done.1.refs_5_), channel_id=1, source_target_pairs={{0,2},{1,3},{2,0},{3,1},{4,6},{5,7},{6,4},{7,5},{8,10},{9,11},{10,... | collective-permute-start | bytes 1179656 | tf_op jit(solution)/shard_map/ppermute | solution.py:62
  32.8 8.6 %collective-permute-done.2.refs_1_ = bf16[128,1152]{1,0:T(8,128)(2,1)S(1)} collective-permute-done((bf16[128,1152]{1,0:T(8,128)(2,1)}, bf16[128,1152]{1,0:T(8,128)(2,1)S(1)}, u32[]{:S(2)}, u32[]{:S(2)}) %collective-permute-start.2) | collective-permute-done | bytes 294944 | tf_op jit(solution)/shard_map/ppermute | solution.py:62
  41.6 0.5 collective-permute-start.14
  42.1 1.4 %collective-permute-start.11 = (bf16[128,1152]{1,0:T(8,128)(2,1)S(1)}, bf16[128,1152]{1,0:T(8,128)(2,1)S(1)}, u32[]{:S(2)}, u32[]{:S(2)}) collective-permute-start(bf16[128,1152]{1,0:T(8,128)(2,1)S(1)} %collective-permute-done.4.refs_5_), channel_id=1, source_target_pairs={{0,2},{1,3},{2,0},{3,1},{4,6},{5,7},{6,4},{7,5},{8,10},{9,11},{10,... | collective-permute-start | bytes 884744 | tf_op jit(solution)/shard_map/ppermute | solution.py:62
  43.5 1.4 %collective-permute-start.10 = (bf16[128,1152]{1,0:T(8,128)(2,1)S(1)}, bf16[128,1152]{1,0:T(8,128)(2,1)S(1)}, u32[]{:S(2)}, u32[]{:S(2)}) collective-permute-start(bf16[128,1152]{1,0:T(8,128)(2,1)S(1)} %collective-permute-done.2.refs_1_), channel_id=1, source_target_pairs={{0,1},{1,0},{2,3},{3,2},{4,5},{5,4},{6,7},{7,6},{8,9},{9,8},{10,11... | collective-permute-start | bytes 884744 | tf_op jit(solution)/shard_map/ppermute | solution.py:62
  44.9 1.0 %copy-done.2 = bf16[128,1536]{1,0:T(8,128)(2,1)S(1)} copy-done((bf16[128,1536]{1,0:T(8,128)(2,1)S(1)}, bf16[128,1536]{1,0:T(8,128)(2,1)}, u32[]{:S(2)}) %copy-start.2) | copy-done | bytes 393240
  45.9 1.0 %copy-done.3 = bf16[128,1536]{1,0:T(8,128)(2,1)S(1)} copy-done((bf16[128,1536]{1,0:T(8,128)(2,1)S(1)}, bf16[128,1536]{1,0:T(8,128)(2,1)}, u32[]{:S(2)}) %copy-start.3) | copy-done | bytes 393240
  46.9 4.2 %teacher_targets.1.refs_12_ = f32[512,1024]{1,0:T(8,128)S(1)} custom-call(bf16[128,1536]{1,0:T(8,128)(2,1)S(1)} %copy-done.2, bf16[128,1536]{1,0:T(8,128)(2,1)S(1)} %collective-permute-done.refs_1_, bf16[128,2688]{1,0:T(8,128)(2,1)S(1)} %collective-permute-done.3.refs_2_, bf16[128,1536]{1,0:T(8,128)(2,1)S(1)} %collective-permute-done.7.refs_3_, ...), custom_call_target="tpu_custom_call" | custom-call | flops 1610612736 | bytes 6815744 | tf_op jit(solution)/shard_map/teacher_targets/pallas_call | solution.py:154
  51.5 1.2 %collective-permute-done.10.refs_3_ = bf16[128,1152]{1,0:T(8,128)(2,1)S(1)} collective-permute-done((bf16[128,1152]{1,0:T(8,128)(2,1)S(1)}, bf16[128,1152]{1,0:T(8,128)(2,1)S(1)}, u32[]{:S(2)}, u32[]{:S(2)}) %collective-permute-start.10) | collective-permute-done | bytes 294944 | tf_op jit(solution)/shard_map/ppermute | solution.py:62
  52.7 0.4 collective-permute-done.15.refs_11_
  53.1 5.4 %pair_and_sent.1 = (bf16[512,1024]{1,0:T(8,128)(2,1)S(1)}, bf16[512,1152]{1,0:T(8,128)(2,1)S(1)}, bf16[1024,1152]{1,0:T(8,128)(2,1)S(1)}, bf16[128,1152]{1,0:T(8...) custom-call(bf16[128,1152]{1,0:T(8,128)(2,1)S(1)} %copy-done.4, ...), custom_call_target="tpu_custom_call" | custom-call | flops 2415919104 | bytes 7733248 | tf_op jit(solution)/shard_map/pair_and_sent/pallas_call | solution.py:217
  58.7 1.3 %collective-permute-start.19 = (bf16[128,1152]{1,0:T(8,128)(2,1)S(1)}, bf16[128,1152]{1,0:T(8,128)(2,1)S(1)}, u32[]{:S(2)}, u32[]{:S(2)}) collective-permute-start(bf16[128,1152]{1,0:T(8,128)(2,1)S(1)} %get-tuple-element.58), channel_id=1, source_target_pairs={{0,1},{1,0},{2,3},{3,2},{4,5},{5,4},{6,7},{7,6},{8,9},{9,8},{10,11... | collective-permute-start | bytes 884744 | tf_op jit(solution)/shard_map/ppermute | solution.py:62
  60.1 1.6 %kept.1 = (f32[128,1152]{1,0:T(8,128)S(1)}, f32[128,1152]{1,0:T(8,128)S(1)}, f32[128,1152]{1,0:T(8,128)S(1)}, f32[128,1152]{1,0:T(8,128)S(1)}, f32[128,1152]{1,0:T(8,128)S(1)}, /*index=5*/f32[128,1152]{1,0:T(8,128)S(1)}) custom-call(bf16[512,1024]{1,0:T(8,128)(2,1)S(1)} %get-tuple-element.49.pair_ref, bf16[512,1152]{1,0:T(8,128)(2,1)S(1)} %get-tuple-element.50.img, ...), custom_call_target="tpu_custom_call" | custom-call | flops 1207959552 | bytes 8126464 | tf_op jit(solution)/shard_map/kept/pallas_call | solution.py:247
  61.8 1.6 %collective-permute-start.22 = (bf16[128,1152]{1,0:T(8,128)(2,1)S(1)}, bf16[128,1152]{1,0:T(8,128)(2,1)S(1)}, u32[]{:S(2)}, u32[]{:S(2)}) collective-permute-start(bf16[128,1152]{1,0:T(8,128)(2,1)S(1)} %get-tuple-element.66), channel_id=1, source_target_pairs={{0,2},{1,3},{2,0},{3,1},{4,6},{5,7},{6,4},{7,5},{8,10},{9,11},{10,... | collective-permute-start | bytes 884744 | tf_op jit(solution)/shard_map/ppermute | solution.py:62
  63.3 4.7 %collective-permute-done.19 = bf16[128,1152]{1,0:T(8,128)(2,1)S(1)} collective-permute-done((bf16[128,1152]{1,0:T(8,128)(2,1)S(1)}, bf16[128,1152]{1,0:T(8,128)(2,1)S(1)}, u32[]{:S(2)}, u32[]{:S(2)}) %collective-permute-start.19) | collective-permute-done | bytes 294944 | tf_op jit(solution)/shard_map/ppermute | solution.py:62
  68.1 2.1 %collective-permute-start.20 = (bf16[128,1152]{1,0:T(8,128)(2,1)S(1)}, bf16[128,1152]{1,0:T(8,128)(2,1)S(1)}, u32[]{:S(2)}, u32[]{:S(2)}) collective-permute-start(bf16[128,1152]{1,0:T(8,128)(2,1)S(1)} %add_convert_fusion.3), channel_id=1, source_target_pairs={{0,16},{1,17},{2,18},{3,19},{4,20},{5,21},{6,22},{7,23},{8,24},{9,... | collective-permute-start | bytes 884744 | tf_op jit(solution)/shard_map/ppermute | solution.py:62
  70.2 1.5 %collective-permute-start.18 = (bf16[128,1152]{1,0:T(8,128)(2,1)S(1)}, bf16[128,1152]{1,0:T(8,128)(2,1)S(1)}, u32[]{:S(2)}, u32[]{:S(2)}) collective-permute-start(bf16[128,1152]{1,0:T(8,128)(2,1)S(1)} %get-tuple-element.56), channel_id=1, source_target_pairs={{0,1},{1,0},{2,3},{3,2},{4,5},{5,4},{6,7},{7,6},{8,9},{9,8},{10,11... | collective-permute-start | bytes 884744 | tf_op jit(solution)/shard_map/ppermute | solution.py:62
  71.6 1.5 %collective-permute-start.21 = (bf16[128,1152]{1,0:T(8,128)(2,1)S(1)}, bf16[128,1152]{1,0:T(8,128)(2,1)S(1)}, u32[]{:S(2)}, u32[]{:S(2)}) collective-permute-start(bf16[128,1152]{1,0:T(8,128)(2,1)S(1)} %get-tuple-element.61), channel_id=1, source_target_pairs={{0,2},{1,3},{2,0},{3,1},{4,6},{5,7},{6,4},{7,5},{8,10},{9,11},{10,... | collective-permute-start | bytes 884744 | tf_op jit(solution)/shard_map/ppermute | solution.py:62
  73.3 1.8 %collective-permute-start.23 = (bf16[128,1152]{1,0:T(8,128)(2,1)S(1)}, bf16[128,1152]{1,0:T(8,128)(2,1)S(1)}, u32[]{:S(2)}, u32[]{:S(2)}) collective-permute-start(bf16[128,1152]{1,0:T(8,128)(2,1)S(1)} %get-tuple-element.64), channel_id=1, source_target_pairs={{0,8},{1,9},{2,10},{3,11},{4,12},{5,13},{6,14},{7,15},{8,0},{9,1},... | collective-permute-start | bytes 884744 | tf_op jit(solution)/shard_map/ppermute | solution.py:62
  75.1 8.9 %collective-permute-done.20.refs_3_ = bf16[128,1152]{1,0:T(8,128)(2,1)S(1)} collective-permute-done((bf16[128,1152]{1,0:T(8,128)(2,1)S(1)}, bf16[128,1152]{1,0:T(8,128)(2,1)S(1)}, u32[]{:S(2)}, u32[]{:S(2)}) %collective-permute-start.20) | collective-permute-done | bytes 294944 | tf_op jit(solution)/shard_map/ppermute | solution.py:62
  83.9 1.2 %final.2 = f32[128,1152]{1,0:T(8,128)} custom-call(bf16[128,1152]{1,0:T(8,128)(2,1)S(1)} %copy-done, f32[128,1152]{1,0:T(8,128)S(1)} %get-tuple-element.52.refs_1_, bf16[128,1152]{1,0:T(8,128)(2,1)S(1)} %collective-permute-done.18.refs_2_, bf16[128,1152]{1,0:T(8,128)(2,1)S(1)} %collective-permute-done.20.refs_3_), custom_call_target="tpu_custom_call" | custom-call | flops 1474560 | bytes 1769472 | tf_op jit(solution)/shard_map/final/pallas_call | solution.py:290
  85.1 1.6 %collective-permute-done.23.refs_3_ = bf16[128,1152]{1,0:T(8,128)(2,1)S(1)} collective-permute-done((bf16[128,1152]{1,0:T(8,128)(2,1)S(1)}, bf16[128,1152]{1,0:T(8,128)(2,1)S(1)}, u32[]{:S(2)}, u32[]{:S(2)}) %collective-permute-start.23) | collective-permute-done | bytes 294944 | tf_op jit(solution)/shard_map/ppermute | solution.py:62
  86.7 1.2 %final.3 = f32[128,1152]{1,0:T(8,128)} custom-call(bf16[128,1152]{1,0:T(8,128)(2,1)S(1)} %copy-done.1, f32[128,1152]{1,0:T(8,128)S(1)} %get-tuple-element.65.refs_1_, bf16[128,1152]{1,0:T(8,128)(2,1)S(1)} %collective-permute-done.21.refs_2_, bf16[128,1152]{1,0:T(8,128)(2,1)S(1)} %collective-permute-done.23.refs_3_), custom_call_target="tpu_custom_call" | custom-call | flops 1474560 | bytes 1769472 | tf_op jit(solution)/shard_map/final/pallas_call | solution.py:290
  (37 shorter events, 1.4 us)
Async XLA Ops:
  3.8 22.0 %collective-permute-start = (bf16[128,1536]{1,0:T(8,128)(2,1)}, bf16[128,1536]{1,0:T(8,128)(2,1)S(1)}, u32[]{:S(2)}, u32[]{:S(2)}) collective-permute-start(bf16[128,1536]{1,0:T(8,128)(2,1)} %get-tuple-element.34.refs_0_), channel_id=1, source_target_pairs={{0,16},{1,17},{2,18},{3,19},{4,20},{5,21},{6,22},{7,23},{8,24},{9,... | collective-permute-start | bytes 1179656 | tf_op jit(solution)/shard_map/ppermute | solution.py:62
  7.9 18.0 %collective-permute-start.1 = (bf16[128,1536]{1,0:T(8,128)(2,1)}, bf16[128,1536]{1,0:T(8,128)(2,1)S(1)}, u32[]{:S(2)}, u32[]{:S(2)}) collective-permute-start(bf16[128,1536]{1,0:T(8,128)(2,1)} %get-tuple-element.35.refs_4_), channel_id=1, source_target_pairs={{0,8},{1,9},{2,10},{3,11},{4,12},{5,13},{6,14},{7,15},{8,0},{9,1},... | collective-permute-start | bytes 1179656 | tf_op jit(solution)/shard_map/ppermute | solution.py:62
  9.5 20.3 %collective-permute-start.6 = (bf16[128,2688]{1,0:T(8,128)(2,1)}, bf16[128,2688]{1,0:T(8,128)(2,1)S(1)}, u32[]{:S(2)}, u32[]{:S(2)}) collective-permute-start(bf16[128,2688]{1,0:T(8,128)(2,1)} %get-tuple-element.40), channel_id=1, source_target_pairs={{0,4},{1,5},{2,6},{3,7},{4,0},{5,1},{6,2},{7,3},{8,12},{9,13},{10,... | collective-permute-start | bytes 2064392 | tf_op jit(solution)/shard_map/ppermute | solution.py:62
  9.5 20.3 %collective-permute-start.5 = (bf16[128,2688]{1,0:T(8,128)(2,1)}, bf16[128,2688]{1,0:T(8,128)(2,1)S(1)}, u32[]{:S(2)}, u32[]{:S(2)}) collective-permute-start(bf16[128,2688]{1,0:T(8,128)(2,1)} %get-tuple-element.40), channel_id=1, source_target_pairs={{0,2},{1,3},{2,0},{3,1},{4,6},{5,7},{6,4},{7,5},{8,10},{9,11},{10,... | collective-permute-start | bytes 2064392 | tf_op jit(solution)/shard_map/ppermute | solution.py:62
  11.0 18.8 %collective-permute-start.3 = (bf16[128,2688]{1,0:T(8,128)(2,1)}, bf16[128,2688]{1,0:T(8,128)(2,1)S(1)}, u32[]{:S(2)}, u32[]{:S(2)}) collective-permute-start(bf16[128,2688]{1,0:T(8,128)(2,1)} %get-tuple-element.37), channel_id=1, source_target_pairs={{0,1},{1,0},{2,3},{3,2},{4,5},{5,4},{6,7},{7,6},{8,9},{9,8},{10,11... | collective-permute-start | bytes 2064392 | tf_op jit(solution)/shard_map/ppermute | solution.py:62
  25.9 15.5 %collective-permute-start.2 = (bf16[128,1152]{1,0:T(8,128)(2,1)}, bf16[128,1152]{1,0:T(8,128)(2,1)S(1)}, u32[]{:S(2)}, u32[]{:S(2)}) collective-permute-start(bf16[128,1152]{1,0:T(8,128)(2,1)} %get-tuple-element.36.refs_0_), channel_id=1, source_target_pairs={{0,16},{1,17},{2,18},{3,19},{4,20},{5,21},{6,22},{7,23},{8,24},{9,... | collective-permute-start | bytes 884744 | tf_op jit(solution)/shard_map/ppermute | solution.py:62
  27.3 14.2 %collective-permute-start.4 = (bf16[128,1152]{1,0:T(8,128)(2,1)}, bf16[128,1152]{1,0:T(8,128)(2,1)S(1)}, u32[]{:S(2)}, u32[]{:S(2)}) collective-permute-start(bf16[128,1152]{1,0:T(8,128)(2,1)} %get-tuple-element.39.refs_4_), channel_id=1, source_target_pairs={{0,8},{1,9},{2,10},{3,11},{4,12},{5,13},{6,14},{7,15},{8,0},{9,1},... | collective-permute-start | bytes 884744 | tf_op jit(solution)/shard_map/ppermute | solution.py:62
  29.7 11.7 %collective-permute-start.7 = (bf16[128,1536]{1,0:T(8,128)(2,1)S(1)}, bf16[128,1536]{1,0:T(8,128)(2,1)S(1)}, u32[]{:S(2)}, u32[]{:S(2)}) collective-permute-start(bf16[128,1536]{1,0:T(8,128)(2,1)S(1)} %collective-permute-done.refs_1_), channel_id=1, source_target_pairs={{0,1},{1,0},{2,3},{3,2},{4,5},{5,4},{6,7},{7,6},{8,9},{9,8},{10,11... | collective-permute-start | bytes 1179656 | tf_op jit(solution)/shard_map/ppermute | solution.py:62
  31.3 10.2 %collective-permute-start.8 = (bf16[128,1536]{1,0:T(8,128)(2,1)S(1)}, bf16[128,1536]{1,0:T(8,128)(2,1)S(1)}, u32[]{:S(2)}, u32[]{:S(2)}) collective-permute-start(bf16[128,1536]{1,0:T(8,128)(2,1)S(1)} %collective-permute-done.1.refs_5_), channel_id=1, source_target_pairs={{0,2},{1,3},{2,0},{3,1},{4,6},{5,7},{6,4},{7,5},{8,10},{9,11},{10,... | collective-permute-start | bytes 1179656 | tf_op jit(solution)/shard_map/ppermute | solution.py:62
  32.8 8.7 %collective-permute-start.9 = (bf16[128,2688]{1,0:T(8,128)(2,1)S(1)}, bf16[128,2688]{1,0:T(8,128)(2,1)S(1)}, u32[]{:S(2)}, u32[]{:S(2)}) collective-permute-start(bf16[128,2688]{1,0:T(8,128)(2,1)S(1)} %collective-permute-done.5.refs_6_), channel_id=1, source_target_pairs={{0,4},{1,5},{2,6},{3,7},{4,0},{5,1},{6,2},{7,3},{8,12},{9,13},{10,... | collective-permute-start | bytes 2064392 | tf_op jit(solution)/shard_map/ppermute | solution.py:62
  41.5 3.4 %collective-permute-start.13 = (bf16[128,1536]{1,0:T(8,128)(2,1)S(1)}, bf16[128,1536]{1,0:T(8,128)(2,1)S(1)}, u32[]{:S(2)}, u32[]{:S(2)}) collective-permute-start(bf16[128,1536]{1,0:T(8,128)(2,1)S(1)} %collective-permute-done.1.refs_5_), channel_id=1, source_target_pairs={{0,4},{1,5},{2,6},{3,7},{4,0},{5,1},{6,2},{7,3},{8,12},{9,13},{10,... | collective-permute-start | bytes 1179656 | tf_op jit(solution)/shard_map/ppermute | solution.py:62
  41.6 3.3 %collective-permute-start.14 = (bf16[128,1536]{1,0:T(8,128)(2,1)S(1)}, bf16[128,1536]{1,0:T(8,128)(2,1)S(1)}, u32[]{:S(2)}, u32[]{:S(2)}) collective-permute-start(bf16[128,1536]{1,0:T(8,128)(2,1)S(1)} %collective-permute-done.8.refs_7_), channel_id=1, source_target_pairs={{0,4},{1,5},{2,6},{3,7},{4,0},{5,1},{6,2},{7,3},{8,12},{9,13},{10,... | collective-permute-start | bytes 1179656 | tf_op jit(solution)/shard_map/ppermute | solution.py:62
  42.1 9.1 %collective-permute-start.12 = (bf16[128,1152]{1,0:T(8,128)(2,1)S(1)}, bf16[128,1152]{1,0:T(8,128)(2,1)S(1)}, u32[]{:S(2)}, u32[]{:S(2)}) collective-permute-start(bf16[128,1152]{1,0:T(8,128)(2,1)S(1)} %collective-permute-done.4.refs_5_), channel_id=1, source_target_pairs={{0,4},{1,5},{2,6},{3,7},{4,0},{5,1},{6,2},{7,3},{8,12},{9,13},{10,... | collective-permute-start | bytes 884744 | tf_op jit(solution)/shard_map/ppermute | solution.py:62
  42.1 9.4 %collective-permute-start.11 = (bf16[128,1152]{1,0:T(8,128)(2,1)S(1)}, bf16[128,1152]{1,0:T(8,128)(2,1)S(1)}, u32[]{:S(2)}, u32[]{:S(2)}) collective-permute-start(bf16[128,1152]{1,0:T(8,128)(2,1)S(1)} %collective-permute-done.4.refs_5_), channel_id=1, source_target_pairs={{0,2},{1,3},{2,0},{3,1},{4,6},{5,7},{6,4},{7,5},{8,10},{9,11},{10,... | collective-permute-start | bytes 884744 | tf_op jit(solution)/shard_map/ppermute | solution.py:62
  43.5 9.1 %collective-permute-start.10 = (bf16[128,1152]{1,0:T(8,128)(2,1)S(1)}, bf16[128,1152]{1,0:T(8,128)(2,1)S(1)}, u32[]{:S(2)}, u32[]{:S(2)}) collective-permute-start(bf16[128,1152]{1,0:T(8,128)(2,1)S(1)} %collective-permute-done.2.refs_1_), channel_id=1, source_target_pairs={{0,1},{1,0},{2,3},{3,2},{4,5},{5,4},{6,7},{7,6},{8,9},{9,8},{10,11... | collective-permute-start | bytes 884744 | tf_op jit(solution)/shard_map/ppermute | solution.py:62
  44.9 1.0 %copy-start.2 = (bf16[128,1536]{1,0:T(8,128)(2,1)S(1)}, bf16[128,1536]{1,0:T(8,128)(2,1)}, u32[]{:S(2)}) copy-start(bf16[128,1536]{1,0:T(8,128)(2,1)} %get-tuple-element.34.refs_0_) | copy-start | bytes 1179652
  45.9 1.0 %copy-start.3 = (bf16[128,1536]{1,0:T(8,128)(2,1)S(1)}, bf16[128,1536]{1,0:T(8,128)(2,1)}, u32[]{:S(2)}) copy-start(bf16[128,1536]{1,0:T(8,128)(2,1)} %get-tuple-element.35.refs_4_) | copy-start | bytes 1179652
  46.9 6.2 %copy-start.4 = (bf16[128,1152]{1,0:T(8,128)(2,1)S(1)}, bf16[128,1152]{1,0:T(8,128)(2,1)}, u32[]{:S(2)}) copy-start(bf16[128,1152]{1,0:T(8,128)(2,1)} %get-tuple-element.36.refs_0_) | copy-start | bytes 884740
  46.9 6.2 %copy-start.5 = (bf16[128,1152]{1,0:T(8,128)(2,1)S(1)}, bf16[128,1152]{1,0:T(8,128)(2,1)}, u32[]{:S(2)}) copy-start(bf16[128,1152]{1,0:T(8,128)(2,1)} %get-tuple-element.39.refs_4_) | copy-start | bytes 884740
  51.5 1.6 %collective-permute-start.15 = (bf16[128,1152]{1,0:T(8,128)(2,1)S(1)}, bf16[128,1152]{1,0:T(8,128)(2,1)S(1)}, u32[]{:S(2)}, u32[]{:S(2)}) collective-permute-start(bf16[128,1152]{1,0:T(8,128)(2,1)S(1)} %collective-permute-done.11.refs_7_), channel_id=1, source_target_pairs={{0,4},{1,5},{2,6},{3,7},{4,0},{5,1},{6,2},{7,3},{8,12},{9,13},{10,... | collective-permute-start | bytes 884744 | tf_op jit(solution)/shard_map/ppermute | solution.py:62
  58.5 3.1 %collective-permute-start.17 = (bf16[256,1152]{1,0:T(8,128)(2,1)S(1)}, bf16[256,1152]{1,0:T(8,128)(2,1)S(1)}, u32[]{:S(2)}, u32[]{:S(2)}) collective-permute-start(bf16[256,1152]{1,0:T(8,128)(2,1)S(1)} %get-tuple-element.55), channel_id=1, source_target_pairs={{0,4},{1,5},{2,6},{3,7},{4,0},{5,1},{6,2},{7,3},{8,12},{9,13},{10,... | collective-permute-start | bytes 1769480 | tf_op jit(solution)/shard_map/ppermute | solution.py:62
  58.7 9.3 %collective-permute-start.19 = (bf16[128,1152]{1,0:T(8,128)(2,1)S(1)}, bf16[128,1152]{1,0:T(8,128)(2,1)S(1)}, u32[]{:S(2)}, u32[]{:S(2)}) collective-permute-start(bf16[128,1152]{1,0:T(8,128)(2,1)S(1)} %get-tuple-element.58), channel_id=1, source_target_pairs={{0,1},{1,0},{2,3},{3,2},{4,5},{5,4},{6,7},{7,6},{8,9},{9,8},{10,11... | collective-permute-start | bytes 884744 | tf_op jit(solution)/shard_map/ppermute | solution.py:62
  60.0 10.2 %collective-permute-start.16 = (bf16[256,1152]{1,0:T(8,128)(2,1)S(1)}, bf16[256,1152]{1,0:T(8,128)(2,1)S(1)}, u32[]{:S(2)}, u32[]{:S(2)}) collective-permute-start(bf16[256,1152]{1,0:T(8,128)(2,1)S(1)} %get-tuple-element.54), channel_id=1, source_target_pairs={{0,4},{1,5},{2,6},{3,7},{4,0},{5,1},{6,2},{7,3},{8,12},{9,13},{10,... | collective-permute-start | bytes 1769480 | tf_op jit(solution)/shard_map/ppermute | solution.py:62
  61.8 22.2 %copy-start = (bf16[128,1152]{1,0:T(8,128)(2,1)S(1)}, bf16[128,1152]{1,0:T(8,128)(2,1)}, u32[]{:S(2)}) copy-start(bf16[128,1152]{1,0:T(8,128)(2,1)} %refs_0_.4) | copy-start | bytes 884740
  61.8 11.4 %collective-permute-start.22 = (bf16[128,1152]{1,0:T(8,128)(2,1)S(1)}, bf16[128,1152]{1,0:T(8,128)(2,1)S(1)}, u32[]{:S(2)}, u32[]{:S(2)}) collective-permute-start(bf16[128,1152]{1,0:T(8,128)(2,1)S(1)} %get-tuple-element.66), channel_id=1, source_target_pairs={{0,2},{1,3},{2,0},{3,1},{4,6},{5,7},{6,4},{7,5},{8,10},{9,11},{10,... | collective-permute-start | bytes 884744 | tf_op jit(solution)/shard_map/ppermute | solution.py:62
  68.1 15.9 %collective-permute-start.20 = (bf16[128,1152]{1,0:T(8,128)(2,1)S(1)}, bf16[128,1152]{1,0:T(8,128)(2,1)S(1)}, u32[]{:S(2)}, u32[]{:S(2)}) collective-permute-start(bf16[128,1152]{1,0:T(8,128)(2,1)S(1)} %add_convert_fusion.3), channel_id=1, source_target_pairs={{0,16},{1,17},{2,18},{3,19},{4,20},{5,21},{6,22},{7,23},{8,24},{9,... | collective-permute-start | bytes 884744 | tf_op jit(solution)/shard_map/ppermute | solution.py:62
  70.2 13.8 %collective-permute-start.18 = (bf16[128,1152]{1,0:T(8,128)(2,1)S(1)}, bf16[128,1152]{1,0:T(8,128)(2,1)S(1)}, u32[]{:S(2)}, u32[]{:S(2)}) collective-permute-start(bf16[128,1152]{1,0:T(8,128)(2,1)S(1)} %get-tuple-element.56), channel_id=1, source_target_pairs={{0,1},{1,0},{2,3},{3,2},{4,5},{5,4},{6,7},{7,6},{8,9},{9,8},{10,11... | collective-permute-start | bytes 884744 | tf_op jit(solution)/shard_map/ppermute | solution.py:62
  71.6 13.4 %collective-permute-start.21 = (bf16[128,1152]{1,0:T(8,128)(2,1)S(1)}, bf16[128,1152]{1,0:T(8,128)(2,1)S(1)}, u32[]{:S(2)}, u32[]{:S(2)}) collective-permute-start(bf16[128,1152]{1,0:T(8,128)(2,1)S(1)} %get-tuple-element.61), channel_id=1, source_target_pairs={{0,2},{1,3},{2,0},{3,1},{4,6},{5,7},{6,4},{7,5},{8,10},{9,11},{10,... | collective-permute-start | bytes 884744 | tf_op jit(solution)/shard_map/ppermute | solution.py:62
  73.2 13.5 %copy-start.1 = (bf16[128,1152]{1,0:T(8,128)(2,1)S(1)}, bf16[128,1152]{1,0:T(8,128)(2,1)}, u32[]{:S(2)}) copy-start(bf16[128,1152]{1,0:T(8,128)(2,1)} %refs_0_.5) | copy-start | bytes 884740
  73.3 13.4 %collective-permute-start.23 = (bf16[128,1152]{1,0:T(8,128)(2,1)S(1)}, bf16[128,1152]{1,0:T(8,128)(2,1)S(1)}, u32[]{:S(2)}, u32[]{:S(2)}) collective-permute-start(bf16[128,1152]{1,0:T(8,128)(2,1)S(1)} %get-tuple-element.64), channel_id=1, source_target_pairs={{0,8},{1,9},{2,10},{3,11},{4,12},{5,13},{6,14},{7,15},{8,0},{9,1},... | collective-permute-start | bytes 884744 | tf_op jit(solution)/shard_map/ppermute | solution.py:62

commit v6 on v5

--- a/solution.py
+++ b/solution.py
@@ -112,7 +112,7 @@
         out_specs=[VMEM] * (len(arrays) + half),
         scratch_shapes=[pltpu.VMEM(a.shape, bf16) for a in arrays]
         + [pltpu.SemaphoreType.DMA((len(arrays),))],
-        compiler_params=pltpu.CompilerParams(vmem_limit_bytes=60 * 2**20),
+        compiler_params=pltpu.CompilerParams(vmem_limit_bytes=int(60 * 2**20)),
         cost_estimate=pl.CostEstimate(
             flops=4 * sum(a.size for a in arrays),
             bytes_accessed=6 * sum(a.size for a in arrays),
@@ -122,19 +122,19 @@
     )(*arrays)
 
 
+def pack(refs, target, columns):
+    rows, width = refs[0].shape[0], target.shape[1]
+    for k, ref in enumerate(refs):
+        first = columns if ref.shape[1] != width else 0
+        target[k * rows : (k + 1) * rows, :] = ref[:, first : first + width]
+
+
 def teacher_kernel(images, texts, *refs):
     img_refs, txt_refs = refs[:images], refs[images : images + texts]
-    p_ref, img, txt, sems = refs[images + texts :]
+    p_ref, img, txt = refs[images + texts :]
     rows = img_refs[0].shape[0]
-    copies = load_all(
-        img_refs + txt_refs,
-        [img.at[pl.ds(k * rows, rows), :] for k in range(images)]
-        + [txt.at[pl.ds(k * rows, rows), :] for k in range(texts)],
-        sems,
-        0,
-    )
-    for copy in copies:
-        copy.wait()
+    pack(img_refs, img, 0)
+    pack(txt_refs, txt, 0)
     step = tile_rows(texts * rows, 256)
 
     def one(j, carry):
@@ -154,14 +154,13 @@
     return pl.pallas_call(
         functools.partial(teacher_kernel, images, texts),
         out_shape=jax.ShapeDtypeStruct((images * rows, texts * rows), f32),
-        in_specs=[ANY] * (images + texts),
+        in_specs=[VMEM] * (images + texts),
         out_specs=VMEM,
         scratch_shapes=[
             pltpu.VMEM((images * rows, width), bf16),
             pltpu.VMEM((texts * rows, width), bf16),
-            pltpu.SemaphoreType.DMA((images + texts,)),
         ],
-        compiler_params=params(((images + texts, rows, width), 2), ((images, rows, texts, rows), 4)),
+        compiler_params=params(((images + texts, rows, width), 2), ((images, rows, texts, rows), 4), *[(v.shape, 2) for v in (*img_blocks, *txt_blocks)]),
         cost_estimate=pl.CostEstimate(
             flops=2 * images * texts * rows * rows * width,
             bytes_accessed=2 * (images + texts) * rows * width + 4 * images * texts * rows * rows,
@@ -185,21 +184,12 @@
 def pair_kernel(images, texts, skip, img_first, txt_first, img_count, *refs):
     img_refs, txt_refs = refs[:images], refs[images : images + texts]
     p_ref, pair_ref, img, txt = refs[images + texts : images + texts + 4]
-    grads, sems = refs[images + texts + 4 : -1], refs[-1]
+    grads = refs[images + texts + 4 :]
     rows = img_refs[0].shape[0]
-    copies = load_all(
-        img_refs + txt_refs,
-        [img.at[pl.ds(k * rows, rows), :] for k in range(images)]
-        + [txt.at[pl.ds(k * rows, rows), :] for k in range(texts)],
-        sems,
-        skip,
-    )
-    for copy in copies[:images]:
-        copy.wait()
+    pack(img_refs, img, skip)
+    pack(txt_refs, txt, skip)
     step = tile_rows(texts * rows, 256)
     for j in range(texts * rows // step):
-        for copy in copies[images + j * step // rows : images + (j + 1) * step // rows]:
-            copy.wait()
         at = slice(j * step, (j + 1) * step)
         dots = lax.dot_general(img[...], txt[at, :], (((1,), (1,)), ((), ())), preferred_element_type=f32)
         pair_ref[:, at] = (2.0 * jax.nn.sigmoid(logit_scale * dots + logit_bias) - p_ref[:, at]).astype(bf16)
@@ -217,12 +207,12 @@
     return pl.pallas_call(
         functools.partial(pair_kernel, images, texts, skip, img_first, txt_first, len(img_out)),
         out_shape=shapes,
-        in_specs=[ANY] * (images + texts) + [VMEM],
+        in_specs=[VMEM] * (images + texts + 1),
         out_specs=[VMEM] * len(shapes),
-        scratch_shapes=[pltpu.SemaphoreType.DMA((images + texts,))],
         compiler_params=params(
             ((images * rows, texts * rows), 6),
             ((images + texts, rows, width), 2),
+            *[(v.shape, 2) for v in (*img_blocks, *txt_blocks)],
             ((sum(img_out) + sum(txt_out), width), 6),
         ),
         cost_estimate=pl.CostEstimate(

time: 88.1 us -> 85.7 us (0.973)
  Pallas kernels: 16.6 us -> 12.9 us
  waiting for transfers between devices: 39.3 us -> 40.7 us
    pallas_call x1, Pallas kernels: 5.42 us -> 3.09 us  [pair_and_sent(): pl.pallas_call(functools.partial(pair_kernel, images, texts, skip, img_fi...]
    pallas_call x1, Pallas kernels: 4.19 us -> 2.78 us  [teacher_targets(): pl.pallas_call(functools.partial(teacher_kernel, images, texts), out_shap...]
    ppermute x24, waiting for transfers between devices: 39.3 us -> 40.7 us  [send(): return lax.ppermute(x, AXES, pairs)]
  transfers between devices with their start and end apart: 24 -> 24, of which waited for: 10 -> 10; matrix products, arithmetic and copies ran while one was open for 0% -> 0% of each run, Pallas kernels for 8% -> 6%
where the time goes in v6:
time: 85.7 us; the launch traced here: 85.5 us
  waiting for transfers between devices  40.7 us (47%)
  starting transfers between devices  29 us (34%)
  Pallas kernels  12.9 us (15%)
  local copies, waits for them, and re-layouts  2.01 us (2%)
    ppermute x24, waiting for transfers between devices, send(): return lax.ppermute(x, AXES, pairs)  40.7 us
    ppermute x24, starting transfers between devices, send(): return lax.ppermute(x, AXES, pairs)  29 us
    pallas_call x1, Pallas kernels, unit_rows(): pl.pallas_call(functools.partial(unit_kernel, len(arrays)), out_shape=[ja...  3.13 us
    pallas_call x1, Pallas kernels, pair_and_sent(): pl.pallas_call(functools.partial(pair_kernel, images, texts, skip, img_fi...  3.09 us
    pallas_call x1, Pallas kernels, teacher_targets(): pl.pallas_call(functools.partial(teacher_kernel, images, texts), out_shap...  2.78 us
    pallas_call x2, Pallas kernels, final(): pl.pallas_call(functools.partial(final_kernel, counts), out_shape=jax.Sha...  2.31 us
    unnamed x12, local copies, waits for them, and re-layouts  2.01 us
  transfers between devices with their start and end apart: 24, of which 10 were waited for; matrix products, arithmetic and copies ran while one was open for 0% of the time, Pallas kernels for 6%

profile of v6, /device:TPU:0, one launch (start us, length us, event | category | flops | bytes accessed | tf_op | source)
XLA Modules:
  0.0 85.5 jit_solution(15667533582540587491)
XLA Ops:
  0.6 3.1 %unit_rows.1 = (bf16[128,1536]{1,0:T(8,128)(2,1)}, bf16[128,1536]{1,0:T(8,128)(2,1)}, bf16[128,1152]{1,0:T(8,128)(2,1)}, bf16[128,1152]{1,0:T(8,128)(2,1)}, bf16...) custom-call(bf16[128,1536]{1,0:T(8,128)(2,1)} %refs_0_.3, bf16[128,1536]{1,0:T(8,128)(2,1)} %refs_1_.1, ...), custom_call_target="tpu_custom_call" | custom-call | flops 2752512 | bytes 4128768 | tf_op jit(solution)/shard_map/unit_rows/pallas_call | solution.py:107
  3.8 4.1 %collective-permute-start = (bf16[128,1536]{1,0:T(8,128)(2,1)}, bf16[128,1536]{1,0:T(8,128)(2,1)S(1)}, u32[]{:S(2)}, u32[]{:S(2)}) collective-permute-start(bf16[128,1536]{1,0:T(8,128)(2,1)} %get-tuple-element.34.refs_0_), channel_id=1, source_target_pairs={{0,16},{1,17},{2,18},{3,19},{4,20},{5,21},{6,22},{7,23},{8,24},{9,... | collective-permute-start | bytes 1179656 | tf_op jit(solution)/shard_map/ppermute | solution.py:62
  7.9 1.6 %collective-permute-start.1 = (bf16[128,1536]{1,0:T(8,128)(2,1)}, bf16[128,1536]{1,0:T(8,128)(2,1)S(1)}, u32[]{:S(2)}, u32[]{:S(2)}) collective-permute-start(bf16[128,1536]{1,0:T(8,128)(2,1)} %get-tuple-element.35.refs_4_), channel_id=1, source_target_pairs={{0,8},{1,9},{2,10},{3,11},{4,12},{5,13},{6,14},{7,15},{8,0},{9,1},... | collective-permute-start | bytes 1179656 | tf_op jit(solution)/shard_map/ppermute | solution.py:62
  9.5 1.5 %collective-permute-start.5 = (bf16[128,2688]{1,0:T(8,128)(2,1)}, bf16[128,2688]{1,0:T(8,128)(2,1)S(1)}, u32[]{:S(2)}, u32[]{:S(2)}) collective-permute-start(bf16[128,2688]{1,0:T(8,128)(2,1)} %get-tuple-element.40), channel_id=1, source_target_pairs={{0,2},{1,3},{2,0},{3,1},{4,6},{5,7},{6,4},{7,5},{8,10},{9,11},{10,... | collective-permute-start | bytes 2064392 | tf_op jit(solution)/shard_map/ppermute | solution.py:62
  11.0 1.5 %collective-permute-start.3 = (bf16[128,2688]{1,0:T(8,128)(2,1)}, bf16[128,2688]{1,0:T(8,128)(2,1)S(1)}, u32[]{:S(2)}, u32[]{:S(2)}) collective-permute-start(bf16[128,2688]{1,0:T(8,128)(2,1)} %get-tuple-element.37), channel_id=1, source_target_pairs={{0,1},{1,0},{2,3},{3,2},{4,5},{5,4},{6,7},{7,6},{8,9},{9,8},{10,11... | collective-permute-start | bytes 2064392 | tf_op jit(solution)/shard_map/ppermute | solution.py:62
  12.5 13.3 %collective-permute-done.refs_1_ = bf16[128,1536]{1,0:T(8,128)(2,1)S(1)} collective-permute-done((bf16[128,1536]{1,0:T(8,128)(2,1)}, bf16[128,1536]{1,0:T(8,128)(2,1)S(1)}, u32[]{:S(2)}, u32[]{:S(2)}) %collective-permute-start) | collective-permute-done | bytes 393248 | tf_op jit(solution)/shard_map/ppermute | solution.py:62
  25.9 1.4 %collective-permute-start.2 = (bf16[128,1152]{1,0:T(8,128)(2,1)}, bf16[128,1152]{1,0:T(8,128)(2,1)S(1)}, u32[]{:S(2)}, u32[]{:S(2)}) collective-permute-start(bf16[128,1152]{1,0:T(8,128)(2,1)} %get-tuple-element.36.refs_0_), channel_id=1, source_target_pairs={{0,16},{1,17},{2,18},{3,19},{4,20},{5,21},{6,22},{7,23},{8,24},{9,... | collective-permute-start | bytes 884744 | tf_op jit(solution)/shard_map/ppermute | solution.py:62
  27.3 2.4 %collective-permute-start.4 = (bf16[128,1152]{1,0:T(8,128)(2,1)}, bf16[128,1152]{1,0:T(8,128)(2,1)S(1)}, u32[]{:S(2)}, u32[]{:S(2)}) collective-permute-start(bf16[128,1152]{1,0:T(8,128)(2,1)} %get-tuple-element.39.refs_4_), channel_id=1, source_target_pairs={{0,8},{1,9},{2,10},{3,11},{4,12},{5,13},{6,14},{7,15},{8,0},{9,1},... | collective-permute-start | bytes 884744 | tf_op jit(solution)/shard_map/ppermute | solution.py:62
  29.7 1.6 %collective-permute-start.7 = (bf16[128,1536]{1,0:T(8,128)(2,1)S(1)}, bf16[128,1536]{1,0:T(8,128)(2,1)S(1)}, u32[]{:S(2)}, u32[]{:S(2)}) collective-permute-start(bf16[128,1536]{1,0:T(8,128)(2,1)S(1)} %collective-permute-done.refs_1_), channel_id=1, source_target_pairs={{0,1},{1,0},{2,3},{3,2},{4,5},{5,4},{6,7},{7,6},{8,9},{9,8},{10,11... | collective-permute-start | bytes 1179656 | tf_op jit(solution)/shard_map/ppermute | solution.py:62
  31.3 1.5 %collective-permute-start.8 = (bf16[128,1536]{1,0:T(8,128)(2,1)S(1)}, bf16[128,1536]{1,0:T(8,128)(2,1)S(1)}, u32[]{:S(2)}, u32[]{:S(2)}) collective-permute-start(bf16[128,1536]{1,0:T(8,128)(2,1)S(1)} %collective-permute-done.1.refs_5_), channel_id=1, source_target_pairs={{0,2},{1,3},{2,0},{3,1},{4,6},{5,7},{6,4},{7,5},{8,10},{9,11},{10,... | collective-permute-start | bytes 1179656 | tf_op jit(solution)/shard_map/ppermute | solution.py:62
  32.8 8.6 %collective-permute-done.2.refs_1_ = bf16[128,1152]{1,0:T(8,128)(2,1)S(1)} collective-permute-done((bf16[128,1152]{1,0:T(8,128)(2,1)}, bf16[128,1152]{1,0:T(8,128)(2,1)S(1)}, u32[]{:S(2)}, u32[]{:S(2)}) %collective-permute-start.2) | collective-permute-done | bytes 294944 | tf_op jit(solution)/shard_map/ppermute | solution.py:62
  41.6 0.5 collective-permute-start.14
  42.1 1.4 %collective-permute-start.11 = (bf16[128,1152]{1,0:T(8,128)(2,1)S(1)}, bf16[128,1152]{1,0:T(8,128)(2,1)S(1)}, u32[]{:S(2)}, u32[]{:S(2)}) collective-permute-start(bf16[128,1152]{1,0:T(8,128)(2,1)S(1)} %collective-permute-done.4.refs_5_), channel_id=1, source_target_pairs={{0,2},{1,3},{2,0},{3,1},{4,6},{5,7},{6,4},{7,5},{8,10},{9,11},{10,... | collective-permute-start | bytes 884744 | tf_op jit(solution)/shard_map/ppermute | solution.py:62
  43.5 1.4 %collective-permute-start.10 = (bf16[128,1152]{1,0:T(8,128)(2,1)S(1)}, bf16[128,1152]{1,0:T(8,128)(2,1)S(1)}, u32[]{:S(2)}, u32[]{:S(2)}) collective-permute-start(bf16[128,1152]{1,0:T(8,128)(2,1)S(1)} %collective-permute-done.2.refs_1_), channel_id=1, source_target_pairs={{0,1},{1,0},{2,3},{3,2},{4,5},{5,4},{6,7},{7,6},{8,9},{9,8},{10,11... | collective-permute-start | bytes 884744 | tf_op jit(solution)/shard_map/ppermute | solution.py:62
  44.9 1.0 %copy-done.2 = bf16[128,1536]{1,0:T(8,128)(2,1)S(1)} copy-done((bf16[128,1536]{1,0:T(8,128)(2,1)S(1)}, bf16[128,1536]{1,0:T(8,128)(2,1)}, u32[]{:S(2)}) %copy-start.2) | copy-done | bytes 393240
  45.9 1.0 %copy-done.3 = bf16[128,1536]{1,0:T(8,128)(2,1)S(1)} copy-done((bf16[128,1536]{1,0:T(8,128)(2,1)S(1)}, bf16[128,1536]{1,0:T(8,128)(2,1)}, u32[]{:S(2)}) %copy-start.3) | copy-done | bytes 393240
  46.9 2.8 %teacher_targets.1.refs_12_ = f32[512,1024]{1,0:T(8,128)S(1)} custom-call(bf16[128,1536]{1,0:T(8,128)(2,1)S(1)} %copy-done.2, bf16[128,1536]{1,0:T(8,128)(2,1)S(1)} %collective-permute-done.refs_1_, bf16[128,2688]{1,0:T(8,128)(2,1)S(1)} %collective-permute-done.3.refs_2_, bf16[128,1536]{1,0:T(8,128)(2,1)S(1)} %collective-permute-done.7.refs_3_, ...), custom_call_target="tpu_custom_call" | custom-call | flops 1610612736 | bytes 6815744 | tf_op jit(solution)/shard_map/teacher_targets/pallas_call | solution.py:154
  49.7 1.8 %collective-permute-done.11.refs_7_ = bf16[128,1152]{1,0:T(8,128)(2,1)S(1)} collective-permute-done((bf16[128,1152]{1,0:T(8,128)(2,1)S(1)}, bf16[128,1152]{1,0:T(8,128)(2,1)S(1)}, u32[]{:S(2)}, u32[]{:S(2)}) %collective-permute-start.11) | collective-permute-done | bytes 294944 | tf_op jit(solution)/shard_map/ppermute | solution.py:62
  51.5 1.2 %collective-permute-done.10.refs_3_ = bf16[128,1152]{1,0:T(8,128)(2,1)S(1)} collective-permute-done((bf16[128,1152]{1,0:T(8,128)(2,1)S(1)}, bf16[128,1152]{1,0:T(8,128)(2,1)S(1)}, u32[]{:S(2)}, u32[]{:S(2)}) %collective-permute-start.10) | collective-permute-done | bytes 294944 | tf_op jit(solution)/shard_map/ppermute | solution.py:62
  53.1 3.1 %pair_and_sent.1 = (bf16[512,1024]{1,0:T(8,128)(2,1)S(1)}, bf16[512,1152]{1,0:T(8,128)(2,1)S(1)}, bf16[1024,1152]{1,0:T(8,128)(2,1)S(1)}, bf16[128,1152]{1,0:T(8...) custom-call(bf16[128,1152]{1,0:T(8,128)(2,1)S(1)} %copy-done.4, ...), custom_call_target="tpu_custom_call" | custom-call | flops 2415919104 | bytes 7733248 | tf_op jit(solution)/shard_map/pair_and_sent/pallas_call | solution.py:207
  56.4 1.3 %collective-permute-start.19 = (bf16[128,1152]{1,0:T(8,128)(2,1)S(1)}, bf16[128,1152]{1,0:T(8,128)(2,1)S(1)}, u32[]{:S(2)}, u32[]{:S(2)}) collective-permute-start(bf16[128,1152]{1,0:T(8,128)(2,1)S(1)} %get-tuple-element.58), channel_id=1, source_target_pairs={{0,1},{1,0},{2,3},{3,2},{4,5},{5,4},{6,7},{7,6},{8,9},{9,8},{10,11... | collective-permute-start | bytes 884744 | tf_op jit(solution)/shard_map/ppermute | solution.py:62
  57.7 1.6 %kept.1 = (f32[128,1152]{1,0:T(8,128)S(1)}, f32[128,1152]{1,0:T(8,128)S(1)}, f32[128,1152]{1,0:T(8,128)S(1)}, f32[128,1152]{1,0:T(8,128)S(1)}, f32[128,1152]{1,0:T(8,128)S(1)}, /*index=5*/f32[128,1152]{1,0:T(8,128)S(1)}) custom-call(bf16[512,1024]{1,0:T(8,128)(2,1)S(1)} %get-tuple-element.49.pair_ref, bf16[512,1152]{1,0:T(8,128)(2,1)S(1)} %get-tuple-element.50.img, ...), custom_call_target="tpu_custom_call" | custom-call | flops 1207959552 | bytes 8126464 | tf_op jit(solution)/shard_map/kept/pallas_call | solution.py:237
  59.4 1.6 %collective-permute-start.22 = (bf16[128,1152]{1,0:T(8,128)(2,1)S(1)}, bf16[128,1152]{1,0:T(8,128)(2,1)S(1)}, u32[]{:S(2)}, u32[]{:S(2)}) collective-permute-start(bf16[128,1152]{1,0:T(8,128)(2,1)S(1)} %get-tuple-element.66), channel_id=1, source_target_pairs={{0,2},{1,3},{2,0},{3,1},{4,6},{5,7},{6,4},{7,5},{8,10},{9,11},{10,... | collective-permute-start | bytes 884744 | tf_op jit(solution)/shard_map/ppermute | solution.py:62
  61.0 4.7 %collective-permute-done.19 = bf16[128,1152]{1,0:T(8,128)(2,1)S(1)} collective-permute-done((bf16[128,1152]{1,0:T(8,128)(2,1)S(1)}, bf16[128,1152]{1,0:T(8,128)(2,1)S(1)}, u32[]{:S(2)}, u32[]{:S(2)}) %collective-permute-start.19) | collective-permute-done | bytes 294944 | tf_op jit(solution)/shard_map/ppermute | solution.py:62
  65.7 2.1 %collective-permute-start.20 = (bf16[128,1152]{1,0:T(8,128)(2,1)S(1)}, bf16[128,1152]{1,0:T(8,128)(2,1)S(1)}, u32[]{:S(2)}, u32[]{:S(2)}) collective-permute-start(bf16[128,1152]{1,0:T(8,128)(2,1)S(1)} %add_convert_fusion.3), channel_id=1, source_target_pairs={{0,16},{1,17},{2,18},{3,19},{4,20},{5,21},{6,22},{7,23},{8,24},{9,... | collective-permute-start | bytes 884744 | tf_op jit(solution)/shard_map/ppermute | solution.py:62
  67.8 1.5 %collective-permute-start.18 = (bf16[128,1152]{1,0:T(8,128)(2,1)S(1)}, bf16[128,1152]{1,0:T(8,128)(2,1)S(1)}, u32[]{:S(2)}, u32[]{:S(2)}) collective-permute-start(bf16[128,1152]{1,0:T(8,128)(2,1)S(1)} %get-tuple-element.56), channel_id=1, source_target_pairs={{0,1},{1,0},{2,3},{3,2},{4,5},{5,4},{6,7},{7,6},{8,9},{9,8},{10,11... | collective-permute-start | bytes 884744 | tf_op jit(solution)/shard_map/ppermute | solution.py:62
  69.3 1.5 %collective-permute-start.21 = (bf16[128,1152]{1,0:T(8,128)(2,1)S(1)}, bf16[128,1152]{1,0:T(8,128)(2,1)S(1)}, u32[]{:S(2)}, u32[]{:S(2)}) collective-permute-start(bf16[128,1152]{1,0:T(8,128)(2,1)S(1)} %get-tuple-element.61), channel_id=1, source_target_pairs={{0,2},{1,3},{2,0},{3,1},{4,6},{5,7},{6,4},{7,5},{8,10},{9,11},{10,... | collective-permute-start | bytes 884744 | tf_op jit(solution)/shard_map/ppermute | solution.py:62
  71.0 1.8 %collective-permute-start.23 = (bf16[128,1152]{1,0:T(8,128)(2,1)S(1)}, bf16[128,1152]{1,0:T(8,128)(2,1)S(1)}, u32[]{:S(2)}, u32[]{:S(2)}) collective-permute-start(bf16[128,1152]{1,0:T(8,128)(2,1)S(1)} %get-tuple-element.64), channel_id=1, source_target_pairs={{0,8},{1,9},{2,10},{3,11},{4,12},{5,13},{6,14},{7,15},{8,0},{9,1},... | collective-permute-start | bytes 884744 | tf_op jit(solution)/shard_map/ppermute | solution.py:62
  72.7 8.9 %collective-permute-done.20.refs_3_ = bf16[128,1152]{1,0:T(8,128)(2,1)S(1)} collective-permute-done((bf16[128,1152]{1,0:T(8,128)(2,1)S(1)}, bf16[128,1152]{1,0:T(8,128)(2,1)S(1)}, u32[]{:S(2)}, u32[]{:S(2)}) %collective-permute-start.20) | collective-permute-done | bytes 294944 | tf_op jit(solution)/shard_map/ppermute | solution.py:62
  81.6 1.2 %final.2 = f32[128,1152]{1,0:T(8,128)} custom-call(bf16[128,1152]{1,0:T(8,128)(2,1)S(1)} %copy-done, f32[128,1152]{1,0:T(8,128)S(1)} %get-tuple-element.52.refs_1_, bf16[128,1152]{1,0:T(8,128)(2,1)S(1)} %collective-permute-done.18.refs_2_, bf16[128,1152]{1,0:T(8,128)(2,1)S(1)} %collective-permute-done.20.refs_3_), custom_call_target="tpu_custom_call" | custom-call | flops 1474560 | bytes 1769472 | tf_op jit(solution)/shard_map/final/pallas_call | solution.py:280
  82.8 1.6 %collective-permute-done.23.refs_3_ = bf16[128,1152]{1,0:T(8,128)(2,1)S(1)} collective-permute-done((bf16[128,1152]{1,0:T(8,128)(2,1)S(1)}, bf16[128,1152]{1,0:T(8,128)(2,1)S(1)}, u32[]{:S(2)}, u32[]{:S(2)}) %collective-permute-start.23) | collective-permute-done | bytes 294944 | tf_op jit(solution)/shard_map/ppermute | solution.py:62
  84.4 1.2 %final.3 = f32[128,1152]{1,0:T(8,128)} custom-call(bf16[128,1152]{1,0:T(8,128)(2,1)S(1)} %copy-done.1, f32[128,1152]{1,0:T(8,128)S(1)} %get-tuple-element.65.refs_1_, bf16[128,1152]{1,0:T(8,128)(2,1)S(1)} %collective-permute-done.21.refs_2_, bf16[128,1152]{1,0:T(8,128)(2,1)S(1)} %collective-permute-done.23.refs_3_), custom_call_target="tpu_custom_call" | custom-call | flops 1474560 | bytes 1769472 | tf_op jit(solution)/shard_map/final/pallas_call | solution.py:280
  (37 shorter events, 1.5 us)
Async XLA Ops:
  3.8 22.0 %collective-permute-start = (bf16[128,1536]{1,0:T(8,128)(2,1)}, bf16[128,1536]{1,0:T(8,128)(2,1)S(1)}, u32[]{:S(2)}, u32[]{:S(2)}) collective-permute-start(bf16[128,1536]{1,0:T(8,128)(2,1)} %get-tuple-element.34.refs_0_), channel_id=1, source_target_pairs={{0,16},{1,17},{2,18},{3,19},{4,20},{5,21},{6,22},{7,23},{8,24},{9,... | collective-permute-start | bytes 1179656 | tf_op jit(solution)/shard_map/ppermute | solution.py:62
  7.9 18.0 %collective-permute-start.1 = (bf16[128,1536]{1,0:T(8,128)(2,1)}, bf16[128,1536]{1,0:T(8,128)(2,1)S(1)}, u32[]{:S(2)}, u32[]{:S(2)}) collective-permute-start(bf16[128,1536]{1,0:T(8,128)(2,1)} %get-tuple-element.35.refs_4_), channel_id=1, source_target_pairs={{0,8},{1,9},{2,10},{3,11},{4,12},{5,13},{6,14},{7,15},{8,0},{9,1},... | collective-permute-start | bytes 1179656 | tf_op jit(solution)/shard_map/ppermute | solution.py:62
  9.5 20.3 %collective-permute-start.6 = (bf16[128,2688]{1,0:T(8,128)(2,1)}, bf16[128,2688]{1,0:T(8,128)(2,1)S(1)}, u32[]{:S(2)}, u32[]{:S(2)}) collective-permute-start(bf16[128,2688]{1,0:T(8,128)(2,1)} %get-tuple-element.40), channel_id=1, source_target_pairs={{0,4},{1,5},{2,6},{3,7},{4,0},{5,1},{6,2},{7,3},{8,12},{9,13},{10,... | collective-permute-start | bytes 2064392 | tf_op jit(solution)/shard_map/ppermute | solution.py:62
  9.5 20.3 %collective-permute-start.5 = (bf16[128,2688]{1,0:T(8,128)(2,1)}, bf16[128,2688]{1,0:T(8,128)(2,1)S(1)}, u32[]{:S(2)}, u32[]{:S(2)}) collective-permute-start(bf16[128,2688]{1,0:T(8,128)(2,1)} %get-tuple-element.40), channel_id=1, source_target_pairs={{0,2},{1,3},{2,0},{3,1},{4,6},{5,7},{6,4},{7,5},{8,10},{9,11},{10,... | collective-permute-start | bytes 2064392 | tf_op jit(solution)/shard_map/ppermute | solution.py:62
  11.0 18.8 %collective-permute-start.3 = (bf16[128,2688]{1,0:T(8,128)(2,1)}, bf16[128,2688]{1,0:T(8,128)(2,1)S(1)}, u32[]{:S(2)}, u32[]{:S(2)}) collective-permute-start(bf16[128,2688]{1,0:T(8,128)(2,1)} %get-tuple-element.37), channel_id=1, source_target_pairs={{0,1},{1,0},{2,3},{3,2},{4,5},{5,4},{6,7},{7,6},{8,9},{9,8},{10,11... | collective-permute-start | bytes 2064392 | tf_op jit(solution)/shard_map/ppermute | solution.py:62
  25.9 15.5 %collective-permute-start.2 = (bf16[128,1152]{1,0:T(8,128)(2,1)}, bf16[128,1152]{1,0:T(8,128)(2,1)S(1)}, u32[]{:S(2)}, u32[]{:S(2)}) collective-permute-start(bf16[128,1152]{1,0:T(8,128)(2,1)} %get-tuple-element.36.refs_0_), channel_id=1, source_target_pairs={{0,16},{1,17},{2,18},{3,19},{4,20},{5,21},{6,22},{7,23},{8,24},{9,... | collective-permute-start | bytes 884744 | tf_op jit(solution)/shard_map/ppermute | solution.py:62
  27.3 14.2 %collective-permute-start.4 = (bf16[128,1152]{1,0:T(8,128)(2,1)}, bf16[128,1152]{1,0:T(8,128)(2,1)S(1)}, u32[]{:S(2)}, u32[]{:S(2)}) collective-permute-start(bf16[128,1152]{1,0:T(8,128)(2,1)} %get-tuple-element.39.refs_4_), channel_id=1, source_target_pairs={{0,8},{1,9},{2,10},{3,11},{4,12},{5,13},{6,14},{7,15},{8,0},{9,1},... | collective-permute-start | bytes 884744 | tf_op jit(solution)/shard_map/ppermute | solution.py:62
  29.7 11.7 %collective-permute-start.7 = (bf16[128,1536]{1,0:T(8,128)(2,1)S(1)}, bf16[128,1536]{1,0:T(8,128)(2,1)S(1)}, u32[]{:S(2)}, u32[]{:S(2)}) collective-permute-start(bf16[128,1536]{1,0:T(8,128)(2,1)S(1)} %collective-permute-done.refs_1_), channel_id=1, source_target_pairs={{0,1},{1,0},{2,3},{3,2},{4,5},{5,4},{6,7},{7,6},{8,9},{9,8},{10,11... | collective-permute-start | bytes 1179656 | tf_op jit(solution)/shard_map/ppermute | solution.py:62
  31.3 10.2 %collective-permute-start.8 = (bf16[128,1536]{1,0:T(8,128)(2,1)S(1)}, bf16[128,1536]{1,0:T(8,128)(2,1)S(1)}, u32[]{:S(2)}, u32[]{:S(2)}) collective-permute-start(bf16[128,1536]{1,0:T(8,128)(2,1)S(1)} %collective-permute-done.1.refs_5_), channel_id=1, source_target_pairs={{0,2},{1,3},{2,0},{3,1},{4,6},{5,7},{6,4},{7,5},{8,10},{9,11},{10,... | collective-permute-start | bytes 1179656 | tf_op jit(solution)/shard_map/ppermute | solution.py:62
  32.8 8.7 %collective-permute-start.9 = (bf16[128,2688]{1,0:T(8,128)(2,1)S(1)}, bf16[128,2688]{1,0:T(8,128)(2,1)S(1)}, u32[]{:S(2)}, u32[]{:S(2)}) collective-permute-start(bf16[128,2688]{1,0:T(8,128)(2,1)S(1)} %collective-permute-done.5.refs_6_), channel_id=1, source_target_pairs={{0,4},{1,5},{2,6},{3,7},{4,0},{5,1},{6,2},{7,3},{8,12},{9,13},{10,... | collective-permute-start | bytes 2064392 | tf_op jit(solution)/shard_map/ppermute | solution.py:62
  41.5 3.4 %collective-permute-start.13 = (bf16[128,1536]{1,0:T(8,128)(2,1)S(1)}, bf16[128,1536]{1,0:T(8,128)(2,1)S(1)}, u32[]{:S(2)}, u32[]{:S(2)}) collective-permute-start(bf16[128,1536]{1,0:T(8,128)(2,1)S(1)} %collective-permute-done.1.refs_5_), channel_id=1, source_target_pairs={{0,4},{1,5},{2,6},{3,7},{4,0},{5,1},{6,2},{7,3},{8,12},{9,13},{10,... | collective-permute-start | bytes 1179656 | tf_op jit(solution)/shard_map/ppermute | solution.py:62
  41.6 3.3 %collective-permute-start.14 = (bf16[128,1536]{1,0:T(8,128)(2,1)S(1)}, bf16[128,1536]{1,0:T(8,128)(2,1)S(1)}, u32[]{:S(2)}, u32[]{:S(2)}) collective-permute-start(bf16[128,1536]{1,0:T(8,128)(2,1)S(1)} %collective-permute-done.8.refs_7_), channel_id=1, source_target_pairs={{0,4},{1,5},{2,6},{3,7},{4,0},{5,1},{6,2},{7,3},{8,12},{9,13},{10,... | collective-permute-start | bytes 1179656 | tf_op jit(solution)/shard_map/ppermute | solution.py:62
  42.1 7.6 %collective-permute-start.12 = (bf16[128,1152]{1,0:T(8,128)(2,1)S(1)}, bf16[128,1152]{1,0:T(8,128)(2,1)S(1)}, u32[]{:S(2)}, u32[]{:S(2)}) collective-permute-start(bf16[128,1152]{1,0:T(8,128)(2,1)S(1)} %collective-permute-done.4.refs_5_), channel_id=1, source_target_pairs={{0,4},{1,5},{2,6},{3,7},{4,0},{5,1},{6,2},{7,3},{8,12},{9,13},{10,... | collective-permute-start | bytes 884744 | tf_op jit(solution)/shard_map/ppermute | solution.py:62
  42.1 9.4 %collective-permute-start.11 = (bf16[128,1152]{1,0:T(8,128)(2,1)S(1)}, bf16[128,1152]{1,0:T(8,128)(2,1)S(1)}, u32[]{:S(2)}, u32[]{:S(2)}) collective-permute-start(bf16[128,1152]{1,0:T(8,128)(2,1)S(1)} %collective-permute-done.4.refs_5_), channel_id=1, source_target_pairs={{0,2},{1,3},{2,0},{3,1},{4,6},{5,7},{6,4},{7,5},{8,10},{9,11},{10,... | collective-permute-start | bytes 884744 | tf_op jit(solution)/shard_map/ppermute | solution.py:62
  43.5 9.1 %collective-permute-start.10 = (bf16[128,1152]{1,0:T(8,128)(2,1)S(1)}, bf16[128,1152]{1,0:T(8,128)(2,1)S(1)}, u32[]{:S(2)}, u32[]{:S(2)}) collective-permute-start(bf16[128,1152]{1,0:T(8,128)(2,1)S(1)} %collective-permute-done.2.refs_1_), channel_id=1, source_target_pairs={{0,1},{1,0},{2,3},{3,2},{4,5},{5,4},{6,7},{7,6},{8,9},{9,8},{10,11... | collective-permute-start | bytes 884744 | tf_op jit(solution)/shard_map/ppermute | solution.py:62
  44.9 1.0 %copy-start.2 = (bf16[128,1536]{1,0:T(8,128)(2,1)S(1)}, bf16[128,1536]{1,0:T(8,128)(2,1)}, u32[]{:S(2)}) copy-start(bf16[128,1536]{1,0:T(8,128)(2,1)} %get-tuple-element.34.refs_0_) | copy-start | bytes 1179652
  45.9 1.0 %copy-start.3 = (bf16[128,1536]{1,0:T(8,128)(2,1)S(1)}, bf16[128,1536]{1,0:T(8,128)(2,1)}, u32[]{:S(2)}) copy-start(bf16[128,1536]{1,0:T(8,128)(2,1)} %get-tuple-element.35.refs_4_) | copy-start | bytes 1179652
  46.9 6.2 %copy-start.4 = (bf16[128,1152]{1,0:T(8,128)(2,1)S(1)}, bf16[128,1152]{1,0:T(8,128)(2,1)}, u32[]{:S(2)}) copy-start(bf16[128,1152]{1,0:T(8,128)(2,1)} %get-tuple-element.36.refs_0_) | copy-start | bytes 884740
  46.9 6.2 %copy-start.5 = (bf16[128,1152]{1,0:T(8,128)(2,1)S(1)}, bf16[128,1152]{1,0:T(8,128)(2,1)}, u32[]{:S(2)}) copy-start(bf16[128,1152]{1,0:T(8,128)(2,1)} %get-tuple-element.39.refs_4_) | copy-start | bytes 884740
  51.5 1.6 %collective-permute-start.15 = (bf16[128,1152]{1,0:T(8,128)(2,1)S(1)}, bf16[128,1152]{1,0:T(8,128)(2,1)S(1)}, u32[]{:S(2)}, u32[]{:S(2)}) collective-permute-start(bf16[128,1152]{1,0:T(8,128)(2,1)S(1)} %collective-permute-done.11.refs_7_), channel_id=1, source_target_pairs={{0,4},{1,5},{2,6},{3,7},{4,0},{5,1},{6,2},{7,3},{8,12},{9,13},{10,... | collective-permute-start | bytes 884744 | tf_op jit(solution)/shard_map/ppermute | solution.py:62
  56.2 3.1 %collective-permute-start.17 = (bf16[256,1152]{1,0:T(8,128)(2,1)S(1)}, bf16[256,1152]{1,0:T(8,128)(2,1)S(1)}, u32[]{:S(2)}, u32[]{:S(2)}) collective-permute-start(bf16[256,1152]{1,0:T(8,128)(2,1)S(1)} %get-tuple-element.55), channel_id=1, source_target_pairs={{0,4},{1,5},{2,6},{3,7},{4,0},{5,1},{6,2},{7,3},{8,12},{9,13},{10,... | collective-permute-start | bytes 1769480 | tf_op jit(solution)/shard_map/ppermute | solution.py:62
  56.4 9.3 %collective-permute-start.19 = (bf16[128,1152]{1,0:T(8,128)(2,1)S(1)}, bf16[128,1152]{1,0:T(8,128)(2,1)S(1)}, u32[]{:S(2)}, u32[]{:S(2)}) collective-permute-start(bf16[128,1152]{1,0:T(8,128)(2,1)S(1)} %get-tuple-element.58), channel_id=1, source_target_pairs={{0,1},{1,0},{2,3},{3,2},{4,5},{5,4},{6,7},{7,6},{8,9},{9,8},{10,11... | collective-permute-start | bytes 884744 | tf_op jit(solution)/shard_map/ppermute | solution.py:62
  57.7 10.2 %collective-permute-start.16 = (bf16[256,1152]{1,0:T(8,128)(2,1)S(1)}, bf16[256,1152]{1,0:T(8,128)(2,1)S(1)}, u32[]{:S(2)}, u32[]{:S(2)}) collective-permute-start(bf16[256,1152]{1,0:T(8,128)(2,1)S(1)} %get-tuple-element.54), channel_id=1, source_target_pairs={{0,4},{1,5},{2,6},{3,7},{4,0},{5,1},{6,2},{7,3},{8,12},{9,13},{10,... | collective-permute-start | bytes 1769480 | tf_op jit(solution)/shard_map/ppermute | solution.py:62
  59.4 22.2 %copy-start = (bf16[128,1152]{1,0:T(8,128)(2,1)S(1)}, bf16[128,1152]{1,0:T(8,128)(2,1)}, u32[]{:S(2)}) copy-start(bf16[128,1152]{1,0:T(8,128)(2,1)} %refs_0_.4) | copy-start | bytes 884740
  59.4 11.4 %collective-permute-start.22 = (bf16[128,1152]{1,0:T(8,128)(2,1)S(1)}, bf16[128,1152]{1,0:T(8,128)(2,1)S(1)}, u32[]{:S(2)}, u32[]{:S(2)}) collective-permute-start(bf16[128,1152]{1,0:T(8,128)(2,1)S(1)} %get-tuple-element.66), channel_id=1, source_target_pairs={{0,2},{1,3},{2,0},{3,1},{4,6},{5,7},{6,4},{7,5},{8,10},{9,11},{10,... | collective-permute-start | bytes 884744 | tf_op jit(solution)/shard_map/ppermute | solution.py:62
  65.7 15.9 %collective-permute-start.20 = (bf16[128,1152]{1,0:T(8,128)(2,1)S(1)}, bf16[128,1152]{1,0:T(8,128)(2,1)S(1)}, u32[]{:S(2)}, u32[]{:S(2)}) collective-permute-start(bf16[128,1152]{1,0:T(8,128)(2,1)S(1)} %add_convert_fusion.3), channel_id=1, source_target_pairs={{0,16},{1,17},{2,18},{3,19},{4,20},{5,21},{6,22},{7,23},{8,24},{9,... | collective-permute-start | bytes 884744 | tf_op jit(solution)/shard_map/ppermute | solution.py:62
  67.8 13.8 %collective-permute-start.18 = (bf16[128,1152]{1,0:T(8,128)(2,1)S(1)}, bf16[128,1152]{1,0:T(8,128)(2,1)S(1)}, u32[]{:S(2)}, u32[]{:S(2)}) collective-permute-start(bf16[128,1152]{1,0:T(8,128)(2,1)S(1)} %get-tuple-element.56), channel_id=1, source_target_pairs={{0,1},{1,0},{2,3},{3,2},{4,5},{5,4},{6,7},{7,6},{8,9},{9,8},{10,11... | collective-permute-start | bytes 884744 | tf_op jit(solution)/shard_map/ppermute | solution.py:62
  69.3 13.4 %collective-permute-start.21 = (bf16[128,1152]{1,0:T(8,128)(2,1)S(1)}, bf16[128,1152]{1,0:T(8,128)(2,1)S(1)}, u32[]{:S(2)}, u32[]{:S(2)}) collective-permute-start(bf16[128,1152]{1,0:T(8,128)(2,1)S(1)} %get-tuple-element.61), channel_id=1, source_target_pairs={{0,2},{1,3},{2,0},{3,1},{4,6},{5,7},{6,4},{7,5},{8,10},{9,11},{10,... | collective-permute-start | bytes 884744 | tf_op jit(solution)/shard_map/ppermute | solution.py:62
  70.8 13.5 %copy-start.1 = (bf16[128,1152]{1,0:T(8,128)(2,1)S(1)}, bf16[128,1152]{1,0:T(8,128)(2,1)}, u32[]{:S(2)}) copy-start(bf16[128,1152]{1,0:T(8,128)(2,1)} %refs_0_.5) | copy-start | bytes 884740
  71.0 13.4 %collective-permute-start.23 = (bf16[128,1152]{1,0:T(8,128)(2,1)S(1)}, bf16[128,1152]{1,0:T(8,128)(2,1)S(1)}, u32[]{:S(2)}, u32[]{:S(2)}) collective-permute-start(bf16[128,1152]{1,0:T(8,128)(2,1)S(1)} %get-tuple-element.64), channel_id=1, source_target_pairs={{0,8},{1,9},{2,10},{3,11},{4,12},{5,13},{6,14},{7,15},{8,0},{9,1},... | collective-permute-start | bytes 884744 | tf_op jit(solution)/shard_map/ppermute | solution.py:62

commit v7 on v6

--- a/solution.py
+++ b/solution.py
@@ -170,22 +170,25 @@
     )(*img_blocks, *txt_blocks)
 
 
-def write_grads(rows, pair, other, axis, first, grads):
-    size = sum(g.shape[0] for g in grads)
-    at = slice(first * rows, first * rows + size)
-    part = pair[at, :] if axis == 1 else pair[:, at]
-    part = lax.dot_general(part, other[...], (((axis,), (0,)), ((), ())), preferred_element_type=f32)
-    done = 0
-    for grad in grads:
-        grad[...] = part[done : done + grad.shape[0], :].astype(grad.dtype)
-        done += grad.shape[0]
-
-
-def pair_kernel(images, texts, skip, img_first, txt_first, img_count, *refs):
+def image_grads(pair, txt, rows, first, count):
+    part = lax.dot_general(
+        pair[first * rows : (first + count) * rows, :], txt, (((1,), (0,)), ((), ())), preferred_element_type=f32
+    )
+    return [part[k * rows : (k + 1) * rows, :] for k in range(count)]
+
+
+def text_grads(pair, img, rows, first, count):
+    part = lax.dot_general(
+        pair[:, first * rows : (first + count) * rows], img, (((0,), (0,)), ((), ())), preferred_element_type=f32
+    )
+    return [part[k * rows : (k + 1) * rows, :] for k in range(count)]
+
+
+def pair_kernel(images, texts, far, skip, half, own_txt, *refs):
     img_refs, txt_refs = refs[:images], refs[images : images + texts]
     p_ref, pair_ref, img, txt = refs[images + texts : images + texts + 4]
-    grads = refs[images + texts + 4 :]
-    rows = img_refs[0].shape[0]
+    outs = list(refs[images + texts + 4 :])
+    rows, col = img_refs[0].shape[0], images // far
     pack(img_refs, img, skip)
     pack(txt_refs, txt, skip)
     step = tile_rows(texts * rows, 256)
@@ -193,27 +196,45 @@
         at = slice(j * step, (j + 1) * step)
         dots = lax.dot_general(img[...], txt[at, :], (((1,), (1,)), ((), ())), preferred_element_type=f32)
         pair_ref[:, at] = (2.0 * jax.nn.sigmoid(logit_scale * dots + logit_bias) - p_ref[:, at]).astype(bf16)
-    if img_count:
-        write_grads(rows, pair_ref, txt, 1, img_first, grads[:img_count])
-    if len(grads) > img_count:
-        write_grads(rows, pair_ref, img, 0, txt_first, grads[img_count:])
-
-
-def pair_and_sent(img_blocks, txt_blocks, skip, targets, img_first, img_out, txt_first, txt_out):
+    others = image_grads(pair_ref, txt[...], rows, far, far * (col - 1)) if col > 1 else []
+    hops = [outs.pop(0) for _ in range(far * (col - 1))]
+    kept = [outs.pop(0) for _ in range(col - 1)]
+    longs = [outs.pop(0) for _ in range(far - 1)]
+    for k, grad in enumerate(others):
+        b, a = 1 + k // far, k % far
+        hops[k][...] = grad[:, :half].astype(bf16)
+        if a:
+            longs[a - 1][b * rows : (b + 1) * rows, :] = grad[:, half:].astype(bf16)
+        else:
+            kept[b - 1][...] = grad[:, half:]
+    if far > 1:
+        for a, grad in enumerate(image_grads(pair_ref, txt[:, half:], rows, 1, far - 1)):
+            longs[a][:rows, :] = grad.astype(bf16)
+    if outs:
+        count = outs[0].shape[0] // rows
+        grads = text_grads(pair_ref, img[...], rows, own_txt, len(outs) * count)
+        for k, grad in enumerate(grads):
+            outs[k // count][(k % count) * rows : (k % count + 1) * rows, :] = grad.astype(bf16)
+
+
+def pair_and_sent(img_blocks, txt_blocks, far, near, own_txt, skip, half, targets):
     images, texts = len(img_blocks), len(txt_blocks)
-    rows, width = img_blocks[0].shape
-    shapes = [jax.ShapeDtypeStruct((images * rows, texts * rows), bf16)]
-    shapes += [jax.ShapeDtypeStruct((n, width), bf16) for n in (images * rows, texts * rows) + img_out + txt_out]
-    return pl.pallas_call(
-        functools.partial(pair_kernel, images, texts, skip, img_first, txt_first, len(img_out)),
-        out_shape=shapes,
+    rows, width = img_blocks[-1].shape
+    col = images // far
+    shapes = [((images * rows, texts * rows), bf16), ((images * rows, width), bf16), ((texts * rows, width), bf16)]
+    shapes += [((rows, half), bf16)] * (far * (col - 1))
+    shapes += [((rows, width - half), f32)] * (col - 1)
+    shapes += [((col * rows, width - half), bf16)] * (far - 1)
+    shapes += [((near * rows, width), bf16)] * ((texts - own_txt) // near)
+    out = pl.pallas_call(
+        functools.partial(pair_kernel, images, texts, far, skip, half, own_txt),
+        out_shape=[jax.ShapeDtypeStruct(*shape) for shape in shapes],
         in_specs=[VMEM] * (images + texts + 1),
         out_specs=[VMEM] * len(shapes),
         compiler_params=params(
             ((images * rows, texts * rows), 6),
-            ((images + texts, rows, width), 2),
+            ((images + texts, rows, width), 6),
             *[(v.shape, 2) for v in (*img_blocks, *txt_blocks)],
-            ((sum(img_out) + sum(txt_out), width), 6),
         ),
         cost_estimate=pl.CostEstimate(
             flops=4 * images * texts * rows * rows * width,
@@ -222,67 +243,107 @@
         ),
         name="pair_and_sent",
     )(*img_blocks, *txt_blocks, targets)
-
-
-def grads_kernel(rows, img_first, img_count, txt_first, pair_ref, img, txt, *grads):
-    if len(grads) > img_count:
-        write_grads(rows, pair_ref, img, 0, txt_first, grads[img_count:])
-    if img_count:
-        write_grads(rows, pair_ref, txt, 1, img_first, grads[:img_count])
-
-
-def some_grads(pair, img, txt, rows, img_first, img_out, txt_first, txt_out, dtype, name):
+    out = list(out)
+    cut = [3, 3 + far * (col - 1), 3 + (far + 1) * (col - 1), 3 + (far + 1) * (col - 1) + far - 1]
+    return out[:3], out[cut[0] : cut[1]], out[cut[1] : cut[2]], out[cut[2] : cut[3]], out[cut[3] :]
+
+
+def kept_kernel(half, pair, img, txt, *outs):
+    rows = outs[0].shape[0]
+    far = len(outs) - 1
+    outs[-1][...] = lax.dot_general(
+        pair[:, : outs[-1].shape[0]], img[...], (((0,), (0,)), ((), ())), preferred_element_type=f32
+    )
+    for out, grad in zip(outs, image_grads(pair, txt[...], rows, 0, far)):
+        out[...] = grad[:, : out.shape[1]]
+
+
+def kept_grads(pair, img, txt, rows, far, own_txt, half):
     width = img.shape[1]
-    shapes = [jax.ShapeDtypeStruct((n * rows, width), dtype) for n in img_out + txt_out]
-    out = pl.pallas_call(
-        functools.partial(grads_kernel, rows, img_first, len(img_out), txt_first),
-        out_shape=shapes,
+    shapes = [(rows, width)] + [(rows, half)] * (far - 1) + [(own_txt * rows, width)]
+    return pl.pallas_call(
+        functools.partial(kept_kernel, half),
+        out_shape=[jax.ShapeDtypeStruct(shape, f32) for shape in shapes],
         in_specs=[VMEM] * 3,
         out_specs=[VMEM] * len(shapes),
-        compiler_params=params(
-            (pair.shape, 2), (img.shape, 2), (txt.shape, 2), ((sum(img_out) + sum(txt_out), rows, width), 8)
-        ),
+        compiler_params=params((pair.shape, 2), (img.shape, 2), (txt.shape, 2), *[(v, 8) for v in shapes]),
         cost_estimate=pl.CostEstimate(
             flops=2 * pair.size * width,
-            bytes_accessed=2 * (pair.size + img.size + txt.size) + 4 * len(shapes) * rows * width,
+            bytes_accessed=2 * (pair.size + img.size + txt.size) + 4 * own_txt * rows * width,
             transcendentals=0,
         ),
-        name=name,
+        name="kept",
     )(pair, img, txt)
-    return out[: len(img_out)], out[len(img_out) :]
-
-
-def final_kernel(counts, *refs):
-    x_ref, out_ref = refs[0], refs[-1]
-    pieces, at = [], 1
-    for count in counts:
-        pieces.append(refs[at : at + count])
-        at += count
-    most = max(counts)
-    step = x_ref.shape[0] // most
-    for k in range(most):
-        rows = slice(k * step, (k + 1) * step)
-        x = x_ref[rows, :].astype(f32)
-        inverse = 1.0 / jnp.sqrt(jnp.sum(x * x, axis=1, keepdims=True) + epsilon)
-        unit = x * inverse
-        grad = None
-        for part in pieces:
-            term = (part[0][rows, :] if len(part) == 1 else part[k][...]).astype(f32)
-            grad = term if grad is None else grad + term
+
+
+def text_sums_kernel(row, near, half, cores, own_ref, *refs):
+    arrived, outs = refs[: cores * row], list(refs[cores * row :])
+    rows = own_ref.shape[0] // (row * near)
+    hops = [outs.pop(0) for _ in range(near * (row - 1))]
+    kept = [outs.pop(0) for _ in range(row - 1)]
+    stay = [outs.pop(0) for _ in range(near)]
+    for b in range(row):
+        for a in range(near):
+            k = b * near + a
+            total = own_ref[k * rows : (k + 1) * rows, :]
+            for c in range(cores):
+                total = total + arrived[c * row + b][a * rows : (a + 1) * rows, :].astype(f32)
+            if b:
+                hops[(b - 1) * near + a][...] = total[:, :half].astype(bf16)
+            else:
+                stay[a][...] = total[:, : stay[a].shape[1]]
+            if a:
+                outs[a - 1][b * rows : (b + 1) * rows, :] = total[:, half:].astype(bf16)
+            elif b:
+                kept[b - 1][...] = total[:, half:]
+
+
+def text_sums(own, arrived, rows, row, near, half):
+    width = own.shape[1]
+    shapes = [((rows, half), bf16)] * (near * (row - 1)) + [((rows, width - half), f32)] * (row - 1)
+    shapes += [((rows, width), f32)] + [((rows, half), f32)] * (near - 1)
+    shapes += [((row * rows, width - half), bf16)] * (near - 1)
+    out = list(
+        pl.pallas_call(
+            functools.partial(text_sums_kernel, row, near, half, len(arrived) // row),
+            out_shape=[jax.ShapeDtypeStruct(*shape) for shape in shapes],
+            in_specs=[VMEM] * (1 + len(arrived)),
+            out_specs=[VMEM] * len(shapes),
+            compiler_params=params((own.shape, 16)),
+            cost_estimate=pl.CostEstimate(flops=2 * own.size, bytes_accessed=10 * own.size, transcendentals=0),
+            name="text_sums",
+        )(own, *arrived)
+    )
+    cut = [near * (row - 1), (near + 1) * (row - 1), (near + 1) * (row - 1) + near]
+    return out[: cut[0]], out[cut[0] : cut[1]], out[cut[1] : cut[2]], out[cut[2] :]
+
+
+def final_kernel(half, lows, x_ref, own_ref, *refs):
+    parts, out_ref = refs[:-1], refs[-1]
+    rows = x_ref.shape[0]
+    x = x_ref[...].astype(f32)
+    inverse = 1.0 / jnp.sqrt(jnp.sum(x * x, axis=1, keepdims=True) + epsilon)
+    sides, along = [], 0.0
+    for at, refs_at in ((slice(0, half), parts[:lows]), (slice(half, None), parts[lows:])):
+        unit = x[:, at] * inverse
+        grad = own_ref[:, at]
+        for part in refs_at:
+            grad = grad + part[:rows, :].astype(f32)
         grad = logit_scale * grad
-        along = jnp.sum(unit * grad, axis=1, keepdims=True)
-        out_ref[rows, :] = (grad - unit * along) * inverse
-
-
-def final(x, parts):
-    counts = tuple(len(part) for part in parts)
-    operands = [x] + [v for part in parts for v in part]
+        along = along + jnp.sum(unit * grad, axis=1, keepdims=True)
+        sides.append((at, unit, grad))
+    for at, unit, grad in sides:
+        out_ref[:, at] = (grad - unit * along) * inverse
+
+
+def final(x, own, lows, highs, half):
+    operands = [x, own, *lows, *highs]
     return pl.pallas_call(
-        functools.partial(final_kernel, counts),
+        functools.partial(final_kernel, half, len(lows)),
         out_shape=jax.ShapeDtypeStruct(x.shape, f32),
         in_specs=[VMEM] * len(operands),
         out_specs=VMEM,
-        compiler_params=params((x.shape, 4 * (4 + len(parts)))),
+        compiler_params=params((x.shape, 4 * (4 + len(operands)))),
         cost_estimate=pl.CostEstimate(flops=10 * x.size, bytes_accessed=12 * x.size, transcendentals=0),
         name="final",
     )(*operands)
@@ -366,68 +427,52 @@
     s_txts = texts(s_txt, s_near, b_row, s_near_row, b_core, s_near_core, b_row_core, s_both_core)
 
     own_txt = row * near
-    pieces = 1 if rows % (16 * 1) == 0 else 1
-    cut = rows // pieces
-
-    def piece(x, i):
-        return x[i * cut : (i + 1) * cut]
-
-    onward_keys = [(b, a) for b in range(1, col) for a in range(1, far)]
-    last_keys = [(b, 0) for b in range(1, col)]
-    img_out = tuple(n for b in range(1, col) for a in range(far) for n in ((cut,) * pieces if a else (rows,)))
-    txt_out = (near * rows,) * (row * (core - 1))
+    half = width // 128 * 2 // 3 * 128
     skip = teacher_img.shape[1]
-    out = pair_and_sent(s_imgs, s_txts, skip, targets, far, img_out, own_txt, txt_out)
-    pair, img_pack, txt_pack = out[:3]
-    img_list, txt_list = list(out[3 : 3 + len(img_out)]), out[3 + len(img_out) :]
-    img_sent = {}
+    packed, img_hops, img_kept, img_longs, txt_out = pair_and_sent(
+        s_imgs, s_txts, far, near, own_txt, skip, half, targets
+    )
+    pair, img_pack, txt_pack = packed
+    img_in = {}
     for b in range(1, col):
-        for a in range(far):
-            img_sent[b, a] = [img_list.pop(0) for _ in range(pieces if a else 1)]
-    txt_sent = {(1 + k // row, k % row): v for k, v in enumerate(txt_list)}
-    img_part, txt_part = some_grads(pair, img_pack, txt_pack, rows, 0, (1,) * far, 0, (1,) * own_txt, f32, "kept")
-    txt_part = {divmod(k, near): v for k, v in enumerate(txt_part)}
-
-    img_in = {key: [plan.send(v, "col", -key[0]) for v in img_sent[key]] for key in onward_keys}
-    txt_in = {key: plan.send(v, "core", -key[0]) for key, v in txt_sent.items()}
-
-    for c in range(1, core):
-        for b in range(row):
-            for a in range(near):
-                txt_part[b, a] = txt_part[b, a] + txt_in[c, b][a * rows : (a + 1) * rows].astype(f32)
-    row_in = {
-        (b, a): [plan.send(piece(txt_part[b, a], i).astype(bf16), "row", -b) for i in range(pieces)]
+        for a in range(1, far):
+            img_in[b, a] = plan.send(img_hops[(b - 1) * far + a], "col", -b)
+    long_in = [plan.send(v, "far", -1 - k) for k, v in enumerate(img_longs)]
+    txt_in = [plan.send(v, "core", -1 - k // row) for k, v in enumerate(txt_out)]
+    *img_stay, txt_own = kept_grads(pair, img_pack, txt_pack, rows, far, own_txt, half)
+    txt_hops, txt_kept, txt_stay, txt_longs = text_sums(txt_own, txt_in, rows, row, near, half)
+
+    row_in = {}
+    for b in range(1, row):
+        for a in range(1, near):
+            row_in[b, a] = plan.send(txt_hops[(b - 1) * near + a], "row", -b)
+    txt_long_in = [plan.send(v, "near", -1 - k) for k, v in enumerate(txt_longs)]
+
+    def total(own, arrived):
+        for v in arrived:
+            own = own + v.astype(f32)
+        return own.astype(bf16)
+
+    img_last = [
+        plan.send(total(after(img_stay[a], *txt_hops, *txt_longs), [img_in[b, a] for b in range(1, col)]), "far", -a) for a in range(1, far)
+    ]
+    txt_last = [
+        plan.send(total(txt_stay[a], [row_in[b, a] for b in range(1, row)]), "near", -a) for a in range(1, near)
+    ]
+    img_side = [
+        plan.send(total(after(img_kept[b - 1], *row_in.values()), [v[b * rows : (b + 1) * rows] for v in long_in]), "col", -b)
+        for b in range(1, col)
+    ]
+    txt_side = [
+        plan.send(total(txt_kept[b - 1], [v[b * rows : (b + 1) * rows] for v in txt_long_in]), "row", -b)
         for b in range(1, row)
-        for a in range(1, near)
-    }
-
-    def summed(own, arrived, i):
-        total = piece(own, i)
-        for v in arrived:
-            total = total + v[i].astype(f32)
-        return total.astype(bf16)
-
-    txt_ready = [
-        [summed(txt_part[0, a], [row_in[b, a] for b in range(1, row)], i) for i in range(pieces)]
-        for a in range(1, near)
     ]
-    txt_last = [[plan.send(v, "near", -a) for v in part] for a, part in zip(range(1, near), txt_ready)]
-    img_last = [
-        [
-            plan.send(summed(img_part[a], [img_in[b, a] for b in range(1, col)], i), "far", -a)
-            for i in range(pieces)
-        ]
-        for a in range(1, far)
-    ]
-    col_ahead = list(txt_in.values())
-    row_ahead = [v for key in onward_keys for v in img_in[key]]
-    for key in last_keys:
-        img_in[key] = [plan.send(after(img_sent[key][0], *col_ahead), "col", -key[0])]
-    for b in range(1, row):
-        row_in[b, 0] = [plan.send(after(txt_part[b, 0].astype(bf16), *row_ahead), "row", -b)]
-    img_own, txt_own = img_part[0], txt_part[0, 0]
-    image_grad = final(student_img, [[img_own]] + [img_in[b, 0] for b in range(1, col)] + img_last)
-    text_grad = final(student_txt, [[txt_own]] + [row_in[b, 0] for b in range(1, row)] + txt_last)
+    col_ahead = list(row_in.values())
+    row_ahead = list(img_in.values())
+    img_ends = [plan.send(after(img_hops[(b - 1) * far], *col_ahead), "col", -b) for b in range(1, col)]
+    txt_ends = [plan.send(after(txt_hops[(b - 1) * near], *row_ahead), "row", -b) for b in range(1, row)]
+    image_grad = final(student_img, img_stay[0], img_ends + img_last, img_side + long_in, half)
+    text_grad = final(student_txt, txt_stay[0], txt_ends + txt_last, txt_side + txt_long_in, half)
     return image_grad, text_grad
 
 

time: 85.7 us -> 84.5 us (0.986)
  waiting for transfers between devices: 40.7 us -> 36.2 us
  starting transfers between devices: 29 us -> 32 us
    ppermute x24 -> x28, waiting for transfers between devices: 40.7 us -> 36.2 us  [send(): return lax.ppermute(x, AXES, pairs)]
    ppermute x24 -> x28, starting transfers between devices: 29 us -> 32 us  [send(): return lax.ppermute(x, AXES, pairs)]
    pallas_call x4 -> x5, Pallas kernels: 6.96 us -> 7.27 us  [the longest x1 3.23 us: pair_and_sent(): pl.pallas_call(functools.partial(pair_kernel, images, texts, far, skip, h...]
  transfers between devices with their start and end apart: 24 -> 28, of which waited for: 10 -> 12; matrix products, arithmetic and copies ran while one was open for 0% -> 0% of each run, Pallas kernels for 6% -> 7%
where the time goes in v7:
time: 84.5 us; the launch traced here: 84.3 us
  waiting for transfers between devices  36.2 us (43%)
  starting transfers between devices  32 us (38%)
  Pallas kernels  13.2 us (16%)
  local copies, waits for them, and re-layouts  2.01 us (2%)
    ppermute x28, waiting for transfers between devices, send(): return lax.ppermute(x, AXES, pairs)  36.2 us
    ppermute x28, starting transfers between devices, send(): return lax.ppermute(x, AXES, pairs)  32 us
    pallas_call x1, Pallas kernels, pair_and_sent(): pl.pallas_call(functools.partial(pair_kernel, images, texts, far, skip, h...  3.23 us
    pallas_call x1, Pallas kernels, unit_rows(): pl.pallas_call(functools.partial(unit_kernel, len(arrays)), out_shape=[ja...  3.15 us
    pallas_call x1, Pallas kernels, teacher_targets(): pl.pallas_call(functools.partial(teacher_kernel, images, texts), out_shap...  2.77 us
    pallas_call x2, Pallas kernels, final(): pl.pallas_call(functools.partial(final_kernel, half, len(lows)), out_shap...  2.3 us
    unnamed x12, local copies, waits for them, and re-layouts  2.01 us
  transfers between devices with their start and end apart: 28, of which 12 were waited for; matrix products, arithmetic and copies ran while one was open for 0% of the time, Pallas kernels for 7%

profile of v7, /device:TPU:0, one launch (start us, length us, event | category | flops | bytes accessed | tf_op | source)
XLA Modules:
  0.0 84.3 jit_solution(190088655822959730)
XLA Ops:
  0.6 3.1 %unit_rows.1 = (bf16[128,1536]{1,0:T(8,128)(2,1)}, bf16[128,1536]{1,0:T(8,128)(2,1)}, bf16[128,1152]{1,0:T(8,128)(2,1)}, bf16[128,1152]{1,0:T(8,128)(2,1)}, bf16...) custom-call(bf16[128,1536]{1,0:T(8,128)(2,1)} %refs_0_.1, bf16[128,1536]{1,0:T(8,128)(2,1)} %refs_1_.1, ...), custom_call_target="tpu_custom_call" | custom-call | flops 2752512 | bytes 4128768 | tf_op jit(solution)/shard_map/unit_rows/pallas_call | solution.py:107
  3.8 4.1 %collective-permute-start = (bf16[128,1536]{1,0:T(8,128)(2,1)}, bf16[128,1536]{1,0:T(8,128)(2,1)S(1)}, u32[]{:S(2)}, u32[]{:S(2)}) collective-permute-start(bf16[128,1536]{1,0:T(8,128)(2,1)} %get-tuple-element.41.refs_0_), channel_id=1, source_target_pairs={{0,16},{1,17},{2,18},{3,19},{4,20},{5,21},{6,22},{7,23},{8,24},{9,... | collective-permute-start | bytes 1179656 | tf_op jit(solution)/shard_map/ppermute | solution.py:62
  7.9 1.6 %collective-permute-start.1 = (bf16[128,1536]{1,0:T(8,128)(2,1)}, bf16[128,1536]{1,0:T(8,128)(2,1)S(1)}, u32[]{:S(2)}, u32[]{:S(2)}) collective-permute-start(bf16[128,1536]{1,0:T(8,128)(2,1)} %get-tuple-element.42.refs_4_), channel_id=1, source_target_pairs={{0,8},{1,9},{2,10},{3,11},{4,12},{5,13},{6,14},{7,15},{8,0},{9,1},... | collective-permute-start | bytes 1179656 | tf_op jit(solution)/shard_map/ppermute | solution.py:62
  9.5 1.5 %collective-permute-start.5 = (bf16[128,2688]{1,0:T(8,128)(2,1)}, bf16[128,2688]{1,0:T(8,128)(2,1)S(1)}, u32[]{:S(2)}, u32[]{:S(2)}) collective-permute-start(bf16[128,2688]{1,0:T(8,128)(2,1)} %get-tuple-element.47), channel_id=1, source_target_pairs={{0,2},{1,3},{2,0},{3,1},{4,6},{5,7},{6,4},{7,5},{8,10},{9,11},{10,... | collective-permute-start | bytes 2064392 | tf_op jit(solution)/shard_map/ppermute | solution.py:62
  11.0 1.5 %collective-permute-start.3 = (bf16[128,2688]{1,0:T(8,128)(2,1)}, bf16[128,2688]{1,0:T(8,128)(2,1)S(1)}, u32[]{:S(2)}, u32[]{:S(2)}) collective-permute-start(bf16[128,2688]{1,0:T(8,128)(2,1)} %get-tuple-element.44), channel_id=1, source_target_pairs={{0,1},{1,0},{2,3},{3,2},{4,5},{5,4},{6,7},{7,6},{8,9},{9,8},{10,11... | collective-permute-start | bytes 2064392 | tf_op jit(solution)/shard_map/ppermute | solution.py:62
  12.5 13.3 %collective-permute-done.refs_1_ = bf16[128,1536]{1,0:T(8,128)(2,1)S(1)} collective-permute-done((bf16[128,1536]{1,0:T(8,128)(2,1)}, bf16[128,1536]{1,0:T(8,128)(2,1)S(1)}, u32[]{:S(2)}, u32[]{:S(2)}) %collective-permute-start) | collective-permute-done | bytes 393248 | tf_op jit(solution)/shard_map/ppermute | solution.py:62
  25.9 1.4 %collective-permute-start.2 = (bf16[128,1152]{1,0:T(8,128)(2,1)}, bf16[128,1152]{1,0:T(8,128)(2,1)S(1)}, u32[]{:S(2)}, u32[]{:S(2)}) collective-permute-start(bf16[128,1152]{1,0:T(8,128)(2,1)} %get-tuple-element.43.refs_0_), channel_id=1, source_target_pairs={{0,16},{1,17},{2,18},{3,19},{4,20},{5,21},{6,22},{7,23},{8,24},{9,... | collective-permute-start | bytes 884744 | tf_op jit(solution)/shard_map/ppermute | solution.py:62
  27.3 2.4 %collective-permute-start.4 = (bf16[128,1152]{1,0:T(8,128)(2,1)}, bf16[128,1152]{1,0:T(8,128)(2,1)S(1)}, u32[]{:S(2)}, u32[]{:S(2)}) collective-permute-start(bf16[128,1152]{1,0:T(8,128)(2,1)} %get-tuple-element.46.refs_4_), channel_id=1, source_target_pairs={{0,8},{1,9},{2,10},{3,11},{4,12},{5,13},{6,14},{7,15},{8,0},{9,1},... | collective-permute-start | bytes 884744 | tf_op jit(solution)/shard_map/ppermute | solution.py:62
  29.8 1.6 %collective-permute-start.7 = (bf16[128,1536]{1,0:T(8,128)(2,1)S(1)}, bf16[128,1536]{1,0:T(8,128)(2,1)S(1)}, u32[]{:S(2)}, u32[]{:S(2)}) collective-permute-start(bf16[128,1536]{1,0:T(8,128)(2,1)S(1)} %collective-permute-done.refs_1_), channel_id=1, source_target_pairs={{0,1},{1,0},{2,3},{3,2},{4,5},{5,4},{6,7},{7,6},{8,9},{9,8},{10,11... | collective-permute-start | bytes 1179656 | tf_op jit(solution)/shard_map/ppermute | solution.py:62
  31.3 1.5 %collective-permute-start.8 = (bf16[128,1536]{1,0:T(8,128)(2,1)S(1)}, bf16[128,1536]{1,0:T(8,128)(2,1)S(1)}, u32[]{:S(2)}, u32[]{:S(2)}) collective-permute-start(bf16[128,1536]{1,0:T(8,128)(2,1)S(1)} %collective-permute-done.1.refs_5_), channel_id=1, source_target_pairs={{0,2},{1,3},{2,0},{3,1},{4,6},{5,7},{6,4},{7,5},{8,10},{9,11},{10,... | collective-permute-start | bytes 1179656 | tf_op jit(solution)/shard_map/ppermute | solution.py:62
  32.8 8.6 %collective-permute-done.2.refs_1_ = bf16[128,1152]{1,0:T(8,128)(2,1)S(1)} collective-permute-done((bf16[128,1152]{1,0:T(8,128)(2,1)}, bf16[128,1152]{1,0:T(8,128)(2,1)S(1)}, u32[]{:S(2)}, u32[]{:S(2)}) %collective-permute-start.2) | collective-permute-done | bytes 294944 | tf_op jit(solution)/shard_map/ppermute | solution.py:62
  42.2 1.4 %collective-permute-start.11 = (bf16[128,1152]{1,0:T(8,128)(2,1)S(1)}, bf16[128,1152]{1,0:T(8,128)(2,1)S(1)}, u32[]{:S(2)}, u32[]{:S(2)}) collective-permute-start(bf16[128,1152]{1,0:T(8,128)(2,1)S(1)} %collective-permute-done.4.refs_5_), channel_id=1, source_target_pairs={{0,2},{1,3},{2,0},{3,1},{4,6},{5,7},{6,4},{7,5},{8,10},{9,11},{10,... | collective-permute-start | bytes 884744 | tf_op jit(solution)/shard_map/ppermute | solution.py:62
  43.6 1.4 %collective-permute-start.10 = (bf16[128,1152]{1,0:T(8,128)(2,1)S(1)}, bf16[128,1152]{1,0:T(8,128)(2,1)S(1)}, u32[]{:S(2)}, u32[]{:S(2)}) collective-permute-start(bf16[128,1152]{1,0:T(8,128)(2,1)S(1)} %collective-permute-done.2.refs_1_), channel_id=1, source_target_pairs={{0,1},{1,0},{2,3},{3,2},{4,5},{5,4},{6,7},{7,6},{8,9},{9,8},{10,11... | collective-permute-start | bytes 884744 | tf_op jit(solution)/shard_map/ppermute | solution.py:62
  45.9 1.0 %copy-done.3 = bf16[128,1536]{1,0:T(8,128)(2,1)S(1)} copy-done((bf16[128,1536]{1,0:T(8,128)(2,1)S(1)}, bf16[128,1536]{1,0:T(8,128)(2,1)}, u32[]{:S(2)}) %copy-start.3) | copy-done | bytes 393240
  46.9 2.8 %teacher_targets.1.refs_12_ = f32[512,1024]{1,0:T(8,128)S(1)} custom-call(bf16[128,1536]{1,0:T(8,128)(2,1)S(1)} %copy-done.2, bf16[128,1536]{1,0:T(8,128)(2,1)S(1)} %collective-permute-done.refs_1_, bf16[128,2688]{1,0:T(8,128)(2,1)S(1)} %collective-permute-done.3.refs_2_, bf16[128,1536]{1,0:T(8,128)(2,1)S(1)} %collective-permute-done.7.refs_3_, ...), custom_call_target="tpu_custom_call" | custom-call | flops 1610612736 | bytes 6815744 | tf_op jit(solution)/shard_map/teacher_targets/pallas_call | solution.py:154
  49.7 1.8 %collective-permute-done.11.refs_7_ = bf16[128,1152]{1,0:T(8,128)(2,1)S(1)} collective-permute-done((bf16[128,1152]{1,0:T(8,128)(2,1)S(1)}, bf16[128,1152]{1,0:T(8,128)(2,1)S(1)}, u32[]{:S(2)}, u32[]{:S(2)}) %collective-permute-start.11) | collective-permute-done | bytes 294944 | tf_op jit(solution)/shard_map/ppermute | solution.py:62
  51.5 1.2 %collective-permute-done.10.refs_3_ = bf16[128,1152]{1,0:T(8,128)(2,1)S(1)} collective-permute-done((bf16[128,1152]{1,0:T(8,128)(2,1)S(1)}, bf16[128,1152]{1,0:T(8,128)(2,1)S(1)}, u32[]{:S(2)}, u32[]{:S(2)}) %collective-permute-start.10) | collective-permute-done | bytes 294944 | tf_op jit(solution)/shard_map/ppermute | solution.py:62
  53.1 3.2 %pair_and_sent.1 = (bf16[512,1024]{1,0:T(8,128)(2,1)S(1)}, bf16[512,1152]{1,0:T(8,128)(2,1)S(1)}, bf16[1024,1152]{1,0:T(8,128)(2,1)S(1)}, bf16[128,768]{1,0:T(8,...) custom-call(bf16[128,1152]{1,0:T(8,128)(2,1)S(1)} %copy-done.4, ...), custom_call_target="tpu_custom_call" | custom-call | flops 2415919104 | bytes 7733248 | tf_op jit(solution)/shard_map/pair_and_sent/pallas_call | solution.py:229
  56.9 1.2 %collective-permute-start.20 = (bf16[128,768]{1,0:T(8,128)(2,1)S(1)}, bf16[128,768]{1,0:T(8,128)(2,1)S(1)}, u32[]{:S(2)}, u32[]{:S(2)}) collective-permute-start(bf16[128,768]{1,0:T(8,128)(2,1)S(1)} %get-tuple-element.70), channel_id=1, source_target_pairs={{0,1},{1,0},{2,3},{3,2},{4,5},{5,4},{6,7},{7,6},{8,9},{9,8},{10,11... | collective-permute-start | bytes 589832 | tf_op jit(solution)/shard_map/ppermute | solution.py:62
  58.2 2.3 %collective-permute-start.22 = (bf16[256,384]{1,0:T(8,128)(2,1)S(1)}, bf16[256,384]{1,0:T(8,128)(2,1)S(1)}, u32[]{:S(2)}, u32[]{:S(2)}) collective-permute-start(bf16[256,384]{1,0:T(8,128)(2,1)S(1)} %get-tuple-element.73), channel_id=1, source_target_pairs={{0,16},{1,17},{2,18},{3,19},{4,20},{5,21},{6,22},{7,23},{8,24},{9,... | collective-permute-start | bytes 589832 | tf_op jit(solution)/shard_map/ppermute | solution.py:62
  60.4 1.5 %kept.1 = (f32[128,1152]{1,0:T(8,128)S(1)}, f32[128,768]{1,0:T(8,128)S(1)}, f32[512,1152]{1,0:T(8,128)S(1)}) custom-call(bf16[512,1024]{1,0:T(8,128)(2,1)S(1)} %get-tuple-element.56.pair, bf16[512,1152]{1,0:T(8,128)(2,1)S(1)} %get-tuple-element.57.img, bf16[1024,1152]{1,0:T(8,128)(2,1)S(1)} %get-tuple-element.58.txt), custom_call_target="tpu_custom_call" | custom-call | flops 1207959552 | bytes 6946816 | tf_op jit(solution)/shard_map/kept/pallas_call | solution.py:264
  62.2 1.6 %collective-permute-start.18 = (bf16[128,768]{1,0:T(8,128)(2,1)S(1)}, bf16[128,768]{1,0:T(8,128)(2,1)S(1)}, u32[]{:S(2)}, u32[]{:S(2)}) collective-permute-start(bf16[128,768]{1,0:T(8,128)(2,1)S(1)} %get-tuple-element.64), channel_id=1, source_target_pairs={{0,2},{1,3},{2,0},{3,1},{4,6},{5,7},{6,4},{7,5},{8,10},{9,11},{10,... | collective-permute-start | bytes 589832 | tf_op jit(solution)/shard_map/ppermute | solution.py:62
  63.8 1.7 %collective-permute-start.26 = (bf16[256,384]{1,0:T(8,128)(2,1)S(1)}, bf16[256,384]{1,0:T(8,128)(2,1)S(1)}, u32[]{:S(2)}, u32[]{:S(2)}) collective-permute-start(bf16[256,384]{1,0:T(8,128)(2,1)S(1)} %get-tuple-element.68), channel_id=1, source_target_pairs={{0,8},{1,9},{2,10},{3,11},{4,12},{5,13},{6,14},{7,15},{8,0},{9,1},... | collective-permute-start | bytes 589832 | tf_op jit(solution)/shard_map/ppermute | solution.py:62
  66.1 1.4 %collective-permute-start.21 = (bf16[128,768]{1,0:T(8,128)(2,1)S(1)}, bf16[128,768]{1,0:T(8,128)(2,1)S(1)}, u32[]{:S(2)}, u32[]{:S(2)}) collective-permute-start(bf16[128,768]{1,0:T(8,128)(2,1)S(1)} %add_convert_fusion.1), channel_id=1, source_target_pairs={{0,16},{1,17},{2,18},{3,19},{4,20},{5,21},{6,22},{7,23},{8,24},{9,... | collective-permute-start | bytes 589832 | tf_op jit(solution)/shard_map/ppermute | solution.py:62
  67.5 2.6 %collective-permute-done.18 = bf16[128,768]{1,0:T(8,128)(2,1)S(1)} collective-permute-done((bf16[128,768]{1,0:T(8,128)(2,1)S(1)}, bf16[128,768]{1,0:T(8,128)(2,1)S(1)}, u32[]{:S(2)}, u32[]{:S(2)}) %collective-permute-start.18) | collective-permute-done | bytes 196640 | tf_op jit(solution)/shard_map/ppermute | solution.py:62
  70.1 4.9 %collective-permute-done.22.refs_3_ = bf16[256,384]{1,0:T(8,128)(2,1)S(1)} collective-permute-done((bf16[256,384]{1,0:T(8,128)(2,1)S(1)}, bf16[256,384]{1,0:T(8,128)(2,1)S(1)}, u32[]{:S(2)}, u32[]{:S(2)}) %collective-permute-start.22) | collective-permute-done | bytes 196640 | tf_op jit(solution)/shard_map/ppermute | solution.py:62
  75.7 1.5 %collective-permute-start.19 = (bf16[128,768]{1,0:T(8,128)(2,1)S(1)}, bf16[128,768]{1,0:T(8,128)(2,1)S(1)}, u32[]{:S(2)}, u32[]{:S(2)}) collective-permute-start(bf16[128,768]{1,0:T(8,128)(2,1)S(1)} %get-tuple-element.65), channel_id=1, source_target_pairs={{0,1},{1,0},{2,3},{3,2},{4,5},{5,4},{6,7},{7,6},{8,9},{9,8},{10,11... | collective-permute-start | bytes 589832 | tf_op jit(solution)/shard_map/ppermute | solution.py:62
  77.3 1.2 %collective-permute-done.21.refs_1_ = bf16[128,768]{1,0:T(8,128)(2,1)S(1)} collective-permute-done((bf16[128,768]{1,0:T(8,128)(2,1)S(1)}, bf16[128,768]{1,0:T(8,128)(2,1)S(1)}, u32[]{:S(2)}, u32[]{:S(2)}) %collective-permute-start.21) | collective-permute-done | bytes 196640 | tf_op jit(solution)/shard_map/ppermute | solution.py:62
  78.5 1.5 %collective-permute-start.27 = (bf16[128,384]{1,0:T(8,128)(2,1)S(1)}, bf16[128,384]{1,0:T(8,128)(2,1)S(1)}, u32[]{:S(2)}, u32[]{:S(2)}) collective-permute-start(bf16[128,384]{1,0:T(8,128)(2,1)S(1)} %add_convert_fusion.2), channel_id=1, source_target_pairs={{0,2},{1,3},{2,0},{3,1},{4,6},{5,7},{6,4},{7,5},{8,10},{9,11},{10,... | collective-permute-start | bytes 294920 | tf_op jit(solution)/shard_map/ppermute | solution.py:62
  80.0 1.8 %collective-permute-done.19.refs_0_ = bf16[128,768]{1,0:T(8,128)(2,1)S(1)} collective-permute-done((bf16[128,768]{1,0:T(8,128)(2,1)S(1)}, bf16[128,768]{1,0:T(8,128)(2,1)S(1)}, u32[]{:S(2)}, u32[]{:S(2)}) %collective-permute-start.19) | collective-permute-done | bytes 196640 | tf_op jit(solution)/shard_map/ppermute | solution.py:62
  81.9 1.1 %final.2 = f32[128,1152]{1,0:T(8,128)} custom-call(bf16[128,1152]{1,0:T(8,128)(2,1)S(1)} %copy-done, f32[128,1152]{1,0:T(8,128)S(1)} %get-tuple-element.59.own_ref, bf16[128,768]{1,0:T(8,128)(2,1)S(1)} %collective-permute-done.19.refs_0_, bf16[128,768]{1,0:T(8,128)(2,1)S(1)} %collective-permute-done.21.refs_1_, ...), custom_call_target="tpu_custom_call" | custom-call | flops 1474560 | bytes 1769472 | tf_op jit(solution)/shard_map/final/pallas_call | solution.py:341
  83.2 1.1 %final.3 = f32[128,1152]{1,0:T(8,128)} custom-call(bf16[128,1152]{1,0:T(8,128)(2,1)S(1)} %copy-done.1, f32[128,1152]{1,0:T(8,128)S(1)} %get-tuple-element.74.own_ref, bf16[128,768]{1,0:T(8,128)(2,1)S(1)} %collective-permute-done.24.refs_0_, bf16[128,768]{1,0:T(8,128)(2,1)S(1)} %collective-permute-done.25.refs_1_, ...), custom_call_target="tpu_custom_call" | custom-call | flops 1474560 | bytes 1769472 | tf_op jit(solution)/shard_map/final/pallas_call | solution.py:341
  (47 shorter events, 4.6 us)
Async XLA Ops:
  3.8 22.0 %collective-permute-start = (bf16[128,1536]{1,0:T(8,128)(2,1)}, bf16[128,1536]{1,0:T(8,128)(2,1)S(1)}, u32[]{:S(2)}, u32[]{:S(2)}) collective-permute-start(bf16[128,1536]{1,0:T(8,128)(2,1)} %get-tuple-element.41.refs_0_), channel_id=1, source_target_pairs={{0,16},{1,17},{2,18},{3,19},{4,20},{5,21},{6,22},{7,23},{8,24},{9,... | collective-permute-start | bytes 1179656 | tf_op jit(solution)/shard_map/ppermute | solution.py:62
  7.9 18.0 %collective-permute-start.1 = (bf16[128,1536]{1,0:T(8,128)(2,1)}, bf16[128,1536]{1,0:T(8,128)(2,1)S(1)}, u32[]{:S(2)}, u32[]{:S(2)}) collective-permute-start(bf16[128,1536]{1,0:T(8,128)(2,1)} %get-tuple-element.42.refs_4_), channel_id=1, source_target_pairs={{0,8},{1,9},{2,10},{3,11},{4,12},{5,13},{6,14},{7,15},{8,0},{9,1},... | collective-permute-start | bytes 1179656 | tf_op jit(solution)/shard_map/ppermute | solution.py:62
  9.5 20.3 %collective-permute-start.6 = (bf16[128,2688]{1,0:T(8,128)(2,1)}, bf16[128,2688]{1,0:T(8,128)(2,1)S(1)}, u32[]{:S(2)}, u32[]{:S(2)}) collective-permute-start(bf16[128,2688]{1,0:T(8,128)(2,1)} %get-tuple-element.47), channel_id=1, source_target_pairs={{0,4},{1,5},{2,6},{3,7},{4,0},{5,1},{6,2},{7,3},{8,12},{9,13},{10,... | collective-permute-start | bytes 2064392 | tf_op jit(solution)/shard_map/ppermute | solution.py:62
  9.5 20.3 %collective-permute-start.5 = (bf16[128,2688]{1,0:T(8,128)(2,1)}, bf16[128,2688]{1,0:T(8,128)(2,1)S(1)}, u32[]{:S(2)}, u32[]{:S(2)}) collective-permute-start(bf16[128,2688]{1,0:T(8,128)(2,1)} %get-tuple-element.47), channel_id=1, source_target_pairs={{0,2},{1,3},{2,0},{3,1},{4,6},{5,7},{6,4},{7,5},{8,10},{9,11},{10,... | collective-permute-start | bytes 2064392 | tf_op jit(solution)/shard_map/ppermute | solution.py:62
  11.0 18.8 %collective-permute-start.3 = (bf16[128,2688]{1,0:T(8,128)(2,1)}, bf16[128,2688]{1,0:T(8,128)(2,1)S(1)}, u32[]{:S(2)}, u32[]{:S(2)}) collective-permute-start(bf16[128,2688]{1,0:T(8,128)(2,1)} %get-tuple-element.44), channel_id=1, source_target_pairs={{0,1},{1,0},{2,3},{3,2},{4,5},{5,4},{6,7},{7,6},{8,9},{9,8},{10,11... | collective-permute-start | bytes 2064392 | tf_op jit(solution)/shard_map/ppermute | solution.py:62
  25.9 15.5 %collective-permute-start.2 = (bf16[128,1152]{1,0:T(8,128)(2,1)}, bf16[128,1152]{1,0:T(8,128)(2,1)S(1)}, u32[]{:S(2)}, u32[]{:S(2)}) collective-permute-start(bf16[128,1152]{1,0:T(8,128)(2,1)} %get-tuple-element.43.refs_0_), channel_id=1, source_target_pairs={{0,16},{1,17},{2,18},{3,19},{4,20},{5,21},{6,22},{7,23},{8,24},{9,... | collective-permute-start | bytes 884744 | tf_op jit(solution)/shard_map/ppermute | solution.py:62
  27.3 14.2 %collective-permute-start.4 = (bf16[128,1152]{1,0:T(8,128)(2,1)}, bf16[128,1152]{1,0:T(8,128)(2,1)S(1)}, u32[]{:S(2)}, u32[]{:S(2)}) collective-permute-start(bf16[128,1152]{1,0:T(8,128)(2,1)} %get-tuple-element.46.refs_4_), channel_id=1, source_target_pairs={{0,8},{1,9},{2,10},{3,11},{4,12},{5,13},{6,14},{7,15},{8,0},{9,1},... | collective-permute-start | bytes 884744 | tf_op jit(solution)/shard_map/ppermute | solution.py:62
  29.8 11.7 %collective-permute-start.7 = (bf16[128,1536]{1,0:T(8,128)(2,1)S(1)}, bf16[128,1536]{1,0:T(8,128)(2,1)S(1)}, u32[]{:S(2)}, u32[]{:S(2)}) collective-permute-start(bf16[128,1536]{1,0:T(8,128)(2,1)S(1)} %collective-permute-done.refs_1_), channel_id=1, source_target_pairs={{0,1},{1,0},{2,3},{3,2},{4,5},{5,4},{6,7},{7,6},{8,9},{9,8},{10,11... | collective-permute-start | bytes 1179656 | tf_op jit(solution)/shard_map/ppermute | solution.py:62
  31.3 10.2 %collective-permute-start.8 = (bf16[128,1536]{1,0:T(8,128)(2,1)S(1)}, bf16[128,1536]{1,0:T(8,128)(2,1)S(1)}, u32[]{:S(2)}, u32[]{:S(2)}) collective-permute-start(bf16[128,1536]{1,0:T(8,128)(2,1)S(1)} %collective-permute-done.1.refs_5_), channel_id=1, source_target_pairs={{0,2},{1,3},{2,0},{3,1},{4,6},{5,7},{6,4},{7,5},{8,10},{9,11},{10,... | collective-permute-start | bytes 1179656 | tf_op jit(solution)/shard_map/ppermute | solution.py:62
  32.8 8.7 %collective-permute-start.9 = (bf16[128,2688]{1,0:T(8,128)(2,1)S(1)}, bf16[128,2688]{1,0:T(8,128)(2,1)S(1)}, u32[]{:S(2)}, u32[]{:S(2)}) collective-permute-start(bf16[128,2688]{1,0:T(8,128)(2,1)S(1)} %collective-permute-done.5.refs_6_), channel_id=1, source_target_pairs={{0,4},{1,5},{2,6},{3,7},{4,0},{5,1},{6,2},{7,3},{8,12},{9,13},{10,... | collective-permute-start | bytes 2064392 | tf_op jit(solution)/shard_map/ppermute | solution.py:62
  41.5 3.4 %collective-permute-start.13 = (bf16[128,1536]{1,0:T(8,128)(2,1)S(1)}, bf16[128,1536]{1,0:T(8,128)(2,1)S(1)}, u32[]{:S(2)}, u32[]{:S(2)}) collective-permute-start(bf16[128,1536]{1,0:T(8,128)(2,1)S(1)} %collective-permute-done.1.refs_5_), channel_id=1, source_target_pairs={{0,4},{1,5},{2,6},{3,7},{4,0},{5,1},{6,2},{7,3},{8,12},{9,13},{10,... | collective-permute-start | bytes 1179656 | tf_op jit(solution)/shard_map/ppermute | solution.py:62
  41.6 3.3 %collective-permute-start.14 = (bf16[128,1536]{1,0:T(8,128)(2,1)S(1)}, bf16[128,1536]{1,0:T(8,128)(2,1)S(1)}, u32[]{:S(2)}, u32[]{:S(2)}) collective-permute-start(bf16[128,1536]{1,0:T(8,128)(2,1)S(1)} %collective-permute-done.8.refs_7_), channel_id=1, source_target_pairs={{0,4},{1,5},{2,6},{3,7},{4,0},{5,1},{6,2},{7,3},{8,12},{9,13},{10,... | collective-permute-start | bytes 1179656 | tf_op jit(solution)/shard_map/ppermute | solution.py:62
  42.1 7.6 %collective-permute-start.12 = (bf16[128,1152]{1,0:T(8,128)(2,1)S(1)}, bf16[128,1152]{1,0:T(8,128)(2,1)S(1)}, u32[]{:S(2)}, u32[]{:S(2)}) collective-permute-start(bf16[128,1152]{1,0:T(8,128)(2,1)S(1)} %collective-permute-done.4.refs_5_), channel_id=1, source_target_pairs={{0,4},{1,5},{2,6},{3,7},{4,0},{5,1},{6,2},{7,3},{8,12},{9,13},{10,... | collective-permute-start | bytes 884744 | tf_op jit(solution)/shard_map/ppermute | solution.py:62
  42.2 9.4 %collective-permute-start.11 = (bf16[128,1152]{1,0:T(8,128)(2,1)S(1)}, bf16[128,1152]{1,0:T(8,128)(2,1)S(1)}, u32[]{:S(2)}, u32[]{:S(2)}) collective-permute-start(bf16[128,1152]{1,0:T(8,128)(2,1)S(1)} %collective-permute-done.4.refs_5_), channel_id=1, source_target_pairs={{0,2},{1,3},{2,0},{3,1},{4,6},{5,7},{6,4},{7,5},{8,10},{9,11},{10,... | collective-permute-start | bytes 884744 | tf_op jit(solution)/shard_map/ppermute | solution.py:62
  43.6 9.1 %collective-permute-start.10 = (bf16[128,1152]{1,0:T(8,128)(2,1)S(1)}, bf16[128,1152]{1,0:T(8,128)(2,1)S(1)}, u32[]{:S(2)}, u32[]{:S(2)}) collective-permute-start(bf16[128,1152]{1,0:T(8,128)(2,1)S(1)} %collective-permute-done.2.refs_1_), channel_id=1, source_target_pairs={{0,1},{1,0},{2,3},{3,2},{4,5},{5,4},{6,7},{7,6},{8,9},{9,8},{10,11... | collective-permute-start | bytes 884744 | tf_op jit(solution)/shard_map/ppermute | solution.py:62
  46.9 6.2 %copy-start.4 = (bf16[128,1152]{1,0:T(8,128)(2,1)S(1)}, bf16[128,1152]{1,0:T(8,128)(2,1)}, u32[]{:S(2)}) copy-start(bf16[128,1152]{1,0:T(8,128)(2,1)} %get-tuple-element.43.refs_0_) | copy-start | bytes 884740
  46.9 6.2 %copy-start.5 = (bf16[128,1152]{1,0:T(8,128)(2,1)S(1)}, bf16[128,1152]{1,0:T(8,128)(2,1)}, u32[]{:S(2)}) copy-start(bf16[128,1152]{1,0:T(8,128)(2,1)} %get-tuple-element.46.refs_4_) | copy-start | bytes 884740
  51.5 1.6 %collective-permute-start.15 = (bf16[128,1152]{1,0:T(8,128)(2,1)S(1)}, bf16[128,1152]{1,0:T(8,128)(2,1)S(1)}, u32[]{:S(2)}, u32[]{:S(2)}) collective-permute-start(bf16[128,1152]{1,0:T(8,128)(2,1)S(1)} %collective-permute-done.11.refs_7_), channel_id=1, source_target_pairs={{0,4},{1,5},{2,6},{3,7},{4,0},{5,1},{6,2},{7,3},{8,12},{9,13},{10,... | collective-permute-start | bytes 884744 | tf_op jit(solution)/shard_map/ppermute | solution.py:62
  56.3 5.6 %collective-permute-start.16 = (bf16[256,1152]{1,0:T(8,128)(2,1)S(1)}, bf16[256,1152]{1,0:T(8,128)(2,1)S(1)}, u32[]{:S(2)}, u32[]{:S(2)}) collective-permute-start(bf16[256,1152]{1,0:T(8,128)(2,1)S(1)} %get-tuple-element.62), channel_id=1, source_target_pairs={{0,4},{1,5},{2,6},{3,7},{4,0},{5,1},{6,2},{7,3},{8,12},{9,13},{10,... | collective-permute-start | bytes 1769480 | tf_op jit(solution)/shard_map/ppermute | solution.py:62
  56.6 5.4 %collective-permute-start.17 = (bf16[256,1152]{1,0:T(8,128)(2,1)S(1)}, bf16[256,1152]{1,0:T(8,128)(2,1)S(1)}, u32[]{:S(2)}, u32[]{:S(2)}) collective-permute-start(bf16[256,1152]{1,0:T(8,128)(2,1)S(1)} %get-tuple-element.63), channel_id=1, source_target_pairs={{0,4},{1,5},{2,6},{3,7},{4,0},{5,1},{6,2},{7,3},{8,12},{9,13},{10,... | collective-permute-start | bytes 1769480 | tf_op jit(solution)/shard_map/ppermute | solution.py:62
  56.9 8.6 %collective-permute-start.20 = (bf16[128,768]{1,0:T(8,128)(2,1)S(1)}, bf16[128,768]{1,0:T(8,128)(2,1)S(1)}, u32[]{:S(2)}, u32[]{:S(2)}) collective-permute-start(bf16[128,768]{1,0:T(8,128)(2,1)S(1)} %get-tuple-element.70), channel_id=1, source_target_pairs={{0,1},{1,0},{2,3},{3,2},{4,5},{5,4},{6,7},{7,6},{8,9},{9,8},{10,11... | collective-permute-start | bytes 589832 | tf_op jit(solution)/shard_map/ppermute | solution.py:62
  58.2 16.9 %collective-permute-start.22 = (bf16[256,384]{1,0:T(8,128)(2,1)S(1)}, bf16[256,384]{1,0:T(8,128)(2,1)S(1)}, u32[]{:S(2)}, u32[]{:S(2)}) collective-permute-start(bf16[256,384]{1,0:T(8,128)(2,1)S(1)} %get-tuple-element.73), channel_id=1, source_target_pairs={{0,16},{1,17},{2,18},{3,19},{4,20},{5,21},{6,22},{7,23},{8,24},{9,... | collective-permute-start | bytes 589832 | tf_op jit(solution)/shard_map/ppermute | solution.py:62
  62.0 19.9 %copy-start = (bf16[128,1152]{1,0:T(8,128)(2,1)S(1)}, bf16[128,1152]{1,0:T(8,128)(2,1)}, u32[]{:S(2)}) copy-start(bf16[128,1152]{1,0:T(8,128)(2,1)} %x_ref.2) | copy-start | bytes 884740
  62.2 20.9 %copy-start.1 = (bf16[128,1152]{1,0:T(8,128)(2,1)S(1)}, bf16[128,1152]{1,0:T(8,128)(2,1)}, u32[]{:S(2)}) copy-start(bf16[128,1152]{1,0:T(8,128)(2,1)} %x_ref.3) | copy-start | bytes 884740
  62.2 7.9 %collective-permute-start.18 = (bf16[128,768]{1,0:T(8,128)(2,1)S(1)}, bf16[128,768]{1,0:T(8,128)(2,1)S(1)}, u32[]{:S(2)}, u32[]{:S(2)}) collective-permute-start(bf16[128,768]{1,0:T(8,128)(2,1)S(1)} %get-tuple-element.64), channel_id=1, source_target_pairs={{0,2},{1,3},{2,0},{3,1},{4,6},{5,7},{6,4},{7,5},{8,10},{9,11},{10,... | collective-permute-start | bytes 589832 | tf_op jit(solution)/shard_map/ppermute | solution.py:62
  63.8 13.4 %collective-permute-start.26 = (bf16[256,384]{1,0:T(8,128)(2,1)S(1)}, bf16[256,384]{1,0:T(8,128)(2,1)S(1)}, u32[]{:S(2)}, u32[]{:S(2)}) collective-permute-start(bf16[256,384]{1,0:T(8,128)(2,1)S(1)} %get-tuple-element.68), channel_id=1, source_target_pairs={{0,8},{1,9},{2,10},{3,11},{4,12},{5,13},{6,14},{7,15},{8,0},{9,1},... | collective-permute-start | bytes 589832 | tf_op jit(solution)/shard_map/ppermute | solution.py:62
  65.5 17.5 %collective-permute-start.24 = (bf16[128,768]{1,0:T(8,128)(2,1)S(1)}, bf16[128,768]{1,0:T(8,128)(2,1)S(1)}, u32[]{:S(2)}, u32[]{:S(2)}) collective-permute-start(bf16[128,768]{1,0:T(8,128)(2,1)S(1)} %get-tuple-element.75), channel_id=1, source_target_pairs={{0,2},{1,3},{2,0},{3,1},{4,6},{5,7},{6,4},{7,5},{8,10},{9,11},{10,... | collective-permute-start | bytes 589832 | tf_op jit(solution)/shard_map/ppermute | solution.py:62
  66.1 12.5 %collective-permute-start.21 = (bf16[128,768]{1,0:T(8,128)(2,1)S(1)}, bf16[128,768]{1,0:T(8,128)(2,1)S(1)}, u32[]{:S(2)}, u32[]{:S(2)}) collective-permute-start(bf16[128,768]{1,0:T(8,128)(2,1)S(1)} %add_convert_fusion.1), channel_id=1, source_target_pairs={{0,16},{1,17},{2,18},{3,19},{4,20},{5,21},{6,22},{7,23},{8,24},{9,... | collective-permute-start | bytes 589832 | tf_op jit(solution)/shard_map/ppermute | solution.py:62
  75.1 5.0 %collective-permute-start.23 = (bf16[128,384]{1,0:T(8,128)(2,1)S(1)}, bf16[128,384]{1,0:T(8,128)(2,1)S(1)}, u32[]{:S(2)}, u32[]{:S(2)}) collective-permute-start(bf16[128,384]{1,0:T(8,128)(2,1)S(1)} %add_convert_fusion.3), channel_id=1, source_target_pairs={{0,1},{1,0},{2,3},{3,2},{4,5},{5,4},{6,7},{7,6},{8,9},{9,8},{10,11... | collective-permute-start | bytes 294920 | tf_op jit(solution)/shard_map/ppermute | solution.py:62
  75.7 6.2 %collective-permute-start.19 = (bf16[128,768]{1,0:T(8,128)(2,1)S(1)}, bf16[128,768]{1,0:T(8,128)(2,1)S(1)}, u32[]{:S(2)}, u32[]{:S(2)}) collective-permute-start(bf16[128,768]{1,0:T(8,128)(2,1)S(1)} %get-tuple-element.65), channel_id=1, source_target_pairs={{0,1},{1,0},{2,3},{3,2},{4,5},{5,4},{6,7},{7,6},{8,9},{9,8},{10,11... | collective-permute-start | bytes 589832 | tf_op jit(solution)/shard_map/ppermute | solution.py:62
  77.2 5.9 %collective-permute-start.25 = (bf16[128,768]{1,0:T(8,128)(2,1)S(1)}, bf16[128,768]{1,0:T(8,128)(2,1)S(1)}, u32[]{:S(2)}, u32[]{:S(2)}) collective-permute-start(bf16[128,768]{1,0:T(8,128)(2,1)S(1)} %add_convert_fusion), channel_id=1, source_target_pairs={{0,8},{1,9},{2,10},{3,11},{4,12},{5,13},{6,14},{7,15},{8,0},{9,1},... | collective-permute-start | bytes 589832 | tf_op jit(solution)/shard_map/ppermute | solution.py:62
  78.5 4.6 %collective-permute-start.27 = (bf16[128,384]{1,0:T(8,128)(2,1)S(1)}, bf16[128,384]{1,0:T(8,128)(2,1)S(1)}, u32[]{:S(2)}, u32[]{:S(2)}) collective-permute-start(bf16[128,384]{1,0:T(8,128)(2,1)S(1)} %add_convert_fusion.2), channel_id=1, source_target_pairs={{0,2},{1,3},{2,0},{3,1},{4,6},{5,7},{6,4},{7,5},{8,10},{9,11},{10,... | collective-permute-start | bytes 294920 | tf_op jit(solution)/shard_map/ppermute | solution.py:62
  (2 other events, 2.0 us)

commit v8 on v7

--- a/solution.py
+++ b/solution.py
@@ -460,11 +460,11 @@
         plan.send(total(txt_stay[a], [row_in[b, a] for b in range(1, row)]), "near", -a) for a in range(1, near)
     ]
     img_side = [
-        plan.send(total(after(img_kept[b - 1], *row_in.values()), [v[b * rows : (b + 1) * rows] for v in long_in]), "col", -b)
+        plan.send(total(after(img_kept[b - 1], *[*txt_long_in, *row_in.values()]), [v[b * rows : (b + 1) * rows] for v in long_in]), "col", -b)
         for b in range(1, col)
     ]
     txt_side = [
-        plan.send(total(txt_kept[b - 1], [v[b * rows : (b + 1) * rows] for v in txt_long_in]), "row", -b)
+        plan.send(total(after(txt_kept[b - 1], *row_in.values()), [v[b * rows : (b + 1) * rows] for v in txt_long_in]), "row", -b)
         for b in range(1, row)
     ]
     col_ahead = list(row_in.values())

time: 84.5 us -> 84.5 us (level)
  no operation moved by 1% of the time
where the time goes in v8:
time: 84.5 us; the launch traced here: 84.3 us
  waiting for transfers between devices  36.7 us (43%)
  starting transfers between devices  31.5 us (37%)
  Pallas kernels  13.2 us (16%)
  local copies, waits for them, and re-layouts  2.01 us (2%)
    ppermute x28, waiting for transfers between devices, send(): return lax.ppermute(x, AXES, pairs)  36.7 us
    ppermute x28, starting transfers between devices, send(): return lax.ppermute(x, AXES, pairs)  31.5 us
    pallas_call x1, Pallas kernels, pair_and_sent(): pl.pallas_call(functools.partial(pair_kernel, images, texts, far, skip, h...  3.23 us
    pallas_call x1, Pallas kernels, unit_rows(): pl.pallas_call(functools.partial(unit_kernel, len(arrays)), out_shape=[ja...  3.15 us
    pallas_call x1, Pallas kernels, teacher_targets(): pl.pallas_call(functools.partial(teacher_kernel, images, texts), out_shap...  2.77 us
    pallas_call x2, Pallas kernels, final(): pl.pallas_call(functools.partial(final_kernel, half, len(lows)), out_shap...  2.3 us
    unnamed x12, local copies, waits for them, and re-layouts  2.01 us
  transfers between devices with their start and end apart: 28, of which 12 were waited for; matrix products, arithmetic and copies ran while one was open for 0% of the time, Pallas kernels for 7%

profile of v8, /device:TPU:0, one launch (start us, length us, event | category | flops | bytes accessed | tf_op | source)
XLA Modules:
  0.0 84.3 jit_solution(10932943236501050788)
XLA Ops:
  0.6 3.1 %unit_rows.1 = (bf16[128,1536]{1,0:T(8,128)(2,1)}, bf16[128,1536]{1,0:T(8,128)(2,1)}, bf16[128,1152]{1,0:T(8,128)(2,1)}, bf16[128,1152]{1,0:T(8,128)(2,1)}, bf16...) custom-call(bf16[128,1536]{1,0:T(8,128)(2,1)} %refs_0_.1, bf16[128,1536]{1,0:T(8,128)(2,1)} %refs_1_.1, ...), custom_call_target="tpu_custom_call" | custom-call | flops 2752512 | bytes 4128768 | tf_op jit(solution)/shard_map/unit_rows/pallas_call | solution.py:107
  3.8 4.1 %collective-permute-start = (bf16[128,1536]{1,0:T(8,128)(2,1)}, bf16[128,1536]{1,0:T(8,128)(2,1)S(1)}, u32[]{:S(2)}, u32[]{:S(2)}) collective-permute-start(bf16[128,1536]{1,0:T(8,128)(2,1)} %get-tuple-element.42.refs_0_), channel_id=1, source_target_pairs={{0,16},{1,17},{2,18},{3,19},{4,20},{5,21},{6,22},{7,23},{8,24},{9,... | collective-permute-start | bytes 1179656 | tf_op jit(solution)/shard_map/ppermute | solution.py:62
  7.9 1.6 %collective-permute-start.1 = (bf16[128,1536]{1,0:T(8,128)(2,1)}, bf16[128,1536]{1,0:T(8,128)(2,1)S(1)}, u32[]{:S(2)}, u32[]{:S(2)}) collective-permute-start(bf16[128,1536]{1,0:T(8,128)(2,1)} %get-tuple-element.43.refs_4_), channel_id=1, source_target_pairs={{0,8},{1,9},{2,10},{3,11},{4,12},{5,13},{6,14},{7,15},{8,0},{9,1},... | collective-permute-start | bytes 1179656 | tf_op jit(solution)/shard_map/ppermute | solution.py:62
  9.5 1.5 %collective-permute-start.5 = (bf16[128,2688]{1,0:T(8,128)(2,1)}, bf16[128,2688]{1,0:T(8,128)(2,1)S(1)}, u32[]{:S(2)}, u32[]{:S(2)}) collective-permute-start(bf16[128,2688]{1,0:T(8,128)(2,1)} %get-tuple-element.48), channel_id=1, source_target_pairs={{0,2},{1,3},{2,0},{3,1},{4,6},{5,7},{6,4},{7,5},{8,10},{9,11},{10,... | collective-permute-start | bytes 2064392 | tf_op jit(solution)/shard_map/ppermute | solution.py:62
  11.0 1.5 %collective-permute-start.3 = (bf16[128,2688]{1,0:T(8,128)(2,1)}, bf16[128,2688]{1,0:T(8,128)(2,1)S(1)}, u32[]{:S(2)}, u32[]{:S(2)}) collective-permute-start(bf16[128,2688]{1,0:T(8,128)(2,1)} %get-tuple-element.45), channel_id=1, source_target_pairs={{0,1},{1,0},{2,3},{3,2},{4,5},{5,4},{6,7},{7,6},{8,9},{9,8},{10,11... | collective-permute-start | bytes 2064392 | tf_op jit(solution)/shard_map/ppermute | solution.py:62
  12.5 13.3 %collective-permute-done.refs_1_ = bf16[128,1536]{1,0:T(8,128)(2,1)S(1)} collective-permute-done((bf16[128,1536]{1,0:T(8,128)(2,1)}, bf16[128,1536]{1,0:T(8,128)(2,1)S(1)}, u32[]{:S(2)}, u32[]{:S(2)}) %collective-permute-start) | collective-permute-done | bytes 393248 | tf_op jit(solution)/shard_map/ppermute | solution.py:62
  25.9 1.4 %collective-permute-start.2 = (bf16[128,1152]{1,0:T(8,128)(2,1)}, bf16[128,1152]{1,0:T(8,128)(2,1)S(1)}, u32[]{:S(2)}, u32[]{:S(2)}) collective-permute-start(bf16[128,1152]{1,0:T(8,128)(2,1)} %get-tuple-element.44.refs_0_), channel_id=1, source_target_pairs={{0,16},{1,17},{2,18},{3,19},{4,20},{5,21},{6,22},{7,23},{8,24},{9,... | collective-permute-start | bytes 884744 | tf_op jit(solution)/shard_map/ppermute | solution.py:62
  27.3 2.4 %collective-permute-start.4 = (bf16[128,1152]{1,0:T(8,128)(2,1)}, bf16[128,1152]{1,0:T(8,128)(2,1)S(1)}, u32[]{:S(2)}, u32[]{:S(2)}) collective-permute-start(bf16[128,1152]{1,0:T(8,128)(2,1)} %get-tuple-element.47.refs_4_), channel_id=1, source_target_pairs={{0,8},{1,9},{2,10},{3,11},{4,12},{5,13},{6,14},{7,15},{8,0},{9,1},... | collective-permute-start | bytes 884744 | tf_op jit(solution)/shard_map/ppermute | solution.py:62
  29.8 1.6 %collective-permute-start.7 = (bf16[128,1536]{1,0:T(8,128)(2,1)S(1)}, bf16[128,1536]{1,0:T(8,128)(2,1)S(1)}, u32[]{:S(2)}, u32[]{:S(2)}) collective-permute-start(bf16[128,1536]{1,0:T(8,128)(2,1)S(1)} %collective-permute-done.refs_1_), channel_id=1, source_target_pairs={{0,1},{1,0},{2,3},{3,2},{4,5},{5,4},{6,7},{7,6},{8,9},{9,8},{10,11... | collective-permute-start | bytes 1179656 | tf_op jit(solution)/shard_map/ppermute | solution.py:62
  31.3 1.5 %collective-permute-start.8 = (bf16[128,1536]{1,0:T(8,128)(2,1)S(1)}, bf16[128,1536]{1,0:T(8,128)(2,1)S(1)}, u32[]{:S(2)}, u32[]{:S(2)}) collective-permute-start(bf16[128,1536]{1,0:T(8,128)(2,1)S(1)} %collective-permute-done.1.refs_5_), channel_id=1, source_target_pairs={{0,2},{1,3},{2,0},{3,1},{4,6},{5,7},{6,4},{7,5},{8,10},{9,11},{10,... | collective-permute-start | bytes 1179656 | tf_op jit(solution)/shard_map/ppermute | solution.py:62
  32.8 8.6 %collective-permute-done.2.refs_1_ = bf16[128,1152]{1,0:T(8,128)(2,1)S(1)} collective-permute-done((bf16[128,1152]{1,0:T(8,128)(2,1)}, bf16[128,1152]{1,0:T(8,128)(2,1)S(1)}, u32[]{:S(2)}, u32[]{:S(2)}) %collective-permute-start.2) | collective-permute-done | bytes 294944 | tf_op jit(solution)/shard_map/ppermute | solution.py:62
  42.2 1.4 %collective-permute-start.11 = (bf16[128,1152]{1,0:T(8,128)(2,1)S(1)}, bf16[128,1152]{1,0:T(8,128)(2,1)S(1)}, u32[]{:S(2)}, u32[]{:S(2)}) collective-permute-start(bf16[128,1152]{1,0:T(8,128)(2,1)S(1)} %collective-permute-done.4.refs_5_), channel_id=1, source_target_pairs={{0,2},{1,3},{2,0},{3,1},{4,6},{5,7},{6,4},{7,5},{8,10},{9,11},{10,... | collective-permute-start | bytes 884744 | tf_op jit(solution)/shard_map/ppermute | solution.py:62
  43.6 1.4 %collective-permute-start.10 = (bf16[128,1152]{1,0:T(8,128)(2,1)S(1)}, bf16[128,1152]{1,0:T(8,128)(2,1)S(1)}, u32[]{:S(2)}, u32[]{:S(2)}) collective-permute-start(bf16[128,1152]{1,0:T(8,128)(2,1)S(1)} %collective-permute-done.2.refs_1_), channel_id=1, source_target_pairs={{0,1},{1,0},{2,3},{3,2},{4,5},{5,4},{6,7},{7,6},{8,9},{9,8},{10,11... | collective-permute-start | bytes 884744 | tf_op jit(solution)/shard_map/ppermute | solution.py:62
  45.9 1.0 %copy-done.3 = bf16[128,1536]{1,0:T(8,128)(2,1)S(1)} copy-done((bf16[128,1536]{1,0:T(8,128)(2,1)S(1)}, bf16[128,1536]{1,0:T(8,128)(2,1)}, u32[]{:S(2)}) %copy-start.3) | copy-done | bytes 393240
  46.9 2.8 %teacher_targets.1.refs_12_ = f32[512,1024]{1,0:T(8,128)S(1)} custom-call(bf16[128,1536]{1,0:T(8,128)(2,1)S(1)} %copy-done.2, bf16[128,1536]{1,0:T(8,128)(2,1)S(1)} %collective-permute-done.refs_1_, bf16[128,2688]{1,0:T(8,128)(2,1)S(1)} %collective-permute-done.3.refs_2_, bf16[128,1536]{1,0:T(8,128)(2,1)S(1)} %collective-permute-done.7.refs_3_, ...), custom_call_target="tpu_custom_call" | custom-call | flops 1610612736 | bytes 6815744 | tf_op jit(solution)/shard_map/teacher_targets/pallas_call | solution.py:154
  49.7 1.8 %collective-permute-done.11.refs_7_ = bf16[128,1152]{1,0:T(8,128)(2,1)S(1)} collective-permute-done((bf16[128,1152]{1,0:T(8,128)(2,1)S(1)}, bf16[128,1152]{1,0:T(8,128)(2,1)S(1)}, u32[]{:S(2)}, u32[]{:S(2)}) %collective-permute-start.11) | collective-permute-done | bytes 294944 | tf_op jit(solution)/shard_map/ppermute | solution.py:62
  51.5 1.2 %collective-permute-done.10.refs_3_ = bf16[128,1152]{1,0:T(8,128)(2,1)S(1)} collective-permute-done((bf16[128,1152]{1,0:T(8,128)(2,1)S(1)}, bf16[128,1152]{1,0:T(8,128)(2,1)S(1)}, u32[]{:S(2)}, u32[]{:S(2)}) %collective-permute-start.10) | collective-permute-done | bytes 294944 | tf_op jit(solution)/shard_map/ppermute | solution.py:62
  53.1 3.2 %pair_and_sent.1 = (bf16[512,1024]{1,0:T(8,128)(2,1)S(1)}, bf16[512,1152]{1,0:T(8,128)(2,1)S(1)}, bf16[1024,1152]{1,0:T(8,128)(2,1)S(1)}, bf16[128,768]{1,0:T(8,...) custom-call(bf16[128,1152]{1,0:T(8,128)(2,1)S(1)} %copy-done.4, ...), custom_call_target="tpu_custom_call" | custom-call | flops 2415919104 | bytes 7733248 | tf_op jit(solution)/shard_map/pair_and_sent/pallas_call | solution.py:229
  56.9 1.2 %collective-permute-start.20 = (bf16[128,768]{1,0:T(8,128)(2,1)S(1)}, bf16[128,768]{1,0:T(8,128)(2,1)S(1)}, u32[]{:S(2)}, u32[]{:S(2)}) collective-permute-start(bf16[128,768]{1,0:T(8,128)(2,1)S(1)} %get-tuple-element.71), channel_id=1, source_target_pairs={{0,1},{1,0},{2,3},{3,2},{4,5},{5,4},{6,7},{7,6},{8,9},{9,8},{10,11... | collective-permute-start | bytes 589832 | tf_op jit(solution)/shard_map/ppermute | solution.py:62
  58.2 2.3 %collective-permute-start.23 = (bf16[256,384]{1,0:T(8,128)(2,1)S(1)}, bf16[256,384]{1,0:T(8,128)(2,1)S(1)}, u32[]{:S(2)}, u32[]{:S(2)}) collective-permute-start(bf16[256,384]{1,0:T(8,128)(2,1)S(1)} %get-tuple-element.74), channel_id=1, source_target_pairs={{0,16},{1,17},{2,18},{3,19},{4,20},{5,21},{6,22},{7,23},{8,24},{9,... | collective-permute-start | bytes 589832 | tf_op jit(solution)/shard_map/ppermute | solution.py:62
  60.4 1.5 %kept.1 = (f32[128,1152]{1,0:T(8,128)S(1)}, f32[128,768]{1,0:T(8,128)S(1)}, f32[512,1152]{1,0:T(8,128)S(1)}) custom-call(bf16[512,1024]{1,0:T(8,128)(2,1)S(1)} %get-tuple-element.57.pair, bf16[512,1152]{1,0:T(8,128)(2,1)S(1)} %get-tuple-element.58.img, bf16[1024,1152]{1,0:T(8,128)(2,1)S(1)} %get-tuple-element.59.txt), custom_call_target="tpu_custom_call" | custom-call | flops 1207959552 | bytes 6946816 | tf_op jit(solution)/shard_map/kept/pallas_call | solution.py:264
  62.2 1.6 %collective-permute-start.18 = (bf16[128,768]{1,0:T(8,128)(2,1)S(1)}, bf16[128,768]{1,0:T(8,128)(2,1)S(1)}, u32[]{:S(2)}, u32[]{:S(2)}) collective-permute-start(bf16[128,768]{1,0:T(8,128)(2,1)S(1)} %get-tuple-element.65), channel_id=1, source_target_pairs={{0,2},{1,3},{2,0},{3,1},{4,6},{5,7},{6,4},{7,5},{8,10},{9,11},{10,... | collective-permute-start | bytes 589832 | tf_op jit(solution)/shard_map/ppermute | solution.py:62
  63.8 1.7 %collective-permute-start.22 = (bf16[256,384]{1,0:T(8,128)(2,1)S(1)}, bf16[256,384]{1,0:T(8,128)(2,1)S(1)}, u32[]{:S(2)}, u32[]{:S(2)}) collective-permute-start(bf16[256,384]{1,0:T(8,128)(2,1)S(1)} %get-tuple-element.69), channel_id=1, source_target_pairs={{0,8},{1,9},{2,10},{3,11},{4,12},{5,13},{6,14},{7,15},{8,0},{9,1},... | collective-permute-start | bytes 589832 | tf_op jit(solution)/shard_map/ppermute | solution.py:62
  66.1 1.4 %collective-permute-start.21 = (bf16[128,768]{1,0:T(8,128)(2,1)S(1)}, bf16[128,768]{1,0:T(8,128)(2,1)S(1)}, u32[]{:S(2)}, u32[]{:S(2)}) collective-permute-start(bf16[128,768]{1,0:T(8,128)(2,1)S(1)} %add_convert_fusion.1), channel_id=1, source_target_pairs={{0,16},{1,17},{2,18},{3,19},{4,20},{5,21},{6,22},{7,23},{8,24},{9,... | collective-permute-start | bytes 589832 | tf_op jit(solution)/shard_map/ppermute | solution.py:62
  67.5 2.6 %collective-permute-done.18 = bf16[128,768]{1,0:T(8,128)(2,1)S(1)} collective-permute-done((bf16[128,768]{1,0:T(8,128)(2,1)S(1)}, bf16[128,768]{1,0:T(8,128)(2,1)S(1)}, u32[]{:S(2)}, u32[]{:S(2)}) %collective-permute-start.18) | collective-permute-done | bytes 196640 | tf_op jit(solution)/shard_map/ppermute | solution.py:62
  70.7 3.4 %collective-permute-done.22.refs_3_ = bf16[256,384]{1,0:T(8,128)(2,1)S(1)} collective-permute-done((bf16[256,384]{1,0:T(8,128)(2,1)S(1)}, bf16[256,384]{1,0:T(8,128)(2,1)S(1)}, u32[]{:S(2)}, u32[]{:S(2)}) %collective-permute-start.22) | collective-permute-done | bytes 196640 | tf_op jit(solution)/shard_map/ppermute | solution.py:62
  74.5 1.2 %collective-permute-start.24 = (bf16[128,384]{1,0:T(8,128)(2,1)S(1)}, bf16[128,384]{1,0:T(8,128)(2,1)S(1)}, u32[]{:S(2)}, u32[]{:S(2)}) collective-permute-start(bf16[128,384]{1,0:T(8,128)(2,1)S(1)} %add_convert_fusion.3), channel_id=1, source_target_pairs={{0,1},{1,0},{2,3},{3,2},{4,5},{5,4},{6,7},{7,6},{8,9},{9,8},{10,11... | collective-permute-start | bytes 294920 | tf_op jit(solution)/shard_map/ppermute | solution.py:62
  75.7 2.8 %collective-permute-done.21.refs_1_ = bf16[128,768]{1,0:T(8,128)(2,1)S(1)} collective-permute-done((bf16[128,768]{1,0:T(8,128)(2,1)S(1)}, bf16[128,768]{1,0:T(8,128)(2,1)S(1)}, u32[]{:S(2)}, u32[]{:S(2)}) %collective-permute-start.21) | collective-permute-done | bytes 196640 | tf_op jit(solution)/shard_map/ppermute | solution.py:62
  78.5 1.5 %collective-permute-start.27 = (bf16[128,384]{1,0:T(8,128)(2,1)S(1)}, bf16[128,384]{1,0:T(8,128)(2,1)S(1)}, u32[]{:S(2)}, u32[]{:S(2)}) collective-permute-start(bf16[128,384]{1,0:T(8,128)(2,1)S(1)} %add_convert_fusion.2), channel_id=1, source_target_pairs={{0,2},{1,3},{2,0},{3,1},{4,6},{5,7},{6,4},{7,5},{8,10},{9,11},{10,... | collective-permute-start | bytes 294920 | tf_op jit(solution)/shard_map/ppermute | solution.py:62
  80.1 1.1 %final.2 = f32[128,1152]{1,0:T(8,128)} custom-call(bf16[128,1152]{1,0:T(8,128)(2,1)S(1)} %copy-done, f32[128,1152]{1,0:T(8,128)S(1)} %get-tuple-element.60.own_ref, bf16[128,768]{1,0:T(8,128)(2,1)S(1)} %collective-permute-done.19.refs_0_, bf16[128,768]{1,0:T(8,128)(2,1)S(1)} %collective-permute-done.21.refs_1_, ...), custom_call_target="tpu_custom_call" | custom-call | flops 1474560 | bytes 1769472 | tf_op jit(solution)/shard_map/final/pallas_call | solution.py:341
  81.2 1.9 %collective-permute-done.27.refs_2_ = bf16[128,384]{1,0:T(8,128)(2,1)S(1)} collective-permute-done((bf16[128,384]{1,0:T(8,128)(2,1)S(1)}, bf16[128,384]{1,0:T(8,128)(2,1)S(1)}, u32[]{:S(2)}, u32[]{:S(2)}) %collective-permute-start.27) | collective-permute-done | bytes 98336 | tf_op jit(solution)/shard_map/ppermute | solution.py:62
  83.2 1.1 %final.3 = f32[128,1152]{1,0:T(8,128)} custom-call(bf16[128,1152]{1,0:T(8,128)(2,1)S(1)} %copy-done.1, f32[128,1152]{1,0:T(8,128)S(1)} %get-tuple-element.75.own_ref, bf16[128,768]{1,0:T(8,128)(2,1)S(1)} %collective-permute-done.25.refs_0_, bf16[128,768]{1,0:T(8,128)(2,1)S(1)} %collective-permute-done.26.refs_1_, ...), custom_call_target="tpu_custom_call" | custom-call | flops 1474560 | bytes 1769472 | tf_op jit(solution)/shard_map/final/pallas_call | solution.py:341
  (47 shorter events, 4.7 us)
Async XLA Ops:
  3.8 22.0 %collective-permute-start = (bf16[128,1536]{1,0:T(8,128)(2,1)}, bf16[128,1536]{1,0:T(8,128)(2,1)S(1)}, u32[]{:S(2)}, u32[]{:S(2)}) collective-permute-start(bf16[128,1536]{1,0:T(8,128)(2,1)} %get-tuple-element.42.refs_0_), channel_id=1, source_target_pairs={{0,16},{1,17},{2,18},{3,19},{4,20},{5,21},{6,22},{7,23},{8,24},{9,... | collective-permute-start | bytes 1179656 | tf_op jit(solution)/shard_map/ppermute | solution.py:62
  7.9 18.0 %collective-permute-start.1 = (bf16[128,1536]{1,0:T(8,128)(2,1)}, bf16[128,1536]{1,0:T(8,128)(2,1)S(1)}, u32[]{:S(2)}, u32[]{:S(2)}) collective-permute-start(bf16[128,1536]{1,0:T(8,128)(2,1)} %get-tuple-element.43.refs_4_), channel_id=1, source_target_pairs={{0,8},{1,9},{2,10},{3,11},{4,12},{5,13},{6,14},{7,15},{8,0},{9,1},... | collective-permute-start | bytes 1179656 | tf_op jit(solution)/shard_map/ppermute | solution.py:62
  9.5 20.3 %collective-permute-start.6 = (bf16[128,2688]{1,0:T(8,128)(2,1)}, bf16[128,2688]{1,0:T(8,128)(2,1)S(1)}, u32[]{:S(2)}, u32[]{:S(2)}) collective-permute-start(bf16[128,2688]{1,0:T(8,128)(2,1)} %get-tuple-element.48), channel_id=1, source_target_pairs={{0,4},{1,5},{2,6},{3,7},{4,0},{5,1},{6,2},{7,3},{8,12},{9,13},{10,... | collective-permute-start | bytes 2064392 | tf_op jit(solution)/shard_map/ppermute | solution.py:62
  9.5 20.3 %collective-permute-start.5 = (bf16[128,2688]{1,0:T(8,128)(2,1)}, bf16[128,2688]{1,0:T(8,128)(2,1)S(1)}, u32[]{:S(2)}, u32[]{:S(2)}) collective-permute-start(bf16[128,2688]{1,0:T(8,128)(2,1)} %get-tuple-element.48), channel_id=1, source_target_pairs={{0,2},{1,3},{2,0},{3,1},{4,6},{5,7},{6,4},{7,5},{8,10},{9,11},{10,... | collective-permute-start | bytes 2064392 | tf_op jit(solution)/shard_map/ppermute | solution.py:62
  11.0 18.8 %collective-permute-start.3 = (bf16[128,2688]{1,0:T(8,128)(2,1)}, bf16[128,2688]{1,0:T(8,128)(2,1)S(1)}, u32[]{:S(2)}, u32[]{:S(2)}) collective-permute-start(bf16[128,2688]{1,0:T(8,128)(2,1)} %get-tuple-element.45), channel_id=1, source_target_pairs={{0,1},{1,0},{2,3},{3,2},{4,5},{5,4},{6,7},{7,6},{8,9},{9,8},{10,11... | collective-permute-start | bytes 2064392 | tf_op jit(solution)/shard_map/ppermute | solution.py:62
  25.9 15.5 %collective-permute-start.2 = (bf16[128,1152]{1,0:T(8,128)(2,1)}, bf16[128,1152]{1,0:T(8,128)(2,1)S(1)}, u32[]{:S(2)}, u32[]{:S(2)}) collective-permute-start(bf16[128,1152]{1,0:T(8,128)(2,1)} %get-tuple-element.44.refs_0_), channel_id=1, source_target_pairs={{0,16},{1,17},{2,18},{3,19},{4,20},{5,21},{6,22},{7,23},{8,24},{9,... | collective-permute-start | bytes 884744 | tf_op jit(solution)/shard_map/ppermute | solution.py:62
  27.3 14.2 %collective-permute-start.4 = (bf16[128,1152]{1,0:T(8,128)(2,1)}, bf16[128,1152]{1,0:T(8,128)(2,1)S(1)}, u32[]{:S(2)}, u32[]{:S(2)}) collective-permute-start(bf16[128,1152]{1,0:T(8,128)(2,1)} %get-tuple-element.47.refs_4_), channel_id=1, source_target_pairs={{0,8},{1,9},{2,10},{3,11},{4,12},{5,13},{6,14},{7,15},{8,0},{9,1},... | collective-permute-start | bytes 884744 | tf_op jit(solution)/shard_map/ppermute | solution.py:62
  29.8 11.7 %collective-permute-start.7 = (bf16[128,1536]{1,0:T(8,128)(2,1)S(1)}, bf16[128,1536]{1,0:T(8,128)(2,1)S(1)}, u32[]{:S(2)}, u32[]{:S(2)}) collective-permute-start(bf16[128,1536]{1,0:T(8,128)(2,1)S(1)} %collective-permute-done.refs_1_), channel_id=1, source_target_pairs={{0,1},{1,0},{2,3},{3,2},{4,5},{5,4},{6,7},{7,6},{8,9},{9,8},{10,11... | collective-permute-start | bytes 1179656 | tf_op jit(solution)/shard_map/ppermute | solution.py:62
  31.3 10.2 %collective-permute-start.8 = (bf16[128,1536]{1,0:T(8,128)(2,1)S(1)}, bf16[128,1536]{1,0:T(8,128)(2,1)S(1)}, u32[]{:S(2)}, u32[]{:S(2)}) collective-permute-start(bf16[128,1536]{1,0:T(8,128)(2,1)S(1)} %collective-permute-done.1.refs_5_), channel_id=1, source_target_pairs={{0,2},{1,3},{2,0},{3,1},{4,6},{5,7},{6,4},{7,5},{8,10},{9,11},{10,... | collective-permute-start | bytes 1179656 | tf_op jit(solution)/shard_map/ppermute | solution.py:62
  32.8 8.7 %collective-permute-start.9 = (bf16[128,2688]{1,0:T(8,128)(2,1)S(1)}, bf16[128,2688]{1,0:T(8,128)(2,1)S(1)}, u32[]{:S(2)}, u32[]{:S(2)}) collective-permute-start(bf16[128,2688]{1,0:T(8,128)(2,1)S(1)} %collective-permute-done.5.refs_6_), channel_id=1, source_target_pairs={{0,4},{1,5},{2,6},{3,7},{4,0},{5,1},{6,2},{7,3},{8,12},{9,13},{10,... | collective-permute-start | bytes 2064392 | tf_op jit(solution)/shard_map/ppermute | solution.py:62
  41.5 3.4 %collective-permute-start.13 = (bf16[128,1536]{1,0:T(8,128)(2,1)S(1)}, bf16[128,1536]{1,0:T(8,128)(2,1)S(1)}, u32[]{:S(2)}, u32[]{:S(2)}) collective-permute-start(bf16[128,1536]{1,0:T(8,128)(2,1)S(1)} %collective-permute-done.1.refs_5_), channel_id=1, source_target_pairs={{0,4},{1,5},{2,6},{3,7},{4,0},{5,1},{6,2},{7,3},{8,12},{9,13},{10,... | collective-permute-start | bytes 1179656 | tf_op jit(solution)/shard_map/ppermute | solution.py:62
  41.6 3.3 %collective-permute-start.14 = (bf16[128,1536]{1,0:T(8,128)(2,1)S(1)}, bf16[128,1536]{1,0:T(8,128)(2,1)S(1)}, u32[]{:S(2)}, u32[]{:S(2)}) collective-permute-start(bf16[128,1536]{1,0:T(8,128)(2,1)S(1)} %collective-permute-done.8.refs_7_), channel_id=1, source_target_pairs={{0,4},{1,5},{2,6},{3,7},{4,0},{5,1},{6,2},{7,3},{8,12},{9,13},{10,... | collective-permute-start | bytes 1179656 | tf_op jit(solution)/shard_map/ppermute | solution.py:62
  42.1 7.6 %collective-permute-start.12 = (bf16[128,1152]{1,0:T(8,128)(2,1)S(1)}, bf16[128,1152]{1,0:T(8,128)(2,1)S(1)}, u32[]{:S(2)}, u32[]{:S(2)}) collective-permute-start(bf16[128,1152]{1,0:T(8,128)(2,1)S(1)} %collective-permute-done.4.refs_5_), channel_id=1, source_target_pairs={{0,4},{1,5},{2,6},{3,7},{4,0},{5,1},{6,2},{7,3},{8,12},{9,13},{10,... | collective-permute-start | bytes 884744 | tf_op jit(solution)/shard_map/ppermute | solution.py:62
  42.2 9.4 %collective-permute-start.11 = (bf16[128,1152]{1,0:T(8,128)(2,1)S(1)}, bf16[128,1152]{1,0:T(8,128)(2,1)S(1)}, u32[]{:S(2)}, u32[]{:S(2)}) collective-permute-start(bf16[128,1152]{1,0:T(8,128)(2,1)S(1)} %collective-permute-done.4.refs_5_), channel_id=1, source_target_pairs={{0,2},{1,3},{2,0},{3,1},{4,6},{5,7},{6,4},{7,5},{8,10},{9,11},{10,... | collective-permute-start | bytes 884744 | tf_op jit(solution)/shard_map/ppermute | solution.py:62
  43.6 9.1 %collective-permute-start.10 = (bf16[128,1152]{1,0:T(8,128)(2,1)S(1)}, bf16[128,1152]{1,0:T(8,128)(2,1)S(1)}, u32[]{:S(2)}, u32[]{:S(2)}) collective-permute-start(bf16[128,1152]{1,0:T(8,128)(2,1)S(1)} %collective-permute-done.2.refs_1_), channel_id=1, source_target_pairs={{0,1},{1,0},{2,3},{3,2},{4,5},{5,4},{6,7},{7,6},{8,9},{9,8},{10,11... | collective-permute-start | bytes 884744 | tf_op jit(solution)/shard_map/ppermute | solution.py:62
  46.9 6.2 %copy-start.4 = (bf16[128,1152]{1,0:T(8,128)(2,1)S(1)}, bf16[128,1152]{1,0:T(8,128)(2,1)}, u32[]{:S(2)}) copy-start(bf16[128,1152]{1,0:T(8,128)(2,1)} %get-tuple-element.44.refs_0_) | copy-start | bytes 884740
  46.9 6.2 %copy-start.5 = (bf16[128,1152]{1,0:T(8,128)(2,1)S(1)}, bf16[128,1152]{1,0:T(8,128)(2,1)}, u32[]{:S(2)}) copy-start(bf16[128,1152]{1,0:T(8,128)(2,1)} %get-tuple-element.47.refs_4_) | copy-start | bytes 884740
  51.5 1.6 %collective-permute-start.15 = (bf16[128,1152]{1,0:T(8,128)(2,1)S(1)}, bf16[128,1152]{1,0:T(8,128)(2,1)S(1)}, u32[]{:S(2)}, u32[]{:S(2)}) collective-permute-start(bf16[128,1152]{1,0:T(8,128)(2,1)S(1)} %collective-permute-done.11.refs_7_), channel_id=1, source_target_pairs={{0,4},{1,5},{2,6},{3,7},{4,0},{5,1},{6,2},{7,3},{8,12},{9,13},{10,... | collective-permute-start | bytes 884744 | tf_op jit(solution)/shard_map/ppermute | solution.py:62
  56.3 5.6 %collective-permute-start.16 = (bf16[256,1152]{1,0:T(8,128)(2,1)S(1)}, bf16[256,1152]{1,0:T(8,128)(2,1)S(1)}, u32[]{:S(2)}, u32[]{:S(2)}) collective-permute-start(bf16[256,1152]{1,0:T(8,128)(2,1)S(1)} %get-tuple-element.63), channel_id=1, source_target_pairs={{0,4},{1,5},{2,6},{3,7},{4,0},{5,1},{6,2},{7,3},{8,12},{9,13},{10,... | collective-permute-start | bytes 1769480 | tf_op jit(solution)/shard_map/ppermute | solution.py:62
  56.6 5.4 %collective-permute-start.17 = (bf16[256,1152]{1,0:T(8,128)(2,1)S(1)}, bf16[256,1152]{1,0:T(8,128)(2,1)S(1)}, u32[]{:S(2)}, u32[]{:S(2)}) collective-permute-start(bf16[256,1152]{1,0:T(8,128)(2,1)S(1)} %get-tuple-element.64), channel_id=1, source_target_pairs={{0,4},{1,5},{2,6},{3,7},{4,0},{5,1},{6,2},{7,3},{8,12},{9,13},{10,... | collective-permute-start | bytes 1769480 | tf_op jit(solution)/shard_map/ppermute | solution.py:62
  56.9 8.6 %collective-permute-start.20 = (bf16[128,768]{1,0:T(8,128)(2,1)S(1)}, bf16[128,768]{1,0:T(8,128)(2,1)S(1)}, u32[]{:S(2)}, u32[]{:S(2)}) collective-permute-start(bf16[128,768]{1,0:T(8,128)(2,1)S(1)} %get-tuple-element.71), channel_id=1, source_target_pairs={{0,1},{1,0},{2,3},{3,2},{4,5},{5,4},{6,7},{7,6},{8,9},{9,8},{10,11... | collective-permute-start | bytes 589832 | tf_op jit(solution)/shard_map/ppermute | solution.py:62
  58.2 16.3 %collective-permute-start.23 = (bf16[256,384]{1,0:T(8,128)(2,1)S(1)}, bf16[256,384]{1,0:T(8,128)(2,1)S(1)}, u32[]{:S(2)}, u32[]{:S(2)}) collective-permute-start(bf16[256,384]{1,0:T(8,128)(2,1)S(1)} %get-tuple-element.74), channel_id=1, source_target_pairs={{0,16},{1,17},{2,18},{3,19},{4,20},{5,21},{6,22},{7,23},{8,24},{9,... | collective-permute-start | bytes 589832 | tf_op jit(solution)/shard_map/ppermute | solution.py:62
  62.0 18.0 %copy-start = (bf16[128,1152]{1,0:T(8,128)(2,1)S(1)}, bf16[128,1152]{1,0:T(8,128)(2,1)}, u32[]{:S(2)}) copy-start(bf16[128,1152]{1,0:T(8,128)(2,1)} %x_ref.2) | copy-start | bytes 884740
  62.2 20.9 %copy-start.1 = (bf16[128,1152]{1,0:T(8,128)(2,1)S(1)}, bf16[128,1152]{1,0:T(8,128)(2,1)}, u32[]{:S(2)}) copy-start(bf16[128,1152]{1,0:T(8,128)(2,1)} %x_ref.3) | copy-start | bytes 884740
  62.2 7.9 %collective-permute-start.18 = (bf16[128,768]{1,0:T(8,128)(2,1)S(1)}, bf16[128,768]{1,0:T(8,128)(2,1)S(1)}, u32[]{:S(2)}, u32[]{:S(2)}) collective-permute-start(bf16[128,768]{1,0:T(8,128)(2,1)S(1)} %get-tuple-element.65), channel_id=1, source_target_pairs={{0,2},{1,3},{2,0},{3,1},{4,6},{5,7},{6,4},{7,5},{8,10},{9,11},{10,... | collective-permute-start | bytes 589832 | tf_op jit(solution)/shard_map/ppermute | solution.py:62
  63.8 10.3 %collective-permute-start.22 = (bf16[256,384]{1,0:T(8,128)(2,1)S(1)}, bf16[256,384]{1,0:T(8,128)(2,1)S(1)}, u32[]{:S(2)}, u32[]{:S(2)}) collective-permute-start(bf16[256,384]{1,0:T(8,128)(2,1)S(1)} %get-tuple-element.69), channel_id=1, source_target_pairs={{0,8},{1,9},{2,10},{3,11},{4,12},{5,13},{6,14},{7,15},{8,0},{9,1},... | collective-permute-start | bytes 589832 | tf_op jit(solution)/shard_map/ppermute | solution.py:62
  65.5 15.7 %collective-permute-start.25 = (bf16[128,768]{1,0:T(8,128)(2,1)S(1)}, bf16[128,768]{1,0:T(8,128)(2,1)S(1)}, u32[]{:S(2)}, u32[]{:S(2)}) collective-permute-start(bf16[128,768]{1,0:T(8,128)(2,1)S(1)} %get-tuple-element.76), channel_id=1, source_target_pairs={{0,2},{1,3},{2,0},{3,1},{4,6},{5,7},{6,4},{7,5},{8,10},{9,11},{10,... | collective-permute-start | bytes 589832 | tf_op jit(solution)/shard_map/ppermute | solution.py:62
  66.1 12.5 %collective-permute-start.21 = (bf16[128,768]{1,0:T(8,128)(2,1)S(1)}, bf16[128,768]{1,0:T(8,128)(2,1)S(1)}, u32[]{:S(2)}, u32[]{:S(2)}) collective-permute-start(bf16[128,768]{1,0:T(8,128)(2,1)S(1)} %add_convert_fusion.1), channel_id=1, source_target_pairs={{0,16},{1,17},{2,18},{3,19},{4,20},{5,21},{6,22},{7,23},{8,24},{9,... | collective-permute-start | bytes 589832 | tf_op jit(solution)/shard_map/ppermute | solution.py:62
  70.1 9.9 %collective-permute-start.19 = (bf16[128,768]{1,0:T(8,128)(2,1)S(1)}, bf16[128,768]{1,0:T(8,128)(2,1)S(1)}, u32[]{:S(2)}, u32[]{:S(2)}) collective-permute-start(bf16[128,768]{1,0:T(8,128)(2,1)S(1)} %get-tuple-element.66), channel_id=1, source_target_pairs={{0,1},{1,0},{2,3},{3,2},{4,5},{5,4},{6,7},{7,6},{8,9},{9,8},{10,11... | collective-permute-start | bytes 589832 | tf_op jit(solution)/shard_map/ppermute | solution.py:62
  74.1 9.0 %collective-permute-start.26 = (bf16[128,768]{1,0:T(8,128)(2,1)S(1)}, bf16[128,768]{1,0:T(8,128)(2,1)S(1)}, u32[]{:S(2)}, u32[]{:S(2)}) collective-permute-start(bf16[128,768]{1,0:T(8,128)(2,1)S(1)} %add_convert_fusion), channel_id=1, source_target_pairs={{0,8},{1,9},{2,10},{3,11},{4,12},{5,13},{6,14},{7,15},{8,0},{9,1},... | collective-permute-start | bytes 589832 | tf_op jit(solution)/shard_map/ppermute | solution.py:62
  74.5 5.5 %collective-permute-start.24 = (bf16[128,384]{1,0:T(8,128)(2,1)S(1)}, bf16[128,384]{1,0:T(8,128)(2,1)S(1)}, u32[]{:S(2)}, u32[]{:S(2)}) collective-permute-start(bf16[128,384]{1,0:T(8,128)(2,1)S(1)} %add_convert_fusion.3), channel_id=1, source_target_pairs={{0,1},{1,0},{2,3},{3,2},{4,5},{5,4},{6,7},{7,6},{8,9},{9,8},{10,11... | collective-permute-start | bytes 294920 | tf_op jit(solution)/shard_map/ppermute | solution.py:62
  78.5 4.6 %collective-permute-start.27 = (bf16[128,384]{1,0:T(8,128)(2,1)S(1)}, bf16[128,384]{1,0:T(8,128)(2,1)S(1)}, u32[]{:S(2)}, u32[]{:S(2)}) collective-permute-start(bf16[128,384]{1,0:T(8,128)(2,1)S(1)} %add_convert_fusion.2), channel_id=1, source_target_pairs={{0,2},{1,3},{2,0},{3,1},{4,6},{5,7},{6,4},{7,5},{8,10},{9,11},{10,... | collective-permute-start | bytes 294920 | tf_op jit(solution)/shard_map/ppermute | solution.py:62
  (2 other events, 2.0 us)

commit v9 on v7

--- a/solution.py
+++ b/solution.py
@@ -248,32 +248,31 @@
     return out[:3], out[cut[0] : cut[1]], out[cut[1] : cut[2]], out[cut[2] : cut[3]], out[cut[3] :]
 
 
-def kept_kernel(half, pair, img, txt, *outs):
+def kept_kernel(of_texts, pair, other, *outs):
     rows = outs[0].shape[0]
-    far = len(outs) - 1
-    outs[-1][...] = lax.dot_general(
-        pair[:, : outs[-1].shape[0]], img[...], (((0,), (0,)), ((), ())), preferred_element_type=f32
-    )
-    for out, grad in zip(outs, image_grads(pair, txt[...], rows, 0, far)):
-        out[...] = grad[:, : out.shape[1]]
-
-
-def kept_grads(pair, img, txt, rows, far, own_txt, half):
-    width = img.shape[1]
-    shapes = [(rows, width)] + [(rows, half)] * (far - 1) + [(own_txt * rows, width)]
+    if of_texts:
+        outs[0][...] = lax.dot_general(
+            pair[:, :rows], other[...], (((0,), (0,)), ((), ())), preferred_element_type=f32
+        )
+    else:
+        for out, grad in zip(outs, image_grads(pair, other[...], rows, 0, len(outs))):
+            out[...] = grad[:, : out.shape[1]]
+
+
+def kept_grads(pair, other, shapes, of_texts):
     return pl.pallas_call(
-        functools.partial(kept_kernel, half),
+        functools.partial(kept_kernel, of_texts),
         out_shape=[jax.ShapeDtypeStruct(shape, f32) for shape in shapes],
-        in_specs=[VMEM] * 3,
+        in_specs=[VMEM] * 2,
         out_specs=[VMEM] * len(shapes),
-        compiler_params=params((pair.shape, 2), (img.shape, 2), (txt.shape, 2), *[(v, 8) for v in shapes]),
+        compiler_params=params((pair.shape, 2), (other.shape, 2), *[(v, 8) for v in shapes]),
         cost_estimate=pl.CostEstimate(
-            flops=2 * pair.size * width,
-            bytes_accessed=2 * (pair.size + img.size + txt.size) + 4 * own_txt * rows * width,
+            flops=pair.size * other.shape[1],
+            bytes_accessed=2 * (pair.size + other.size) + 4 * sum(math.prod(v) for v in shapes),
             transcendentals=0,
         ),
-        name="kept",
-    )(pair, img, txt)
+        name="kept_texts" if of_texts else "kept_images",
+    )(pair, other)
 
 
 def text_sums_kernel(row, near, half, cores, own_ref, *refs):
@@ -439,8 +438,9 @@
             img_in[b, a] = plan.send(img_hops[(b - 1) * far + a], "col", -b)
     long_in = [plan.send(v, "far", -1 - k) for k, v in enumerate(img_longs)]
     txt_in = [plan.send(v, "core", -1 - k // row) for k, v in enumerate(txt_out)]
-    *img_stay, txt_own = kept_grads(pair, img_pack, txt_pack, rows, far, own_txt, half)
+    (txt_own,) = kept_grads(pair, img_pack, [(own_txt * rows, width)], True)
     txt_hops, txt_kept, txt_stay, txt_longs = text_sums(txt_own, txt_in, rows, row, near, half)
+    img_stay = kept_grads(after(pair, *txt_hops), txt_pack, [(rows, width)] + [(rows, half)] * (far - 1), False)
 
     row_in = {}
     for b in range(1, row):

time: 84.5 us -> 84.5 us (level)
  waiting for transfers between devices: 36.2 us -> 34.5 us
  starting transfers between devices: 32 us -> 33.5 us
    ppermute x28, waiting for transfers between devices: 36.2 us -> 34.5 us  [send(): return lax.ppermute(x, AXES, pairs)]
    ppermute x28, starting transfers between devices: 32 us -> 33.5 us  [send(): return lax.ppermute(x, AXES, pairs)]
    pallas_call x1 -> x2, Pallas kernels: 1.55 us -> 1.72 us  [kept_grads(): pl.pallas_call(functools.partial(kept_kernel, of_texts), out_shape=[jax.S...]
where the time goes in v9:
time: 84.5 us; the launch traced here: 84.3 us
  waiting for transfers between devices  34.5 us (41%)
  starting transfers between devices  33.5 us (40%)
  Pallas kernels  13.4 us (16%)
  local copies, waits for them, and re-layouts  2.01 us (2%)
    ppermute x28, waiting for transfers between devices, send(): return lax.ppermute(x, AXES, pairs)  34.5 us
    ppermute x28, starting transfers between devices, send(): return lax.ppermute(x, AXES, pairs)  33.5 us
    pallas_call x1, Pallas kernels, pair_and_sent(): pl.pallas_call(functools.partial(pair_kernel, images, texts, far, skip, h...  3.23 us
    pallas_call x1, Pallas kernels, unit_rows(): pl.pallas_call(functools.partial(unit_kernel, len(arrays)), out_shape=[ja...  3.15 us
    pallas_call x1, Pallas kernels, teacher_targets(): pl.pallas_call(functools.partial(teacher_kernel, images, texts), out_shap...  2.77 us
    pallas_call x2, Pallas kernels, final(): pl.pallas_call(functools.partial(final_kernel, half, len(lows)), out_shap...  2.3 us
    unnamed x12, local copies, waits for them, and re-layouts  2.01 us
    pallas_call x2, Pallas kernels, kept_grads(): pl.pallas_call(functools.partial(kept_kernel, of_texts), out_shape=[jax.S...  1.72 us
  transfers between devices with their start and end apart: 28, of which 12 were waited for; matrix products, arithmetic and copies ran while one was open for 0% of the time, Pallas kernels for 7%

profile of v9, /device:TPU:0, one launch (start us, length us, event | category | flops | bytes accessed | tf_op | source)
XLA Modules:
  0.0 84.3 jit_solution(10431753435117301468)
XLA Ops:
  0.6 3.1 %unit_rows.1 = (bf16[128,1536]{1,0:T(8,128)(2,1)}, bf16[128,1536]{1,0:T(8,128)(2,1)}, bf16[128,1152]{1,0:T(8,128)(2,1)}, bf16[128,1152]{1,0:T(8,128)(2,1)}, bf16...) custom-call(bf16[128,1536]{1,0:T(8,128)(2,1)} %refs_0_.1, bf16[128,1536]{1,0:T(8,128)(2,1)} %refs_1_.1, ...), custom_call_target="tpu_custom_call" | custom-call | flops 2752512 | bytes 4128768 | tf_op jit(solution)/shard_map/unit_rows/pallas_call | solution.py:107
  3.8 4.1 %collective-permute-start = (bf16[128,1536]{1,0:T(8,128)(2,1)}, bf16[128,1536]{1,0:T(8,128)(2,1)S(1)}, u32[]{:S(2)}, u32[]{:S(2)}) collective-permute-start(bf16[128,1536]{1,0:T(8,128)(2,1)} %get-tuple-element.41.refs_0_), channel_id=1, source_target_pairs={{0,16},{1,17},{2,18},{3,19},{4,20},{5,21},{6,22},{7,23},{8,24},{9,... | collective-permute-start | bytes 1179656 | tf_op jit(solution)/shard_map/ppermute | solution.py:62
  7.9 1.6 %collective-permute-start.1 = (bf16[128,1536]{1,0:T(8,128)(2,1)}, bf16[128,1536]{1,0:T(8,128)(2,1)S(1)}, u32[]{:S(2)}, u32[]{:S(2)}) collective-permute-start(bf16[128,1536]{1,0:T(8,128)(2,1)} %get-tuple-element.42.refs_4_), channel_id=1, source_target_pairs={{0,8},{1,9},{2,10},{3,11},{4,12},{5,13},{6,14},{7,15},{8,0},{9,1},... | collective-permute-start | bytes 1179656 | tf_op jit(solution)/shard_map/ppermute | solution.py:62
  9.5 1.5 %collective-permute-start.5 = (bf16[128,2688]{1,0:T(8,128)(2,1)}, bf16[128,2688]{1,0:T(8,128)(2,1)S(1)}, u32[]{:S(2)}, u32[]{:S(2)}) collective-permute-start(bf16[128,2688]{1,0:T(8,128)(2,1)} %get-tuple-element.47), channel_id=1, source_target_pairs={{0,2},{1,3},{2,0},{3,1},{4,6},{5,7},{6,4},{7,5},{8,10},{9,11},{10,... | collective-permute-start | bytes 2064392 | tf_op jit(solution)/shard_map/ppermute | solution.py:62
  11.0 1.5 %collective-permute-start.3 = (bf16[128,2688]{1,0:T(8,128)(2,1)}, bf16[128,2688]{1,0:T(8,128)(2,1)S(1)}, u32[]{:S(2)}, u32[]{:S(2)}) collective-permute-start(bf16[128,2688]{1,0:T(8,128)(2,1)} %get-tuple-element.44), channel_id=1, source_target_pairs={{0,1},{1,0},{2,3},{3,2},{4,5},{5,4},{6,7},{7,6},{8,9},{9,8},{10,11... | collective-permute-start | bytes 2064392 | tf_op jit(solution)/shard_map/ppermute | solution.py:62
  12.5 13.3 %collective-permute-done.refs_1_ = bf16[128,1536]{1,0:T(8,128)(2,1)S(1)} collective-permute-done((bf16[128,1536]{1,0:T(8,128)(2,1)}, bf16[128,1536]{1,0:T(8,128)(2,1)S(1)}, u32[]{:S(2)}, u32[]{:S(2)}) %collective-permute-start) | collective-permute-done | bytes 393248 | tf_op jit(solution)/shard_map/ppermute | solution.py:62
  25.9 1.4 %collective-permute-start.2 = (bf16[128,1152]{1,0:T(8,128)(2,1)}, bf16[128,1152]{1,0:T(8,128)(2,1)S(1)}, u32[]{:S(2)}, u32[]{:S(2)}) collective-permute-start(bf16[128,1152]{1,0:T(8,128)(2,1)} %get-tuple-element.43.refs_0_), channel_id=1, source_target_pairs={{0,16},{1,17},{2,18},{3,19},{4,20},{5,21},{6,22},{7,23},{8,24},{9,... | collective-permute-start | bytes 884744 | tf_op jit(solution)/shard_map/ppermute | solution.py:62
  27.3 2.4 %collective-permute-start.4 = (bf16[128,1152]{1,0:T(8,128)(2,1)}, bf16[128,1152]{1,0:T(8,128)(2,1)S(1)}, u32[]{:S(2)}, u32[]{:S(2)}) collective-permute-start(bf16[128,1152]{1,0:T(8,128)(2,1)} %get-tuple-element.46.refs_4_), channel_id=1, source_target_pairs={{0,8},{1,9},{2,10},{3,11},{4,12},{5,13},{6,14},{7,15},{8,0},{9,1},... | collective-permute-start | bytes 884744 | tf_op jit(solution)/shard_map/ppermute | solution.py:62
  29.8 1.6 %collective-permute-start.7 = (bf16[128,1536]{1,0:T(8,128)(2,1)S(1)}, bf16[128,1536]{1,0:T(8,128)(2,1)S(1)}, u32[]{:S(2)}, u32[]{:S(2)}) collective-permute-start(bf16[128,1536]{1,0:T(8,128)(2,1)S(1)} %collective-permute-done.refs_1_), channel_id=1, source_target_pairs={{0,1},{1,0},{2,3},{3,2},{4,5},{5,4},{6,7},{7,6},{8,9},{9,8},{10,11... | collective-permute-start | bytes 1179656 | tf_op jit(solution)/shard_map/ppermute | solution.py:62
  31.3 1.5 %collective-permute-start.8 = (bf16[128,1536]{1,0:T(8,128)(2,1)S(1)}, bf16[128,1536]{1,0:T(8,128)(2,1)S(1)}, u32[]{:S(2)}, u32[]{:S(2)}) collective-permute-start(bf16[128,1536]{1,0:T(8,128)(2,1)S(1)} %collective-permute-done.1.refs_5_), channel_id=1, source_target_pairs={{0,2},{1,3},{2,0},{3,1},{4,6},{5,7},{6,4},{7,5},{8,10},{9,11},{10,... | collective-permute-start | bytes 1179656 | tf_op jit(solution)/shard_map/ppermute | solution.py:62
  32.8 8.6 %collective-permute-done.2.refs_1_ = bf16[128,1152]{1,0:T(8,128)(2,1)S(1)} collective-permute-done((bf16[128,1152]{1,0:T(8,128)(2,1)}, bf16[128,1152]{1,0:T(8,128)(2,1)S(1)}, u32[]{:S(2)}, u32[]{:S(2)}) %collective-permute-start.2) | collective-permute-done | bytes 294944 | tf_op jit(solution)/shard_map/ppermute | solution.py:62
  42.2 1.4 %collective-permute-start.11 = (bf16[128,1152]{1,0:T(8,128)(2,1)S(1)}, bf16[128,1152]{1,0:T(8,128)(2,1)S(1)}, u32[]{:S(2)}, u32[]{:S(2)}) collective-permute-start(bf16[128,1152]{1,0:T(8,128)(2,1)S(1)} %collective-permute-done.4.refs_5_), channel_id=1, source_target_pairs={{0,2},{1,3},{2,0},{3,1},{4,6},{5,7},{6,4},{7,5},{8,10},{9,11},{10,... | collective-permute-start | bytes 884744 | tf_op jit(solution)/shard_map/ppermute | solution.py:62
  43.6 1.4 %collective-permute-start.10 = (bf16[128,1152]{1,0:T(8,128)(2,1)S(1)}, bf16[128,1152]{1,0:T(8,128)(2,1)S(1)}, u32[]{:S(2)}, u32[]{:S(2)}) collective-permute-start(bf16[128,1152]{1,0:T(8,128)(2,1)S(1)} %collective-permute-done.2.refs_1_), channel_id=1, source_target_pairs={{0,1},{1,0},{2,3},{3,2},{4,5},{5,4},{6,7},{7,6},{8,9},{9,8},{10,11... | collective-permute-start | bytes 884744 | tf_op jit(solution)/shard_map/ppermute | solution.py:62
  44.9 1.0 %copy-done.2 = bf16[128,1536]{1,0:T(8,128)(2,1)S(1)} copy-done((bf16[128,1536]{1,0:T(8,128)(2,1)S(1)}, bf16[128,1536]{1,0:T(8,128)(2,1)}, u32[]{:S(2)}) %copy-start.2) | copy-done | bytes 393240
  45.9 1.0 %copy-done.3 = bf16[128,1536]{1,0:T(8,128)(2,1)S(1)} copy-done((bf16[128,1536]{1,0:T(8,128)(2,1)S(1)}, bf16[128,1536]{1,0:T(8,128)(2,1)}, u32[]{:S(2)}) %copy-start.3) | copy-done | bytes 393240
  46.9 2.8 %teacher_targets.1.refs_12_ = f32[512,1024]{1,0:T(8,128)S(1)} custom-call(bf16[128,1536]{1,0:T(8,128)(2,1)S(1)} %copy-done.2, bf16[128,1536]{1,0:T(8,128)(2,1)S(1)} %collective-permute-done.refs_1_, bf16[128,2688]{1,0:T(8,128)(2,1)S(1)} %collective-permute-done.3.refs_2_, bf16[128,1536]{1,0:T(8,128)(2,1)S(1)} %collective-permute-done.7.refs_3_, ...), custom_call_target="tpu_custom_call" | custom-call | flops 1610612736 | bytes 6815744 | tf_op jit(solution)/shard_map/teacher_targets/pallas_call | solution.py:154
  49.7 1.8 %collective-permute-done.11.refs_7_ = bf16[128,1152]{1,0:T(8,128)(2,1)S(1)} collective-permute-done((bf16[128,1152]{1,0:T(8,128)(2,1)S(1)}, bf16[128,1152]{1,0:T(8,128)(2,1)S(1)}, u32[]{:S(2)}, u32[]{:S(2)}) %collective-permute-start.11) | collective-permute-done | bytes 294944 | tf_op jit(solution)/shard_map/ppermute | solution.py:62
  51.5 1.2 %collective-permute-done.10.refs_3_ = bf16[128,1152]{1,0:T(8,128)(2,1)S(1)} collective-permute-done((bf16[128,1152]{1,0:T(8,128)(2,1)S(1)}, bf16[128,1152]{1,0:T(8,128)(2,1)S(1)}, u32[]{:S(2)}, u32[]{:S(2)}) %collective-permute-start.10) | collective-permute-done | bytes 294944 | tf_op jit(solution)/shard_map/ppermute | solution.py:62
  53.1 3.2 %pair_and_sent.1 = (bf16[512,1024]{1,0:T(8,128)(2,1)S(1)}, bf16[512,1152]{1,0:T(8,128)(2,1)S(1)}, bf16[1024,1152]{1,0:T(8,128)(2,1)S(1)}, bf16[128,768]{1,0:T(8,...) custom-call(bf16[128,1152]{1,0:T(8,128)(2,1)S(1)} %copy-done.4, ...), custom_call_target="tpu_custom_call" | custom-call | flops 2415919104 | bytes 7733248 | tf_op jit(solution)/shard_map/pair_and_sent/pallas_call | solution.py:229
  56.9 1.2 %collective-permute-start.20 = (bf16[128,768]{1,0:T(8,128)(2,1)S(1)}, bf16[128,768]{1,0:T(8,128)(2,1)S(1)}, u32[]{:S(2)}, u32[]{:S(2)}) collective-permute-start(bf16[128,768]{1,0:T(8,128)(2,1)S(1)} %get-tuple-element.70), channel_id=1, source_target_pairs={{0,1},{1,0},{2,3},{3,2},{4,5},{5,4},{6,7},{7,6},{8,9},{9,8},{10,11... | collective-permute-start | bytes 589832 | tf_op jit(solution)/shard_map/ppermute | solution.py:62
  58.2 2.3 %collective-permute-start.22 = (bf16[256,384]{1,0:T(8,128)(2,1)S(1)}, bf16[256,384]{1,0:T(8,128)(2,1)S(1)}, u32[]{:S(2)}, u32[]{:S(2)}) collective-permute-start(bf16[256,384]{1,0:T(8,128)(2,1)S(1)} %get-tuple-element.73), channel_id=1, source_target_pairs={{0,16},{1,17},{2,18},{3,19},{4,20},{5,21},{6,22},{7,23},{8,24},{9,... | collective-permute-start | bytes 589832 | tf_op jit(solution)/shard_map/ppermute | solution.py:62
  61.5 1.6 %collective-permute-start.18 = (bf16[128,768]{1,0:T(8,128)(2,1)S(1)}, bf16[128,768]{1,0:T(8,128)(2,1)S(1)}, u32[]{:S(2)}, u32[]{:S(2)}) collective-permute-start(bf16[128,768]{1,0:T(8,128)(2,1)S(1)} %get-tuple-element.61), channel_id=1, source_target_pairs={{0,2},{1,3},{2,0},{3,1},{4,6},{5,7},{6,4},{7,5},{8,10},{9,11},{10,... | collective-permute-start | bytes 589832 | tf_op jit(solution)/shard_map/ppermute | solution.py:62
  63.9 1.0 %collective-permute-start.26 = (bf16[256,384]{1,0:T(8,128)(2,1)S(1)}, bf16[256,384]{1,0:T(8,128)(2,1)S(1)}, u32[]{:S(2)}, u32[]{:S(2)}) collective-permute-start(bf16[256,384]{1,0:T(8,128)(2,1)S(1)} %get-tuple-element.68), channel_id=1, source_target_pairs={{0,8},{1,9},{2,10},{3,11},{4,12},{5,13},{6,14},{7,15},{8,0},{9,1},... | collective-permute-start | bytes 589832 | tf_op jit(solution)/shard_map/ppermute | solution.py:62
  65.7 2.8 %collective-permute-start.21 = (bf16[128,768]{1,0:T(8,128)(2,1)S(1)}, bf16[128,768]{1,0:T(8,128)(2,1)S(1)}, u32[]{:S(2)}, u32[]{:S(2)}) collective-permute-start(bf16[128,768]{1,0:T(8,128)(2,1)S(1)} %add_convert_fusion.1), channel_id=1, source_target_pairs={{0,16},{1,17},{2,18},{3,19},{4,20},{5,21},{6,22},{7,23},{8,24},{9,... | collective-permute-start | bytes 589832 | tf_op jit(solution)/shard_map/ppermute | solution.py:62
  68.5 1.5 %collective-permute-start.24 = (bf16[128,768]{1,0:T(8,128)(2,1)S(1)}, bf16[128,768]{1,0:T(8,128)(2,1)S(1)}, u32[]{:S(2)}, u32[]{:S(2)}) collective-permute-start(bf16[128,768]{1,0:T(8,128)(2,1)S(1)} %get-tuple-element.75), channel_id=1, source_target_pairs={{0,2},{1,3},{2,0},{3,1},{4,6},{5,7},{6,4},{7,5},{8,10},{9,11},{10,... | collective-permute-start | bytes 589832 | tf_op jit(solution)/shard_map/ppermute | solution.py:62
  70.1 1.9 %collective-permute-done.22.refs_3_ = bf16[256,384]{1,0:T(8,128)(2,1)S(1)} collective-permute-done((bf16[256,384]{1,0:T(8,128)(2,1)S(1)}, bf16[256,384]{1,0:T(8,128)(2,1)S(1)}, u32[]{:S(2)}, u32[]{:S(2)}) %collective-permute-start.22) | collective-permute-done | bytes 196640 | tf_op jit(solution)/shard_map/ppermute | solution.py:62
  72.1 2.0 %collective-permute-start.19 = (bf16[128,768]{1,0:T(8,128)(2,1)S(1)}, bf16[128,768]{1,0:T(8,128)(2,1)S(1)}, u32[]{:S(2)}, u32[]{:S(2)}) collective-permute-start(bf16[128,768]{1,0:T(8,128)(2,1)S(1)} %get-tuple-element.66), channel_id=1, source_target_pairs={{0,1},{1,0},{2,3},{3,2},{4,5},{5,4},{6,7},{7,6},{8,9},{9,8},{10,11... | collective-permute-start | bytes 589832 | tf_op jit(solution)/shard_map/ppermute | solution.py:62
  74.9 3.6 %collective-permute-done.21.refs_1_ = bf16[128,768]{1,0:T(8,128)(2,1)S(1)} collective-permute-done((bf16[128,768]{1,0:T(8,128)(2,1)S(1)}, bf16[128,768]{1,0:T(8,128)(2,1)S(1)}, u32[]{:S(2)}, u32[]{:S(2)}) %collective-permute-start.21) | collective-permute-done | bytes 196640 | tf_op jit(solution)/shard_map/ppermute | solution.py:62
  78.5 1.5 %collective-permute-start.27 = (bf16[128,384]{1,0:T(8,128)(2,1)S(1)}, bf16[128,384]{1,0:T(8,128)(2,1)S(1)}, u32[]{:S(2)}, u32[]{:S(2)}) collective-permute-start(bf16[128,384]{1,0:T(8,128)(2,1)S(1)} %add_convert_fusion.2), channel_id=1, source_target_pairs={{0,2},{1,3},{2,0},{3,1},{4,6},{5,7},{6,4},{7,5},{8,10},{9,11},{10,... | collective-permute-start | bytes 294920 | tf_op jit(solution)/shard_map/ppermute | solution.py:62
  80.1 1.1 %final.2 = f32[128,1152]{1,0:T(8,128)} custom-call(bf16[128,1152]{1,0:T(8,128)(2,1)S(1)} %copy-done, f32[128,1152]{1,0:T(8,128)S(1)} %get-tuple-element.64.own_ref, bf16[128,768]{1,0:T(8,128)(2,1)S(1)} %collective-permute-done.19.refs_0_, bf16[128,768]{1,0:T(8,128)(2,1)S(1)} %collective-permute-done.21.refs_1_, ...), custom_call_target="tpu_custom_call" | custom-call | flops 1474560 | bytes 1769472 | tf_op jit(solution)/shard_map/final/pallas_call | solution.py:340
  81.2 1.9 %collective-permute-done.27.refs_2_ = bf16[128,384]{1,0:T(8,128)(2,1)S(1)} collective-permute-done((bf16[128,384]{1,0:T(8,128)(2,1)S(1)}, bf16[128,384]{1,0:T(8,128)(2,1)S(1)}, u32[]{:S(2)}, u32[]{:S(2)}) %collective-permute-start.27) | collective-permute-done | bytes 98336 | tf_op jit(solution)/shard_map/ppermute | solution.py:62
  83.2 1.1 %final.3 = f32[128,1152]{1,0:T(8,128)} custom-call(bf16[128,1152]{1,0:T(8,128)(2,1)S(1)} %copy-done.1, f32[128,1152]{1,0:T(8,128)S(1)} %get-tuple-element.74.own_ref, bf16[128,768]{1,0:T(8,128)(2,1)S(1)} %collective-permute-done.24.refs_0_, bf16[128,768]{1,0:T(8,128)(2,1)S(1)} %collective-permute-done.25.refs_1_, ...), custom_call_target="tpu_custom_call" | custom-call | flops 1474560 | bytes 1769472 | tf_op jit(solution)/shard_map/final/pallas_call | solution.py:340
  (48 shorter events, 5.6 us)
Async XLA Ops:
  3.8 22.0 %collective-permute-start = (bf16[128,1536]{1,0:T(8,128)(2,1)}, bf16[128,1536]{1,0:T(8,128)(2,1)S(1)}, u32[]{:S(2)}, u32[]{:S(2)}) collective-permute-start(bf16[128,1536]{1,0:T(8,128)(2,1)} %get-tuple-element.41.refs_0_), channel_id=1, source_target_pairs={{0,16},{1,17},{2,18},{3,19},{4,20},{5,21},{6,22},{7,23},{8,24},{9,... | collective-permute-start | bytes 1179656 | tf_op jit(solution)/shard_map/ppermute | solution.py:62
  7.9 18.0 %collective-permute-start.1 = (bf16[128,1536]{1,0:T(8,128)(2,1)}, bf16[128,1536]{1,0:T(8,128)(2,1)S(1)}, u32[]{:S(2)}, u32[]{:S(2)}) collective-permute-start(bf16[128,1536]{1,0:T(8,128)(2,1)} %get-tuple-element.42.refs_4_), channel_id=1, source_target_pairs={{0,8},{1,9},{2,10},{3,11},{4,12},{5,13},{6,14},{7,15},{8,0},{9,1},... | collective-permute-start | bytes 1179656 | tf_op jit(solution)/shard_map/ppermute | solution.py:62
  9.5 20.3 %collective-permute-start.6 = (bf16[128,2688]{1,0:T(8,128)(2,1)}, bf16[128,2688]{1,0:T(8,128)(2,1)S(1)}, u32[]{:S(2)}, u32[]{:S(2)}) collective-permute-start(bf16[128,2688]{1,0:T(8,128)(2,1)} %get-tuple-element.47), channel_id=1, source_target_pairs={{0,4},{1,5},{2,6},{3,7},{4,0},{5,1},{6,2},{7,3},{8,12},{9,13},{10,... | collective-permute-start | bytes 2064392 | tf_op jit(solution)/shard_map/ppermute | solution.py:62
  9.5 20.3 %collective-permute-start.5 = (bf16[128,2688]{1,0:T(8,128)(2,1)}, bf16[128,2688]{1,0:T(8,128)(2,1)S(1)}, u32[]{:S(2)}, u32[]{:S(2)}) collective-permute-start(bf16[128,2688]{1,0:T(8,128)(2,1)} %get-tuple-element.47), channel_id=1, source_target_pairs={{0,2},{1,3},{2,0},{3,1},{4,6},{5,7},{6,4},{7,5},{8,10},{9,11},{10,... | collective-permute-start | bytes 2064392 | tf_op jit(solution)/shard_map/ppermute | solution.py:62
  11.0 18.8 %collective-permute-start.3 = (bf16[128,2688]{1,0:T(8,128)(2,1)}, bf16[128,2688]{1,0:T(8,128)(2,1)S(1)}, u32[]{:S(2)}, u32[]{:S(2)}) collective-permute-start(bf16[128,2688]{1,0:T(8,128)(2,1)} %get-tuple-element.44), channel_id=1, source_target_pairs={{0,1},{1,0},{2,3},{3,2},{4,5},{5,4},{6,7},{7,6},{8,9},{9,8},{10,11... | collective-permute-start | bytes 2064392 | tf_op jit(solution)/shard_map/ppermute | solution.py:62
  25.9 15.5 %collective-permute-start.2 = (bf16[128,1152]{1,0:T(8,128)(2,1)}, bf16[128,1152]{1,0:T(8,128)(2,1)S(1)}, u32[]{:S(2)}, u32[]{:S(2)}) collective-permute-start(bf16[128,1152]{1,0:T(8,128)(2,1)} %get-tuple-element.43.refs_0_), channel_id=1, source_target_pairs={{0,16},{1,17},{2,18},{3,19},{4,20},{5,21},{6,22},{7,23},{8,24},{9,... | collective-permute-start | bytes 884744 | tf_op jit(solution)/shard_map/ppermute | solution.py:62
  27.3 14.2 %collective-permute-start.4 = (bf16[128,1152]{1,0:T(8,128)(2,1)}, bf16[128,1152]{1,0:T(8,128)(2,1)S(1)}, u32[]{:S(2)}, u32[]{:S(2)}) collective-permute-start(bf16[128,1152]{1,0:T(8,128)(2,1)} %get-tuple-element.46.refs_4_), channel_id=1, source_target_pairs={{0,8},{1,9},{2,10},{3,11},{4,12},{5,13},{6,14},{7,15},{8,0},{9,1},... | collective-permute-start | bytes 884744 | tf_op jit(solution)/shard_map/ppermute | solution.py:62
  29.8 11.7 %collective-permute-start.7 = (bf16[128,1536]{1,0:T(8,128)(2,1)S(1)}, bf16[128,1536]{1,0:T(8,128)(2,1)S(1)}, u32[]{:S(2)}, u32[]{:S(2)}) collective-permute-start(bf16[128,1536]{1,0:T(8,128)(2,1)S(1)} %collective-permute-done.refs_1_), channel_id=1, source_target_pairs={{0,1},{1,0},{2,3},{3,2},{4,5},{5,4},{6,7},{7,6},{8,9},{9,8},{10,11... | collective-permute-start | bytes 1179656 | tf_op jit(solution)/shard_map/ppermute | solution.py:62
  31.3 10.2 %collective-permute-start.8 = (bf16[128,1536]{1,0:T(8,128)(2,1)S(1)}, bf16[128,1536]{1,0:T(8,128)(2,1)S(1)}, u32[]{:S(2)}, u32[]{:S(2)}) collective-permute-start(bf16[128,1536]{1,0:T(8,128)(2,1)S(1)} %collective-permute-done.1.refs_5_), channel_id=1, source_target_pairs={{0,2},{1,3},{2,0},{3,1},{4,6},{5,7},{6,4},{7,5},{8,10},{9,11},{10,... | collective-permute-start | bytes 1179656 | tf_op jit(solution)/shard_map/ppermute | solution.py:62
  32.8 8.7 %collective-permute-start.9 = (bf16[128,2688]{1,0:T(8,128)(2,1)S(1)}, bf16[128,2688]{1,0:T(8,128)(2,1)S(1)}, u32[]{:S(2)}, u32[]{:S(2)}) collective-permute-start(bf16[128,2688]{1,0:T(8,128)(2,1)S(1)} %collective-permute-done.5.refs_6_), channel_id=1, source_target_pairs={{0,4},{1,5},{2,6},{3,7},{4,0},{5,1},{6,2},{7,3},{8,12},{9,13},{10,... | collective-permute-start | bytes 2064392 | tf_op jit(solution)/shard_map/ppermute | solution.py:62
  41.5 3.4 %collective-permute-start.13 = (bf16[128,1536]{1,0:T(8,128)(2,1)S(1)}, bf16[128,1536]{1,0:T(8,128)(2,1)S(1)}, u32[]{:S(2)}, u32[]{:S(2)}) collective-permute-start(bf16[128,1536]{1,0:T(8,128)(2,1)S(1)} %collective-permute-done.1.refs_5_), channel_id=1, source_target_pairs={{0,4},{1,5},{2,6},{3,7},{4,0},{5,1},{6,2},{7,3},{8,12},{9,13},{10,... | collective-permute-start | bytes 1179656 | tf_op jit(solution)/shard_map/ppermute | solution.py:62
  41.6 3.3 %collective-permute-start.14 = (bf16[128,1536]{1,0:T(8,128)(2,1)S(1)}, bf16[128,1536]{1,0:T(8,128)(2,1)S(1)}, u32[]{:S(2)}, u32[]{:S(2)}) collective-permute-start(bf16[128,1536]{1,0:T(8,128)(2,1)S(1)} %collective-permute-done.8.refs_7_), channel_id=1, source_target_pairs={{0,4},{1,5},{2,6},{3,7},{4,0},{5,1},{6,2},{7,3},{8,12},{9,13},{10,... | collective-permute-start | bytes 1179656 | tf_op jit(solution)/shard_map/ppermute | solution.py:62
  42.1 7.6 %collective-permute-start.12 = (bf16[128,1152]{1,0:T(8,128)(2,1)S(1)}, bf16[128,1152]{1,0:T(8,128)(2,1)S(1)}, u32[]{:S(2)}, u32[]{:S(2)}) collective-permute-start(bf16[128,1152]{1,0:T(8,128)(2,1)S(1)} %collective-permute-done.4.refs_5_), channel_id=1, source_target_pairs={{0,4},{1,5},{2,6},{3,7},{4,0},{5,1},{6,2},{7,3},{8,12},{9,13},{10,... | collective-permute-start | bytes 884744 | tf_op jit(solution)/shard_map/ppermute | solution.py:62
  42.2 9.4 %collective-permute-start.11 = (bf16[128,1152]{1,0:T(8,128)(2,1)S(1)}, bf16[128,1152]{1,0:T(8,128)(2,1)S(1)}, u32[]{:S(2)}, u32[]{:S(2)}) collective-permute-start(bf16[128,1152]{1,0:T(8,128)(2,1)S(1)} %collective-permute-done.4.refs_5_), channel_id=1, source_target_pairs={{0,2},{1,3},{2,0},{3,1},{4,6},{5,7},{6,4},{7,5},{8,10},{9,11},{10,... | collective-permute-start | bytes 884744 | tf_op jit(solution)/shard_map/ppermute | solution.py:62
  43.6 9.1 %collective-permute-start.10 = (bf16[128,1152]{1,0:T(8,128)(2,1)S(1)}, bf16[128,1152]{1,0:T(8,128)(2,1)S(1)}, u32[]{:S(2)}, u32[]{:S(2)}) collective-permute-start(bf16[128,1152]{1,0:T(8,128)(2,1)S(1)} %collective-permute-done.2.refs_1_), channel_id=1, source_target_pairs={{0,1},{1,0},{2,3},{3,2},{4,5},{5,4},{6,7},{7,6},{8,9},{9,8},{10,11... | collective-permute-start | bytes 884744 | tf_op jit(solution)/shard_map/ppermute | solution.py:62
  46.9 6.2 %copy-start.4 = (bf16[128,1152]{1,0:T(8,128)(2,1)S(1)}, bf16[128,1152]{1,0:T(8,128)(2,1)}, u32[]{:S(2)}) copy-start(bf16[128,1152]{1,0:T(8,128)(2,1)} %get-tuple-element.43.refs_0_) | copy-start | bytes 884740
  46.9 6.2 %copy-start.5 = (bf16[128,1152]{1,0:T(8,128)(2,1)S(1)}, bf16[128,1152]{1,0:T(8,128)(2,1)}, u32[]{:S(2)}) copy-start(bf16[128,1152]{1,0:T(8,128)(2,1)} %get-tuple-element.46.refs_4_) | copy-start | bytes 884740
  51.5 1.6 %collective-permute-start.15 = (bf16[128,1152]{1,0:T(8,128)(2,1)S(1)}, bf16[128,1152]{1,0:T(8,128)(2,1)S(1)}, u32[]{:S(2)}, u32[]{:S(2)}) collective-permute-start(bf16[128,1152]{1,0:T(8,128)(2,1)S(1)} %collective-permute-done.11.refs_7_), channel_id=1, source_target_pairs={{0,4},{1,5},{2,6},{3,7},{4,0},{5,1},{6,2},{7,3},{8,12},{9,13},{10,... | collective-permute-start | bytes 884744 | tf_op jit(solution)/shard_map/ppermute | solution.py:62
  56.3 5.0 %collective-permute-start.16 = (bf16[256,1152]{1,0:T(8,128)(2,1)S(1)}, bf16[256,1152]{1,0:T(8,128)(2,1)S(1)}, u32[]{:S(2)}, u32[]{:S(2)}) collective-permute-start(bf16[256,1152]{1,0:T(8,128)(2,1)S(1)} %get-tuple-element.58), channel_id=1, source_target_pairs={{0,4},{1,5},{2,6},{3,7},{4,0},{5,1},{6,2},{7,3},{8,12},{9,13},{10,... | collective-permute-start | bytes 1769480 | tf_op jit(solution)/shard_map/ppermute | solution.py:62
  56.6 4.8 %collective-permute-start.17 = (bf16[256,1152]{1,0:T(8,128)(2,1)S(1)}, bf16[256,1152]{1,0:T(8,128)(2,1)S(1)}, u32[]{:S(2)}, u32[]{:S(2)}) collective-permute-start(bf16[256,1152]{1,0:T(8,128)(2,1)S(1)} %get-tuple-element.59), channel_id=1, source_target_pairs={{0,4},{1,5},{2,6},{3,7},{4,0},{5,1},{6,2},{7,3},{8,12},{9,13},{10,... | collective-permute-start | bytes 1769480 | tf_op jit(solution)/shard_map/ppermute | solution.py:62
  56.9 7.0 %collective-permute-start.20 = (bf16[128,768]{1,0:T(8,128)(2,1)S(1)}, bf16[128,768]{1,0:T(8,128)(2,1)S(1)}, u32[]{:S(2)}, u32[]{:S(2)}) collective-permute-start(bf16[128,768]{1,0:T(8,128)(2,1)S(1)} %get-tuple-element.70), channel_id=1, source_target_pairs={{0,1},{1,0},{2,3},{3,2},{4,5},{5,4},{6,7},{7,6},{8,9},{9,8},{10,11... | collective-permute-start | bytes 589832 | tf_op jit(solution)/shard_map/ppermute | solution.py:62
  58.2 13.8 %collective-permute-start.22 = (bf16[256,384]{1,0:T(8,128)(2,1)S(1)}, bf16[256,384]{1,0:T(8,128)(2,1)S(1)}, u32[]{:S(2)}, u32[]{:S(2)}) collective-permute-start(bf16[256,384]{1,0:T(8,128)(2,1)S(1)} %get-tuple-element.73), channel_id=1, source_target_pairs={{0,16},{1,17},{2,18},{3,19},{4,20},{5,21},{6,22},{7,23},{8,24},{9,... | collective-permute-start | bytes 589832 | tf_op jit(solution)/shard_map/ppermute | solution.py:62
  61.5 8.5 %collective-permute-start.18 = (bf16[128,768]{1,0:T(8,128)(2,1)S(1)}, bf16[128,768]{1,0:T(8,128)(2,1)S(1)}, u32[]{:S(2)}, u32[]{:S(2)}) collective-permute-start(bf16[128,768]{1,0:T(8,128)(2,1)S(1)} %get-tuple-element.61), channel_id=1, source_target_pairs={{0,2},{1,3},{2,0},{3,1},{4,6},{5,7},{6,4},{7,5},{8,10},{9,11},{10,... | collective-permute-start | bytes 589832 | tf_op jit(solution)/shard_map/ppermute | solution.py:62
  63.9 11.0 %collective-permute-start.26 = (bf16[256,384]{1,0:T(8,128)(2,1)S(1)}, bf16[256,384]{1,0:T(8,128)(2,1)S(1)}, u32[]{:S(2)}, u32[]{:S(2)}) collective-permute-start(bf16[256,384]{1,0:T(8,128)(2,1)S(1)} %get-tuple-element.68), channel_id=1, source_target_pairs={{0,8},{1,9},{2,10},{3,11},{4,12},{5,13},{6,14},{7,15},{8,0},{9,1},... | collective-permute-start | bytes 589832 | tf_op jit(solution)/shard_map/ppermute | solution.py:62
  64.8 15.2 %copy-start = (bf16[128,1152]{1,0:T(8,128)(2,1)S(1)}, bf16[128,1152]{1,0:T(8,128)(2,1)}, u32[]{:S(2)}) copy-start(bf16[128,1152]{1,0:T(8,128)(2,1)} %x_ref.2) | copy-start | bytes 884740
  65.7 17.5 %copy-start.1 = (bf16[128,1152]{1,0:T(8,128)(2,1)S(1)}, bf16[128,1152]{1,0:T(8,128)(2,1)}, u32[]{:S(2)}) copy-start(bf16[128,1152]{1,0:T(8,128)(2,1)} %x_ref.3) | copy-start | bytes 884740
  65.7 12.8 %collective-permute-start.21 = (bf16[128,768]{1,0:T(8,128)(2,1)S(1)}, bf16[128,768]{1,0:T(8,128)(2,1)S(1)}, u32[]{:S(2)}, u32[]{:S(2)}) collective-permute-start(bf16[128,768]{1,0:T(8,128)(2,1)S(1)} %add_convert_fusion.1), channel_id=1, source_target_pairs={{0,16},{1,17},{2,18},{3,19},{4,20},{5,21},{6,22},{7,23},{8,24},{9,... | collective-permute-start | bytes 589832 | tf_op jit(solution)/shard_map/ppermute | solution.py:62
  68.5 12.7 %collective-permute-start.24 = (bf16[128,768]{1,0:T(8,128)(2,1)S(1)}, bf16[128,768]{1,0:T(8,128)(2,1)S(1)}, u32[]{:S(2)}, u32[]{:S(2)}) collective-permute-start(bf16[128,768]{1,0:T(8,128)(2,1)S(1)} %get-tuple-element.75), channel_id=1, source_target_pairs={{0,2},{1,3},{2,0},{3,1},{4,6},{5,7},{6,4},{7,5},{8,10},{9,11},{10,... | collective-permute-start | bytes 589832 | tf_op jit(solution)/shard_map/ppermute | solution.py:62
  72.0 8.0 %collective-permute-start.23 = (bf16[128,384]{1,0:T(8,128)(2,1)S(1)}, bf16[128,384]{1,0:T(8,128)(2,1)S(1)}, u32[]{:S(2)}, u32[]{:S(2)}) collective-permute-start(bf16[128,384]{1,0:T(8,128)(2,1)S(1)} %add_convert_fusion.3), channel_id=1, source_target_pairs={{0,1},{1,0},{2,3},{3,2},{4,5},{5,4},{6,7},{7,6},{8,9},{9,8},{10,11... | collective-permute-start | bytes 294920 | tf_op jit(solution)/shard_map/ppermute | solution.py:62
  72.1 8.0 %collective-permute-start.19 = (bf16[128,768]{1,0:T(8,128)(2,1)S(1)}, bf16[128,768]{1,0:T(8,128)(2,1)S(1)}, u32[]{:S(2)}, u32[]{:S(2)}) collective-permute-start(bf16[128,768]{1,0:T(8,128)(2,1)S(1)} %get-tuple-element.66), channel_id=1, source_target_pairs={{0,1},{1,0},{2,3},{3,2},{4,5},{5,4},{6,7},{7,6},{8,9},{9,8},{10,11... | collective-permute-start | bytes 589832 | tf_op jit(solution)/shard_map/ppermute | solution.py:62
  74.9 8.2 %collective-permute-start.25 = (bf16[128,768]{1,0:T(8,128)(2,1)S(1)}, bf16[128,768]{1,0:T(8,128)(2,1)S(1)}, u32[]{:S(2)}, u32[]{:S(2)}) collective-permute-start(bf16[128,768]{1,0:T(8,128)(2,1)S(1)} %add_convert_fusion), channel_id=1, source_target_pairs={{0,8},{1,9},{2,10},{3,11},{4,12},{5,13},{6,14},{7,15},{8,0},{9,1},... | collective-permute-start | bytes 589832 | tf_op jit(solution)/shard_map/ppermute | solution.py:62
  78.5 4.6 %collective-permute-start.27 = (bf16[128,384]{1,0:T(8,128)(2,1)S(1)}, bf16[128,384]{1,0:T(8,128)(2,1)S(1)}, u32[]{:S(2)}, u32[]{:S(2)}) collective-permute-start(bf16[128,384]{1,0:T(8,128)(2,1)S(1)} %add_convert_fusion.2), channel_id=1, source_target_pairs={{0,2},{1,3},{2,0},{3,1},{4,6},{5,7},{6,4},{7,5},{8,10},{9,11},{10,... | collective-permute-start | bytes 294920 | tf_op jit(solution)/shard_map/ppermute | solution.py:62
  (2 other events, 2.0 us)

commit v10 on v8

--- a/solution.py
+++ b/solution.py
@@ -318,33 +318,40 @@
     return out[: cut[0]], out[cut[0] : cut[1]], out[cut[1] : cut[2]], out[cut[2] :]
 
 
-def final_kernel(half, lows, x_ref, own_ref, *refs):
-    parts, out_ref = refs[:-1], refs[-1]
-    rows = x_ref.shape[0]
-    x = x_ref[...].astype(f32)
-    inverse = 1.0 / jnp.sqrt(jnp.sum(x * x, axis=1, keepdims=True) + epsilon)
-    sides, along = [], 0.0
-    for at, refs_at in ((slice(0, half), parts[:lows]), (slice(half, None), parts[lows:])):
-        unit = x[:, at] * inverse
-        grad = own_ref[:, at]
-        for part in refs_at:
-            grad = grad + part[:rows, :].astype(f32)
-        grad = logit_scale * grad
-        along = along + jnp.sum(unit * grad, axis=1, keepdims=True)
-        sides.append((at, unit, grad))
-    for at, unit, grad in sides:
-        out_ref[:, at] = (grad - unit * along) * inverse
-
-
-def final(x, own, lows, highs, half):
-    operands = [x, own, *lows, *highs]
+def final_kernel(half, counts, *refs):
+    outs = refs[-len(counts) :]
+    for (lows, highs), out_ref in zip(counts, outs):
+        x_ref, own_ref, parts = refs[0], refs[1], refs[2 : 2 + lows + highs]
+        refs = refs[2 + lows + highs :]
+        rows = x_ref.shape[0]
+        x = x_ref[...].astype(f32)
+        inverse = 1.0 / jnp.sqrt(jnp.sum(x * x, axis=1, keepdims=True) + epsilon)
+        sides, along = [], 0.0
+        for at, refs_at in ((slice(0, half), parts[:lows]), (slice(half, None), parts[lows:])):
+            unit = x[:, at] * inverse
+            grad = own_ref[:, at]
+            for part in refs_at:
+                grad = grad + part[:rows, :].astype(f32)
+            grad = logit_scale * grad
+            along = along + jnp.sum(unit * grad, axis=1, keepdims=True)
+            sides.append((at, unit, grad))
+        for at, unit, grad in sides:
+            out_ref[:, at] = (grad - unit * along) * inverse
+
+
+def final(half, *sides):
+    operands = [v for x, own, lows, highs in sides for v in (x, own, *lows, *highs)]
     return pl.pallas_call(
-        functools.partial(final_kernel, half, len(lows)),
-        out_shape=jax.ShapeDtypeStruct(x.shape, f32),
+        functools.partial(final_kernel, half, tuple((len(lows), len(highs)) for _, _, lows, highs in sides)),
+        out_shape=[jax.ShapeDtypeStruct(side[0].shape, f32) for side in sides],
         in_specs=[VMEM] * len(operands),
-        out_specs=VMEM,
-        compiler_params=params((x.shape, 4 * (4 + len(operands)))),
-        cost_estimate=pl.CostEstimate(flops=10 * x.size, bytes_accessed=12 * x.size, transcendentals=0),
+        out_specs=[VMEM] * len(sides),
+        compiler_params=params(*[(v.shape, 8) for v in operands]),
+        cost_estimate=pl.CostEstimate(
+            flops=10 * sum(side[0].size for side in sides),
+            bytes_accessed=12 * sum(side[0].size for side in sides),
+            transcendentals=0,
+        ),
         name="final",
     )(*operands)
 
@@ -471,9 +478,9 @@
     row_ahead = list(img_in.values())
     img_ends = [plan.send(after(img_hops[(b - 1) * far], *col_ahead), "col", -b) for b in range(1, col)]
     txt_ends = [plan.send(after(txt_hops[(b - 1) * near], *row_ahead), "row", -b) for b in range(1, row)]
-    image_grad = final(student_img, img_stay[0], img_ends + img_last, img_side + long_in, half)
-    text_grad = final(student_txt, txt_stay[0], txt_ends + txt_last, txt_side + txt_long_in, half)
-    return image_grad, text_grad
+    image_side = (student_img, img_stay[0], img_ends + img_last, img_side + long_in)
+    text_side = (student_txt, txt_stay[0], txt_ends + txt_last, txt_side + txt_long_in)
+    return tuple(final(half, image_side, text_side))
 
 
 def solution(mesh):

time: 84.5 us -> 84.4 us (level)
  waiting for transfers between devices: 36.7 us -> 37.7 us
    ppermute x28, waiting for transfers between devices: 36.7 us -> 37.7 us  [send(): return lax.ppermute(x, AXES, pairs)]
    pallas_call x2 -> x1, Pallas kernels: 2.3 us -> 1.56 us  [final(): pl.pallas_call(functools.partial(final_kernel, half, tuple(((len(lows), l...]
  transfers between devices with their start and end apart: 28 -> 28, of which waited for: 12 -> 14; matrix products, arithmetic and copies ran while one was open for 0% -> 0% of each run, Pallas kernels for 7% -> 5%
where the time goes in v10:
time: 84.4 us; the launch traced here: 84.2 us
  waiting for transfers between devices  37.7 us (45%)
  starting transfers between devices  31.1 us (37%)
  Pallas kernels  12.5 us (15%)
  local copies, waits for them, and re-layouts  2.01 us (2%)
    ppermute x28, waiting for transfers between devices, send(): return lax.ppermute(x, AXES, pairs)  37.7 us
    ppermute x28, starting transfers between devices, send(): return lax.ppermute(x, AXES, pairs)  31.1 us
    pallas_call x1, Pallas kernels, pair_and_sent(): pl.pallas_call(functools.partial(pair_kernel, images, texts, far, skip, h...  3.23 us
    pallas_call x1, Pallas kernels, unit_rows(): pl.pallas_call(functools.partial(unit_kernel, len(arrays)), out_shape=[ja...  3.15 us
    pallas_call x1, Pallas kernels, teacher_targets(): pl.pallas_call(functools.partial(teacher_kernel, images, texts), out_shap...  2.77 us
    unnamed x12, local copies, waits for them, and re-layouts  2.01 us
  transfers between devices with their start and end apart: 28, of which 14 were waited for; matrix products, arithmetic and copies ran while one was open for 0% of the time, Pallas kernels for 5%

profile of v10, /device:TPU:0, one launch (start us, length us, event | category | flops | bytes accessed | tf_op | source)
XLA Modules:
  0.0 84.2 jit_solution(13862643666490159028)
XLA Ops:
  0.6 3.1 %unit_rows.1 = (bf16[128,1536]{1,0:T(8,128)(2,1)}, bf16[128,1536]{1,0:T(8,128)(2,1)}, bf16[128,1152]{1,0:T(8,128)(2,1)}, bf16[128,1152]{1,0:T(8,128)(2,1)}, bf16...) custom-call(bf16[128,1536]{1,0:T(8,128)(2,1)} %refs_0_.2, bf16[128,1536]{1,0:T(8,128)(2,1)} %refs_1_.1, ...), custom_call_target="tpu_custom_call" | custom-call | flops 2752512 | bytes 4128768 | tf_op jit(solution)/shard_map/unit_rows/pallas_call | solution.py:107
  3.8 4.1 %collective-permute-start = (bf16[128,1536]{1,0:T(8,128)(2,1)}, bf16[128,1536]{1,0:T(8,128)(2,1)S(1)}, u32[]{:S(2)}, u32[]{:S(2)}) collective-permute-start(bf16[128,1536]{1,0:T(8,128)(2,1)} %get-tuple-element.42.refs_0_), channel_id=1, source_target_pairs={{0,16},{1,17},{2,18},{3,19},{4,20},{5,21},{6,22},{7,23},{8,24},{9,... | collective-permute-start | bytes 1179656 | tf_op jit(solution)/shard_map/ppermute | solution.py:62
  7.9 1.6 %collective-permute-start.1 = (bf16[128,1536]{1,0:T(8,128)(2,1)}, bf16[128,1536]{1,0:T(8,128)(2,1)S(1)}, u32[]{:S(2)}, u32[]{:S(2)}) collective-permute-start(bf16[128,1536]{1,0:T(8,128)(2,1)} %get-tuple-element.43.refs_4_), channel_id=1, source_target_pairs={{0,8},{1,9},{2,10},{3,11},{4,12},{5,13},{6,14},{7,15},{8,0},{9,1},... | collective-permute-start | bytes 1179656 | tf_op jit(solution)/shard_map/ppermute | solution.py:62
  9.5 1.5 %collective-permute-start.5 = (bf16[128,2688]{1,0:T(8,128)(2,1)}, bf16[128,2688]{1,0:T(8,128)(2,1)S(1)}, u32[]{:S(2)}, u32[]{:S(2)}) collective-permute-start(bf16[128,2688]{1,0:T(8,128)(2,1)} %get-tuple-element.48), channel_id=1, source_target_pairs={{0,2},{1,3},{2,0},{3,1},{4,6},{5,7},{6,4},{7,5},{8,10},{9,11},{10,... | collective-permute-start | bytes 2064392 | tf_op jit(solution)/shard_map/ppermute | solution.py:62
  11.0 1.5 %collective-permute-start.3 = (bf16[128,2688]{1,0:T(8,128)(2,1)}, bf16[128,2688]{1,0:T(8,128)(2,1)S(1)}, u32[]{:S(2)}, u32[]{:S(2)}) collective-permute-start(bf16[128,2688]{1,0:T(8,128)(2,1)} %get-tuple-element.45), channel_id=1, source_target_pairs={{0,1},{1,0},{2,3},{3,2},{4,5},{5,4},{6,7},{7,6},{8,9},{9,8},{10,11... | collective-permute-start | bytes 2064392 | tf_op jit(solution)/shard_map/ppermute | solution.py:62
  12.5 13.3 %collective-permute-done.refs_1_ = bf16[128,1536]{1,0:T(8,128)(2,1)S(1)} collective-permute-done((bf16[128,1536]{1,0:T(8,128)(2,1)}, bf16[128,1536]{1,0:T(8,128)(2,1)S(1)}, u32[]{:S(2)}, u32[]{:S(2)}) %collective-permute-start) | collective-permute-done | bytes 393248 | tf_op jit(solution)/shard_map/ppermute | solution.py:62
  25.9 1.4 %collective-permute-start.2 = (bf16[128,1152]{1,0:T(8,128)(2,1)}, bf16[128,1152]{1,0:T(8,128)(2,1)S(1)}, u32[]{:S(2)}, u32[]{:S(2)}) collective-permute-start(bf16[128,1152]{1,0:T(8,128)(2,1)} %get-tuple-element.44.refs_0_), channel_id=1, source_target_pairs={{0,16},{1,17},{2,18},{3,19},{4,20},{5,21},{6,22},{7,23},{8,24},{9,... | collective-permute-start | bytes 884744 | tf_op jit(solution)/shard_map/ppermute | solution.py:62
  27.3 2.4 %collective-permute-start.4 = (bf16[128,1152]{1,0:T(8,128)(2,1)}, bf16[128,1152]{1,0:T(8,128)(2,1)S(1)}, u32[]{:S(2)}, u32[]{:S(2)}) collective-permute-start(bf16[128,1152]{1,0:T(8,128)(2,1)} %get-tuple-element.47.refs_4_), channel_id=1, source_target_pairs={{0,8},{1,9},{2,10},{3,11},{4,12},{5,13},{6,14},{7,15},{8,0},{9,1},... | collective-permute-start | bytes 884744 | tf_op jit(solution)/shard_map/ppermute | solution.py:62
  29.8 1.6 %collective-permute-start.7 = (bf16[128,1536]{1,0:T(8,128)(2,1)S(1)}, bf16[128,1536]{1,0:T(8,128)(2,1)S(1)}, u32[]{:S(2)}, u32[]{:S(2)}) collective-permute-start(bf16[128,1536]{1,0:T(8,128)(2,1)S(1)} %collective-permute-done.refs_1_), channel_id=1, source_target_pairs={{0,1},{1,0},{2,3},{3,2},{4,5},{5,4},{6,7},{7,6},{8,9},{9,8},{10,11... | collective-permute-start | bytes 1179656 | tf_op jit(solution)/shard_map/ppermute | solution.py:62
  31.3 1.5 %collective-permute-start.8 = (bf16[128,1536]{1,0:T(8,128)(2,1)S(1)}, bf16[128,1536]{1,0:T(8,128)(2,1)S(1)}, u32[]{:S(2)}, u32[]{:S(2)}) collective-permute-start(bf16[128,1536]{1,0:T(8,128)(2,1)S(1)} %collective-permute-done.1.refs_5_), channel_id=1, source_target_pairs={{0,2},{1,3},{2,0},{3,1},{4,6},{5,7},{6,4},{7,5},{8,10},{9,11},{10,... | collective-permute-start | bytes 1179656 | tf_op jit(solution)/shard_map/ppermute | solution.py:62
  32.8 8.6 %collective-permute-done.2.refs_1_ = bf16[128,1152]{1,0:T(8,128)(2,1)S(1)} collective-permute-done((bf16[128,1152]{1,0:T(8,128)(2,1)}, bf16[128,1152]{1,0:T(8,128)(2,1)S(1)}, u32[]{:S(2)}, u32[]{:S(2)}) %collective-permute-start.2) | collective-permute-done | bytes 294944 | tf_op jit(solution)/shard_map/ppermute | solution.py:62
  42.2 1.4 %collective-permute-start.11 = (bf16[128,1152]{1,0:T(8,128)(2,1)S(1)}, bf16[128,1152]{1,0:T(8,128)(2,1)S(1)}, u32[]{:S(2)}, u32[]{:S(2)}) collective-permute-start(bf16[128,1152]{1,0:T(8,128)(2,1)S(1)} %collective-permute-done.4.refs_5_), channel_id=1, source_target_pairs={{0,2},{1,3},{2,0},{3,1},{4,6},{5,7},{6,4},{7,5},{8,10},{9,11},{10,... | collective-permute-start | bytes 884744 | tf_op jit(solution)/shard_map/ppermute | solution.py:62
  43.6 1.4 %collective-permute-start.10 = (bf16[128,1152]{1,0:T(8,128)(2,1)S(1)}, bf16[128,1152]{1,0:T(8,128)(2,1)S(1)}, u32[]{:S(2)}, u32[]{:S(2)}) collective-permute-start(bf16[128,1152]{1,0:T(8,128)(2,1)S(1)} %collective-permute-done.2.refs_1_), channel_id=1, source_target_pairs={{0,1},{1,0},{2,3},{3,2},{4,5},{5,4},{6,7},{7,6},{8,9},{9,8},{10,11... | collective-permute-start | bytes 884744 | tf_op jit(solution)/shard_map/ppermute | solution.py:62
  45.9 1.0 %copy-done.3 = bf16[128,1536]{1,0:T(8,128)(2,1)S(1)} copy-done((bf16[128,1536]{1,0:T(8,128)(2,1)S(1)}, bf16[128,1536]{1,0:T(8,128)(2,1)}, u32[]{:S(2)}) %copy-start.3) | copy-done | bytes 393240
  46.9 2.8 %teacher_targets.1.refs_12_ = f32[512,1024]{1,0:T(8,128)S(1)} custom-call(bf16[128,1536]{1,0:T(8,128)(2,1)S(1)} %copy-done.2, bf16[128,1536]{1,0:T(8,128)(2,1)S(1)} %collective-permute-done.refs_1_, bf16[128,2688]{1,0:T(8,128)(2,1)S(1)} %collective-permute-done.3.refs_2_, bf16[128,1536]{1,0:T(8,128)(2,1)S(1)} %collective-permute-done.7.refs_3_, ...), custom_call_target="tpu_custom_call" | custom-call | flops 1610612736 | bytes 6815744 | tf_op jit(solution)/shard_map/teacher_targets/pallas_call | solution.py:154
  49.7 1.8 %collective-permute-done.11.refs_7_ = bf16[128,1152]{1,0:T(8,128)(2,1)S(1)} collective-permute-done((bf16[128,1152]{1,0:T(8,128)(2,1)S(1)}, bf16[128,1152]{1,0:T(8,128)(2,1)S(1)}, u32[]{:S(2)}, u32[]{:S(2)}) %collective-permute-start.11) | collective-permute-done | bytes 294944 | tf_op jit(solution)/shard_map/ppermute | solution.py:62
  51.5 1.2 %collective-permute-done.10.refs_3_ = bf16[128,1152]{1,0:T(8,128)(2,1)S(1)} collective-permute-done((bf16[128,1152]{1,0:T(8,128)(2,1)S(1)}, bf16[128,1152]{1,0:T(8,128)(2,1)S(1)}, u32[]{:S(2)}, u32[]{:S(2)}) %collective-permute-start.10) | collective-permute-done | bytes 294944 | tf_op jit(solution)/shard_map/ppermute | solution.py:62
  53.1 3.2 %pair_and_sent.1 = (bf16[512,1024]{1,0:T(8,128)(2,1)S(1)}, bf16[512,1152]{1,0:T(8,128)(2,1)S(1)}, bf16[1024,1152]{1,0:T(8,128)(2,1)S(1)}, bf16[128,768]{1,0:T(8,...) custom-call(bf16[128,1152]{1,0:T(8,128)(2,1)S(1)} %copy-done.4, ...), custom_call_target="tpu_custom_call" | custom-call | flops 2415919104 | bytes 7733248 | tf_op jit(solution)/shard_map/pair_and_sent/pallas_call | solution.py:229
  56.9 1.2 %collective-permute-start.20 = (bf16[128,768]{1,0:T(8,128)(2,1)S(1)}, bf16[128,768]{1,0:T(8,128)(2,1)S(1)}, u32[]{:S(2)}, u32[]{:S(2)}) collective-permute-start(bf16[128,768]{1,0:T(8,128)(2,1)S(1)} %get-tuple-element.71), channel_id=1, source_target_pairs={{0,1},{1,0},{2,3},{3,2},{4,5},{5,4},{6,7},{7,6},{8,9},{9,8},{10,11... | collective-permute-start | bytes 589832 | tf_op jit(solution)/shard_map/ppermute | solution.py:62
  58.2 2.3 %collective-permute-start.23 = (bf16[256,384]{1,0:T(8,128)(2,1)S(1)}, bf16[256,384]{1,0:T(8,128)(2,1)S(1)}, u32[]{:S(2)}, u32[]{:S(2)}) collective-permute-start(bf16[256,384]{1,0:T(8,128)(2,1)S(1)} %get-tuple-element.74), channel_id=1, source_target_pairs={{0,16},{1,17},{2,18},{3,19},{4,20},{5,21},{6,22},{7,23},{8,24},{9,... | collective-permute-start | bytes 589832 | tf_op jit(solution)/shard_map/ppermute | solution.py:62
  60.4 1.5 %kept.1 = (f32[128,1152]{1,0:T(8,128)S(1)}, f32[128,768]{1,0:T(8,128)S(1)}, f32[512,1152]{1,0:T(8,128)S(1)}) custom-call(bf16[512,1024]{1,0:T(8,128)(2,1)S(1)} %get-tuple-element.57.pair, bf16[512,1152]{1,0:T(8,128)(2,1)S(1)} %get-tuple-element.58.img, bf16[1024,1152]{1,0:T(8,128)(2,1)S(1)} %get-tuple-element.59.txt), custom_call_target="tpu_custom_call" | custom-call | flops 1207959552 | bytes 6946816 | tf_op jit(solution)/shard_map/kept/pallas_call | solution.py:264
  62.2 1.6 %collective-permute-start.18 = (bf16[128,768]{1,0:T(8,128)(2,1)S(1)}, bf16[128,768]{1,0:T(8,128)(2,1)S(1)}, u32[]{:S(2)}, u32[]{:S(2)}) collective-permute-start(bf16[128,768]{1,0:T(8,128)(2,1)S(1)} %get-tuple-element.65), channel_id=1, source_target_pairs={{0,2},{1,3},{2,0},{3,1},{4,6},{5,7},{6,4},{7,5},{8,10},{9,11},{10,... | collective-permute-start | bytes 589832 | tf_op jit(solution)/shard_map/ppermute | solution.py:62
  63.8 1.7 %collective-permute-start.22 = (bf16[256,384]{1,0:T(8,128)(2,1)S(1)}, bf16[256,384]{1,0:T(8,128)(2,1)S(1)}, u32[]{:S(2)}, u32[]{:S(2)}) collective-permute-start(bf16[256,384]{1,0:T(8,128)(2,1)S(1)} %get-tuple-element.69), channel_id=1, source_target_pairs={{0,8},{1,9},{2,10},{3,11},{4,12},{5,13},{6,14},{7,15},{8,0},{9,1},... | collective-permute-start | bytes 589832 | tf_op jit(solution)/shard_map/ppermute | solution.py:62
  66.1 1.4 %collective-permute-start.21 = (bf16[128,768]{1,0:T(8,128)(2,1)S(1)}, bf16[128,768]{1,0:T(8,128)(2,1)S(1)}, u32[]{:S(2)}, u32[]{:S(2)}) collective-permute-start(bf16[128,768]{1,0:T(8,128)(2,1)S(1)} %add_convert_fusion.1), channel_id=1, source_target_pairs={{0,16},{1,17},{2,18},{3,19},{4,20},{5,21},{6,22},{7,23},{8,24},{9,... | collective-permute-start | bytes 589832 | tf_op jit(solution)/shard_map/ppermute | solution.py:62
  67.5 2.6 %collective-permute-done.18 = bf16[128,768]{1,0:T(8,128)(2,1)S(1)} collective-permute-done((bf16[128,768]{1,0:T(8,128)(2,1)S(1)}, bf16[128,768]{1,0:T(8,128)(2,1)S(1)}, u32[]{:S(2)}, u32[]{:S(2)}) %collective-permute-start.18) | collective-permute-done | bytes 196640 | tf_op jit(solution)/shard_map/ppermute | solution.py:62
  70.7 3.4 %collective-permute-done.22.refs_11_ = bf16[256,384]{1,0:T(8,128)(2,1)S(1)} collective-permute-done((bf16[256,384]{1,0:T(8,128)(2,1)S(1)}, bf16[256,384]{1,0:T(8,128)(2,1)S(1)}, u32[]{:S(2)}, u32[]{:S(2)}) %collective-permute-start.22) | collective-permute-done | bytes 196640 | tf_op jit(solution)/shard_map/ppermute | solution.py:62
  74.5 1.2 %collective-permute-start.24 = (bf16[128,384]{1,0:T(8,128)(2,1)S(1)}, bf16[128,384]{1,0:T(8,128)(2,1)S(1)}, u32[]{:S(2)}, u32[]{:S(2)}) collective-permute-start(bf16[128,384]{1,0:T(8,128)(2,1)S(1)} %add_convert_fusion.3), channel_id=1, source_target_pairs={{0,1},{1,0},{2,3},{3,2},{4,5},{5,4},{6,7},{7,6},{8,9},{9,8},{10,11... | collective-permute-start | bytes 294920 | tf_op jit(solution)/shard_map/ppermute | solution.py:62
  75.7 1.1 %collective-permute-start.27 = (bf16[128,384]{1,0:T(8,128)(2,1)S(1)}, bf16[128,384]{1,0:T(8,128)(2,1)S(1)}, u32[]{:S(2)}, u32[]{:S(2)}) collective-permute-start(bf16[128,384]{1,0:T(8,128)(2,1)S(1)} %add_convert_fusion.2), channel_id=1, source_target_pairs={{0,2},{1,3},{2,0},{3,1},{4,6},{5,7},{6,4},{7,5},{8,10},{9,11},{10,... | collective-permute-start | bytes 294920 | tf_op jit(solution)/shard_map/ppermute | solution.py:62
  76.8 1.7 %collective-permute-done.21.refs_3_ = bf16[128,768]{1,0:T(8,128)(2,1)S(1)} collective-permute-done((bf16[128,768]{1,0:T(8,128)(2,1)S(1)}, bf16[128,768]{1,0:T(8,128)(2,1)S(1)}, u32[]{:S(2)}, u32[]{:S(2)}) %collective-permute-start.21) | collective-permute-done | bytes 196640 | tf_op jit(solution)/shard_map/ppermute | solution.py:62
  79.2 1.2 %collective-permute-done.27.refs_10_ = bf16[128,384]{1,0:T(8,128)(2,1)S(1)} collective-permute-done((bf16[128,384]{1,0:T(8,128)(2,1)S(1)}, bf16[128,384]{1,0:T(8,128)(2,1)S(1)}, u32[]{:S(2)}, u32[]{:S(2)}) %collective-permute-start.27) | collective-permute-done | bytes 98336 | tf_op jit(solution)/shard_map/ppermute | solution.py:62
  80.4 2.2 %collective-permute-done.26.refs_9_ = bf16[128,768]{1,0:T(8,128)(2,1)S(1)} collective-permute-done((bf16[128,768]{1,0:T(8,128)(2,1)S(1)}, bf16[128,768]{1,0:T(8,128)(2,1)S(1)}, u32[]{:S(2)}, u32[]{:S(2)}) %collective-permute-start.26) | collective-permute-done | bytes 196640 | tf_op jit(solution)/shard_map/ppermute | solution.py:62
  82.6 1.6 %final.1 = (f32[128,1152]{1,0:T(8,128)}, f32[128,1152]{1,0:T(8,128)}) custom-call(bf16[128,1152]{1,0:T(8,128)(2,1)S(1)} %copy-done, f32[128,1152]{1,0:T(8,128)S(1)} %get-tuple-element.60.refs_1_, bf16[128,768]{1,0:T(8,128)(2,1)S(1)} %collective-permute-done.19.refs_2_, bf16[128,768]{1,0:T(8,128)(2,1)S(1)} %collective-permute-done.21.refs_3_, ...), custom_call_target="tpu_custom_call" | custom-call | flops 2949120 | bytes 3538944 | tf_op jit(solution)/shard_map/final/pallas_call | solution.py:344
  (46 shorter events, 5.3 us)
Async XLA Ops:
  3.8 22.0 %collective-permute-start = (bf16[128,1536]{1,0:T(8,128)(2,1)}, bf16[128,1536]{1,0:T(8,128)(2,1)S(1)}, u32[]{:S(2)}, u32[]{:S(2)}) collective-permute-start(bf16[128,1536]{1,0:T(8,128)(2,1)} %get-tuple-element.42.refs_0_), channel_id=1, source_target_pairs={{0,16},{1,17},{2,18},{3,19},{4,20},{5,21},{6,22},{7,23},{8,24},{9,... | collective-permute-start | bytes 1179656 | tf_op jit(solution)/shard_map/ppermute | solution.py:62
  7.9 18.0 %collective-permute-start.1 = (bf16[128,1536]{1,0:T(8,128)(2,1)}, bf16[128,1536]{1,0:T(8,128)(2,1)S(1)}, u32[]{:S(2)}, u32[]{:S(2)}) collective-permute-start(bf16[128,1536]{1,0:T(8,128)(2,1)} %get-tuple-element.43.refs_4_), channel_id=1, source_target_pairs={{0,8},{1,9},{2,10},{3,11},{4,12},{5,13},{6,14},{7,15},{8,0},{9,1},... | collective-permute-start | bytes 1179656 | tf_op jit(solution)/shard_map/ppermute | solution.py:62
  9.5 20.3 %collective-permute-start.6 = (bf16[128,2688]{1,0:T(8,128)(2,1)}, bf16[128,2688]{1,0:T(8,128)(2,1)S(1)}, u32[]{:S(2)}, u32[]{:S(2)}) collective-permute-start(bf16[128,2688]{1,0:T(8,128)(2,1)} %get-tuple-element.48), channel_id=1, source_target_pairs={{0,4},{1,5},{2,6},{3,7},{4,0},{5,1},{6,2},{7,3},{8,12},{9,13},{10,... | collective-permute-start | bytes 2064392 | tf_op jit(solution)/shard_map/ppermute | solution.py:62
  9.5 20.3 %collective-permute-start.5 = (bf16[128,2688]{1,0:T(8,128)(2,1)}, bf16[128,2688]{1,0:T(8,128)(2,1)S(1)}, u32[]{:S(2)}, u32[]{:S(2)}) collective-permute-start(bf16[128,2688]{1,0:T(8,128)(2,1)} %get-tuple-element.48), channel_id=1, source_target_pairs={{0,2},{1,3},{2,0},{3,1},{4,6},{5,7},{6,4},{7,5},{8,10},{9,11},{10,... | collective-permute-start | bytes 2064392 | tf_op jit(solution)/shard_map/ppermute | solution.py:62
  11.0 18.8 %collective-permute-start.3 = (bf16[128,2688]{1,0:T(8,128)(2,1)}, bf16[128,2688]{1,0:T(8,128)(2,1)S(1)}, u32[]{:S(2)}, u32[]{:S(2)}) collective-permute-start(bf16[128,2688]{1,0:T(8,128)(2,1)} %get-tuple-element.45), channel_id=1, source_target_pairs={{0,1},{1,0},{2,3},{3,2},{4,5},{5,4},{6,7},{7,6},{8,9},{9,8},{10,11... | collective-permute-start | bytes 2064392 | tf_op jit(solution)/shard_map/ppermute | solution.py:62
  25.9 15.5 %collective-permute-start.2 = (bf16[128,1152]{1,0:T(8,128)(2,1)}, bf16[128,1152]{1,0:T(8,128)(2,1)S(1)}, u32[]{:S(2)}, u32[]{:S(2)}) collective-permute-start(bf16[128,1152]{1,0:T(8,128)(2,1)} %get-tuple-element.44.refs_0_), channel_id=1, source_target_pairs={{0,16},{1,17},{2,18},{3,19},{4,20},{5,21},{6,22},{7,23},{8,24},{9,... | collective-permute-start | bytes 884744 | tf_op jit(solution)/shard_map/ppermute | solution.py:62
  27.3 14.2 %collective-permute-start.4 = (bf16[128,1152]{1,0:T(8,128)(2,1)}, bf16[128,1152]{1,0:T(8,128)(2,1)S(1)}, u32[]{:S(2)}, u32[]{:S(2)}) collective-permute-start(bf16[128,1152]{1,0:T(8,128)(2,1)} %get-tuple-element.47.refs_4_), channel_id=1, source_target_pairs={{0,8},{1,9},{2,10},{3,11},{4,12},{5,13},{6,14},{7,15},{8,0},{9,1},... | collective-permute-start | bytes 884744 | tf_op jit(solution)/shard_map/ppermute | solution.py:62
  29.8 11.7 %collective-permute-start.7 = (bf16[128,1536]{1,0:T(8,128)(2,1)S(1)}, bf16[128,1536]{1,0:T(8,128)(2,1)S(1)}, u32[]{:S(2)}, u32[]{:S(2)}) collective-permute-start(bf16[128,1536]{1,0:T(8,128)(2,1)S(1)} %collective-permute-done.refs_1_), channel_id=1, source_target_pairs={{0,1},{1,0},{2,3},{3,2},{4,5},{5,4},{6,7},{7,6},{8,9},{9,8},{10,11... | collective-permute-start | bytes 1179656 | tf_op jit(solution)/shard_map/ppermute | solution.py:62
  31.3 10.2 %collective-permute-start.8 = (bf16[128,1536]{1,0:T(8,128)(2,1)S(1)}, bf16[128,1536]{1,0:T(8,128)(2,1)S(1)}, u32[]{:S(2)}, u32[]{:S(2)}) collective-permute-start(bf16[128,1536]{1,0:T(8,128)(2,1)S(1)} %collective-permute-done.1.refs_5_), channel_id=1, source_target_pairs={{0,2},{1,3},{2,0},{3,1},{4,6},{5,7},{6,4},{7,5},{8,10},{9,11},{10,... | collective-permute-start | bytes 1179656 | tf_op jit(solution)/shard_map/ppermute | solution.py:62
  32.8 8.7 %collective-permute-start.9 = (bf16[128,2688]{1,0:T(8,128)(2,1)S(1)}, bf16[128,2688]{1,0:T(8,128)(2,1)S(1)}, u32[]{:S(2)}, u32[]{:S(2)}) collective-permute-start(bf16[128,2688]{1,0:T(8,128)(2,1)S(1)} %collective-permute-done.5.refs_6_), channel_id=1, source_target_pairs={{0,4},{1,5},{2,6},{3,7},{4,0},{5,1},{6,2},{7,3},{8,12},{9,13},{10,... | collective-permute-start | bytes 2064392 | tf_op jit(solution)/shard_map/ppermute | solution.py:62
  41.5 3.4 %collective-permute-start.13 = (bf16[128,1536]{1,0:T(8,128)(2,1)S(1)}, bf16[128,1536]{1,0:T(8,128)(2,1)S(1)}, u32[]{:S(2)}, u32[]{:S(2)}) collective-permute-start(bf16[128,1536]{1,0:T(8,128)(2,1)S(1)} %collective-permute-done.1.refs_5_), channel_id=1, source_target_pairs={{0,4},{1,5},{2,6},{3,7},{4,0},{5,1},{6,2},{7,3},{8,12},{9,13},{10,... | collective-permute-start | bytes 1179656 | tf_op jit(solution)/shard_map/ppermute | solution.py:62
  41.6 3.3 %collective-permute-start.14 = (bf16[128,1536]{1,0:T(8,128)(2,1)S(1)}, bf16[128,1536]{1,0:T(8,128)(2,1)S(1)}, u32[]{:S(2)}, u32[]{:S(2)}) collective-permute-start(bf16[128,1536]{1,0:T(8,128)(2,1)S(1)} %collective-permute-done.8.refs_7_), channel_id=1, source_target_pairs={{0,4},{1,5},{2,6},{3,7},{4,0},{5,1},{6,2},{7,3},{8,12},{9,13},{10,... | collective-permute-start | bytes 1179656 | tf_op jit(solution)/shard_map/ppermute | solution.py:62
  42.1 7.6 %collective-permute-start.12 = (bf16[128,1152]{1,0:T(8,128)(2,1)S(1)}, bf16[128,1152]{1,0:T(8,128)(2,1)S(1)}, u32[]{:S(2)}, u32[]{:S(2)}) collective-permute-start(bf16[128,1152]{1,0:T(8,128)(2,1)S(1)} %collective-permute-done.4.refs_5_), channel_id=1, source_target_pairs={{0,4},{1,5},{2,6},{3,7},{4,0},{5,1},{6,2},{7,3},{8,12},{9,13},{10,... | collective-permute-start | bytes 884744 | tf_op jit(solution)/shard_map/ppermute | solution.py:62
  42.2 9.4 %collective-permute-start.11 = (bf16[128,1152]{1,0:T(8,128)(2,1)S(1)}, bf16[128,1152]{1,0:T(8,128)(2,1)S(1)}, u32[]{:S(2)}, u32[]{:S(2)}) collective-permute-start(bf16[128,1152]{1,0:T(8,128)(2,1)S(1)} %collective-permute-done.4.refs_5_), channel_id=1, source_target_pairs={{0,2},{1,3},{2,0},{3,1},{4,6},{5,7},{6,4},{7,5},{8,10},{9,11},{10,... | collective-permute-start | bytes 884744 | tf_op jit(solution)/shard_map/ppermute | solution.py:62
  43.6 9.1 %collective-permute-start.10 = (bf16[128,1152]{1,0:T(8,128)(2,1)S(1)}, bf16[128,1152]{1,0:T(8,128)(2,1)S(1)}, u32[]{:S(2)}, u32[]{:S(2)}) collective-permute-start(bf16[128,1152]{1,0:T(8,128)(2,1)S(1)} %collective-permute-done.2.refs_1_), channel_id=1, source_target_pairs={{0,1},{1,0},{2,3},{3,2},{4,5},{5,4},{6,7},{7,6},{8,9},{9,8},{10,11... | collective-permute-start | bytes 884744 | tf_op jit(solution)/shard_map/ppermute | solution.py:62
  46.9 6.2 %copy-start.4 = (bf16[128,1152]{1,0:T(8,128)(2,1)S(1)}, bf16[128,1152]{1,0:T(8,128)(2,1)}, u32[]{:S(2)}) copy-start(bf16[128,1152]{1,0:T(8,128)(2,1)} %get-tuple-element.44.refs_0_) | copy-start | bytes 884740
  46.9 6.2 %copy-start.5 = (bf16[128,1152]{1,0:T(8,128)(2,1)S(1)}, bf16[128,1152]{1,0:T(8,128)(2,1)}, u32[]{:S(2)}) copy-start(bf16[128,1152]{1,0:T(8,128)(2,1)} %get-tuple-element.47.refs_4_) | copy-start | bytes 884740
  51.5 1.6 %collective-permute-start.15 = (bf16[128,1152]{1,0:T(8,128)(2,1)S(1)}, bf16[128,1152]{1,0:T(8,128)(2,1)S(1)}, u32[]{:S(2)}, u32[]{:S(2)}) collective-permute-start(bf16[128,1152]{1,0:T(8,128)(2,1)S(1)} %collective-permute-done.11.refs_7_), channel_id=1, source_target_pairs={{0,4},{1,5},{2,6},{3,7},{4,0},{5,1},{6,2},{7,3},{8,12},{9,13},{10,... | collective-permute-start | bytes 884744 | tf_op jit(solution)/shard_map/ppermute | solution.py:62
  56.3 5.6 %collective-permute-start.16 = (bf16[256,1152]{1,0:T(8,128)(2,1)S(1)}, bf16[256,1152]{1,0:T(8,128)(2,1)S(1)}, u32[]{:S(2)}, u32[]{:S(2)}) collective-permute-start(bf16[256,1152]{1,0:T(8,128)(2,1)S(1)} %get-tuple-element.63), channel_id=1, source_target_pairs={{0,4},{1,5},{2,6},{3,7},{4,0},{5,1},{6,2},{7,3},{8,12},{9,13},{10,... | collective-permute-start | bytes 1769480 | tf_op jit(solution)/shard_map/ppermute | solution.py:62
  56.6 5.4 %collective-permute-start.17 = (bf16[256,1152]{1,0:T(8,128)(2,1)S(1)}, bf16[256,1152]{1,0:T(8,128)(2,1)S(1)}, u32[]{:S(2)}, u32[]{:S(2)}) collective-permute-start(bf16[256,1152]{1,0:T(8,128)(2,1)S(1)} %get-tuple-element.64), channel_id=1, source_target_pairs={{0,4},{1,5},{2,6},{3,7},{4,0},{5,1},{6,2},{7,3},{8,12},{9,13},{10,... | collective-permute-start | bytes 1769480 | tf_op jit(solution)/shard_map/ppermute | solution.py:62
  56.9 8.6 %collective-permute-start.20 = (bf16[128,768]{1,0:T(8,128)(2,1)S(1)}, bf16[128,768]{1,0:T(8,128)(2,1)S(1)}, u32[]{:S(2)}, u32[]{:S(2)}) collective-permute-start(bf16[128,768]{1,0:T(8,128)(2,1)S(1)} %get-tuple-element.71), channel_id=1, source_target_pairs={{0,1},{1,0},{2,3},{3,2},{4,5},{5,4},{6,7},{7,6},{8,9},{9,8},{10,11... | collective-permute-start | bytes 589832 | tf_op jit(solution)/shard_map/ppermute | solution.py:62
  58.2 16.3 %collective-permute-start.23 = (bf16[256,384]{1,0:T(8,128)(2,1)S(1)}, bf16[256,384]{1,0:T(8,128)(2,1)S(1)}, u32[]{:S(2)}, u32[]{:S(2)}) collective-permute-start(bf16[256,384]{1,0:T(8,128)(2,1)S(1)} %get-tuple-element.74), channel_id=1, source_target_pairs={{0,16},{1,17},{2,18},{3,19},{4,20},{5,21},{6,22},{7,23},{8,24},{9,... | collective-permute-start | bytes 589832 | tf_op jit(solution)/shard_map/ppermute | solution.py:62
  62.0 20.6 %copy-start = (bf16[128,1152]{1,0:T(8,128)(2,1)S(1)}, bf16[128,1152]{1,0:T(8,128)(2,1)}, u32[]{:S(2)}) copy-start(bf16[128,1152]{1,0:T(8,128)(2,1)} %refs_0_.3) | copy-start | bytes 884740
  62.0 20.6 %copy-start.1 = (bf16[128,1152]{1,0:T(8,128)(2,1)S(1)}, bf16[128,1152]{1,0:T(8,128)(2,1)}, u32[]{:S(2)}) copy-start(bf16[128,1152]{1,0:T(8,128)(2,1)} %refs_6_.1) | copy-start | bytes 884740
  62.2 7.9 %collective-permute-start.18 = (bf16[128,768]{1,0:T(8,128)(2,1)S(1)}, bf16[128,768]{1,0:T(8,128)(2,1)S(1)}, u32[]{:S(2)}, u32[]{:S(2)}) collective-permute-start(bf16[128,768]{1,0:T(8,128)(2,1)S(1)} %get-tuple-element.65), channel_id=1, source_target_pairs={{0,2},{1,3},{2,0},{3,1},{4,6},{5,7},{6,4},{7,5},{8,10},{9,11},{10,... | collective-permute-start | bytes 589832 | tf_op jit(solution)/shard_map/ppermute | solution.py:62
  63.8 10.3 %collective-permute-start.22 = (bf16[256,384]{1,0:T(8,128)(2,1)S(1)}, bf16[256,384]{1,0:T(8,128)(2,1)S(1)}, u32[]{:S(2)}, u32[]{:S(2)}) collective-permute-start(bf16[256,384]{1,0:T(8,128)(2,1)S(1)} %get-tuple-element.69), channel_id=1, source_target_pairs={{0,8},{1,9},{2,10},{3,11},{4,12},{5,13},{6,14},{7,15},{8,0},{9,1},... | collective-permute-start | bytes 589832 | tf_op jit(solution)/shard_map/ppermute | solution.py:62
  65.5 10.2 %collective-permute-start.25 = (bf16[128,768]{1,0:T(8,128)(2,1)S(1)}, bf16[128,768]{1,0:T(8,128)(2,1)S(1)}, u32[]{:S(2)}, u32[]{:S(2)}) collective-permute-start(bf16[128,768]{1,0:T(8,128)(2,1)S(1)} %get-tuple-element.76), channel_id=1, source_target_pairs={{0,2},{1,3},{2,0},{3,1},{4,6},{5,7},{6,4},{7,5},{8,10},{9,11},{10,... | collective-permute-start | bytes 589832 | tf_op jit(solution)/shard_map/ppermute | solution.py:62
  66.1 12.5 %collective-permute-start.21 = (bf16[128,768]{1,0:T(8,128)(2,1)S(1)}, bf16[128,768]{1,0:T(8,128)(2,1)S(1)}, u32[]{:S(2)}, u32[]{:S(2)}) collective-permute-start(bf16[128,768]{1,0:T(8,128)(2,1)S(1)} %add_convert_fusion.1), channel_id=1, source_target_pairs={{0,16},{1,17},{2,18},{3,19},{4,20},{5,21},{6,22},{7,23},{8,24},{9,... | collective-permute-start | bytes 589832 | tf_op jit(solution)/shard_map/ppermute | solution.py:62
  70.1 10.3 %collective-permute-start.19 = (bf16[128,768]{1,0:T(8,128)(2,1)S(1)}, bf16[128,768]{1,0:T(8,128)(2,1)S(1)}, u32[]{:S(2)}, u32[]{:S(2)}) collective-permute-start(bf16[128,768]{1,0:T(8,128)(2,1)S(1)} %get-tuple-element.66), channel_id=1, source_target_pairs={{0,1},{1,0},{2,3},{3,2},{4,5},{5,4},{6,7},{7,6},{8,9},{9,8},{10,11... | collective-permute-start | bytes 589832 | tf_op jit(solution)/shard_map/ppermute | solution.py:62
  74.1 8.5 %collective-permute-start.26 = (bf16[128,768]{1,0:T(8,128)(2,1)S(1)}, bf16[128,768]{1,0:T(8,128)(2,1)S(1)}, u32[]{:S(2)}, u32[]{:S(2)}) collective-permute-start(bf16[128,768]{1,0:T(8,128)(2,1)S(1)} %add_convert_fusion), channel_id=1, source_target_pairs={{0,8},{1,9},{2,10},{3,11},{4,12},{5,13},{6,14},{7,15},{8,0},{9,1},... | collective-permute-start | bytes 589832 | tf_op jit(solution)/shard_map/ppermute | solution.py:62
  74.5 4.7 %collective-permute-start.24 = (bf16[128,384]{1,0:T(8,128)(2,1)S(1)}, bf16[128,384]{1,0:T(8,128)(2,1)S(1)}, u32[]{:S(2)}, u32[]{:S(2)}) collective-permute-start(bf16[128,384]{1,0:T(8,128)(2,1)S(1)} %add_convert_fusion.3), channel_id=1, source_target_pairs={{0,1},{1,0},{2,3},{3,2},{4,5},{5,4},{6,7},{7,6},{8,9},{9,8},{10,11... | collective-permute-start | bytes 294920 | tf_op jit(solution)/shard_map/ppermute | solution.py:62
  75.7 4.7 %collective-permute-start.27 = (bf16[128,384]{1,0:T(8,128)(2,1)S(1)}, bf16[128,384]{1,0:T(8,128)(2,1)S(1)}, u32[]{:S(2)}, u32[]{:S(2)}) collective-permute-start(bf16[128,384]{1,0:T(8,128)(2,1)S(1)} %add_convert_fusion.2), channel_id=1, source_target_pairs={{0,2},{1,3},{2,0},{3,1},{4,6},{5,7},{6,4},{7,5},{8,10},{9,11},{10,... | collective-permute-start | bytes 294920 | tf_op jit(solution)/shard_map/ppermute | solution.py:62
  (2 other events, 2.0 us)

commit v11 on v10

--- a/solution.py
+++ b/solution.py
@@ -248,32 +248,31 @@
     return out[:3], out[cut[0] : cut[1]], out[cut[1] : cut[2]], out[cut[2] : cut[3]], out[cut[3] :]
 
 
-def kept_kernel(half, pair, img, txt, *outs):
+def kept_kernel(of_texts, pair, other, *outs):
     rows = outs[0].shape[0]
-    far = len(outs) - 1
-    outs[-1][...] = lax.dot_general(
-        pair[:, : outs[-1].shape[0]], img[...], (((0,), (0,)), ((), ())), preferred_element_type=f32
-    )
-    for out, grad in zip(outs, image_grads(pair, txt[...], rows, 0, far)):
-        out[...] = grad[:, : out.shape[1]]
-
-
-def kept_grads(pair, img, txt, rows, far, own_txt, half):
-    width = img.shape[1]
-    shapes = [(rows, width)] + [(rows, half)] * (far - 1) + [(own_txt * rows, width)]
+    if of_texts:
+        outs[0][...] = lax.dot_general(
+            pair[:, :rows], other[...], (((0,), (0,)), ((), ())), preferred_element_type=f32
+        )
+    else:
+        for out, grad in zip(outs, image_grads(pair, other[...], rows, 0, len(outs))):
+            out[...] = grad[:, : out.shape[1]]
+
+
+def kept_grads(pair, other, shapes, of_texts):
     return pl.pallas_call(
-        functools.partial(kept_kernel, half),
+        functools.partial(kept_kernel, of_texts),
         out_shape=[jax.ShapeDtypeStruct(shape, f32) for shape in shapes],
-        in_specs=[VMEM] * 3,
+        in_specs=[VMEM] * 2,
         out_specs=[VMEM] * len(shapes),
-        compiler_params=params((pair.shape, 2), (img.shape, 2), (txt.shape, 2), *[(v, 8) for v in shapes]),
+        compiler_params=params((pair.shape, 2), (other.shape, 2), *[(v, 8) for v in shapes]),
         cost_estimate=pl.CostEstimate(
-            flops=2 * pair.size * width,
-            bytes_accessed=2 * (pair.size + img.size + txt.size) + 4 * own_txt * rows * width,
+            flops=pair.size * other.shape[1],
+            bytes_accessed=2 * (pair.size + other.size) + 4 * sum(math.prod(v) for v in shapes),
             transcendentals=0,
         ),
-        name="kept",
-    )(pair, img, txt)
+        name="kept_texts" if of_texts else "kept_images",
+    )(pair, other)
 
 
 def text_sums_kernel(row, near, half, cores, own_ref, *refs):
@@ -446,8 +445,9 @@
             img_in[b, a] = plan.send(img_hops[(b - 1) * far + a], "col", -b)
     long_in = [plan.send(v, "far", -1 - k) for k, v in enumerate(img_longs)]
     txt_in = [plan.send(v, "core", -1 - k // row) for k, v in enumerate(txt_out)]
-    *img_stay, txt_own = kept_grads(pair, img_pack, txt_pack, rows, far, own_txt, half)
+    (txt_own,) = kept_grads(pair, img_pack, [(own_txt * rows, width)], True)
     txt_hops, txt_kept, txt_stay, txt_longs = text_sums(txt_own, txt_in, rows, row, near, half)
+    img_stay = kept_grads(pair, txt_pack, [(rows, width)] + [(rows, half)] * (far - 1), False)
 
     row_in = {}
     for b in range(1, row):
@@ -467,11 +467,11 @@
         plan.send(total(txt_stay[a], [row_in[b, a] for b in range(1, row)]), "near", -a) for a in range(1, near)
     ]
     img_side = [
-        plan.send(total(after(img_kept[b - 1], *[*txt_long_in, *row_in.values()]), [v[b * rows : (b + 1) * rows] for v in long_in]), "col", -b)
+        plan.send(total(after(img_kept[b - 1], *row_in.values()), [v[b * rows : (b + 1) * rows] for v in long_in]), "col", -b)
         for b in range(1, col)
     ]
     txt_side = [
-        plan.send(total(after(txt_kept[b - 1], *row_in.values()), [v[b * rows : (b + 1) * rows] for v in txt_long_in]), "row", -b)
+        plan.send(total(txt_kept[b - 1], [v[b * rows : (b + 1) * rows] for v in txt_long_in]), "row", -b)
         for b in range(1, row)
     ]
     col_ahead = list(row_in.values())

time: 84.4 us -> 84.7 us (level)
    pallas_call x1 -> x2, Pallas kernels: 1.55 us -> 1.72 us  [kept_grads(): pl.pallas_call(functools.partial(kept_kernel, of_texts), out_shape=[jax.S...]
  transfers between devices with their start and end apart: 28 -> 28, of which waited for: 14 -> 12; matrix products, arithmetic and copies ran while one was open for 0% -> 0% of each run, Pallas kernels for 5% -> 6%
where the time goes in v11:
time: 84.7 us; the launch traced here: 84.5 us
  waiting for transfers between devices  37.1 us (44%)
  starting transfers between devices  31.9 us (38%)
  Pallas kernels  12.6 us (15%)
  local copies, waits for them, and re-layouts  2.01 us (2%)
    ppermute x28, waiting for transfers between devices, send(): return lax.ppermute(x, AXES, pairs)  37.1 us
    ppermute x28, starting transfers between devices, send(): return lax.ppermute(x, AXES, pairs)  31.9 us
    pallas_call x1, Pallas kernels, pair_and_sent(): pl.pallas_call(functools.partial(pair_kernel, images, texts, far, skip, h...  3.23 us
    pallas_call x1, Pallas kernels, unit_rows(): pl.pallas_call(functools.partial(unit_kernel, len(arrays)), out_shape=[ja...  3.15 us
    pallas_call x1, Pallas kernels, teacher_targets(): pl.pallas_call(functools.partial(teacher_kernel, images, texts), out_shap...  2.77 us
    unnamed x12, local copies, waits for them, and re-layouts  2.01 us
    pallas_call x2, Pallas kernels, kept_grads(): pl.pallas_call(functools.partial(kept_kernel, of_texts), out_shape=[jax.S...  1.72 us
  transfers between devices with their start and end apart: 28, of which 12 were waited for; matrix products, arithmetic and copies ran while one was open for 0% of the time, Pallas kernels for 6%

profile of v11, /device:TPU:0, one launch (start us, length us, event | category | flops | bytes accessed | tf_op | source)
XLA Modules:
  0.0 84.5 jit_solution(15591695604407109473)
XLA Ops:
  0.6 3.1 %unit_rows.1 = (bf16[128,1536]{1,0:T(8,128)(2,1)}, bf16[128,1536]{1,0:T(8,128)(2,1)}, bf16[128,1152]{1,0:T(8,128)(2,1)}, bf16[128,1152]{1,0:T(8,128)(2,1)}, bf16...) custom-call(bf16[128,1536]{1,0:T(8,128)(2,1)} %refs_0_.2, bf16[128,1536]{1,0:T(8,128)(2,1)} %refs_1_.1, ...), custom_call_target="tpu_custom_call" | custom-call | flops 2752512 | bytes 4128768 | tf_op jit(solution)/shard_map/unit_rows/pallas_call | solution.py:107
  3.8 4.1 %collective-permute-start = (bf16[128,1536]{1,0:T(8,128)(2,1)}, bf16[128,1536]{1,0:T(8,128)(2,1)S(1)}, u32[]{:S(2)}, u32[]{:S(2)}) collective-permute-start(bf16[128,1536]{1,0:T(8,128)(2,1)} %get-tuple-element.40.refs_0_), channel_id=1, source_target_pairs={{0,16},{1,17},{2,18},{3,19},{4,20},{5,21},{6,22},{7,23},{8,24},{9,... | collective-permute-start | bytes 1179656 | tf_op jit(solution)/shard_map/ppermute | solution.py:62
  7.9 1.6 %collective-permute-start.1 = (bf16[128,1536]{1,0:T(8,128)(2,1)}, bf16[128,1536]{1,0:T(8,128)(2,1)S(1)}, u32[]{:S(2)}, u32[]{:S(2)}) collective-permute-start(bf16[128,1536]{1,0:T(8,128)(2,1)} %get-tuple-element.41.refs_4_), channel_id=1, source_target_pairs={{0,8},{1,9},{2,10},{3,11},{4,12},{5,13},{6,14},{7,15},{8,0},{9,1},... | collective-permute-start | bytes 1179656 | tf_op jit(solution)/shard_map/ppermute | solution.py:62
  9.5 1.5 %collective-permute-start.5 = (bf16[128,2688]{1,0:T(8,128)(2,1)}, bf16[128,2688]{1,0:T(8,128)(2,1)S(1)}, u32[]{:S(2)}, u32[]{:S(2)}) collective-permute-start(bf16[128,2688]{1,0:T(8,128)(2,1)} %get-tuple-element.46), channel_id=1, source_target_pairs={{0,2},{1,3},{2,0},{3,1},{4,6},{5,7},{6,4},{7,5},{8,10},{9,11},{10,... | collective-permute-start | bytes 2064392 | tf_op jit(solution)/shard_map/ppermute | solution.py:62
  11.0 1.5 %collective-permute-start.3 = (bf16[128,2688]{1,0:T(8,128)(2,1)}, bf16[128,2688]{1,0:T(8,128)(2,1)S(1)}, u32[]{:S(2)}, u32[]{:S(2)}) collective-permute-start(bf16[128,2688]{1,0:T(8,128)(2,1)} %get-tuple-element.43), channel_id=1, source_target_pairs={{0,1},{1,0},{2,3},{3,2},{4,5},{5,4},{6,7},{7,6},{8,9},{9,8},{10,11... | collective-permute-start | bytes 2064392 | tf_op jit(solution)/shard_map/ppermute | solution.py:62
  12.5 13.3 %collective-permute-done.refs_1_ = bf16[128,1536]{1,0:T(8,128)(2,1)S(1)} collective-permute-done((bf16[128,1536]{1,0:T(8,128)(2,1)}, bf16[128,1536]{1,0:T(8,128)(2,1)S(1)}, u32[]{:S(2)}, u32[]{:S(2)}) %collective-permute-start) | collective-permute-done | bytes 393248 | tf_op jit(solution)/shard_map/ppermute | solution.py:62
  25.9 1.4 %collective-permute-start.2 = (bf16[128,1152]{1,0:T(8,128)(2,1)}, bf16[128,1152]{1,0:T(8,128)(2,1)S(1)}, u32[]{:S(2)}, u32[]{:S(2)}) collective-permute-start(bf16[128,1152]{1,0:T(8,128)(2,1)} %get-tuple-element.42.refs_0_), channel_id=1, source_target_pairs={{0,16},{1,17},{2,18},{3,19},{4,20},{5,21},{6,22},{7,23},{8,24},{9,... | collective-permute-start | bytes 884744 | tf_op jit(solution)/shard_map/ppermute | solution.py:62
  27.3 2.4 %collective-permute-start.4 = (bf16[128,1152]{1,0:T(8,128)(2,1)}, bf16[128,1152]{1,0:T(8,128)(2,1)S(1)}, u32[]{:S(2)}, u32[]{:S(2)}) collective-permute-start(bf16[128,1152]{1,0:T(8,128)(2,1)} %get-tuple-element.45.refs_4_), channel_id=1, source_target_pairs={{0,8},{1,9},{2,10},{3,11},{4,12},{5,13},{6,14},{7,15},{8,0},{9,1},... | collective-permute-start | bytes 884744 | tf_op jit(solution)/shard_map/ppermute | solution.py:62
  29.8 1.6 %collective-permute-start.7 = (bf16[128,1536]{1,0:T(8,128)(2,1)S(1)}, bf16[128,1536]{1,0:T(8,128)(2,1)S(1)}, u32[]{:S(2)}, u32[]{:S(2)}) collective-permute-start(bf16[128,1536]{1,0:T(8,128)(2,1)S(1)} %collective-permute-done.refs_1_), channel_id=1, source_target_pairs={{0,1},{1,0},{2,3},{3,2},{4,5},{5,4},{6,7},{7,6},{8,9},{9,8},{10,11... | collective-permute-start | bytes 1179656 | tf_op jit(solution)/shard_map/ppermute | solution.py:62
  31.3 1.5 %collective-permute-start.8 = (bf16[128,1536]{1,0:T(8,128)(2,1)S(1)}, bf16[128,1536]{1,0:T(8,128)(2,1)S(1)}, u32[]{:S(2)}, u32[]{:S(2)}) collective-permute-start(bf16[128,1536]{1,0:T(8,128)(2,1)S(1)} %collective-permute-done.1.refs_5_), channel_id=1, source_target_pairs={{0,2},{1,3},{2,0},{3,1},{4,6},{5,7},{6,4},{7,5},{8,10},{9,11},{10,... | collective-permute-start | bytes 1179656 | tf_op jit(solution)/shard_map/ppermute | solution.py:62
  32.8 8.6 %collective-permute-done.2.refs_1_ = bf16[128,1152]{1,0:T(8,128)(2,1)S(1)} collective-permute-done((bf16[128,1152]{1,0:T(8,128)(2,1)}, bf16[128,1152]{1,0:T(8,128)(2,1)S(1)}, u32[]{:S(2)}, u32[]{:S(2)}) %collective-permute-start.2) | collective-permute-done | bytes 294944 | tf_op jit(solution)/shard_map/ppermute | solution.py:62
  42.2 1.4 %collective-permute-start.11 = (bf16[128,1152]{1,0:T(8,128)(2,1)S(1)}, bf16[128,1152]{1,0:T(8,128)(2,1)S(1)}, u32[]{:S(2)}, u32[]{:S(2)}) collective-permute-start(bf16[128,1152]{1,0:T(8,128)(2,1)S(1)} %collective-permute-done.4.refs_5_), channel_id=1, source_target_pairs={{0,2},{1,3},{2,0},{3,1},{4,6},{5,7},{6,4},{7,5},{8,10},{9,11},{10,... | collective-permute-start | bytes 884744 | tf_op jit(solution)/shard_map/ppermute | solution.py:62
  43.6 1.4 %collective-permute-start.10 = (bf16[128,1152]{1,0:T(8,128)(2,1)S(1)}, bf16[128,1152]{1,0:T(8,128)(2,1)S(1)}, u32[]{:S(2)}, u32[]{:S(2)}) collective-permute-start(bf16[128,1152]{1,0:T(8,128)(2,1)S(1)} %collective-permute-done.2.refs_1_), channel_id=1, source_target_pairs={{0,1},{1,0},{2,3},{3,2},{4,5},{5,4},{6,7},{7,6},{8,9},{9,8},{10,11... | collective-permute-start | bytes 884744 | tf_op jit(solution)/shard_map/ppermute | solution.py:62
  44.9 1.0 %copy-done.2 = bf16[128,1536]{1,0:T(8,128)(2,1)S(1)} copy-done((bf16[128,1536]{1,0:T(8,128)(2,1)S(1)}, bf16[128,1536]{1,0:T(8,128)(2,1)}, u32[]{:S(2)}) %copy-start.2) | copy-done | bytes 393240
  45.9 1.0 %copy-done.3 = bf16[128,1536]{1,0:T(8,128)(2,1)S(1)} copy-done((bf16[128,1536]{1,0:T(8,128)(2,1)S(1)}, bf16[128,1536]{1,0:T(8,128)(2,1)}, u32[]{:S(2)}) %copy-start.3) | copy-done | bytes 393240
  46.9 2.8 %teacher_targets.1.refs_12_ = f32[512,1024]{1,0:T(8,128)S(1)} custom-call(bf16[128,1536]{1,0:T(8,128)(2,1)S(1)} %copy-done.2, bf16[128,1536]{1,0:T(8,128)(2,1)S(1)} %collective-permute-done.refs_1_, bf16[128,2688]{1,0:T(8,128)(2,1)S(1)} %collective-permute-done.3.refs_2_, bf16[128,1536]{1,0:T(8,128)(2,1)S(1)} %collective-permute-done.7.refs_3_, ...), custom_call_target="tpu_custom_call" | custom-call | flops 1610612736 | bytes 6815744 | tf_op jit(solution)/shard_map/teacher_targets/pallas_call | solution.py:154
  49.7 1.8 %collective-permute-done.11.refs_7_ = bf16[128,1152]{1,0:T(8,128)(2,1)S(1)} collective-permute-done((bf16[128,1152]{1,0:T(8,128)(2,1)S(1)}, bf16[128,1152]{1,0:T(8,128)(2,1)S(1)}, u32[]{:S(2)}, u32[]{:S(2)}) %collective-permute-start.11) | collective-permute-done | bytes 294944 | tf_op jit(solution)/shard_map/ppermute | solution.py:62
  51.5 1.2 %collective-permute-done.10.refs_3_ = bf16[128,1152]{1,0:T(8,128)(2,1)S(1)} collective-permute-done((bf16[128,1152]{1,0:T(8,128)(2,1)S(1)}, bf16[128,1152]{1,0:T(8,128)(2,1)S(1)}, u32[]{:S(2)}, u32[]{:S(2)}) %collective-permute-start.10) | collective-permute-done | bytes 294944 | tf_op jit(solution)/shard_map/ppermute | solution.py:62
  53.1 3.2 %pair_and_sent.1 = (bf16[512,1024]{1,0:T(8,128)(2,1)S(1)}, bf16[512,1152]{1,0:T(8,128)(2,1)S(1)}, bf16[1024,1152]{1,0:T(8,128)(2,1)S(1)}, bf16[128,768]{1,0:T(8,...) custom-call(bf16[128,1152]{1,0:T(8,128)(2,1)S(1)} %copy-done.4, ...), custom_call_target="tpu_custom_call" | custom-call | flops 2415919104 | bytes 7733248 | tf_op jit(solution)/shard_map/pair_and_sent/pallas_call | solution.py:229
  56.9 1.2 %collective-permute-start.20 = (bf16[128,768]{1,0:T(8,128)(2,1)S(1)}, bf16[128,768]{1,0:T(8,128)(2,1)S(1)}, u32[]{:S(2)}, u32[]{:S(2)}) collective-permute-start(bf16[128,768]{1,0:T(8,128)(2,1)S(1)} %get-tuple-element.68), channel_id=1, source_target_pairs={{0,1},{1,0},{2,3},{3,2},{4,5},{5,4},{6,7},{7,6},{8,9},{9,8},{10,11... | collective-permute-start | bytes 589832 | tf_op jit(solution)/shard_map/ppermute | solution.py:62
  58.2 2.3 %collective-permute-start.22 = (bf16[256,384]{1,0:T(8,128)(2,1)S(1)}, bf16[256,384]{1,0:T(8,128)(2,1)S(1)}, u32[]{:S(2)}, u32[]{:S(2)}) collective-permute-start(bf16[256,384]{1,0:T(8,128)(2,1)S(1)} %get-tuple-element.71), channel_id=1, source_target_pairs={{0,16},{1,17},{2,18},{3,19},{4,20},{5,21},{6,22},{7,23},{8,24},{9,... | collective-permute-start | bytes 589832 | tf_op jit(solution)/shard_map/ppermute | solution.py:62
  61.3 0.9 %kept_texts.1.own_ref = f32[512,1152]{1,0:T(8,128)S(1)} custom-call(bf16[512,1024]{1,0:T(8,128)(2,1)S(1)} %get-tuple-element.55.pair, bf16[512,1152]{1,0:T(8,128)(2,1)S(1)} %get-tuple-element.59.other), custom_call_target="tpu_custom_call" | custom-call | flops 603979776 | bytes 4587520 | tf_op jit(solution)/shard_map/kept_texts/pallas_call | solution.py:263
  62.4 1.6 %collective-permute-start.18 = (bf16[128,768]{1,0:T(8,128)(2,1)S(1)}, bf16[128,768]{1,0:T(8,128)(2,1)S(1)}, u32[]{:S(2)}, u32[]{:S(2)}) collective-permute-start(bf16[128,768]{1,0:T(8,128)(2,1)S(1)} %get-tuple-element.62), channel_id=1, source_target_pairs={{0,2},{1,3},{2,0},{3,1},{4,6},{5,7},{6,4},{7,5},{8,10},{9,11},{10,... | collective-permute-start | bytes 589832 | tf_op jit(solution)/shard_map/ppermute | solution.py:62
  64.0 1.7 %collective-permute-start.26 = (bf16[256,384]{1,0:T(8,128)(2,1)S(1)}, bf16[256,384]{1,0:T(8,128)(2,1)S(1)}, u32[]{:S(2)}, u32[]{:S(2)}) collective-permute-start(bf16[256,384]{1,0:T(8,128)(2,1)S(1)} %get-tuple-element.66), channel_id=1, source_target_pairs={{0,8},{1,9},{2,10},{3,11},{4,12},{5,13},{6,14},{7,15},{8,0},{9,1},... | collective-permute-start | bytes 589832 | tf_op jit(solution)/shard_map/ppermute | solution.py:62
  66.3 1.3 %collective-permute-start.21 = (bf16[128,768]{1,0:T(8,128)(2,1)S(1)}, bf16[128,768]{1,0:T(8,128)(2,1)S(1)}, u32[]{:S(2)}, u32[]{:S(2)}) collective-permute-start(bf16[128,768]{1,0:T(8,128)(2,1)S(1)} %add_convert_fusion.1), channel_id=1, source_target_pairs={{0,16},{1,17},{2,18},{3,19},{4,20},{5,21},{6,22},{7,23},{8,24},{9,... | collective-permute-start | bytes 589832 | tf_op jit(solution)/shard_map/ppermute | solution.py:62
  67.5 2.8 %collective-permute-done.18 = bf16[128,768]{1,0:T(8,128)(2,1)S(1)} collective-permute-done((bf16[128,768]{1,0:T(8,128)(2,1)S(1)}, bf16[128,768]{1,0:T(8,128)(2,1)S(1)}, u32[]{:S(2)}, u32[]{:S(2)}) %collective-permute-start.18) | collective-permute-done | bytes 196640 | tf_op jit(solution)/shard_map/ppermute | solution.py:62
  70.3 4.8 %collective-permute-done.22.refs_5_ = bf16[256,384]{1,0:T(8,128)(2,1)S(1)} collective-permute-done((bf16[256,384]{1,0:T(8,128)(2,1)S(1)}, bf16[256,384]{1,0:T(8,128)(2,1)S(1)}, u32[]{:S(2)}, u32[]{:S(2)}) %collective-permute-start.22) | collective-permute-done | bytes 196640 | tf_op jit(solution)/shard_map/ppermute | solution.py:62
  75.7 1.5 %collective-permute-start.19 = (bf16[128,768]{1,0:T(8,128)(2,1)S(1)}, bf16[128,768]{1,0:T(8,128)(2,1)S(1)}, u32[]{:S(2)}, u32[]{:S(2)}) collective-permute-start(bf16[128,768]{1,0:T(8,128)(2,1)S(1)} %get-tuple-element.63), channel_id=1, source_target_pairs={{0,1},{1,0},{2,3},{3,2},{4,5},{5,4},{6,7},{7,6},{8,9},{9,8},{10,11... | collective-permute-start | bytes 589832 | tf_op jit(solution)/shard_map/ppermute | solution.py:62
  77.3 1.6 %collective-permute-start.27 = (bf16[128,384]{1,0:T(8,128)(2,1)S(1)}, bf16[128,384]{1,0:T(8,128)(2,1)S(1)}, u32[]{:S(2)}, u32[]{:S(2)}) collective-permute-start(bf16[128,384]{1,0:T(8,128)(2,1)S(1)} %add_convert_fusion.2), channel_id=1, source_target_pairs={{0,2},{1,3},{2,0},{3,1},{4,6},{5,7},{6,4},{7,5},{8,10},{9,11},{10,... | collective-permute-start | bytes 294920 | tf_op jit(solution)/shard_map/ppermute | solution.py:62
  79.8 2.3 %collective-permute-done.27.refs_10_ = bf16[128,384]{1,0:T(8,128)(2,1)S(1)} collective-permute-done((bf16[128,384]{1,0:T(8,128)(2,1)S(1)}, bf16[128,384]{1,0:T(8,128)(2,1)S(1)}, u32[]{:S(2)}, u32[]{:S(2)}) %collective-permute-start.27) | collective-permute-done | bytes 98336 | tf_op jit(solution)/shard_map/ppermute | solution.py:62
  82.0 0.9 %collective-permute-done.25.refs_9_ = bf16[128,768]{1,0:T(8,128)(2,1)S(1)} collective-permute-done((bf16[128,768]{1,0:T(8,128)(2,1)S(1)}, bf16[128,768]{1,0:T(8,128)(2,1)S(1)}, u32[]{:S(2)}, u32[]{:S(2)}) %collective-permute-start.25) | collective-permute-done | bytes 196640 | tf_op jit(solution)/shard_map/ppermute | solution.py:62
  83.0 1.6 %final.1 = (f32[128,1152]{1,0:T(8,128)}, f32[128,1152]{1,0:T(8,128)}) custom-call(bf16[128,1152]{1,0:T(8,128)(2,1)S(1)} %copy-done, f32[128,1152]{1,0:T(8,128)S(1)} %get-tuple-element.57.refs_1_, bf16[128,768]{1,0:T(8,128)(2,1)S(1)} %collective-permute-done.19.refs_2_, bf16[128,768]{1,0:T(8,128)(2,1)S(1)} %collective-permute-done.21.refs_3_, ...), custom_call_target="tpu_custom_call" | custom-call | flops 2949120 | bytes 3538944 | tf_op jit(solution)/shard_map/final/pallas_call | solution.py:343
  (47 shorter events, 5.1 us)
Async XLA Ops:
  3.8 22.0 %collective-permute-start = (bf16[128,1536]{1,0:T(8,128)(2,1)}, bf16[128,1536]{1,0:T(8,128)(2,1)S(1)}, u32[]{:S(2)}, u32[]{:S(2)}) collective-permute-start(bf16[128,1536]{1,0:T(8,128)(2,1)} %get-tuple-element.40.refs_0_), channel_id=1, source_target_pairs={{0,16},{1,17},{2,18},{3,19},{4,20},{5,21},{6,22},{7,23},{8,24},{9,... | collective-permute-start | bytes 1179656 | tf_op jit(solution)/shard_map/ppermute | solution.py:62
  7.9 18.0 %collective-permute-start.1 = (bf16[128,1536]{1,0:T(8,128)(2,1)}, bf16[128,1536]{1,0:T(8,128)(2,1)S(1)}, u32[]{:S(2)}, u32[]{:S(2)}) collective-permute-start(bf16[128,1536]{1,0:T(8,128)(2,1)} %get-tuple-element.41.refs_4_), channel_id=1, source_target_pairs={{0,8},{1,9},{2,10},{3,11},{4,12},{5,13},{6,14},{7,15},{8,0},{9,1},... | collective-permute-start | bytes 1179656 | tf_op jit(solution)/shard_map/ppermute | solution.py:62
  9.5 20.3 %collective-permute-start.6 = (bf16[128,2688]{1,0:T(8,128)(2,1)}, bf16[128,2688]{1,0:T(8,128)(2,1)S(1)}, u32[]{:S(2)}, u32[]{:S(2)}) collective-permute-start(bf16[128,2688]{1,0:T(8,128)(2,1)} %get-tuple-element.46), channel_id=1, source_target_pairs={{0,4},{1,5},{2,6},{3,7},{4,0},{5,1},{6,2},{7,3},{8,12},{9,13},{10,... | collective-permute-start | bytes 2064392 | tf_op jit(solution)/shard_map/ppermute | solution.py:62
  9.5 20.3 %collective-permute-start.5 = (bf16[128,2688]{1,0:T(8,128)(2,1)}, bf16[128,2688]{1,0:T(8,128)(2,1)S(1)}, u32[]{:S(2)}, u32[]{:S(2)}) collective-permute-start(bf16[128,2688]{1,0:T(8,128)(2,1)} %get-tuple-element.46), channel_id=1, source_target_pairs={{0,2},{1,3},{2,0},{3,1},{4,6},{5,7},{6,4},{7,5},{8,10},{9,11},{10,... | collective-permute-start | bytes 2064392 | tf_op jit(solution)/shard_map/ppermute | solution.py:62
  11.0 18.8 %collective-permute-start.3 = (bf16[128,2688]{1,0:T(8,128)(2,1)}, bf16[128,2688]{1,0:T(8,128)(2,1)S(1)}, u32[]{:S(2)}, u32[]{:S(2)}) collective-permute-start(bf16[128,2688]{1,0:T(8,128)(2,1)} %get-tuple-element.43), channel_id=1, source_target_pairs={{0,1},{1,0},{2,3},{3,2},{4,5},{5,4},{6,7},{7,6},{8,9},{9,8},{10,11... | collective-permute-start | bytes 2064392 | tf_op jit(solution)/shard_map/ppermute | solution.py:62
  25.9 15.5 %collective-permute-start.2 = (bf16[128,1152]{1,0:T(8,128)(2,1)}, bf16[128,1152]{1,0:T(8,128)(2,1)S(1)}, u32[]{:S(2)}, u32[]{:S(2)}) collective-permute-start(bf16[128,1152]{1,0:T(8,128)(2,1)} %get-tuple-element.42.refs_0_), channel_id=1, source_target_pairs={{0,16},{1,17},{2,18},{3,19},{4,20},{5,21},{6,22},{7,23},{8,24},{9,... | collective-permute-start | bytes 884744 | tf_op jit(solution)/shard_map/ppermute | solution.py:62
  27.3 14.2 %collective-permute-start.4 = (bf16[128,1152]{1,0:T(8,128)(2,1)}, bf16[128,1152]{1,0:T(8,128)(2,1)S(1)}, u32[]{:S(2)}, u32[]{:S(2)}) collective-permute-start(bf16[128,1152]{1,0:T(8,128)(2,1)} %get-tuple-element.45.refs_4_), channel_id=1, source_target_pairs={{0,8},{1,9},{2,10},{3,11},{4,12},{5,13},{6,14},{7,15},{8,0},{9,1},... | collective-permute-start | bytes 884744 | tf_op jit(solution)/shard_map/ppermute | solution.py:62
  29.8 11.7 %collective-permute-start.7 = (bf16[128,1536]{1,0:T(8,128)(2,1)S(1)}, bf16[128,1536]{1,0:T(8,128)(2,1)S(1)}, u32[]{:S(2)}, u32[]{:S(2)}) collective-permute-start(bf16[128,1536]{1,0:T(8,128)(2,1)S(1)} %collective-permute-done.refs_1_), channel_id=1, source_target_pairs={{0,1},{1,0},{2,3},{3,2},{4,5},{5,4},{6,7},{7,6},{8,9},{9,8},{10,11... | collective-permute-start | bytes 1179656 | tf_op jit(solution)/shard_map/ppermute | solution.py:62
  31.3 10.2 %collective-permute-start.8 = (bf16[128,1536]{1,0:T(8,128)(2,1)S(1)}, bf16[128,1536]{1,0:T(8,128)(2,1)S(1)}, u32[]{:S(2)}, u32[]{:S(2)}) collective-permute-start(bf16[128,1536]{1,0:T(8,128)(2,1)S(1)} %collective-permute-done.1.refs_5_), channel_id=1, source_target_pairs={{0,2},{1,3},{2,0},{3,1},{4,6},{5,7},{6,4},{7,5},{8,10},{9,11},{10,... | collective-permute-start | bytes 1179656 | tf_op jit(solution)/shard_map/ppermute | solution.py:62
  32.8 8.7 %collective-permute-start.9 = (bf16[128,2688]{1,0:T(8,128)(2,1)S(1)}, bf16[128,2688]{1,0:T(8,128)(2,1)S(1)}, u32[]{:S(2)}, u32[]{:S(2)}) collective-permute-start(bf16[128,2688]{1,0:T(8,128)(2,1)S(1)} %collective-permute-done.5.refs_6_), channel_id=1, source_target_pairs={{0,4},{1,5},{2,6},{3,7},{4,0},{5,1},{6,2},{7,3},{8,12},{9,13},{10,... | collective-permute-start | bytes 2064392 | tf_op jit(solution)/shard_map/ppermute | solution.py:62
  41.5 3.4 %collective-permute-start.13 = (bf16[128,1536]{1,0:T(8,128)(2,1)S(1)}, bf16[128,1536]{1,0:T(8,128)(2,1)S(1)}, u32[]{:S(2)}, u32[]{:S(2)}) collective-permute-start(bf16[128,1536]{1,0:T(8,128)(2,1)S(1)} %collective-permute-done.1.refs_5_), channel_id=1, source_target_pairs={{0,4},{1,5},{2,6},{3,7},{4,0},{5,1},{6,2},{7,3},{8,12},{9,13},{10,... | collective-permute-start | bytes 1179656 | tf_op jit(solution)/shard_map/ppermute | solution.py:62
  41.6 3.3 %collective-permute-start.14 = (bf16[128,1536]{1,0:T(8,128)(2,1)S(1)}, bf16[128,1536]{1,0:T(8,128)(2,1)S(1)}, u32[]{:S(2)}, u32[]{:S(2)}) collective-permute-start(bf16[128,1536]{1,0:T(8,128)(2,1)S(1)} %collective-permute-done.8.refs_7_), channel_id=1, source_target_pairs={{0,4},{1,5},{2,6},{3,7},{4,0},{5,1},{6,2},{7,3},{8,12},{9,13},{10,... | collective-permute-start | bytes 1179656 | tf_op jit(solution)/shard_map/ppermute | solution.py:62
  42.1 7.6 %collective-permute-start.12 = (bf16[128,1152]{1,0:T(8,128)(2,1)S(1)}, bf16[128,1152]{1,0:T(8,128)(2,1)S(1)}, u32[]{:S(2)}, u32[]{:S(2)}) collective-permute-start(bf16[128,1152]{1,0:T(8,128)(2,1)S(1)} %collective-permute-done.4.refs_5_), channel_id=1, source_target_pairs={{0,4},{1,5},{2,6},{3,7},{4,0},{5,1},{6,2},{7,3},{8,12},{9,13},{10,... | collective-permute-start | bytes 884744 | tf_op jit(solution)/shard_map/ppermute | solution.py:62
  42.2 9.4 %collective-permute-start.11 = (bf16[128,1152]{1,0:T(8,128)(2,1)S(1)}, bf16[128,1152]{1,0:T(8,128)(2,1)S(1)}, u32[]{:S(2)}, u32[]{:S(2)}) collective-permute-start(bf16[128,1152]{1,0:T(8,128)(2,1)S(1)} %collective-permute-done.4.refs_5_), channel_id=1, source_target_pairs={{0,2},{1,3},{2,0},{3,1},{4,6},{5,7},{6,4},{7,5},{8,10},{9,11},{10,... | collective-permute-start | bytes 884744 | tf_op jit(solution)/shard_map/ppermute | solution.py:62
  43.6 9.1 %collective-permute-start.10 = (bf16[128,1152]{1,0:T(8,128)(2,1)S(1)}, bf16[128,1152]{1,0:T(8,128)(2,1)S(1)}, u32[]{:S(2)}, u32[]{:S(2)}) collective-permute-start(bf16[128,1152]{1,0:T(8,128)(2,1)S(1)} %collective-permute-done.2.refs_1_), channel_id=1, source_target_pairs={{0,1},{1,0},{2,3},{3,2},{4,5},{5,4},{6,7},{7,6},{8,9},{9,8},{10,11... | collective-permute-start | bytes 884744 | tf_op jit(solution)/shard_map/ppermute | solution.py:62
  46.9 6.2 %copy-start.4 = (bf16[128,1152]{1,0:T(8,128)(2,1)S(1)}, bf16[128,1152]{1,0:T(8,128)(2,1)}, u32[]{:S(2)}) copy-start(bf16[128,1152]{1,0:T(8,128)(2,1)} %get-tuple-element.42.refs_0_) | copy-start | bytes 884740
  46.9 6.2 %copy-start.5 = (bf16[128,1152]{1,0:T(8,128)(2,1)S(1)}, bf16[128,1152]{1,0:T(8,128)(2,1)}, u32[]{:S(2)}) copy-start(bf16[128,1152]{1,0:T(8,128)(2,1)} %get-tuple-element.45.refs_4_) | copy-start | bytes 884740
  51.5 1.6 %collective-permute-start.15 = (bf16[128,1152]{1,0:T(8,128)(2,1)S(1)}, bf16[128,1152]{1,0:T(8,128)(2,1)S(1)}, u32[]{:S(2)}, u32[]{:S(2)}) collective-permute-start(bf16[128,1152]{1,0:T(8,128)(2,1)S(1)} %collective-permute-done.11.refs_7_), channel_id=1, source_target_pairs={{0,4},{1,5},{2,6},{3,7},{4,0},{5,1},{6,2},{7,3},{8,12},{9,13},{10,... | collective-permute-start | bytes 884744 | tf_op jit(solution)/shard_map/ppermute | solution.py:62
  56.3 5.8 %collective-permute-start.16 = (bf16[256,1152]{1,0:T(8,128)(2,1)S(1)}, bf16[256,1152]{1,0:T(8,128)(2,1)S(1)}, u32[]{:S(2)}, u32[]{:S(2)}) collective-permute-start(bf16[256,1152]{1,0:T(8,128)(2,1)S(1)} %get-tuple-element.60), channel_id=1, source_target_pairs={{0,4},{1,5},{2,6},{3,7},{4,0},{5,1},{6,2},{7,3},{8,12},{9,13},{10,... | collective-permute-start | bytes 1769480 | tf_op jit(solution)/shard_map/ppermute | solution.py:62
  56.6 5.6 %collective-permute-start.17 = (bf16[256,1152]{1,0:T(8,128)(2,1)S(1)}, bf16[256,1152]{1,0:T(8,128)(2,1)S(1)}, u32[]{:S(2)}, u32[]{:S(2)}) collective-permute-start(bf16[256,1152]{1,0:T(8,128)(2,1)S(1)} %get-tuple-element.61), channel_id=1, source_target_pairs={{0,4},{1,5},{2,6},{3,7},{4,0},{5,1},{6,2},{7,3},{8,12},{9,13},{10,... | collective-permute-start | bytes 1769480 | tf_op jit(solution)/shard_map/ppermute | solution.py:62
  56.9 8.8 %collective-permute-start.20 = (bf16[128,768]{1,0:T(8,128)(2,1)S(1)}, bf16[128,768]{1,0:T(8,128)(2,1)S(1)}, u32[]{:S(2)}, u32[]{:S(2)}) collective-permute-start(bf16[128,768]{1,0:T(8,128)(2,1)S(1)} %get-tuple-element.68), channel_id=1, source_target_pairs={{0,1},{1,0},{2,3},{3,2},{4,5},{5,4},{6,7},{7,6},{8,9},{9,8},{10,11... | collective-permute-start | bytes 589832 | tf_op jit(solution)/shard_map/ppermute | solution.py:62
  58.2 16.9 %collective-permute-start.22 = (bf16[256,384]{1,0:T(8,128)(2,1)S(1)}, bf16[256,384]{1,0:T(8,128)(2,1)S(1)}, u32[]{:S(2)}, u32[]{:S(2)}) collective-permute-start(bf16[256,384]{1,0:T(8,128)(2,1)S(1)} %get-tuple-element.71), channel_id=1, source_target_pairs={{0,16},{1,17},{2,18},{3,19},{4,20},{5,21},{6,22},{7,23},{8,24},{9,... | collective-permute-start | bytes 589832 | tf_op jit(solution)/shard_map/ppermute | solution.py:62
  62.2 20.8 %copy-start = (bf16[128,1152]{1,0:T(8,128)(2,1)S(1)}, bf16[128,1152]{1,0:T(8,128)(2,1)}, u32[]{:S(2)}) copy-start(bf16[128,1152]{1,0:T(8,128)(2,1)} %refs_0_.3) | copy-start | bytes 884740
  62.2 20.8 %copy-start.1 = (bf16[128,1152]{1,0:T(8,128)(2,1)S(1)}, bf16[128,1152]{1,0:T(8,128)(2,1)}, u32[]{:S(2)}) copy-start(bf16[128,1152]{1,0:T(8,128)(2,1)} %refs_6_.1) | copy-start | bytes 884740
  62.4 7.9 %collective-permute-start.18 = (bf16[128,768]{1,0:T(8,128)(2,1)S(1)}, bf16[128,768]{1,0:T(8,128)(2,1)S(1)}, u32[]{:S(2)}, u32[]{:S(2)}) collective-permute-start(bf16[128,768]{1,0:T(8,128)(2,1)S(1)} %get-tuple-element.62), channel_id=1, source_target_pairs={{0,2},{1,3},{2,0},{3,1},{4,6},{5,7},{6,4},{7,5},{8,10},{9,11},{10,... | collective-permute-start | bytes 589832 | tf_op jit(solution)/shard_map/ppermute | solution.py:62
  64.0 13.2 %collective-permute-start.26 = (bf16[256,384]{1,0:T(8,128)(2,1)S(1)}, bf16[256,384]{1,0:T(8,128)(2,1)S(1)}, u32[]{:S(2)}, u32[]{:S(2)}) collective-permute-start(bf16[256,384]{1,0:T(8,128)(2,1)S(1)} %get-tuple-element.66), channel_id=1, source_target_pairs={{0,8},{1,9},{2,10},{3,11},{4,12},{5,13},{6,14},{7,15},{8,0},{9,1},... | collective-permute-start | bytes 589832 | tf_op jit(solution)/shard_map/ppermute | solution.py:62
  65.7 11.6 %collective-permute-start.24 = (bf16[128,768]{1,0:T(8,128)(2,1)S(1)}, bf16[128,768]{1,0:T(8,128)(2,1)S(1)}, u32[]{:S(2)}, u32[]{:S(2)}) collective-permute-start(bf16[128,768]{1,0:T(8,128)(2,1)S(1)} %get-tuple-element.73), channel_id=1, source_target_pairs={{0,2},{1,3},{2,0},{3,1},{4,6},{5,7},{6,4},{7,5},{8,10},{9,11},{10,... | collective-permute-start | bytes 589832 | tf_op jit(solution)/shard_map/ppermute | solution.py:62
  66.3 12.7 %collective-permute-start.21 = (bf16[128,768]{1,0:T(8,128)(2,1)S(1)}, bf16[128,768]{1,0:T(8,128)(2,1)S(1)}, u32[]{:S(2)}, u32[]{:S(2)}) collective-permute-start(bf16[128,768]{1,0:T(8,128)(2,1)S(1)} %add_convert_fusion.1), channel_id=1, source_target_pairs={{0,16},{1,17},{2,18},{3,19},{4,20},{5,21},{6,22},{7,23},{8,24},{9,... | collective-permute-start | bytes 589832 | tf_op jit(solution)/shard_map/ppermute | solution.py:62
  75.1 4.7 %collective-permute-start.23 = (bf16[128,384]{1,0:T(8,128)(2,1)S(1)}, bf16[128,384]{1,0:T(8,128)(2,1)S(1)}, u32[]{:S(2)}, u32[]{:S(2)}) collective-permute-start(bf16[128,384]{1,0:T(8,128)(2,1)S(1)} %add_convert_fusion.3), channel_id=1, source_target_pairs={{0,1},{1,0},{2,3},{3,2},{4,5},{5,4},{6,7},{7,6},{8,9},{9,8},{10,11... | collective-permute-start | bytes 294920 | tf_op jit(solution)/shard_map/ppermute | solution.py:62
  75.7 6.3 %collective-permute-start.19 = (bf16[128,768]{1,0:T(8,128)(2,1)S(1)}, bf16[128,768]{1,0:T(8,128)(2,1)S(1)}, u32[]{:S(2)}, u32[]{:S(2)}) collective-permute-start(bf16[128,768]{1,0:T(8,128)(2,1)S(1)} %get-tuple-element.63), channel_id=1, source_target_pairs={{0,1},{1,0},{2,3},{3,2},{4,5},{5,4},{6,7},{7,6},{8,9},{9,8},{10,11... | collective-permute-start | bytes 589832 | tf_op jit(solution)/shard_map/ppermute | solution.py:62
  77.2 5.7 %collective-permute-start.25 = (bf16[128,768]{1,0:T(8,128)(2,1)S(1)}, bf16[128,768]{1,0:T(8,128)(2,1)S(1)}, u32[]{:S(2)}, u32[]{:S(2)}) collective-permute-start(bf16[128,768]{1,0:T(8,128)(2,1)S(1)} %add_convert_fusion), channel_id=1, source_target_pairs={{0,8},{1,9},{2,10},{3,11},{4,12},{5,13},{6,14},{7,15},{8,0},{9,1},... | collective-permute-start | bytes 589832 | tf_op jit(solution)/shard_map/ppermute | solution.py:62
  77.3 4.7 %collective-permute-start.27 = (bf16[128,384]{1,0:T(8,128)(2,1)S(1)}, bf16[128,384]{1,0:T(8,128)(2,1)S(1)}, u32[]{:S(2)}, u32[]{:S(2)}) collective-permute-start(bf16[128,384]{1,0:T(8,128)(2,1)S(1)} %add_convert_fusion.2), channel_id=1, source_target_pairs={{0,2},{1,3},{2,0},{3,1},{4,6},{5,7},{6,4},{7,5},{8,10},{9,11},{10,... | collective-permute-start | bytes 294920 | tf_op jit(solution)/shard_map/ppermute | solution.py:62
  (2 other events, 2.0 us)

commit v12 on v10

--- a/solution.py
+++ b/solution.py
@@ -434,7 +434,7 @@
     s_txts = texts(s_txt, s_near, b_row, s_near_row, b_core, s_near_core, b_row_core, s_both_core)
 
     own_txt = row * near
-    half = width // 128 * 2 // 3 * 128
+    half = width // 128 * 7 // 9 * 128
     skip = teacher_img.shape[1]
     packed, img_hops, img_kept, img_longs, txt_out = pair_and_sent(
         s_imgs, s_txts, far, near, own_txt, skip, half, targets
@@ -474,8 +474,8 @@
         plan.send(total(after(txt_kept[b - 1], *row_in.values()), [v[b * rows : (b + 1) * rows] for v in txt_long_in]), "row", -b)
         for b in range(1, row)
     ]
-    col_ahead = list(row_in.values())
-    row_ahead = list(img_in.values())
+    col_ahead = list(txt_long_in)
+    row_ahead = list(txt_long_in)
     img_ends = [plan.send(after(img_hops[(b - 1) * far], *col_ahead), "col", -b) for b in range(1, col)]
     txt_ends = [plan.send(after(txt_hops[(b - 1) * near], *row_ahead), "row", -b) for b in range(1, row)]
     image_side = (student_img, img_stay[0], img_ends + img_last, img_side + long_in)

time: 84.4 us -> 84.5 us (level)
  starting transfers between devices: 31.1 us -> 32.7 us
  waiting for transfers between devices: 37.7 us -> 36.2 us
    ppermute x28, starting transfers between devices: 31.1 us -> 32.7 us  [send(): return lax.ppermute(x, AXES, pairs)]
    ppermute x28, waiting for transfers between devices: 37.7 us -> 36.2 us  [send(): return lax.ppermute(x, AXES, pairs)]
  transfers between devices with their start and end apart: 28 -> 28, of which waited for: 14 -> 11; matrix products, arithmetic and copies ran while one was open for 0% -> 0% of each run, Pallas kernels for 5% -> 5%
where the time goes in v12:
time: 84.5 us; the launch traced here: 84.2 us
  waiting for transfers between devices  36.2 us (43%)
  starting transfers between devices  32.7 us (39%)
  Pallas kernels  12.4 us (15%)
  local copies, waits for them, and re-layouts  2.01 us (2%)
    ppermute x28, waiting for transfers between devices, send(): return lax.ppermute(x, AXES, pairs)  36.2 us
    ppermute x28, starting transfers between devices, send(): return lax.ppermute(x, AXES, pairs)  32.7 us
    pallas_call x1, Pallas kernels, pair_and_sent(): pl.pallas_call(functools.partial(pair_kernel, images, texts, far, skip, h...  3.19 us
    pallas_call x1, Pallas kernels, unit_rows(): pl.pallas_call(functools.partial(unit_kernel, len(arrays)), out_shape=[ja...  3.15 us
    pallas_call x1, Pallas kernels, teacher_targets(): pl.pallas_call(functools.partial(teacher_kernel, images, texts), out_shap...  2.77 us
    unnamed x12, local copies, waits for them, and re-layouts  2.01 us
  transfers between devices with their start and end apart: 28, of which 11 were waited for; matrix products, arithmetic and copies ran while one was open for 0% of the time, Pallas kernels for 5%

profile of v12, /device:TPU:0, one launch (start us, length us, event | category | flops | bytes accessed | tf_op | source)
XLA Modules:
  0.0 84.2 jit_solution(2915556424132358839)
XLA Ops:
  0.6 3.1 %unit_rows.1 = (bf16[128,1536]{1,0:T(8,128)(2,1)}, bf16[128,1536]{1,0:T(8,128)(2,1)}, bf16[128,1152]{1,0:T(8,128)(2,1)}, bf16[128,1152]{1,0:T(8,128)(2,1)}, bf16...) custom-call(bf16[128,1536]{1,0:T(8,128)(2,1)} %refs_0_.2, bf16[128,1536]{1,0:T(8,128)(2,1)} %refs_1_.1, ...), custom_call_target="tpu_custom_call" | custom-call | flops 2752512 | bytes 4128768 | tf_op jit(solution)/shard_map/unit_rows/pallas_call | solution.py:107
  3.8 4.1 %collective-permute-start = (bf16[128,1536]{1,0:T(8,128)(2,1)}, bf16[128,1536]{1,0:T(8,128)(2,1)S(1)}, u32[]{:S(2)}, u32[]{:S(2)}) collective-permute-start(bf16[128,1536]{1,0:T(8,128)(2,1)} %get-tuple-element.42.refs_0_), channel_id=1, source_target_pairs={{0,16},{1,17},{2,18},{3,19},{4,20},{5,21},{6,22},{7,23},{8,24},{9,... | collective-permute-start | bytes 1179656 | tf_op jit(solution)/shard_map/ppermute | solution.py:62
  7.9 1.6 %collective-permute-start.1 = (bf16[128,1536]{1,0:T(8,128)(2,1)}, bf16[128,1536]{1,0:T(8,128)(2,1)S(1)}, u32[]{:S(2)}, u32[]{:S(2)}) collective-permute-start(bf16[128,1536]{1,0:T(8,128)(2,1)} %get-tuple-element.43.refs_4_), channel_id=1, source_target_pairs={{0,8},{1,9},{2,10},{3,11},{4,12},{5,13},{6,14},{7,15},{8,0},{9,1},... | collective-permute-start | bytes 1179656 | tf_op jit(solution)/shard_map/ppermute | solution.py:62
  9.5 1.5 %collective-permute-start.5 = (bf16[128,2688]{1,0:T(8,128)(2,1)}, bf16[128,2688]{1,0:T(8,128)(2,1)S(1)}, u32[]{:S(2)}, u32[]{:S(2)}) collective-permute-start(bf16[128,2688]{1,0:T(8,128)(2,1)} %get-tuple-element.48), channel_id=1, source_target_pairs={{0,2},{1,3},{2,0},{3,1},{4,6},{5,7},{6,4},{7,5},{8,10},{9,11},{10,... | collective-permute-start | bytes 2064392 | tf_op jit(solution)/shard_map/ppermute | solution.py:62
  11.0 1.5 %collective-permute-start.3 = (bf16[128,2688]{1,0:T(8,128)(2,1)}, bf16[128,2688]{1,0:T(8,128)(2,1)S(1)}, u32[]{:S(2)}, u32[]{:S(2)}) collective-permute-start(bf16[128,2688]{1,0:T(8,128)(2,1)} %get-tuple-element.45), channel_id=1, source_target_pairs={{0,1},{1,0},{2,3},{3,2},{4,5},{5,4},{6,7},{7,6},{8,9},{9,8},{10,11... | collective-permute-start | bytes 2064392 | tf_op jit(solution)/shard_map/ppermute | solution.py:62
  12.5 13.3 %collective-permute-done.refs_1_ = bf16[128,1536]{1,0:T(8,128)(2,1)S(1)} collective-permute-done((bf16[128,1536]{1,0:T(8,128)(2,1)}, bf16[128,1536]{1,0:T(8,128)(2,1)S(1)}, u32[]{:S(2)}, u32[]{:S(2)}) %collective-permute-start) | collective-permute-done | bytes 393248 | tf_op jit(solution)/shard_map/ppermute | solution.py:62
  25.9 1.4 %collective-permute-start.2 = (bf16[128,1152]{1,0:T(8,128)(2,1)}, bf16[128,1152]{1,0:T(8,128)(2,1)S(1)}, u32[]{:S(2)}, u32[]{:S(2)}) collective-permute-start(bf16[128,1152]{1,0:T(8,128)(2,1)} %get-tuple-element.44.refs_0_), channel_id=1, source_target_pairs={{0,16},{1,17},{2,18},{3,19},{4,20},{5,21},{6,22},{7,23},{8,24},{9,... | collective-permute-start | bytes 884744 | tf_op jit(solution)/shard_map/ppermute | solution.py:62
  27.3 2.4 %collective-permute-start.4 = (bf16[128,1152]{1,0:T(8,128)(2,1)}, bf16[128,1152]{1,0:T(8,128)(2,1)S(1)}, u32[]{:S(2)}, u32[]{:S(2)}) collective-permute-start(bf16[128,1152]{1,0:T(8,128)(2,1)} %get-tuple-element.47.refs_4_), channel_id=1, source_target_pairs={{0,8},{1,9},{2,10},{3,11},{4,12},{5,13},{6,14},{7,15},{8,0},{9,1},... | collective-permute-start | bytes 884744 | tf_op jit(solution)/shard_map/ppermute | solution.py:62
  29.8 1.6 %collective-permute-start.7 = (bf16[128,1536]{1,0:T(8,128)(2,1)S(1)}, bf16[128,1536]{1,0:T(8,128)(2,1)S(1)}, u32[]{:S(2)}, u32[]{:S(2)}) collective-permute-start(bf16[128,1536]{1,0:T(8,128)(2,1)S(1)} %collective-permute-done.refs_1_), channel_id=1, source_target_pairs={{0,1},{1,0},{2,3},{3,2},{4,5},{5,4},{6,7},{7,6},{8,9},{9,8},{10,11... | collective-permute-start | bytes 1179656 | tf_op jit(solution)/shard_map/ppermute | solution.py:62
  31.3 1.5 %collective-permute-start.8 = (bf16[128,1536]{1,0:T(8,128)(2,1)S(1)}, bf16[128,1536]{1,0:T(8,128)(2,1)S(1)}, u32[]{:S(2)}, u32[]{:S(2)}) collective-permute-start(bf16[128,1536]{1,0:T(8,128)(2,1)S(1)} %collective-permute-done.1.refs_5_), channel_id=1, source_target_pairs={{0,2},{1,3},{2,0},{3,1},{4,6},{5,7},{6,4},{7,5},{8,10},{9,11},{10,... | collective-permute-start | bytes 1179656 | tf_op jit(solution)/shard_map/ppermute | solution.py:62
  32.8 8.6 %collective-permute-done.2.refs_1_ = bf16[128,1152]{1,0:T(8,128)(2,1)S(1)} collective-permute-done((bf16[128,1152]{1,0:T(8,128)(2,1)}, bf16[128,1152]{1,0:T(8,128)(2,1)S(1)}, u32[]{:S(2)}, u32[]{:S(2)}) %collective-permute-start.2) | collective-permute-done | bytes 294944 | tf_op jit(solution)/shard_map/ppermute | solution.py:62
  42.2 1.4 %collective-permute-start.11 = (bf16[128,1152]{1,0:T(8,128)(2,1)S(1)}, bf16[128,1152]{1,0:T(8,128)(2,1)S(1)}, u32[]{:S(2)}, u32[]{:S(2)}) collective-permute-start(bf16[128,1152]{1,0:T(8,128)(2,1)S(1)} %collective-permute-done.4.refs_5_), channel_id=1, source_target_pairs={{0,2},{1,3},{2,0},{3,1},{4,6},{5,7},{6,4},{7,5},{8,10},{9,11},{10,... | collective-permute-start | bytes 884744 | tf_op jit(solution)/shard_map/ppermute | solution.py:62
  43.6 1.4 %collective-permute-start.10 = (bf16[128,1152]{1,0:T(8,128)(2,1)S(1)}, bf16[128,1152]{1,0:T(8,128)(2,1)S(1)}, u32[]{:S(2)}, u32[]{:S(2)}) collective-permute-start(bf16[128,1152]{1,0:T(8,128)(2,1)S(1)} %collective-permute-done.2.refs_1_), channel_id=1, source_target_pairs={{0,1},{1,0},{2,3},{3,2},{4,5},{5,4},{6,7},{7,6},{8,9},{9,8},{10,11... | collective-permute-start | bytes 884744 | tf_op jit(solution)/shard_map/ppermute | solution.py:62
  44.9 1.0 %copy-done.2 = bf16[128,1536]{1,0:T(8,128)(2,1)S(1)} copy-done((bf16[128,1536]{1,0:T(8,128)(2,1)S(1)}, bf16[128,1536]{1,0:T(8,128)(2,1)}, u32[]{:S(2)}) %copy-start.2) | copy-done | bytes 393240
  45.9 1.0 %copy-done.3 = bf16[128,1536]{1,0:T(8,128)(2,1)S(1)} copy-done((bf16[128,1536]{1,0:T(8,128)(2,1)S(1)}, bf16[128,1536]{1,0:T(8,128)(2,1)}, u32[]{:S(2)}) %copy-start.3) | copy-done | bytes 393240
  46.9 2.8 %teacher_targets.1.refs_12_ = f32[512,1024]{1,0:T(8,128)S(1)} custom-call(bf16[128,1536]{1,0:T(8,128)(2,1)S(1)} %copy-done.2, bf16[128,1536]{1,0:T(8,128)(2,1)S(1)} %collective-permute-done.refs_1_, bf16[128,2688]{1,0:T(8,128)(2,1)S(1)} %collective-permute-done.3.refs_2_, bf16[128,1536]{1,0:T(8,128)(2,1)S(1)} %collective-permute-done.7.refs_3_, ...), custom_call_target="tpu_custom_call" | custom-call | flops 1610612736 | bytes 6815744 | tf_op jit(solution)/shard_map/teacher_targets/pallas_call | solution.py:154
  49.7 1.8 %collective-permute-done.11.refs_7_ = bf16[128,1152]{1,0:T(8,128)(2,1)S(1)} collective-permute-done((bf16[128,1152]{1,0:T(8,128)(2,1)S(1)}, bf16[128,1152]{1,0:T(8,128)(2,1)S(1)}, u32[]{:S(2)}, u32[]{:S(2)}) %collective-permute-start.11) | collective-permute-done | bytes 294944 | tf_op jit(solution)/shard_map/ppermute | solution.py:62
  51.5 1.2 %collective-permute-done.10.refs_3_ = bf16[128,1152]{1,0:T(8,128)(2,1)S(1)} collective-permute-done((bf16[128,1152]{1,0:T(8,128)(2,1)S(1)}, bf16[128,1152]{1,0:T(8,128)(2,1)S(1)}, u32[]{:S(2)}, u32[]{:S(2)}) %collective-permute-start.10) | collective-permute-done | bytes 294944 | tf_op jit(solution)/shard_map/ppermute | solution.py:62
  53.1 3.2 %pair_and_sent.1 = (bf16[512,1024]{1,0:T(8,128)(2,1)S(1)}, bf16[512,1152]{1,0:T(8,128)(2,1)S(1)}, bf16[1024,1152]{1,0:T(8,128)(2,1)S(1)}, bf16[128,896]{1,0:T(8,...) custom-call(bf16[128,1152]{1,0:T(8,128)(2,1)S(1)} %copy-done.4, ...), custom_call_target="tpu_custom_call" | custom-call | flops 2415919104 | bytes 7733248 | tf_op jit(solution)/shard_map/pair_and_sent/pallas_call | solution.py:229
  56.9 1.2 %collective-permute-start.20 = (bf16[128,896]{1,0:T(8,128)(2,1)S(1)}, bf16[128,896]{1,0:T(8,128)(2,1)S(1)}, u32[]{:S(2)}, u32[]{:S(2)}) collective-permute-start(bf16[128,896]{1,0:T(8,128)(2,1)S(1)} %get-tuple-element.71), channel_id=1, source_target_pairs={{0,1},{1,0},{2,3},{3,2},{4,5},{5,4},{6,7},{7,6},{8,9},{9,8},{10,11... | collective-permute-start | bytes 688136 | tf_op jit(solution)/shard_map/ppermute | solution.py:62
  58.1 2.3 %collective-permute-start.23 = (bf16[256,256]{1,0:T(8,128)(2,1)S(1)}, bf16[256,256]{1,0:T(8,128)(2,1)S(1)}, u32[]{:S(2)}, u32[]{:S(2)}) collective-permute-start(bf16[256,256]{1,0:T(8,128)(2,1)S(1)} %get-tuple-element.74), channel_id=1, source_target_pairs={{0,16},{1,17},{2,18},{3,19},{4,20},{5,21},{6,22},{7,23},{8,24},{9,... | collective-permute-start | bytes 393224 | tf_op jit(solution)/shard_map/ppermute | solution.py:62
  60.4 1.5 %kept.1 = (f32[128,1152]{1,0:T(8,128)S(1)}, f32[128,896]{1,0:T(8,128)S(1)}, f32[512,1152]{1,0:T(8,128)S(1)}) custom-call(bf16[512,1024]{1,0:T(8,128)(2,1)S(1)} %get-tuple-element.57.pair, bf16[512,1152]{1,0:T(8,128)(2,1)S(1)} %get-tuple-element.58.img, bf16[1024,1152]{1,0:T(8,128)(2,1)S(1)} %get-tuple-element.59.txt), custom_call_target="tpu_custom_call" | custom-call | flops 1207959552 | bytes 6946816 | tf_op jit(solution)/shard_map/kept/pallas_call | solution.py:264
  62.2 1.8 %collective-permute-start.18 = (bf16[256,256]{1,0:T(8,128)(2,1)S(1)}, bf16[256,256]{1,0:T(8,128)(2,1)S(1)}, u32[]{:S(2)}, u32[]{:S(2)}) collective-permute-start(bf16[256,256]{1,0:T(8,128)(2,1)S(1)} %get-tuple-element.65), channel_id=1, source_target_pairs={{0,8},{1,9},{2,10},{3,11},{4,12},{5,13},{6,14},{7,15},{8,0},{9,1},... | collective-permute-start | bytes 393224 | tf_op jit(solution)/shard_map/ppermute | solution.py:62
  63.9 1.5 %collective-permute-start.22 = (bf16[128,896]{1,0:T(8,128)(2,1)S(1)}, bf16[128,896]{1,0:T(8,128)(2,1)S(1)}, u32[]{:S(2)}, u32[]{:S(2)}) collective-permute-start(bf16[128,896]{1,0:T(8,128)(2,1)S(1)} %get-tuple-element.69), channel_id=1, source_target_pairs={{0,2},{1,3},{2,0},{3,1},{4,6},{5,7},{6,4},{7,5},{8,10},{9,11},{10,... | collective-permute-start | bytes 688136 | tf_op jit(solution)/shard_map/ppermute | solution.py:62
  65.5 1.1 %collective-permute-start.21 = (bf16[128,896]{1,0:T(8,128)(2,1)S(1)}, bf16[128,896]{1,0:T(8,128)(2,1)S(1)}, u32[]{:S(2)}, u32[]{:S(2)}) collective-permute-start(bf16[128,896]{1,0:T(8,128)(2,1)S(1)} %add_convert_fusion.1), channel_id=1, source_target_pairs={{0,16},{1,17},{2,18},{3,19},{4,20},{5,21},{6,22},{7,23},{8,24},{9,... | collective-permute-start | bytes 688136 | tf_op jit(solution)/shard_map/ppermute | solution.py:62
  66.7 2.6 %collective-permute-done.18.refs_11_ = bf16[256,256]{1,0:T(8,128)(2,1)S(1)} collective-permute-done((bf16[256,256]{1,0:T(8,128)(2,1)S(1)}, bf16[256,256]{1,0:T(8,128)(2,1)S(1)}, u32[]{:S(2)}, u32[]{:S(2)}) %collective-permute-start.18) | collective-permute-done | bytes 131104 | tf_op jit(solution)/shard_map/ppermute | solution.py:62
  69.3 1.6 %collective-permute-start.19 = (bf16[128,896]{1,0:T(8,128)(2,1)S(1)}, bf16[128,896]{1,0:T(8,128)(2,1)S(1)}, u32[]{:S(2)}, u32[]{:S(2)}) collective-permute-start(bf16[128,896]{1,0:T(8,128)(2,1)S(1)} %get-tuple-element.66), channel_id=1, source_target_pairs={{0,1},{1,0},{2,3},{3,2},{4,5},{5,4},{6,7},{7,6},{8,9},{9,8},{10,11... | collective-permute-start | bytes 688136 | tf_op jit(solution)/shard_map/ppermute | solution.py:62
  70.8 1.4 %collective-permute-start.25 = (bf16[128,896]{1,0:T(8,128)(2,1)S(1)}, bf16[128,896]{1,0:T(8,128)(2,1)S(1)}, u32[]{:S(2)}, u32[]{:S(2)}) collective-permute-start(bf16[128,896]{1,0:T(8,128)(2,1)S(1)} %get-tuple-element.76), channel_id=1, source_target_pairs={{0,2},{1,3},{2,0},{3,1},{4,6},{5,7},{6,4},{7,5},{8,10},{9,11},{10,... | collective-permute-start | bytes 688136 | tf_op jit(solution)/shard_map/ppermute | solution.py:62
  72.3 1.2 %collective-permute-start.24 = (bf16[128,256]{1,0:T(8,128)(2,1)S(1)}, bf16[128,256]{1,0:T(8,128)(2,1)S(1)}, u32[]{:S(2)}, u32[]{:S(2)}) collective-permute-start(bf16[128,256]{1,0:T(8,128)(2,1)S(1)} %add_convert_fusion.3), channel_id=1, source_target_pairs={{0,1},{1,0},{2,3},{3,2},{4,5},{5,4},{6,7},{7,6},{8,9},{9,8},{10,11... | collective-permute-start | bytes 196616 | tf_op jit(solution)/shard_map/ppermute | solution.py:62
  73.7 4.2 %collective-permute-done.21.refs_3_ = bf16[128,896]{1,0:T(8,128)(2,1)S(1)} collective-permute-done((bf16[128,896]{1,0:T(8,128)(2,1)S(1)}, bf16[128,896]{1,0:T(8,128)(2,1)S(1)}, u32[]{:S(2)}, u32[]{:S(2)}) %collective-permute-start.21) | collective-permute-done | bytes 229408 | tf_op jit(solution)/shard_map/ppermute | solution.py:62
  78.8 3.3 %collective-permute-done.27.refs_10_ = bf16[128,256]{1,0:T(8,128)(2,1)S(1)} collective-permute-done((bf16[128,256]{1,0:T(8,128)(2,1)S(1)}, bf16[128,256]{1,0:T(8,128)(2,1)S(1)}, u32[]{:S(2)}, u32[]{:S(2)}) %collective-permute-start.27) | collective-permute-done | bytes 65568 | tf_op jit(solution)/shard_map/ppermute | solution.py:62
  82.7 1.6 %final.1 = (f32[128,1152]{1,0:T(8,128)}, f32[128,1152]{1,0:T(8,128)}) custom-call(bf16[128,1152]{1,0:T(8,128)(2,1)S(1)} %copy-done, f32[128,1152]{1,0:T(8,128)S(1)} %get-tuple-element.60.refs_1_, bf16[128,896]{1,0:T(8,128)(2,1)S(1)} %collective-permute-done.19.refs_2_, bf16[128,896]{1,0:T(8,128)(2,1)S(1)} %collective-permute-done.21.refs_3_, ...), custom_call_target="tpu_custom_call" | custom-call | flops 2949120 | bytes 3538944 | tf_op jit(solution)/shard_map/final/pallas_call | solution.py:344
  (46 shorter events, 3.8 us)
Async XLA Ops:
  3.8 22.0 %collective-permute-start = (bf16[128,1536]{1,0:T(8,128)(2,1)}, bf16[128,1536]{1,0:T(8,128)(2,1)S(1)}, u32[]{:S(2)}, u32[]{:S(2)}) collective-permute-start(bf16[128,1536]{1,0:T(8,128)(2,1)} %get-tuple-element.42.refs_0_), channel_id=1, source_target_pairs={{0,16},{1,17},{2,18},{3,19},{4,20},{5,21},{6,22},{7,23},{8,24},{9,... | collective-permute-start | bytes 1179656 | tf_op jit(solution)/shard_map/ppermute | solution.py:62
  7.9 18.0 %collective-permute-start.1 = (bf16[128,1536]{1,0:T(8,128)(2,1)}, bf16[128,1536]{1,0:T(8,128)(2,1)S(1)}, u32[]{:S(2)}, u32[]{:S(2)}) collective-permute-start(bf16[128,1536]{1,0:T(8,128)(2,1)} %get-tuple-element.43.refs_4_), channel_id=1, source_target_pairs={{0,8},{1,9},{2,10},{3,11},{4,12},{5,13},{6,14},{7,15},{8,0},{9,1},... | collective-permute-start | bytes 1179656 | tf_op jit(solution)/shard_map/ppermute | solution.py:62
  9.5 20.3 %collective-permute-start.6 = (bf16[128,2688]{1,0:T(8,128)(2,1)}, bf16[128,2688]{1,0:T(8,128)(2,1)S(1)}, u32[]{:S(2)}, u32[]{:S(2)}) collective-permute-start(bf16[128,2688]{1,0:T(8,128)(2,1)} %get-tuple-element.48), channel_id=1, source_target_pairs={{0,4},{1,5},{2,6},{3,7},{4,0},{5,1},{6,2},{7,3},{8,12},{9,13},{10,... | collective-permute-start | bytes 2064392 | tf_op jit(solution)/shard_map/ppermute | solution.py:62
  9.5 20.3 %collective-permute-start.5 = (bf16[128,2688]{1,0:T(8,128)(2,1)}, bf16[128,2688]{1,0:T(8,128)(2,1)S(1)}, u32[]{:S(2)}, u32[]{:S(2)}) collective-permute-start(bf16[128,2688]{1,0:T(8,128)(2,1)} %get-tuple-element.48), channel_id=1, source_target_pairs={{0,2},{1,3},{2,0},{3,1},{4,6},{5,7},{6,4},{7,5},{8,10},{9,11},{10,... | collective-permute-start | bytes 2064392 | tf_op jit(solution)/shard_map/ppermute | solution.py:62
  11.0 18.8 %collective-permute-start.3 = (bf16[128,2688]{1,0:T(8,128)(2,1)}, bf16[128,2688]{1,0:T(8,128)(2,1)S(1)}, u32[]{:S(2)}, u32[]{:S(2)}) collective-permute-start(bf16[128,2688]{1,0:T(8,128)(2,1)} %get-tuple-element.45), channel_id=1, source_target_pairs={{0,1},{1,0},{2,3},{3,2},{4,5},{5,4},{6,7},{7,6},{8,9},{9,8},{10,11... | collective-permute-start | bytes 2064392 | tf_op jit(solution)/shard_map/ppermute | solution.py:62
  25.9 15.5 %collective-permute-start.2 = (bf16[128,1152]{1,0:T(8,128)(2,1)}, bf16[128,1152]{1,0:T(8,128)(2,1)S(1)}, u32[]{:S(2)}, u32[]{:S(2)}) collective-permute-start(bf16[128,1152]{1,0:T(8,128)(2,1)} %get-tuple-element.44.refs_0_), channel_id=1, source_target_pairs={{0,16},{1,17},{2,18},{3,19},{4,20},{5,21},{6,22},{7,23},{8,24},{9,... | collective-permute-start | bytes 884744 | tf_op jit(solution)/shard_map/ppermute | solution.py:62
  27.3 14.2 %collective-permute-start.4 = (bf16[128,1152]{1,0:T(8,128)(2,1)}, bf16[128,1152]{1,0:T(8,128)(2,1)S(1)}, u32[]{:S(2)}, u32[]{:S(2)}) collective-permute-start(bf16[128,1152]{1,0:T(8,128)(2,1)} %get-tuple-element.47.refs_4_), channel_id=1, source_target_pairs={{0,8},{1,9},{2,10},{3,11},{4,12},{5,13},{6,14},{7,15},{8,0},{9,1},... | collective-permute-start | bytes 884744 | tf_op jit(solution)/shard_map/ppermute | solution.py:62
  29.8 11.7 %collective-permute-start.7 = (bf16[128,1536]{1,0:T(8,128)(2,1)S(1)}, bf16[128,1536]{1,0:T(8,128)(2,1)S(1)}, u32[]{:S(2)}, u32[]{:S(2)}) collective-permute-start(bf16[128,1536]{1,0:T(8,128)(2,1)S(1)} %collective-permute-done.refs_1_), channel_id=1, source_target_pairs={{0,1},{1,0},{2,3},{3,2},{4,5},{5,4},{6,7},{7,6},{8,9},{9,8},{10,11... | collective-permute-start | bytes 1179656 | tf_op jit(solution)/shard_map/ppermute | solution.py:62
  31.3 10.2 %collective-permute-start.8 = (bf16[128,1536]{1,0:T(8,128)(2,1)S(1)}, bf16[128,1536]{1,0:T(8,128)(2,1)S(1)}, u32[]{:S(2)}, u32[]{:S(2)}) collective-permute-start(bf16[128,1536]{1,0:T(8,128)(2,1)S(1)} %collective-permute-done.1.refs_5_), channel_id=1, source_target_pairs={{0,2},{1,3},{2,0},{3,1},{4,6},{5,7},{6,4},{7,5},{8,10},{9,11},{10,... | collective-permute-start | bytes 1179656 | tf_op jit(solution)/shard_map/ppermute | solution.py:62
  32.8 8.7 %collective-permute-start.9 = (bf16[128,2688]{1,0:T(8,128)(2,1)S(1)}, bf16[128,2688]{1,0:T(8,128)(2,1)S(1)}, u32[]{:S(2)}, u32[]{:S(2)}) collective-permute-start(bf16[128,2688]{1,0:T(8,128)(2,1)S(1)} %collective-permute-done.5.refs_6_), channel_id=1, source_target_pairs={{0,4},{1,5},{2,6},{3,7},{4,0},{5,1},{6,2},{7,3},{8,12},{9,13},{10,... | collective-permute-start | bytes 2064392 | tf_op jit(solution)/shard_map/ppermute | solution.py:62
  41.5 3.4 %collective-permute-start.13 = (bf16[128,1536]{1,0:T(8,128)(2,1)S(1)}, bf16[128,1536]{1,0:T(8,128)(2,1)S(1)}, u32[]{:S(2)}, u32[]{:S(2)}) collective-permute-start(bf16[128,1536]{1,0:T(8,128)(2,1)S(1)} %collective-permute-done.1.refs_5_), channel_id=1, source_target_pairs={{0,4},{1,5},{2,6},{3,7},{4,0},{5,1},{6,2},{7,3},{8,12},{9,13},{10,... | collective-permute-start | bytes 1179656 | tf_op jit(solution)/shard_map/ppermute | solution.py:62
  41.6 3.3 %collective-permute-start.14 = (bf16[128,1536]{1,0:T(8,128)(2,1)S(1)}, bf16[128,1536]{1,0:T(8,128)(2,1)S(1)}, u32[]{:S(2)}, u32[]{:S(2)}) collective-permute-start(bf16[128,1536]{1,0:T(8,128)(2,1)S(1)} %collective-permute-done.8.refs_7_), channel_id=1, source_target_pairs={{0,4},{1,5},{2,6},{3,7},{4,0},{5,1},{6,2},{7,3},{8,12},{9,13},{10,... | collective-permute-start | bytes 1179656 | tf_op jit(solution)/shard_map/ppermute | solution.py:62
  42.1 7.6 %collective-permute-start.12 = (bf16[128,1152]{1,0:T(8,128)(2,1)S(1)}, bf16[128,1152]{1,0:T(8,128)(2,1)S(1)}, u32[]{:S(2)}, u32[]{:S(2)}) collective-permute-start(bf16[128,1152]{1,0:T(8,128)(2,1)S(1)} %collective-permute-done.4.refs_5_), channel_id=1, source_target_pairs={{0,4},{1,5},{2,6},{3,7},{4,0},{5,1},{6,2},{7,3},{8,12},{9,13},{10,... | collective-permute-start | bytes 884744 | tf_op jit(solution)/shard_map/ppermute | solution.py:62
  42.2 9.4 %collective-permute-start.11 = (bf16[128,1152]{1,0:T(8,128)(2,1)S(1)}, bf16[128,1152]{1,0:T(8,128)(2,1)S(1)}, u32[]{:S(2)}, u32[]{:S(2)}) collective-permute-start(bf16[128,1152]{1,0:T(8,128)(2,1)S(1)} %collective-permute-done.4.refs_5_), channel_id=1, source_target_pairs={{0,2},{1,3},{2,0},{3,1},{4,6},{5,7},{6,4},{7,5},{8,10},{9,11},{10,... | collective-permute-start | bytes 884744 | tf_op jit(solution)/shard_map/ppermute | solution.py:62
  43.6 9.1 %collective-permute-start.10 = (bf16[128,1152]{1,0:T(8,128)(2,1)S(1)}, bf16[128,1152]{1,0:T(8,128)(2,1)S(1)}, u32[]{:S(2)}, u32[]{:S(2)}) collective-permute-start(bf16[128,1152]{1,0:T(8,128)(2,1)S(1)} %collective-permute-done.2.refs_1_), channel_id=1, source_target_pairs={{0,1},{1,0},{2,3},{3,2},{4,5},{5,4},{6,7},{7,6},{8,9},{9,8},{10,11... | collective-permute-start | bytes 884744 | tf_op jit(solution)/shard_map/ppermute | solution.py:62
  46.9 6.2 %copy-start.4 = (bf16[128,1152]{1,0:T(8,128)(2,1)S(1)}, bf16[128,1152]{1,0:T(8,128)(2,1)}, u32[]{:S(2)}) copy-start(bf16[128,1152]{1,0:T(8,128)(2,1)} %get-tuple-element.44.refs_0_) | copy-start | bytes 884740
  46.9 6.2 %copy-start.5 = (bf16[128,1152]{1,0:T(8,128)(2,1)S(1)}, bf16[128,1152]{1,0:T(8,128)(2,1)}, u32[]{:S(2)}) copy-start(bf16[128,1152]{1,0:T(8,128)(2,1)} %get-tuple-element.47.refs_4_) | copy-start | bytes 884740
  51.5 1.6 %collective-permute-start.15 = (bf16[128,1152]{1,0:T(8,128)(2,1)S(1)}, bf16[128,1152]{1,0:T(8,128)(2,1)S(1)}, u32[]{:S(2)}, u32[]{:S(2)}) collective-permute-start(bf16[128,1152]{1,0:T(8,128)(2,1)S(1)} %collective-permute-done.11.refs_7_), channel_id=1, source_target_pairs={{0,4},{1,5},{2,6},{3,7},{4,0},{5,1},{6,2},{7,3},{8,12},{9,13},{10,... | collective-permute-start | bytes 884744 | tf_op jit(solution)/shard_map/ppermute | solution.py:62
  56.3 5.6 %collective-permute-start.16 = (bf16[256,1152]{1,0:T(8,128)(2,1)S(1)}, bf16[256,1152]{1,0:T(8,128)(2,1)S(1)}, u32[]{:S(2)}, u32[]{:S(2)}) collective-permute-start(bf16[256,1152]{1,0:T(8,128)(2,1)S(1)} %get-tuple-element.63), channel_id=1, source_target_pairs={{0,4},{1,5},{2,6},{3,7},{4,0},{5,1},{6,2},{7,3},{8,12},{9,13},{10,... | collective-permute-start | bytes 1769480 | tf_op jit(solution)/shard_map/ppermute | solution.py:62
  56.5 5.5 %collective-permute-start.17 = (bf16[256,1152]{1,0:T(8,128)(2,1)S(1)}, bf16[256,1152]{1,0:T(8,128)(2,1)S(1)}, u32[]{:S(2)}, u32[]{:S(2)}) collective-permute-start(bf16[256,1152]{1,0:T(8,128)(2,1)S(1)} %get-tuple-element.64), channel_id=1, source_target_pairs={{0,4},{1,5},{2,6},{3,7},{4,0},{5,1},{6,2},{7,3},{8,12},{9,13},{10,... | collective-permute-start | bytes 1769480 | tf_op jit(solution)/shard_map/ppermute | solution.py:62
  56.9 8.6 %collective-permute-start.20 = (bf16[128,896]{1,0:T(8,128)(2,1)S(1)}, bf16[128,896]{1,0:T(8,128)(2,1)S(1)}, u32[]{:S(2)}, u32[]{:S(2)}) collective-permute-start(bf16[128,896]{1,0:T(8,128)(2,1)S(1)} %get-tuple-element.71), channel_id=1, source_target_pairs={{0,1},{1,0},{2,3},{3,2},{4,5},{5,4},{6,7},{7,6},{8,9},{9,8},{10,11... | collective-permute-start | bytes 688136 | tf_op jit(solution)/shard_map/ppermute | solution.py:62
  58.1 14.2 %collective-permute-start.23 = (bf16[256,256]{1,0:T(8,128)(2,1)S(1)}, bf16[256,256]{1,0:T(8,128)(2,1)S(1)}, u32[]{:S(2)}, u32[]{:S(2)}) collective-permute-start(bf16[256,256]{1,0:T(8,128)(2,1)S(1)} %get-tuple-element.74), channel_id=1, source_target_pairs={{0,16},{1,17},{2,18},{3,19},{4,20},{5,21},{6,22},{7,23},{8,24},{9,... | collective-permute-start | bytes 393224 | tf_op jit(solution)/shard_map/ppermute | solution.py:62
  62.0 20.7 %copy-start = (bf16[128,1152]{1,0:T(8,128)(2,1)S(1)}, bf16[128,1152]{1,0:T(8,128)(2,1)}, u32[]{:S(2)}) copy-start(bf16[128,1152]{1,0:T(8,128)(2,1)} %refs_0_.3) | copy-start | bytes 884740
  62.0 20.7 %copy-start.1 = (bf16[128,1152]{1,0:T(8,128)(2,1)S(1)}, bf16[128,1152]{1,0:T(8,128)(2,1)}, u32[]{:S(2)}) copy-start(bf16[128,1152]{1,0:T(8,128)(2,1)} %refs_6_.1) | copy-start | bytes 884740
  62.2 7.1 %collective-permute-start.18 = (bf16[256,256]{1,0:T(8,128)(2,1)S(1)}, bf16[256,256]{1,0:T(8,128)(2,1)S(1)}, u32[]{:S(2)}, u32[]{:S(2)}) collective-permute-start(bf16[256,256]{1,0:T(8,128)(2,1)S(1)} %get-tuple-element.65), channel_id=1, source_target_pairs={{0,8},{1,9},{2,10},{3,11},{4,12},{5,13},{6,14},{7,15},{8,0},{9,1},... | collective-permute-start | bytes 393224 | tf_op jit(solution)/shard_map/ppermute | solution.py:62
  63.9 8.3 %collective-permute-start.22 = (bf16[128,896]{1,0:T(8,128)(2,1)S(1)}, bf16[128,896]{1,0:T(8,128)(2,1)S(1)}, u32[]{:S(2)}, u32[]{:S(2)}) collective-permute-start(bf16[128,896]{1,0:T(8,128)(2,1)S(1)} %get-tuple-element.69), channel_id=1, source_target_pairs={{0,2},{1,3},{2,0},{3,1},{4,6},{5,7},{6,4},{7,5},{8,10},{9,11},{10,... | collective-permute-start | bytes 688136 | tf_op jit(solution)/shard_map/ppermute | solution.py:62
  65.5 12.3 %collective-permute-start.21 = (bf16[128,896]{1,0:T(8,128)(2,1)S(1)}, bf16[128,896]{1,0:T(8,128)(2,1)S(1)}, u32[]{:S(2)}, u32[]{:S(2)}) collective-permute-start(bf16[128,896]{1,0:T(8,128)(2,1)S(1)} %add_convert_fusion.1), channel_id=1, source_target_pairs={{0,16},{1,17},{2,18},{3,19},{4,20},{5,21},{6,22},{7,23},{8,24},{9,... | collective-permute-start | bytes 688136 | tf_op jit(solution)/shard_map/ppermute | solution.py:62
  69.3 12.9 %collective-permute-start.19 = (bf16[128,896]{1,0:T(8,128)(2,1)S(1)}, bf16[128,896]{1,0:T(8,128)(2,1)S(1)}, u32[]{:S(2)}, u32[]{:S(2)}) collective-permute-start(bf16[128,896]{1,0:T(8,128)(2,1)S(1)} %get-tuple-element.66), channel_id=1, source_target_pairs={{0,1},{1,0},{2,3},{3,2},{4,5},{5,4},{6,7},{7,6},{8,9},{9,8},{10,11... | collective-permute-start | bytes 688136 | tf_op jit(solution)/shard_map/ppermute | solution.py:62
  70.8 11.3 %collective-permute-start.25 = (bf16[128,896]{1,0:T(8,128)(2,1)S(1)}, bf16[128,896]{1,0:T(8,128)(2,1)S(1)}, u32[]{:S(2)}, u32[]{:S(2)}) collective-permute-start(bf16[128,896]{1,0:T(8,128)(2,1)S(1)} %get-tuple-element.76), channel_id=1, source_target_pairs={{0,2},{1,3},{2,0},{3,1},{4,6},{5,7},{6,4},{7,5},{8,10},{9,11},{10,... | collective-permute-start | bytes 688136 | tf_op jit(solution)/shard_map/ppermute | solution.py:62
  72.3 6.5 %collective-permute-start.24 = (bf16[128,256]{1,0:T(8,128)(2,1)S(1)}, bf16[128,256]{1,0:T(8,128)(2,1)S(1)}, u32[]{:S(2)}, u32[]{:S(2)}) collective-permute-start(bf16[128,256]{1,0:T(8,128)(2,1)S(1)} %add_convert_fusion.3), channel_id=1, source_target_pairs={{0,1},{1,0},{2,3},{3,2},{4,5},{5,4},{6,7},{7,6},{8,9},{9,8},{10,11... | collective-permute-start | bytes 196616 | tf_op jit(solution)/shard_map/ppermute | solution.py:62
  73.6 9.1 %collective-permute-start.26 = (bf16[128,896]{1,0:T(8,128)(2,1)S(1)}, bf16[128,896]{1,0:T(8,128)(2,1)S(1)}, u32[]{:S(2)}, u32[]{:S(2)}) collective-permute-start(bf16[128,896]{1,0:T(8,128)(2,1)S(1)} %add_convert_fusion), channel_id=1, source_target_pairs={{0,8},{1,9},{2,10},{3,11},{4,12},{5,13},{6,14},{7,15},{8,0},{9,1},... | collective-permute-start | bytes 688136 | tf_op jit(solution)/shard_map/ppermute | solution.py:62
  77.9 4.3 %collective-permute-start.27 = (bf16[128,256]{1,0:T(8,128)(2,1)S(1)}, bf16[128,256]{1,0:T(8,128)(2,1)S(1)}, u32[]{:S(2)}, u32[]{:S(2)}) collective-permute-start(bf16[128,256]{1,0:T(8,128)(2,1)S(1)} %add_convert_fusion.2), channel_id=1, source_target_pairs={{0,2},{1,3},{2,0},{3,1},{4,6},{5,7},{6,4},{7,5},{8,10},{9,11},{10,... | collective-permute-start | bytes 196616 | tf_op jit(solution)/shard_map/ppermute | solution.py:62
  (2 other events, 2.0 us)

commit v13 on v11

--- a/solution.py
+++ b/solution.py
@@ -433,7 +433,7 @@
     s_txts = texts(s_txt, s_near, b_row, s_near_row, b_core, s_near_core, b_row_core, s_both_core)
 
     own_txt = row * near
-    half = width // 128 * 2 // 3 * 128
+    half = width // 128 * 7 // 9 * 128
     skip = teacher_img.shape[1]
     packed, img_hops, img_kept, img_longs, txt_out = pair_and_sent(
         s_imgs, s_txts, far, near, own_txt, skip, half, targets
@@ -447,7 +447,7 @@
     txt_in = [plan.send(v, "core", -1 - k // row) for k, v in enumerate(txt_out)]
     (txt_own,) = kept_grads(pair, img_pack, [(own_txt * rows, width)], True)
     txt_hops, txt_kept, txt_stay, txt_longs = text_sums(txt_own, txt_in, rows, row, near, half)
-    img_stay = kept_grads(pair, txt_pack, [(rows, width)] + [(rows, half)] * (far - 1), False)
+    img_stay = kept_grads(after(pair, *txt_hops), txt_pack, [(rows, width)] + [(rows, half)] * (far - 1), False)
 
     row_in = {}
     for b in range(1, row):
@@ -467,15 +467,15 @@
         plan.send(total(txt_stay[a], [row_in[b, a] for b in range(1, row)]), "near", -a) for a in range(1, near)
     ]
     img_side = [
-        plan.send(total(after(img_kept[b - 1], *row_in.values()), [v[b * rows : (b + 1) * rows] for v in long_in]), "col", -b)
+        plan.send(total(after(img_kept[b - 1], *[*txt_long_in, *row_in.values()]), [v[b * rows : (b + 1) * rows] for v in long_in]), "col", -b)
         for b in range(1, col)
     ]
     txt_side = [
-        plan.send(total(txt_kept[b - 1], [v[b * rows : (b + 1) * rows] for v in txt_long_in]), "row", -b)
+        plan.send(total(after(txt_kept[b - 1], *row_in.values()), [v[b * rows : (b + 1) * rows] for v in txt_long_in]), "row", -b)
         for b in range(1, row)
     ]
-    col_ahead = list(row_in.values())
-    row_ahead = list(img_in.values())
+    col_ahead = list(txt_long_in)
+    row_ahead = list(txt_long_in)
     img_ends = [plan.send(after(img_hops[(b - 1) * far], *col_ahead), "col", -b) for b in range(1, col)]
     txt_ends = [plan.send(after(txt_hops[(b - 1) * near], *row_ahead), "row", -b) for b in range(1, row)]
     image_side = (student_img, img_stay[0], img_ends + img_last, img_side + long_in)

time: 84.7 us -> 84.7 us (level)
  transfers between devices with their start and end apart: 28 -> 28, of which waited for: 12 -> 11; matrix products, arithmetic and copies ran while one was open for 0% -> 0% of each run, Pallas kernels for 6% -> 6%
where the time goes in v13:
time: 84.7 us; the launch traced here: 84.5 us
  waiting for transfers between devices  37.7 us (45%)
  starting transfers between devices  31.3 us (37%)
  Pallas kernels  12.6 us (15%)
  local copies, waits for them, and re-layouts  2 us (2%)
    ppermute x28, waiting for transfers between devices, send(): return lax.ppermute(x, AXES, pairs)  37.7 us
    ppermute x28, starting transfers between devices, send(): return lax.ppermute(x, AXES, pairs)  31.3 us
    pallas_call x1, Pallas kernels, pair_and_sent(): pl.pallas_call(functools.partial(pair_kernel, images, texts, far, skip, h...  3.19 us
    pallas_call x1, Pallas kernels, unit_rows(): pl.pallas_call(functools.partial(unit_kernel, len(arrays)), out_shape=[ja...  3.15 us
    pallas_call x1, Pallas kernels, teacher_targets(): pl.pallas_call(functools.partial(teacher_kernel, images, texts), out_shap...  2.77 us
    unnamed x12, local copies, waits for them, and re-layouts  2 us
    pallas_call x2, Pallas kernels, kept_grads(): pl.pallas_call(functools.partial(kept_kernel, of_texts), out_shape=[jax.S...  1.71 us
  transfers between devices with their start and end apart: 28, of which 11 were waited for; matrix products, arithmetic and copies ran while one was open for 0% of the time, Pallas kernels for 6%

profile of v13, /device:TPU:0, one launch (start us, length us, event | category | flops | bytes accessed | tf_op | source)
XLA Modules:
  0.0 84.5 jit_solution(10170509337258442066)
XLA Ops:
  0.6 3.1 %unit_rows.1 = (bf16[128,1536]{1,0:T(8,128)(2,1)}, bf16[128,1536]{1,0:T(8,128)(2,1)}, bf16[128,1152]{1,0:T(8,128)(2,1)}, bf16[128,1152]{1,0:T(8,128)(2,1)}, bf16...) custom-call(bf16[128,1536]{1,0:T(8,128)(2,1)} %refs_0_.2, bf16[128,1536]{1,0:T(8,128)(2,1)} %refs_1_.1, ...), custom_call_target="tpu_custom_call" | custom-call | flops 2752512 | bytes 4128768 | tf_op jit(solution)/shard_map/unit_rows/pallas_call | solution.py:107
  3.8 4.1 %collective-permute-start = (bf16[128,1536]{1,0:T(8,128)(2,1)}, bf16[128,1536]{1,0:T(8,128)(2,1)S(1)}, u32[]{:S(2)}, u32[]{:S(2)}) collective-permute-start(bf16[128,1536]{1,0:T(8,128)(2,1)} %get-tuple-element.42.refs_0_), channel_id=1, source_target_pairs={{0,16},{1,17},{2,18},{3,19},{4,20},{5,21},{6,22},{7,23},{8,24},{9,... | collective-permute-start | bytes 1179656 | tf_op jit(solution)/shard_map/ppermute | solution.py:62
  7.9 1.6 %collective-permute-start.1 = (bf16[128,1536]{1,0:T(8,128)(2,1)}, bf16[128,1536]{1,0:T(8,128)(2,1)S(1)}, u32[]{:S(2)}, u32[]{:S(2)}) collective-permute-start(bf16[128,1536]{1,0:T(8,128)(2,1)} %get-tuple-element.43.refs_4_), channel_id=1, source_target_pairs={{0,8},{1,9},{2,10},{3,11},{4,12},{5,13},{6,14},{7,15},{8,0},{9,1},... | collective-permute-start | bytes 1179656 | tf_op jit(solution)/shard_map/ppermute | solution.py:62
  9.5 1.5 %collective-permute-start.5 = (bf16[128,2688]{1,0:T(8,128)(2,1)}, bf16[128,2688]{1,0:T(8,128)(2,1)S(1)}, u32[]{:S(2)}, u32[]{:S(2)}) collective-permute-start(bf16[128,2688]{1,0:T(8,128)(2,1)} %get-tuple-element.48), channel_id=1, source_target_pairs={{0,2},{1,3},{2,0},{3,1},{4,6},{5,7},{6,4},{7,5},{8,10},{9,11},{10,... | collective-permute-start | bytes 2064392 | tf_op jit(solution)/shard_map/ppermute | solution.py:62
  11.0 1.5 %collective-permute-start.3 = (bf16[128,2688]{1,0:T(8,128)(2,1)}, bf16[128,2688]{1,0:T(8,128)(2,1)S(1)}, u32[]{:S(2)}, u32[]{:S(2)}) collective-permute-start(bf16[128,2688]{1,0:T(8,128)(2,1)} %get-tuple-element.45), channel_id=1, source_target_pairs={{0,1},{1,0},{2,3},{3,2},{4,5},{5,4},{6,7},{7,6},{8,9},{9,8},{10,11... | collective-permute-start | bytes 2064392 | tf_op jit(solution)/shard_map/ppermute | solution.py:62
  12.5 13.3 %collective-permute-done.refs_1_ = bf16[128,1536]{1,0:T(8,128)(2,1)S(1)} collective-permute-done((bf16[128,1536]{1,0:T(8,128)(2,1)}, bf16[128,1536]{1,0:T(8,128)(2,1)S(1)}, u32[]{:S(2)}, u32[]{:S(2)}) %collective-permute-start) | collective-permute-done | bytes 393248 | tf_op jit(solution)/shard_map/ppermute | solution.py:62
  25.9 1.4 %collective-permute-start.2 = (bf16[128,1152]{1,0:T(8,128)(2,1)}, bf16[128,1152]{1,0:T(8,128)(2,1)S(1)}, u32[]{:S(2)}, u32[]{:S(2)}) collective-permute-start(bf16[128,1152]{1,0:T(8,128)(2,1)} %get-tuple-element.44.refs_0_), channel_id=1, source_target_pairs={{0,16},{1,17},{2,18},{3,19},{4,20},{5,21},{6,22},{7,23},{8,24},{9,... | collective-permute-start | bytes 884744 | tf_op jit(solution)/shard_map/ppermute | solution.py:62
  27.3 2.4 %collective-permute-start.4 = (bf16[128,1152]{1,0:T(8,128)(2,1)}, bf16[128,1152]{1,0:T(8,128)(2,1)S(1)}, u32[]{:S(2)}, u32[]{:S(2)}) collective-permute-start(bf16[128,1152]{1,0:T(8,128)(2,1)} %get-tuple-element.47.refs_4_), channel_id=1, source_target_pairs={{0,8},{1,9},{2,10},{3,11},{4,12},{5,13},{6,14},{7,15},{8,0},{9,1},... | collective-permute-start | bytes 884744 | tf_op jit(solution)/shard_map/ppermute | solution.py:62
  29.8 1.6 %collective-permute-start.7 = (bf16[128,1536]{1,0:T(8,128)(2,1)S(1)}, bf16[128,1536]{1,0:T(8,128)(2,1)S(1)}, u32[]{:S(2)}, u32[]{:S(2)}) collective-permute-start(bf16[128,1536]{1,0:T(8,128)(2,1)S(1)} %collective-permute-done.refs_1_), channel_id=1, source_target_pairs={{0,1},{1,0},{2,3},{3,2},{4,5},{5,4},{6,7},{7,6},{8,9},{9,8},{10,11... | collective-permute-start | bytes 1179656 | tf_op jit(solution)/shard_map/ppermute | solution.py:62
  31.3 1.5 %collective-permute-start.8 = (bf16[128,1536]{1,0:T(8,128)(2,1)S(1)}, bf16[128,1536]{1,0:T(8,128)(2,1)S(1)}, u32[]{:S(2)}, u32[]{:S(2)}) collective-permute-start(bf16[128,1536]{1,0:T(8,128)(2,1)S(1)} %collective-permute-done.1.refs_5_), channel_id=1, source_target_pairs={{0,2},{1,3},{2,0},{3,1},{4,6},{5,7},{6,4},{7,5},{8,10},{9,11},{10,... | collective-permute-start | bytes 1179656 | tf_op jit(solution)/shard_map/ppermute | solution.py:62
  32.8 8.6 %collective-permute-done.2.refs_1_ = bf16[128,1152]{1,0:T(8,128)(2,1)S(1)} collective-permute-done((bf16[128,1152]{1,0:T(8,128)(2,1)}, bf16[128,1152]{1,0:T(8,128)(2,1)S(1)}, u32[]{:S(2)}, u32[]{:S(2)}) %collective-permute-start.2) | collective-permute-done | bytes 294944 | tf_op jit(solution)/shard_map/ppermute | solution.py:62
  42.2 1.4 %collective-permute-start.11 = (bf16[128,1152]{1,0:T(8,128)(2,1)S(1)}, bf16[128,1152]{1,0:T(8,128)(2,1)S(1)}, u32[]{:S(2)}, u32[]{:S(2)}) collective-permute-start(bf16[128,1152]{1,0:T(8,128)(2,1)S(1)} %collective-permute-done.4.refs_5_), channel_id=1, source_target_pairs={{0,2},{1,3},{2,0},{3,1},{4,6},{5,7},{6,4},{7,5},{8,10},{9,11},{10,... | collective-permute-start | bytes 884744 | tf_op jit(solution)/shard_map/ppermute | solution.py:62
  43.6 1.4 %collective-permute-start.10 = (bf16[128,1152]{1,0:T(8,128)(2,1)S(1)}, bf16[128,1152]{1,0:T(8,128)(2,1)S(1)}, u32[]{:S(2)}, u32[]{:S(2)}) collective-permute-start(bf16[128,1152]{1,0:T(8,128)(2,1)S(1)} %collective-permute-done.2.refs_1_), channel_id=1, source_target_pairs={{0,1},{1,0},{2,3},{3,2},{4,5},{5,4},{6,7},{7,6},{8,9},{9,8},{10,11... | collective-permute-start | bytes 884744 | tf_op jit(solution)/shard_map/ppermute | solution.py:62
  44.9 1.0 %copy-done.2 = bf16[128,1536]{1,0:T(8,128)(2,1)S(1)} copy-done((bf16[128,1536]{1,0:T(8,128)(2,1)S(1)}, bf16[128,1536]{1,0:T(8,128)(2,1)}, u32[]{:S(2)}) %copy-start.2) | copy-done | bytes 393240
  45.9 1.0 %copy-done.3 = bf16[128,1536]{1,0:T(8,128)(2,1)S(1)} copy-done((bf16[128,1536]{1,0:T(8,128)(2,1)S(1)}, bf16[128,1536]{1,0:T(8,128)(2,1)}, u32[]{:S(2)}) %copy-start.3) | copy-done | bytes 393240
  46.9 2.8 %teacher_targets.1.refs_12_ = f32[512,1024]{1,0:T(8,128)S(1)} custom-call(bf16[128,1536]{1,0:T(8,128)(2,1)S(1)} %copy-done.2, bf16[128,1536]{1,0:T(8,128)(2,1)S(1)} %collective-permute-done.refs_1_, bf16[128,2688]{1,0:T(8,128)(2,1)S(1)} %collective-permute-done.3.refs_2_, bf16[128,1536]{1,0:T(8,128)(2,1)S(1)} %collective-permute-done.7.refs_3_, ...), custom_call_target="tpu_custom_call" | custom-call | flops 1610612736 | bytes 6815744 | tf_op jit(solution)/shard_map/teacher_targets/pallas_call | solution.py:154
  49.7 1.8 %collective-permute-done.11.refs_7_ = bf16[128,1152]{1,0:T(8,128)(2,1)S(1)} collective-permute-done((bf16[128,1152]{1,0:T(8,128)(2,1)S(1)}, bf16[128,1152]{1,0:T(8,128)(2,1)S(1)}, u32[]{:S(2)}, u32[]{:S(2)}) %collective-permute-start.11) | collective-permute-done | bytes 294944 | tf_op jit(solution)/shard_map/ppermute | solution.py:62
  51.5 1.2 %collective-permute-done.10.refs_3_ = bf16[128,1152]{1,0:T(8,128)(2,1)S(1)} collective-permute-done((bf16[128,1152]{1,0:T(8,128)(2,1)S(1)}, bf16[128,1152]{1,0:T(8,128)(2,1)S(1)}, u32[]{:S(2)}, u32[]{:S(2)}) %collective-permute-start.10) | collective-permute-done | bytes 294944 | tf_op jit(solution)/shard_map/ppermute | solution.py:62
  53.1 3.2 %pair_and_sent.1 = (bf16[512,1024]{1,0:T(8,128)(2,1)S(1)}, bf16[512,1152]{1,0:T(8,128)(2,1)S(1)}, bf16[1024,1152]{1,0:T(8,128)(2,1)S(1)}, bf16[128,896]{1,0:T(8,...) custom-call(bf16[128,1152]{1,0:T(8,128)(2,1)S(1)} %copy-done.4, ...), custom_call_target="tpu_custom_call" | custom-call | flops 2415919104 | bytes 7733248 | tf_op jit(solution)/shard_map/pair_and_sent/pallas_call | solution.py:229
  56.9 1.2 %collective-permute-start.20 = (bf16[128,896]{1,0:T(8,128)(2,1)S(1)}, bf16[128,896]{1,0:T(8,128)(2,1)S(1)}, u32[]{:S(2)}, u32[]{:S(2)}) collective-permute-start(bf16[128,896]{1,0:T(8,128)(2,1)S(1)} %get-tuple-element.71), channel_id=1, source_target_pairs={{0,1},{1,0},{2,3},{3,2},{4,5},{5,4},{6,7},{7,6},{8,9},{9,8},{10,11... | collective-permute-start | bytes 688136 | tf_op jit(solution)/shard_map/ppermute | solution.py:62
  58.1 2.3 %collective-permute-start.23 = (bf16[256,256]{1,0:T(8,128)(2,1)S(1)}, bf16[256,256]{1,0:T(8,128)(2,1)S(1)}, u32[]{:S(2)}, u32[]{:S(2)}) collective-permute-start(bf16[256,256]{1,0:T(8,128)(2,1)S(1)} %get-tuple-element.74), channel_id=1, source_target_pairs={{0,16},{1,17},{2,18},{3,19},{4,20},{5,21},{6,22},{7,23},{8,24},{9,... | collective-permute-start | bytes 393224 | tf_op jit(solution)/shard_map/ppermute | solution.py:62
  60.4 0.9 %kept_texts.1.own_ref = f32[512,1152]{1,0:T(8,128)S(1)} custom-call(bf16[512,1024]{1,0:T(8,128)(2,1)S(1)} %get-tuple-element.63.pair, bf16[512,1152]{1,0:T(8,128)(2,1)S(1)} %get-tuple-element.58.other), custom_call_target="tpu_custom_call" | custom-call | flops 603979776 | bytes 4587520 | tf_op jit(solution)/shard_map/kept_texts/pallas_call | solution.py:263
  61.5 1.6 %collective-permute-start.22 = (bf16[128,896]{1,0:T(8,128)(2,1)S(1)}, bf16[128,896]{1,0:T(8,128)(2,1)S(1)}, u32[]{:S(2)}, u32[]{:S(2)}) collective-permute-start(bf16[128,896]{1,0:T(8,128)(2,1)S(1)} %get-tuple-element.62), channel_id=1, source_target_pairs={{0,2},{1,3},{2,0},{3,1},{4,6},{5,7},{6,4},{7,5},{8,10},{9,11},{10,... | collective-permute-start | bytes 688136 | tf_op jit(solution)/shard_map/ppermute | solution.py:62
  63.1 1.7 %collective-permute-start.18 = (bf16[256,256]{1,0:T(8,128)(2,1)S(1)}, bf16[256,256]{1,0:T(8,128)(2,1)S(1)}, u32[]{:S(2)}, u32[]{:S(2)}) collective-permute-start(bf16[256,256]{1,0:T(8,128)(2,1)S(1)} %get-tuple-element.67), channel_id=1, source_target_pairs={{0,8},{1,9},{2,10},{3,11},{4,12},{5,13},{6,14},{7,15},{8,0},{9,1},... | collective-permute-start | bytes 393224 | tf_op jit(solution)/shard_map/ppermute | solution.py:62
  64.8 0.8 kept_images.1
  65.7 1.0 %collective-permute-start.21 = (bf16[128,896]{1,0:T(8,128)(2,1)S(1)}, bf16[128,896]{1,0:T(8,128)(2,1)S(1)}, u32[]{:S(2)}, u32[]{:S(2)}) collective-permute-start(bf16[128,896]{1,0:T(8,128)(2,1)S(1)} %add_convert_fusion.1), channel_id=1, source_target_pairs={{0,16},{1,17},{2,18},{3,19},{4,20},{5,21},{6,22},{7,23},{8,24},{9,... | collective-permute-start | bytes 688136 | tf_op jit(solution)/shard_map/ppermute | solution.py:62
  66.7 3.2 %collective-permute-done.18.refs_11_ = bf16[256,256]{1,0:T(8,128)(2,1)S(1)} collective-permute-done((bf16[256,256]{1,0:T(8,128)(2,1)S(1)}, bf16[256,256]{1,0:T(8,128)(2,1)S(1)}, u32[]{:S(2)}, u32[]{:S(2)}) %collective-permute-start.18) | collective-permute-done | bytes 131104 | tf_op jit(solution)/shard_map/ppermute | solution.py:62
  69.8 1.4 %collective-permute-start.19 = (bf16[128,896]{1,0:T(8,128)(2,1)S(1)}, bf16[128,896]{1,0:T(8,128)(2,1)S(1)}, u32[]{:S(2)}, u32[]{:S(2)}) collective-permute-start(bf16[128,896]{1,0:T(8,128)(2,1)S(1)} %get-tuple-element.68), channel_id=1, source_target_pairs={{0,1},{1,0},{2,3},{3,2},{4,5},{5,4},{6,7},{7,6},{8,9},{9,8},{10,11... | collective-permute-start | bytes 688136 | tf_op jit(solution)/shard_map/ppermute | solution.py:62
  71.8 1.2 %collective-permute-start.24 = (bf16[128,256]{1,0:T(8,128)(2,1)S(1)}, bf16[128,256]{1,0:T(8,128)(2,1)S(1)}, u32[]{:S(2)}, u32[]{:S(2)}) collective-permute-start(bf16[128,256]{1,0:T(8,128)(2,1)S(1)} %add_convert_fusion.3), channel_id=1, source_target_pairs={{0,1},{1,0},{2,3},{3,2},{4,5},{5,4},{6,7},{7,6},{8,9},{9,8},{10,11... | collective-permute-start | bytes 196616 | tf_op jit(solution)/shard_map/ppermute | solution.py:62
  73.2 4.9 %collective-permute-done.21.refs_3_ = bf16[128,896]{1,0:T(8,128)(2,1)S(1)} collective-permute-done((bf16[128,896]{1,0:T(8,128)(2,1)S(1)}, bf16[128,896]{1,0:T(8,128)(2,1)S(1)}, u32[]{:S(2)}, u32[]{:S(2)}) %collective-permute-start.21) | collective-permute-done | bytes 229408 | tf_op jit(solution)/shard_map/ppermute | solution.py:62
  78.8 3.5 %collective-permute-done.27.refs_10_ = bf16[128,256]{1,0:T(8,128)(2,1)S(1)} collective-permute-done((bf16[128,256]{1,0:T(8,128)(2,1)S(1)}, bf16[128,256]{1,0:T(8,128)(2,1)S(1)}, u32[]{:S(2)}, u32[]{:S(2)}) %collective-permute-start.27) | collective-permute-done | bytes 65568 | tf_op jit(solution)/shard_map/ppermute | solution.py:62
  82.9 1.6 %final.1 = (f32[128,1152]{1,0:T(8,128)}, f32[128,1152]{1,0:T(8,128)}) custom-call(bf16[128,1152]{1,0:T(8,128)(2,1)S(1)} %copy-done, f32[128,1152]{1,0:T(8,128)S(1)} %get-tuple-element.65.refs_1_, bf16[128,896]{1,0:T(8,128)(2,1)S(1)} %collective-permute-done.19.refs_2_, bf16[128,896]{1,0:T(8,128)(2,1)S(1)} %collective-permute-done.21.refs_3_, ...), custom_call_target="tpu_custom_call" | custom-call | flops 2949120 | bytes 3538944 | tf_op jit(solution)/shard_map/final/pallas_call | solution.py:343
  (47 shorter events, 4.2 us)
Async XLA Ops:
  3.8 22.0 %collective-permute-start = (bf16[128,1536]{1,0:T(8,128)(2,1)}, bf16[128,1536]{1,0:T(8,128)(2,1)S(1)}, u32[]{:S(2)}, u32[]{:S(2)}) collective-permute-start(bf16[128,1536]{1,0:T(8,128)(2,1)} %get-tuple-element.42.refs_0_), channel_id=1, source_target_pairs={{0,16},{1,17},{2,18},{3,19},{4,20},{5,21},{6,22},{7,23},{8,24},{9,... | collective-permute-start | bytes 1179656 | tf_op jit(solution)/shard_map/ppermute | solution.py:62
  7.9 18.0 %collective-permute-start.1 = (bf16[128,1536]{1,0:T(8,128)(2,1)}, bf16[128,1536]{1,0:T(8,128)(2,1)S(1)}, u32[]{:S(2)}, u32[]{:S(2)}) collective-permute-start(bf16[128,1536]{1,0:T(8,128)(2,1)} %get-tuple-element.43.refs_4_), channel_id=1, source_target_pairs={{0,8},{1,9},{2,10},{3,11},{4,12},{5,13},{6,14},{7,15},{8,0},{9,1},... | collective-permute-start | bytes 1179656 | tf_op jit(solution)/shard_map/ppermute | solution.py:62
  9.5 20.3 %collective-permute-start.6 = (bf16[128,2688]{1,0:T(8,128)(2,1)}, bf16[128,2688]{1,0:T(8,128)(2,1)S(1)}, u32[]{:S(2)}, u32[]{:S(2)}) collective-permute-start(bf16[128,2688]{1,0:T(8,128)(2,1)} %get-tuple-element.48), channel_id=1, source_target_pairs={{0,4},{1,5},{2,6},{3,7},{4,0},{5,1},{6,2},{7,3},{8,12},{9,13},{10,... | collective-permute-start | bytes 2064392 | tf_op jit(solution)/shard_map/ppermute | solution.py:62
  9.5 20.3 %collective-permute-start.5 = (bf16[128,2688]{1,0:T(8,128)(2,1)}, bf16[128,2688]{1,0:T(8,128)(2,1)S(1)}, u32[]{:S(2)}, u32[]{:S(2)}) collective-permute-start(bf16[128,2688]{1,0:T(8,128)(2,1)} %get-tuple-element.48), channel_id=1, source_target_pairs={{0,2},{1,3},{2,0},{3,1},{4,6},{5,7},{6,4},{7,5},{8,10},{9,11},{10,... | collective-permute-start | bytes 2064392 | tf_op jit(solution)/shard_map/ppermute | solution.py:62
  11.0 18.8 %collective-permute-start.3 = (bf16[128,2688]{1,0:T(8,128)(2,1)}, bf16[128,2688]{1,0:T(8,128)(2,1)S(1)}, u32[]{:S(2)}, u32[]{:S(2)}) collective-permute-start(bf16[128,2688]{1,0:T(8,128)(2,1)} %get-tuple-element.45), channel_id=1, source_target_pairs={{0,1},{1,0},{2,3},{3,2},{4,5},{5,4},{6,7},{7,6},{8,9},{9,8},{10,11... | collective-permute-start | bytes 2064392 | tf_op jit(solution)/shard_map/ppermute | solution.py:62
  25.9 15.5 %collective-permute-start.2 = (bf16[128,1152]{1,0:T(8,128)(2,1)}, bf16[128,1152]{1,0:T(8,128)(2,1)S(1)}, u32[]{:S(2)}, u32[]{:S(2)}) collective-permute-start(bf16[128,1152]{1,0:T(8,128)(2,1)} %get-tuple-element.44.refs_0_), channel_id=1, source_target_pairs={{0,16},{1,17},{2,18},{3,19},{4,20},{5,21},{6,22},{7,23},{8,24},{9,... | collective-permute-start | bytes 884744 | tf_op jit(solution)/shard_map/ppermute | solution.py:62
  27.3 14.2 %collective-permute-start.4 = (bf16[128,1152]{1,0:T(8,128)(2,1)}, bf16[128,1152]{1,0:T(8,128)(2,1)S(1)}, u32[]{:S(2)}, u32[]{:S(2)}) collective-permute-start(bf16[128,1152]{1,0:T(8,128)(2,1)} %get-tuple-element.47.refs_4_), channel_id=1, source_target_pairs={{0,8},{1,9},{2,10},{3,11},{4,12},{5,13},{6,14},{7,15},{8,0},{9,1},... | collective-permute-start | bytes 884744 | tf_op jit(solution)/shard_map/ppermute | solution.py:62
  29.8 11.7 %collective-permute-start.7 = (bf16[128,1536]{1,0:T(8,128)(2,1)S(1)}, bf16[128,1536]{1,0:T(8,128)(2,1)S(1)}, u32[]{:S(2)}, u32[]{:S(2)}) collective-permute-start(bf16[128,1536]{1,0:T(8,128)(2,1)S(1)} %collective-permute-done.refs_1_), channel_id=1, source_target_pairs={{0,1},{1,0},{2,3},{3,2},{4,5},{5,4},{6,7},{7,6},{8,9},{9,8},{10,11... | collective-permute-start | bytes 1179656 | tf_op jit(solution)/shard_map/ppermute | solution.py:62
  31.3 10.2 %collective-permute-start.8 = (bf16[128,1536]{1,0:T(8,128)(2,1)S(1)}, bf16[128,1536]{1,0:T(8,128)(2,1)S(1)}, u32[]{:S(2)}, u32[]{:S(2)}) collective-permute-start(bf16[128,1536]{1,0:T(8,128)(2,1)S(1)} %collective-permute-done.1.refs_5_), channel_id=1, source_target_pairs={{0,2},{1,3},{2,0},{3,1},{4,6},{5,7},{6,4},{7,5},{8,10},{9,11},{10,... | collective-permute-start | bytes 1179656 | tf_op jit(solution)/shard_map/ppermute | solution.py:62
  32.8 8.7 %collective-permute-start.9 = (bf16[128,2688]{1,0:T(8,128)(2,1)S(1)}, bf16[128,2688]{1,0:T(8,128)(2,1)S(1)}, u32[]{:S(2)}, u32[]{:S(2)}) collective-permute-start(bf16[128,2688]{1,0:T(8,128)(2,1)S(1)} %collective-permute-done.5.refs_6_), channel_id=1, source_target_pairs={{0,4},{1,5},{2,6},{3,7},{4,0},{5,1},{6,2},{7,3},{8,12},{9,13},{10,... | collective-permute-start | bytes 2064392 | tf_op jit(solution)/shard_map/ppermute | solution.py:62
  41.5 3.4 %collective-permute-start.13 = (bf16[128,1536]{1,0:T(8,128)(2,1)S(1)}, bf16[128,1536]{1,0:T(8,128)(2,1)S(1)}, u32[]{:S(2)}, u32[]{:S(2)}) collective-permute-start(bf16[128,1536]{1,0:T(8,128)(2,1)S(1)} %collective-permute-done.1.refs_5_), channel_id=1, source_target_pairs={{0,4},{1,5},{2,6},{3,7},{4,0},{5,1},{6,2},{7,3},{8,12},{9,13},{10,... | collective-permute-start | bytes 1179656 | tf_op jit(solution)/shard_map/ppermute | solution.py:62
  41.6 3.3 %collective-permute-start.14 = (bf16[128,1536]{1,0:T(8,128)(2,1)S(1)}, bf16[128,1536]{1,0:T(8,128)(2,1)S(1)}, u32[]{:S(2)}, u32[]{:S(2)}) collective-permute-start(bf16[128,1536]{1,0:T(8,128)(2,1)S(1)} %collective-permute-done.8.refs_7_), channel_id=1, source_target_pairs={{0,4},{1,5},{2,6},{3,7},{4,0},{5,1},{6,2},{7,3},{8,12},{9,13},{10,... | collective-permute-start | bytes 1179656 | tf_op jit(solution)/shard_map/ppermute | solution.py:62
  42.1 7.6 %collective-permute-start.12 = (bf16[128,1152]{1,0:T(8,128)(2,1)S(1)}, bf16[128,1152]{1,0:T(8,128)(2,1)S(1)}, u32[]{:S(2)}, u32[]{:S(2)}) collective-permute-start(bf16[128,1152]{1,0:T(8,128)(2,1)S(1)} %collective-permute-done.4.refs_5_), channel_id=1, source_target_pairs={{0,4},{1,5},{2,6},{3,7},{4,0},{5,1},{6,2},{7,3},{8,12},{9,13},{10,... | collective-permute-start | bytes 884744 | tf_op jit(solution)/shard_map/ppermute | solution.py:62
  42.2 9.4 %collective-permute-start.11 = (bf16[128,1152]{1,0:T(8,128)(2,1)S(1)}, bf16[128,1152]{1,0:T(8,128)(2,1)S(1)}, u32[]{:S(2)}, u32[]{:S(2)}) collective-permute-start(bf16[128,1152]{1,0:T(8,128)(2,1)S(1)} %collective-permute-done.4.refs_5_), channel_id=1, source_target_pairs={{0,2},{1,3},{2,0},{3,1},{4,6},{5,7},{6,4},{7,5},{8,10},{9,11},{10,... | collective-permute-start | bytes 884744 | tf_op jit(solution)/shard_map/ppermute | solution.py:62
  43.6 9.1 %collective-permute-start.10 = (bf16[128,1152]{1,0:T(8,128)(2,1)S(1)}, bf16[128,1152]{1,0:T(8,128)(2,1)S(1)}, u32[]{:S(2)}, u32[]{:S(2)}) collective-permute-start(bf16[128,1152]{1,0:T(8,128)(2,1)S(1)} %collective-permute-done.2.refs_1_), channel_id=1, source_target_pairs={{0,1},{1,0},{2,3},{3,2},{4,5},{5,4},{6,7},{7,6},{8,9},{9,8},{10,11... | collective-permute-start | bytes 884744 | tf_op jit(solution)/shard_map/ppermute | solution.py:62
  46.9 6.2 %copy-start.4 = (bf16[128,1152]{1,0:T(8,128)(2,1)S(1)}, bf16[128,1152]{1,0:T(8,128)(2,1)}, u32[]{:S(2)}) copy-start(bf16[128,1152]{1,0:T(8,128)(2,1)} %get-tuple-element.44.refs_0_) | copy-start | bytes 884740
  46.9 6.2 %copy-start.5 = (bf16[128,1152]{1,0:T(8,128)(2,1)S(1)}, bf16[128,1152]{1,0:T(8,128)(2,1)}, u32[]{:S(2)}) copy-start(bf16[128,1152]{1,0:T(8,128)(2,1)} %get-tuple-element.47.refs_4_) | copy-start | bytes 884740
  51.5 1.6 %collective-permute-start.15 = (bf16[128,1152]{1,0:T(8,128)(2,1)S(1)}, bf16[128,1152]{1,0:T(8,128)(2,1)S(1)}, u32[]{:S(2)}, u32[]{:S(2)}) collective-permute-start(bf16[128,1152]{1,0:T(8,128)(2,1)S(1)} %collective-permute-done.11.refs_7_), channel_id=1, source_target_pairs={{0,4},{1,5},{2,6},{3,7},{4,0},{5,1},{6,2},{7,3},{8,12},{9,13},{10,... | collective-permute-start | bytes 884744 | tf_op jit(solution)/shard_map/ppermute | solution.py:62
  56.3 5.0 %collective-permute-start.16 = (bf16[256,1152]{1,0:T(8,128)(2,1)S(1)}, bf16[256,1152]{1,0:T(8,128)(2,1)S(1)}, u32[]{:S(2)}, u32[]{:S(2)}) collective-permute-start(bf16[256,1152]{1,0:T(8,128)(2,1)S(1)} %get-tuple-element.59), channel_id=1, source_target_pairs={{0,4},{1,5},{2,6},{3,7},{4,0},{5,1},{6,2},{7,3},{8,12},{9,13},{10,... | collective-permute-start | bytes 1769480 | tf_op jit(solution)/shard_map/ppermute | solution.py:62
  56.5 4.8 %collective-permute-start.17 = (bf16[256,1152]{1,0:T(8,128)(2,1)S(1)}, bf16[256,1152]{1,0:T(8,128)(2,1)S(1)}, u32[]{:S(2)}, u32[]{:S(2)}) collective-permute-start(bf16[256,1152]{1,0:T(8,128)(2,1)S(1)} %get-tuple-element.60), channel_id=1, source_target_pairs={{0,4},{1,5},{2,6},{3,7},{4,0},{5,1},{6,2},{7,3},{8,12},{9,13},{10,... | collective-permute-start | bytes 1769480 | tf_op jit(solution)/shard_map/ppermute | solution.py:62
  56.9 8.7 %collective-permute-start.20 = (bf16[128,896]{1,0:T(8,128)(2,1)S(1)}, bf16[128,896]{1,0:T(8,128)(2,1)S(1)}, u32[]{:S(2)}, u32[]{:S(2)}) collective-permute-start(bf16[128,896]{1,0:T(8,128)(2,1)S(1)} %get-tuple-element.71), channel_id=1, source_target_pairs={{0,1},{1,0},{2,3},{3,2},{4,5},{5,4},{6,7},{7,6},{8,9},{9,8},{10,11... | collective-permute-start | bytes 688136 | tf_op jit(solution)/shard_map/ppermute | solution.py:62
  58.1 13.7 %collective-permute-start.23 = (bf16[256,256]{1,0:T(8,128)(2,1)S(1)}, bf16[256,256]{1,0:T(8,128)(2,1)S(1)}, u32[]{:S(2)}, u32[]{:S(2)}) collective-permute-start(bf16[256,256]{1,0:T(8,128)(2,1)S(1)} %get-tuple-element.74), channel_id=1, source_target_pairs={{0,16},{1,17},{2,18},{3,19},{4,20},{5,21},{6,22},{7,23},{8,24},{9,... | collective-permute-start | bytes 393224 | tf_op jit(solution)/shard_map/ppermute | solution.py:62
  61.5 10.3 %collective-permute-start.22 = (bf16[128,896]{1,0:T(8,128)(2,1)S(1)}, bf16[128,896]{1,0:T(8,128)(2,1)S(1)}, u32[]{:S(2)}, u32[]{:S(2)}) collective-permute-start(bf16[128,896]{1,0:T(8,128)(2,1)S(1)} %get-tuple-element.62), channel_id=1, source_target_pairs={{0,2},{1,3},{2,0},{3,1},{4,6},{5,7},{6,4},{7,5},{8,10},{9,11},{10,... | collective-permute-start | bytes 688136 | tf_op jit(solution)/shard_map/ppermute | solution.py:62
  63.1 6.7 %collective-permute-start.18 = (bf16[256,256]{1,0:T(8,128)(2,1)S(1)}, bf16[256,256]{1,0:T(8,128)(2,1)S(1)}, u32[]{:S(2)}, u32[]{:S(2)}) collective-permute-start(bf16[256,256]{1,0:T(8,128)(2,1)S(1)} %get-tuple-element.67), channel_id=1, source_target_pairs={{0,8},{1,9},{2,10},{3,11},{4,12},{5,13},{6,14},{7,15},{8,0},{9,1},... | collective-permute-start | bytes 393224 | tf_op jit(solution)/shard_map/ppermute | solution.py:62
  64.8 18.1 %copy-start = (bf16[128,1152]{1,0:T(8,128)(2,1)S(1)}, bf16[128,1152]{1,0:T(8,128)(2,1)}, u32[]{:S(2)}) copy-start(bf16[128,1152]{1,0:T(8,128)(2,1)} %refs_0_.3) | copy-start | bytes 884740
  64.8 18.1 %copy-start.1 = (bf16[128,1152]{1,0:T(8,128)(2,1)S(1)}, bf16[128,1152]{1,0:T(8,128)(2,1)}, u32[]{:S(2)}) copy-start(bf16[128,1152]{1,0:T(8,128)(2,1)} %refs_6_.1) | copy-start | bytes 884740
  65.7 12.4 %collective-permute-start.21 = (bf16[128,896]{1,0:T(8,128)(2,1)S(1)}, bf16[128,896]{1,0:T(8,128)(2,1)S(1)}, u32[]{:S(2)}, u32[]{:S(2)}) collective-permute-start(bf16[128,896]{1,0:T(8,128)(2,1)S(1)} %add_convert_fusion.1), channel_id=1, source_target_pairs={{0,16},{1,17},{2,18},{3,19},{4,20},{5,21},{6,22},{7,23},{8,24},{9,... | collective-permute-start | bytes 688136 | tf_op jit(solution)/shard_map/ppermute | solution.py:62
  69.8 12.5 %collective-permute-start.19 = (bf16[128,896]{1,0:T(8,128)(2,1)S(1)}, bf16[128,896]{1,0:T(8,128)(2,1)S(1)}, u32[]{:S(2)}, u32[]{:S(2)}) collective-permute-start(bf16[128,896]{1,0:T(8,128)(2,1)S(1)} %get-tuple-element.68), channel_id=1, source_target_pairs={{0,1},{1,0},{2,3},{3,2},{4,5},{5,4},{6,7},{7,6},{8,9},{9,8},{10,11... | collective-permute-start | bytes 688136 | tf_op jit(solution)/shard_map/ppermute | solution.py:62
  71.3 11.1 %collective-permute-start.25 = (bf16[128,896]{1,0:T(8,128)(2,1)S(1)}, bf16[128,896]{1,0:T(8,128)(2,1)S(1)}, u32[]{:S(2)}, u32[]{:S(2)}) collective-permute-start(bf16[128,896]{1,0:T(8,128)(2,1)S(1)} %get-tuple-element.76), channel_id=1, source_target_pairs={{0,2},{1,3},{2,0},{3,1},{4,6},{5,7},{6,4},{7,5},{8,10},{9,11},{10,... | collective-permute-start | bytes 688136 | tf_op jit(solution)/shard_map/ppermute | solution.py:62
  71.8 7.0 %collective-permute-start.24 = (bf16[128,256]{1,0:T(8,128)(2,1)S(1)}, bf16[128,256]{1,0:T(8,128)(2,1)S(1)}, u32[]{:S(2)}, u32[]{:S(2)}) collective-permute-start(bf16[128,256]{1,0:T(8,128)(2,1)S(1)} %add_convert_fusion.3), channel_id=1, source_target_pairs={{0,1},{1,0},{2,3},{3,2},{4,5},{5,4},{6,7},{7,6},{8,9},{9,8},{10,11... | collective-permute-start | bytes 196616 | tf_op jit(solution)/shard_map/ppermute | solution.py:62
  73.1 9.8 %collective-permute-start.26 = (bf16[128,896]{1,0:T(8,128)(2,1)S(1)}, bf16[128,896]{1,0:T(8,128)(2,1)S(1)}, u32[]{:S(2)}, u32[]{:S(2)}) collective-permute-start(bf16[128,896]{1,0:T(8,128)(2,1)S(1)} %add_convert_fusion), channel_id=1, source_target_pairs={{0,8},{1,9},{2,10},{3,11},{4,12},{5,13},{6,14},{7,15},{8,0},{9,1},... | collective-permute-start | bytes 688136 | tf_op jit(solution)/shard_map/ppermute | solution.py:62
  78.1 4.3 %collective-permute-start.27 = (bf16[128,256]{1,0:T(8,128)(2,1)S(1)}, bf16[128,256]{1,0:T(8,128)(2,1)S(1)}, u32[]{:S(2)}, u32[]{:S(2)}) collective-permute-start(bf16[128,256]{1,0:T(8,128)(2,1)S(1)} %add_convert_fusion.2), channel_id=1, source_target_pairs={{0,2},{1,3},{2,0},{3,1},{4,6},{5,7},{6,4},{7,5},{8,10},{9,11},{10,... | collective-permute-start | bytes 196616 | tf_op jit(solution)/shard_map/ppermute | solution.py:62
  (2 other events, 2.0 us)

commit v14 on v8

--- a/solution.py
+++ b/solution.py
@@ -427,7 +427,7 @@
     s_txts = texts(s_txt, s_near, b_row, s_near_row, b_core, s_near_core, b_row_core, s_both_core)
 
     own_txt = row * near
-    half = width // 128 * 2 // 3 * 128
+    half = width // 128 * 7 // 9 * 128
     skip = teacher_img.shape[1]
     packed, img_hops, img_kept, img_longs, txt_out = pair_and_sent(
         s_imgs, s_txts, far, near, own_txt, skip, half, targets
@@ -467,8 +467,8 @@
         plan.send(total(after(txt_kept[b - 1], *row_in.values()), [v[b * rows : (b + 1) * rows] for v in txt_long_in]), "row", -b)
         for b in range(1, row)
     ]
-    col_ahead = list(row_in.values())
-    row_ahead = list(img_in.values())
+    col_ahead = list(txt_long_in)
+    row_ahead = list(txt_long_in)
     img_ends = [plan.send(after(img_hops[(b - 1) * far], *col_ahead), "col", -b) for b in range(1, col)]
     txt_ends = [plan.send(after(txt_hops[(b - 1) * near], *row_ahead), "row", -b) for b in range(1, row)]
     image_grad = final(student_img, img_stay[0], img_ends + img_last, img_side + long_in, half)

time: 84.5 us -> 84.1 us (level)
  waiting for transfers between devices: 36.7 us -> 35.1 us
  starting transfers between devices: 31.5 us -> 32.7 us
    ppermute x28, waiting for transfers between devices: 36.7 us -> 35.1 us  [send(): return lax.ppermute(x, AXES, pairs)]
    ppermute x28, starting transfers between devices: 31.5 us -> 32.7 us  [send(): return lax.ppermute(x, AXES, pairs)]
  transfers between devices with their start and end apart: 28 -> 28, of which waited for: 12 -> 11; matrix products, arithmetic and copies ran while one was open for 0% -> 0% of each run, Pallas kernels for 7% -> 7%
where the time goes in v14:
time: 84.1 us; the launch traced here: 83.8 us
  waiting for transfers between devices  35.1 us (42%)
  starting transfers between devices  32.7 us (39%)
  Pallas kernels  13.2 us (16%)
  local copies, waits for them, and re-layouts  2.01 us (2%)
    ppermute x28, waiting for transfers between devices, send(): return lax.ppermute(x, AXES, pairs)  35.1 us
    ppermute x28, starting transfers between devices, send(): return lax.ppermute(x, AXES, pairs)  32.7 us
    pallas_call x1, Pallas kernels, pair_and_sent(): pl.pallas_call(functools.partial(pair_kernel, images, texts, far, skip, h...  3.19 us
    pallas_call x1, Pallas kernels, unit_rows(): pl.pallas_call(functools.partial(unit_kernel, len(arrays)), out_shape=[ja...  3.15 us
    pallas_call x1, Pallas kernels, teacher_targets(): pl.pallas_call(functools.partial(teacher_kernel, images, texts), out_shap...  2.77 us
    pallas_call x2, Pallas kernels, final(): pl.pallas_call(functools.partial(final_kernel, half, len(lows)), out_shap...  2.3 us
    unnamed x12, local copies, waits for them, and re-layouts  2.01 us
  transfers between devices with their start and end apart: 28, of which 11 were waited for; matrix products, arithmetic and copies ran while one was open for 0% of the time, Pallas kernels for 7%

profile of v14, /device:TPU:0, one launch (start us, length us, event | category | flops | bytes accessed | tf_op | source)
XLA Modules:
  0.0 83.8 jit_solution(11176655683607259978)
XLA Ops:
  0.6 3.1 %unit_rows.1 = (bf16[128,1536]{1,0:T(8,128)(2,1)}, bf16[128,1536]{1,0:T(8,128)(2,1)}, bf16[128,1152]{1,0:T(8,128)(2,1)}, bf16[128,1152]{1,0:T(8,128)(2,1)}, bf16...) custom-call(bf16[128,1536]{1,0:T(8,128)(2,1)} %refs_0_.1, bf16[128,1536]{1,0:T(8,128)(2,1)} %refs_1_.1, ...), custom_call_target="tpu_custom_call" | custom-call | flops 2752512 | bytes 4128768 | tf_op jit(solution)/shard_map/unit_rows/pallas_call | solution.py:107
  3.8 4.1 %collective-permute-start = (bf16[128,1536]{1,0:T(8,128)(2,1)}, bf16[128,1536]{1,0:T(8,128)(2,1)S(1)}, u32[]{:S(2)}, u32[]{:S(2)}) collective-permute-start(bf16[128,1536]{1,0:T(8,128)(2,1)} %get-tuple-element.42.refs_0_), channel_id=1, source_target_pairs={{0,16},{1,17},{2,18},{3,19},{4,20},{5,21},{6,22},{7,23},{8,24},{9,... | collective-permute-start | bytes 1179656 | tf_op jit(solution)/shard_map/ppermute | solution.py:62
  7.9 1.6 %collective-permute-start.1 = (bf16[128,1536]{1,0:T(8,128)(2,1)}, bf16[128,1536]{1,0:T(8,128)(2,1)S(1)}, u32[]{:S(2)}, u32[]{:S(2)}) collective-permute-start(bf16[128,1536]{1,0:T(8,128)(2,1)} %get-tuple-element.43.refs_4_), channel_id=1, source_target_pairs={{0,8},{1,9},{2,10},{3,11},{4,12},{5,13},{6,14},{7,15},{8,0},{9,1},... | collective-permute-start | bytes 1179656 | tf_op jit(solution)/shard_map/ppermute | solution.py:62
  9.5 1.5 %collective-permute-start.5 = (bf16[128,2688]{1,0:T(8,128)(2,1)}, bf16[128,2688]{1,0:T(8,128)(2,1)S(1)}, u32[]{:S(2)}, u32[]{:S(2)}) collective-permute-start(bf16[128,2688]{1,0:T(8,128)(2,1)} %get-tuple-element.48), channel_id=1, source_target_pairs={{0,2},{1,3},{2,0},{3,1},{4,6},{5,7},{6,4},{7,5},{8,10},{9,11},{10,... | collective-permute-start | bytes 2064392 | tf_op jit(solution)/shard_map/ppermute | solution.py:62
  11.0 1.5 %collective-permute-start.3 = (bf16[128,2688]{1,0:T(8,128)(2,1)}, bf16[128,2688]{1,0:T(8,128)(2,1)S(1)}, u32[]{:S(2)}, u32[]{:S(2)}) collective-permute-start(bf16[128,2688]{1,0:T(8,128)(2,1)} %get-tuple-element.45), channel_id=1, source_target_pairs={{0,1},{1,0},{2,3},{3,2},{4,5},{5,4},{6,7},{7,6},{8,9},{9,8},{10,11... | collective-permute-start | bytes 2064392 | tf_op jit(solution)/shard_map/ppermute | solution.py:62
  12.5 13.3 %collective-permute-done.refs_1_ = bf16[128,1536]{1,0:T(8,128)(2,1)S(1)} collective-permute-done((bf16[128,1536]{1,0:T(8,128)(2,1)}, bf16[128,1536]{1,0:T(8,128)(2,1)S(1)}, u32[]{:S(2)}, u32[]{:S(2)}) %collective-permute-start) | collective-permute-done | bytes 393248 | tf_op jit(solution)/shard_map/ppermute | solution.py:62
  25.9 1.4 %collective-permute-start.2 = (bf16[128,1152]{1,0:T(8,128)(2,1)}, bf16[128,1152]{1,0:T(8,128)(2,1)S(1)}, u32[]{:S(2)}, u32[]{:S(2)}) collective-permute-start(bf16[128,1152]{1,0:T(8,128)(2,1)} %get-tuple-element.44.refs_0_), channel_id=1, source_target_pairs={{0,16},{1,17},{2,18},{3,19},{4,20},{5,21},{6,22},{7,23},{8,24},{9,... | collective-permute-start | bytes 884744 | tf_op jit(solution)/shard_map/ppermute | solution.py:62
  27.3 2.4 %collective-permute-start.4 = (bf16[128,1152]{1,0:T(8,128)(2,1)}, bf16[128,1152]{1,0:T(8,128)(2,1)S(1)}, u32[]{:S(2)}, u32[]{:S(2)}) collective-permute-start(bf16[128,1152]{1,0:T(8,128)(2,1)} %get-tuple-element.47.refs_4_), channel_id=1, source_target_pairs={{0,8},{1,9},{2,10},{3,11},{4,12},{5,13},{6,14},{7,15},{8,0},{9,1},... | collective-permute-start | bytes 884744 | tf_op jit(solution)/shard_map/ppermute | solution.py:62
  29.8 1.6 %collective-permute-start.7 = (bf16[128,1536]{1,0:T(8,128)(2,1)S(1)}, bf16[128,1536]{1,0:T(8,128)(2,1)S(1)}, u32[]{:S(2)}, u32[]{:S(2)}) collective-permute-start(bf16[128,1536]{1,0:T(8,128)(2,1)S(1)} %collective-permute-done.refs_1_), channel_id=1, source_target_pairs={{0,1},{1,0},{2,3},{3,2},{4,5},{5,4},{6,7},{7,6},{8,9},{9,8},{10,11... | collective-permute-start | bytes 1179656 | tf_op jit(solution)/shard_map/ppermute | solution.py:62
  31.3 1.5 %collective-permute-start.8 = (bf16[128,1536]{1,0:T(8,128)(2,1)S(1)}, bf16[128,1536]{1,0:T(8,128)(2,1)S(1)}, u32[]{:S(2)}, u32[]{:S(2)}) collective-permute-start(bf16[128,1536]{1,0:T(8,128)(2,1)S(1)} %collective-permute-done.1.refs_5_), channel_id=1, source_target_pairs={{0,2},{1,3},{2,0},{3,1},{4,6},{5,7},{6,4},{7,5},{8,10},{9,11},{10,... | collective-permute-start | bytes 1179656 | tf_op jit(solution)/shard_map/ppermute | solution.py:62
  32.8 8.6 %collective-permute-done.2.refs_1_ = bf16[128,1152]{1,0:T(8,128)(2,1)S(1)} collective-permute-done((bf16[128,1152]{1,0:T(8,128)(2,1)}, bf16[128,1152]{1,0:T(8,128)(2,1)S(1)}, u32[]{:S(2)}, u32[]{:S(2)}) %collective-permute-start.2) | collective-permute-done | bytes 294944 | tf_op jit(solution)/shard_map/ppermute | solution.py:62
  42.2 1.4 %collective-permute-start.11 = (bf16[128,1152]{1,0:T(8,128)(2,1)S(1)}, bf16[128,1152]{1,0:T(8,128)(2,1)S(1)}, u32[]{:S(2)}, u32[]{:S(2)}) collective-permute-start(bf16[128,1152]{1,0:T(8,128)(2,1)S(1)} %collective-permute-done.4.refs_5_), channel_id=1, source_target_pairs={{0,2},{1,3},{2,0},{3,1},{4,6},{5,7},{6,4},{7,5},{8,10},{9,11},{10,... | collective-permute-start | bytes 884744 | tf_op jit(solution)/shard_map/ppermute | solution.py:62
  43.6 1.4 %collective-permute-start.10 = (bf16[128,1152]{1,0:T(8,128)(2,1)S(1)}, bf16[128,1152]{1,0:T(8,128)(2,1)S(1)}, u32[]{:S(2)}, u32[]{:S(2)}) collective-permute-start(bf16[128,1152]{1,0:T(8,128)(2,1)S(1)} %collective-permute-done.2.refs_1_), channel_id=1, source_target_pairs={{0,1},{1,0},{2,3},{3,2},{4,5},{5,4},{6,7},{7,6},{8,9},{9,8},{10,11... | collective-permute-start | bytes 884744 | tf_op jit(solution)/shard_map/ppermute | solution.py:62
  45.9 1.0 %copy-done.3 = bf16[128,1536]{1,0:T(8,128)(2,1)S(1)} copy-done((bf16[128,1536]{1,0:T(8,128)(2,1)S(1)}, bf16[128,1536]{1,0:T(8,128)(2,1)}, u32[]{:S(2)}) %copy-start.3) | copy-done | bytes 393240
  46.9 2.8 %teacher_targets.1.refs_12_ = f32[512,1024]{1,0:T(8,128)S(1)} custom-call(bf16[128,1536]{1,0:T(8,128)(2,1)S(1)} %copy-done.2, bf16[128,1536]{1,0:T(8,128)(2,1)S(1)} %collective-permute-done.refs_1_, bf16[128,2688]{1,0:T(8,128)(2,1)S(1)} %collective-permute-done.3.refs_2_, bf16[128,1536]{1,0:T(8,128)(2,1)S(1)} %collective-permute-done.7.refs_3_, ...), custom_call_target="tpu_custom_call" | custom-call | flops 1610612736 | bytes 6815744 | tf_op jit(solution)/shard_map/teacher_targets/pallas_call | solution.py:154
  49.7 1.8 %collective-permute-done.11.refs_7_ = bf16[128,1152]{1,0:T(8,128)(2,1)S(1)} collective-permute-done((bf16[128,1152]{1,0:T(8,128)(2,1)S(1)}, bf16[128,1152]{1,0:T(8,128)(2,1)S(1)}, u32[]{:S(2)}, u32[]{:S(2)}) %collective-permute-start.11) | collective-permute-done | bytes 294944 | tf_op jit(solution)/shard_map/ppermute | solution.py:62
  51.5 1.2 %collective-permute-done.10.refs_3_ = bf16[128,1152]{1,0:T(8,128)(2,1)S(1)} collective-permute-done((bf16[128,1152]{1,0:T(8,128)(2,1)S(1)}, bf16[128,1152]{1,0:T(8,128)(2,1)S(1)}, u32[]{:S(2)}, u32[]{:S(2)}) %collective-permute-start.10) | collective-permute-done | bytes 294944 | tf_op jit(solution)/shard_map/ppermute | solution.py:62
  53.1 3.2 %pair_and_sent.1 = (bf16[512,1024]{1,0:T(8,128)(2,1)S(1)}, bf16[512,1152]{1,0:T(8,128)(2,1)S(1)}, bf16[1024,1152]{1,0:T(8,128)(2,1)S(1)}, bf16[128,896]{1,0:T(8,...) custom-call(bf16[128,1152]{1,0:T(8,128)(2,1)S(1)} %copy-done.4, ...), custom_call_target="tpu_custom_call" | custom-call | flops 2415919104 | bytes 7733248 | tf_op jit(solution)/shard_map/pair_and_sent/pallas_call | solution.py:229
  56.9 1.2 %collective-permute-start.20 = (bf16[128,896]{1,0:T(8,128)(2,1)S(1)}, bf16[128,896]{1,0:T(8,128)(2,1)S(1)}, u32[]{:S(2)}, u32[]{:S(2)}) collective-permute-start(bf16[128,896]{1,0:T(8,128)(2,1)S(1)} %get-tuple-element.71), channel_id=1, source_target_pairs={{0,1},{1,0},{2,3},{3,2},{4,5},{5,4},{6,7},{7,6},{8,9},{9,8},{10,11... | collective-permute-start | bytes 688136 | tf_op jit(solution)/shard_map/ppermute | solution.py:62
  58.1 2.3 %collective-permute-start.23 = (bf16[256,256]{1,0:T(8,128)(2,1)S(1)}, bf16[256,256]{1,0:T(8,128)(2,1)S(1)}, u32[]{:S(2)}, u32[]{:S(2)}) collective-permute-start(bf16[256,256]{1,0:T(8,128)(2,1)S(1)} %get-tuple-element.74), channel_id=1, source_target_pairs={{0,16},{1,17},{2,18},{3,19},{4,20},{5,21},{6,22},{7,23},{8,24},{9,... | collective-permute-start | bytes 393224 | tf_op jit(solution)/shard_map/ppermute | solution.py:62
  60.4 1.5 %kept.1 = (f32[128,1152]{1,0:T(8,128)S(1)}, f32[128,896]{1,0:T(8,128)S(1)}, f32[512,1152]{1,0:T(8,128)S(1)}) custom-call(bf16[512,1024]{1,0:T(8,128)(2,1)S(1)} %get-tuple-element.57.pair, bf16[512,1152]{1,0:T(8,128)(2,1)S(1)} %get-tuple-element.58.img, bf16[1024,1152]{1,0:T(8,128)(2,1)S(1)} %get-tuple-element.59.txt), custom_call_target="tpu_custom_call" | custom-call | flops 1207959552 | bytes 6946816 | tf_op jit(solution)/shard_map/kept/pallas_call | solution.py:264
  62.2 1.8 %collective-permute-start.18 = (bf16[256,256]{1,0:T(8,128)(2,1)S(1)}, bf16[256,256]{1,0:T(8,128)(2,1)S(1)}, u32[]{:S(2)}, u32[]{:S(2)}) collective-permute-start(bf16[256,256]{1,0:T(8,128)(2,1)S(1)} %get-tuple-element.65), channel_id=1, source_target_pairs={{0,8},{1,9},{2,10},{3,11},{4,12},{5,13},{6,14},{7,15},{8,0},{9,1},... | collective-permute-start | bytes 393224 | tf_op jit(solution)/shard_map/ppermute | solution.py:62
  63.9 1.5 %collective-permute-start.22 = (bf16[128,896]{1,0:T(8,128)(2,1)S(1)}, bf16[128,896]{1,0:T(8,128)(2,1)S(1)}, u32[]{:S(2)}, u32[]{:S(2)}) collective-permute-start(bf16[128,896]{1,0:T(8,128)(2,1)S(1)} %get-tuple-element.69), channel_id=1, source_target_pairs={{0,2},{1,3},{2,0},{3,1},{4,6},{5,7},{6,4},{7,5},{8,10},{9,11},{10,... | collective-permute-start | bytes 688136 | tf_op jit(solution)/shard_map/ppermute | solution.py:62
  65.5 1.1 %collective-permute-start.21 = (bf16[128,896]{1,0:T(8,128)(2,1)S(1)}, bf16[128,896]{1,0:T(8,128)(2,1)S(1)}, u32[]{:S(2)}, u32[]{:S(2)}) collective-permute-start(bf16[128,896]{1,0:T(8,128)(2,1)S(1)} %add_convert_fusion.1), channel_id=1, source_target_pairs={{0,16},{1,17},{2,18},{3,19},{4,20},{5,21},{6,22},{7,23},{8,24},{9,... | collective-permute-start | bytes 688136 | tf_op jit(solution)/shard_map/ppermute | solution.py:62
  66.7 2.6 %collective-permute-done.18.refs_3_ = bf16[256,256]{1,0:T(8,128)(2,1)S(1)} collective-permute-done((bf16[256,256]{1,0:T(8,128)(2,1)S(1)}, bf16[256,256]{1,0:T(8,128)(2,1)S(1)}, u32[]{:S(2)}, u32[]{:S(2)}) %collective-permute-start.18) | collective-permute-done | bytes 131104 | tf_op jit(solution)/shard_map/ppermute | solution.py:62
  69.3 1.6 %collective-permute-start.19 = (bf16[128,896]{1,0:T(8,128)(2,1)S(1)}, bf16[128,896]{1,0:T(8,128)(2,1)S(1)}, u32[]{:S(2)}, u32[]{:S(2)}) collective-permute-start(bf16[128,896]{1,0:T(8,128)(2,1)S(1)} %get-tuple-element.66), channel_id=1, source_target_pairs={{0,1},{1,0},{2,3},{3,2},{4,5},{5,4},{6,7},{7,6},{8,9},{9,8},{10,11... | collective-permute-start | bytes 688136 | tf_op jit(solution)/shard_map/ppermute | solution.py:62
  70.8 1.4 %collective-permute-start.25 = (bf16[128,896]{1,0:T(8,128)(2,1)S(1)}, bf16[128,896]{1,0:T(8,128)(2,1)S(1)}, u32[]{:S(2)}, u32[]{:S(2)}) collective-permute-start(bf16[128,896]{1,0:T(8,128)(2,1)S(1)} %get-tuple-element.76), channel_id=1, source_target_pairs={{0,2},{1,3},{2,0},{3,1},{4,6},{5,7},{6,4},{7,5},{8,10},{9,11},{10,... | collective-permute-start | bytes 688136 | tf_op jit(solution)/shard_map/ppermute | solution.py:62
  72.3 1.2 %collective-permute-start.24 = (bf16[128,256]{1,0:T(8,128)(2,1)S(1)}, bf16[128,256]{1,0:T(8,128)(2,1)S(1)}, u32[]{:S(2)}, u32[]{:S(2)}) collective-permute-start(bf16[128,256]{1,0:T(8,128)(2,1)S(1)} %add_convert_fusion.3), channel_id=1, source_target_pairs={{0,1},{1,0},{2,3},{3,2},{4,5},{5,4},{6,7},{7,6},{8,9},{9,8},{10,11... | collective-permute-start | bytes 196616 | tf_op jit(solution)/shard_map/ppermute | solution.py:62
  73.7 4.2 %collective-permute-done.21.refs_1_ = bf16[128,896]{1,0:T(8,128)(2,1)S(1)} collective-permute-done((bf16[128,896]{1,0:T(8,128)(2,1)S(1)}, bf16[128,896]{1,0:T(8,128)(2,1)S(1)}, u32[]{:S(2)}, u32[]{:S(2)}) %collective-permute-start.21) | collective-permute-done | bytes 229408 | tf_op jit(solution)/shard_map/ppermute | solution.py:62
  78.8 1.2 %final.2 = f32[128,1152]{1,0:T(8,128)} custom-call(bf16[128,1152]{1,0:T(8,128)(2,1)S(1)} %copy-done, f32[128,1152]{1,0:T(8,128)S(1)} %get-tuple-element.60.own_ref, bf16[128,896]{1,0:T(8,128)(2,1)S(1)} %collective-permute-done.19.refs_0_, bf16[128,896]{1,0:T(8,128)(2,1)S(1)} %collective-permute-done.21.refs_1_, ...), custom_call_target="tpu_custom_call" | custom-call | flops 1474560 | bytes 1769472 | tf_op jit(solution)/shard_map/final/pallas_call | solution.py:341
  80.0 2.2 %collective-permute-done.27.refs_2_ = bf16[128,256]{1,0:T(8,128)(2,1)S(1)} collective-permute-done((bf16[128,256]{1,0:T(8,128)(2,1)S(1)}, bf16[128,256]{1,0:T(8,128)(2,1)S(1)}, u32[]{:S(2)}, u32[]{:S(2)}) %collective-permute-start.27) | collective-permute-done | bytes 65568 | tf_op jit(solution)/shard_map/ppermute | solution.py:62
  82.7 1.1 %final.3 = f32[128,1152]{1,0:T(8,128)} custom-call(bf16[128,1152]{1,0:T(8,128)(2,1)S(1)} %copy-done.1, f32[128,1152]{1,0:T(8,128)S(1)} %get-tuple-element.75.own_ref, bf16[128,896]{1,0:T(8,128)(2,1)S(1)} %collective-permute-done.25.refs_0_, bf16[128,896]{1,0:T(8,128)(2,1)S(1)} %collective-permute-done.26.refs_1_, ...), custom_call_target="tpu_custom_call" | custom-call | flops 1474560 | bytes 1769472 | tf_op jit(solution)/shard_map/final/pallas_call | solution.py:341
  (47 shorter events, 4.8 us)
Async XLA Ops:
  3.8 22.0 %collective-permute-start = (bf16[128,1536]{1,0:T(8,128)(2,1)}, bf16[128,1536]{1,0:T(8,128)(2,1)S(1)}, u32[]{:S(2)}, u32[]{:S(2)}) collective-permute-start(bf16[128,1536]{1,0:T(8,128)(2,1)} %get-tuple-element.42.refs_0_), channel_id=1, source_target_pairs={{0,16},{1,17},{2,18},{3,19},{4,20},{5,21},{6,22},{7,23},{8,24},{9,... | collective-permute-start | bytes 1179656 | tf_op jit(solution)/shard_map/ppermute | solution.py:62
  7.9 18.0 %collective-permute-start.1 = (bf16[128,1536]{1,0:T(8,128)(2,1)}, bf16[128,1536]{1,0:T(8,128)(2,1)S(1)}, u32[]{:S(2)}, u32[]{:S(2)}) collective-permute-start(bf16[128,1536]{1,0:T(8,128)(2,1)} %get-tuple-element.43.refs_4_), channel_id=1, source_target_pairs={{0,8},{1,9},{2,10},{3,11},{4,12},{5,13},{6,14},{7,15},{8,0},{9,1},... | collective-permute-start | bytes 1179656 | tf_op jit(solution)/shard_map/ppermute | solution.py:62
  9.5 20.3 %collective-permute-start.6 = (bf16[128,2688]{1,0:T(8,128)(2,1)}, bf16[128,2688]{1,0:T(8,128)(2,1)S(1)}, u32[]{:S(2)}, u32[]{:S(2)}) collective-permute-start(bf16[128,2688]{1,0:T(8,128)(2,1)} %get-tuple-element.48), channel_id=1, source_target_pairs={{0,4},{1,5},{2,6},{3,7},{4,0},{5,1},{6,2},{7,3},{8,12},{9,13},{10,... | collective-permute-start | bytes 2064392 | tf_op jit(solution)/shard_map/ppermute | solution.py:62
  9.5 20.3 %collective-permute-start.5 = (bf16[128,2688]{1,0:T(8,128)(2,1)}, bf16[128,2688]{1,0:T(8,128)(2,1)S(1)}, u32[]{:S(2)}, u32[]{:S(2)}) collective-permute-start(bf16[128,2688]{1,0:T(8,128)(2,1)} %get-tuple-element.48), channel_id=1, source_target_pairs={{0,2},{1,3},{2,0},{3,1},{4,6},{5,7},{6,4},{7,5},{8,10},{9,11},{10,... | collective-permute-start | bytes 2064392 | tf_op jit(solution)/shard_map/ppermute | solution.py:62
  11.0 18.8 %collective-permute-start.3 = (bf16[128,2688]{1,0:T(8,128)(2,1)}, bf16[128,2688]{1,0:T(8,128)(2,1)S(1)}, u32[]{:S(2)}, u32[]{:S(2)}) collective-permute-start(bf16[128,2688]{1,0:T(8,128)(2,1)} %get-tuple-element.45), channel_id=1, source_target_pairs={{0,1},{1,0},{2,3},{3,2},{4,5},{5,4},{6,7},{7,6},{8,9},{9,8},{10,11... | collective-permute-start | bytes 2064392 | tf_op jit(solution)/shard_map/ppermute | solution.py:62
  25.9 15.5 %collective-permute-start.2 = (bf16[128,1152]{1,0:T(8,128)(2,1)}, bf16[128,1152]{1,0:T(8,128)(2,1)S(1)}, u32[]{:S(2)}, u32[]{:S(2)}) collective-permute-start(bf16[128,1152]{1,0:T(8,128)(2,1)} %get-tuple-element.44.refs_0_), channel_id=1, source_target_pairs={{0,16},{1,17},{2,18},{3,19},{4,20},{5,21},{6,22},{7,23},{8,24},{9,... | collective-permute-start | bytes 884744 | tf_op jit(solution)/shard_map/ppermute | solution.py:62
  27.3 14.2 %collective-permute-start.4 = (bf16[128,1152]{1,0:T(8,128)(2,1)}, bf16[128,1152]{1,0:T(8,128)(2,1)S(1)}, u32[]{:S(2)}, u32[]{:S(2)}) collective-permute-start(bf16[128,1152]{1,0:T(8,128)(2,1)} %get-tuple-element.47.refs_4_), channel_id=1, source_target_pairs={{0,8},{1,9},{2,10},{3,11},{4,12},{5,13},{6,14},{7,15},{8,0},{9,1},... | collective-permute-start | bytes 884744 | tf_op jit(solution)/shard_map/ppermute | solution.py:62
  29.8 11.7 %collective-permute-start.7 = (bf16[128,1536]{1,0:T(8,128)(2,1)S(1)}, bf16[128,1536]{1,0:T(8,128)(2,1)S(1)}, u32[]{:S(2)}, u32[]{:S(2)}) collective-permute-start(bf16[128,1536]{1,0:T(8,128)(2,1)S(1)} %collective-permute-done.refs_1_), channel_id=1, source_target_pairs={{0,1},{1,0},{2,3},{3,2},{4,5},{5,4},{6,7},{7,6},{8,9},{9,8},{10,11... | collective-permute-start | bytes 1179656 | tf_op jit(solution)/shard_map/ppermute | solution.py:62
  31.3 10.2 %collective-permute-start.8 = (bf16[128,1536]{1,0:T(8,128)(2,1)S(1)}, bf16[128,1536]{1,0:T(8,128)(2,1)S(1)}, u32[]{:S(2)}, u32[]{:S(2)}) collective-permute-start(bf16[128,1536]{1,0:T(8,128)(2,1)S(1)} %collective-permute-done.1.refs_5_), channel_id=1, source_target_pairs={{0,2},{1,3},{2,0},{3,1},{4,6},{5,7},{6,4},{7,5},{8,10},{9,11},{10,... | collective-permute-start | bytes 1179656 | tf_op jit(solution)/shard_map/ppermute | solution.py:62
  32.8 8.7 %collective-permute-start.9 = (bf16[128,2688]{1,0:T(8,128)(2,1)S(1)}, bf16[128,2688]{1,0:T(8,128)(2,1)S(1)}, u32[]{:S(2)}, u32[]{:S(2)}) collective-permute-start(bf16[128,2688]{1,0:T(8,128)(2,1)S(1)} %collective-permute-done.5.refs_6_), channel_id=1, source_target_pairs={{0,4},{1,5},{2,6},{3,7},{4,0},{5,1},{6,2},{7,3},{8,12},{9,13},{10,... | collective-permute-start | bytes 2064392 | tf_op jit(solution)/shard_map/ppermute | solution.py:62
  41.5 3.4 %collective-permute-start.13 = (bf16[128,1536]{1,0:T(8,128)(2,1)S(1)}, bf16[128,1536]{1,0:T(8,128)(2,1)S(1)}, u32[]{:S(2)}, u32[]{:S(2)}) collective-permute-start(bf16[128,1536]{1,0:T(8,128)(2,1)S(1)} %collective-permute-done.1.refs_5_), channel_id=1, source_target_pairs={{0,4},{1,5},{2,6},{3,7},{4,0},{5,1},{6,2},{7,3},{8,12},{9,13},{10,... | collective-permute-start | bytes 1179656 | tf_op jit(solution)/shard_map/ppermute | solution.py:62
  41.6 3.3 %collective-permute-start.14 = (bf16[128,1536]{1,0:T(8,128)(2,1)S(1)}, bf16[128,1536]{1,0:T(8,128)(2,1)S(1)}, u32[]{:S(2)}, u32[]{:S(2)}) collective-permute-start(bf16[128,1536]{1,0:T(8,128)(2,1)S(1)} %collective-permute-done.8.refs_7_), channel_id=1, source_target_pairs={{0,4},{1,5},{2,6},{3,7},{4,0},{5,1},{6,2},{7,3},{8,12},{9,13},{10,... | collective-permute-start | bytes 1179656 | tf_op jit(solution)/shard_map/ppermute | solution.py:62
  42.1 7.6 %collective-permute-start.12 = (bf16[128,1152]{1,0:T(8,128)(2,1)S(1)}, bf16[128,1152]{1,0:T(8,128)(2,1)S(1)}, u32[]{:S(2)}, u32[]{:S(2)}) collective-permute-start(bf16[128,1152]{1,0:T(8,128)(2,1)S(1)} %collective-permute-done.4.refs_5_), channel_id=1, source_target_pairs={{0,4},{1,5},{2,6},{3,7},{4,0},{5,1},{6,2},{7,3},{8,12},{9,13},{10,... | collective-permute-start | bytes 884744 | tf_op jit(solution)/shard_map/ppermute | solution.py:62
  42.2 9.4 %collective-permute-start.11 = (bf16[128,1152]{1,0:T(8,128)(2,1)S(1)}, bf16[128,1152]{1,0:T(8,128)(2,1)S(1)}, u32[]{:S(2)}, u32[]{:S(2)}) collective-permute-start(bf16[128,1152]{1,0:T(8,128)(2,1)S(1)} %collective-permute-done.4.refs_5_), channel_id=1, source_target_pairs={{0,2},{1,3},{2,0},{3,1},{4,6},{5,7},{6,4},{7,5},{8,10},{9,11},{10,... | collective-permute-start | bytes 884744 | tf_op jit(solution)/shard_map/ppermute | solution.py:62
  43.6 9.1 %collective-permute-start.10 = (bf16[128,1152]{1,0:T(8,128)(2,1)S(1)}, bf16[128,1152]{1,0:T(8,128)(2,1)S(1)}, u32[]{:S(2)}, u32[]{:S(2)}) collective-permute-start(bf16[128,1152]{1,0:T(8,128)(2,1)S(1)} %collective-permute-done.2.refs_1_), channel_id=1, source_target_pairs={{0,1},{1,0},{2,3},{3,2},{4,5},{5,4},{6,7},{7,6},{8,9},{9,8},{10,11... | collective-permute-start | bytes 884744 | tf_op jit(solution)/shard_map/ppermute | solution.py:62
  46.9 6.2 %copy-start.4 = (bf16[128,1152]{1,0:T(8,128)(2,1)S(1)}, bf16[128,1152]{1,0:T(8,128)(2,1)}, u32[]{:S(2)}) copy-start(bf16[128,1152]{1,0:T(8,128)(2,1)} %get-tuple-element.44.refs_0_) | copy-start | bytes 884740
  46.9 6.2 %copy-start.5 = (bf16[128,1152]{1,0:T(8,128)(2,1)S(1)}, bf16[128,1152]{1,0:T(8,128)(2,1)}, u32[]{:S(2)}) copy-start(bf16[128,1152]{1,0:T(8,128)(2,1)} %get-tuple-element.47.refs_4_) | copy-start | bytes 884740
  51.5 1.6 %collective-permute-start.15 = (bf16[128,1152]{1,0:T(8,128)(2,1)S(1)}, bf16[128,1152]{1,0:T(8,128)(2,1)S(1)}, u32[]{:S(2)}, u32[]{:S(2)}) collective-permute-start(bf16[128,1152]{1,0:T(8,128)(2,1)S(1)} %collective-permute-done.11.refs_7_), channel_id=1, source_target_pairs={{0,4},{1,5},{2,6},{3,7},{4,0},{5,1},{6,2},{7,3},{8,12},{9,13},{10,... | collective-permute-start | bytes 884744 | tf_op jit(solution)/shard_map/ppermute | solution.py:62
  56.3 5.6 %collective-permute-start.16 = (bf16[256,1152]{1,0:T(8,128)(2,1)S(1)}, bf16[256,1152]{1,0:T(8,128)(2,1)S(1)}, u32[]{:S(2)}, u32[]{:S(2)}) collective-permute-start(bf16[256,1152]{1,0:T(8,128)(2,1)S(1)} %get-tuple-element.63), channel_id=1, source_target_pairs={{0,4},{1,5},{2,6},{3,7},{4,0},{5,1},{6,2},{7,3},{8,12},{9,13},{10,... | collective-permute-start | bytes 1769480 | tf_op jit(solution)/shard_map/ppermute | solution.py:62
  56.5 5.5 %collective-permute-start.17 = (bf16[256,1152]{1,0:T(8,128)(2,1)S(1)}, bf16[256,1152]{1,0:T(8,128)(2,1)S(1)}, u32[]{:S(2)}, u32[]{:S(2)}) collective-permute-start(bf16[256,1152]{1,0:T(8,128)(2,1)S(1)} %get-tuple-element.64), channel_id=1, source_target_pairs={{0,4},{1,5},{2,6},{3,7},{4,0},{5,1},{6,2},{7,3},{8,12},{9,13},{10,... | collective-permute-start | bytes 1769480 | tf_op jit(solution)/shard_map/ppermute | solution.py:62
  56.9 8.6 %collective-permute-start.20 = (bf16[128,896]{1,0:T(8,128)(2,1)S(1)}, bf16[128,896]{1,0:T(8,128)(2,1)S(1)}, u32[]{:S(2)}, u32[]{:S(2)}) collective-permute-start(bf16[128,896]{1,0:T(8,128)(2,1)S(1)} %get-tuple-element.71), channel_id=1, source_target_pairs={{0,1},{1,0},{2,3},{3,2},{4,5},{5,4},{6,7},{7,6},{8,9},{9,8},{10,11... | collective-permute-start | bytes 688136 | tf_op jit(solution)/shard_map/ppermute | solution.py:62
  58.1 14.2 %collective-permute-start.23 = (bf16[256,256]{1,0:T(8,128)(2,1)S(1)}, bf16[256,256]{1,0:T(8,128)(2,1)S(1)}, u32[]{:S(2)}, u32[]{:S(2)}) collective-permute-start(bf16[256,256]{1,0:T(8,128)(2,1)S(1)} %get-tuple-element.74), channel_id=1, source_target_pairs={{0,16},{1,17},{2,18},{3,19},{4,20},{5,21},{6,22},{7,23},{8,24},{9,... | collective-permute-start | bytes 393224 | tf_op jit(solution)/shard_map/ppermute | solution.py:62
  62.0 16.9 %copy-start = (bf16[128,1152]{1,0:T(8,128)(2,1)S(1)}, bf16[128,1152]{1,0:T(8,128)(2,1)}, u32[]{:S(2)}) copy-start(bf16[128,1152]{1,0:T(8,128)(2,1)} %x_ref.2) | copy-start | bytes 884740
  62.2 20.5 %copy-start.1 = (bf16[128,1152]{1,0:T(8,128)(2,1)S(1)}, bf16[128,1152]{1,0:T(8,128)(2,1)}, u32[]{:S(2)}) copy-start(bf16[128,1152]{1,0:T(8,128)(2,1)} %x_ref.3) | copy-start | bytes 884740
  62.2 7.1 %collective-permute-start.18 = (bf16[256,256]{1,0:T(8,128)(2,1)S(1)}, bf16[256,256]{1,0:T(8,128)(2,1)S(1)}, u32[]{:S(2)}, u32[]{:S(2)}) collective-permute-start(bf16[256,256]{1,0:T(8,128)(2,1)S(1)} %get-tuple-element.65), channel_id=1, source_target_pairs={{0,8},{1,9},{2,10},{3,11},{4,12},{5,13},{6,14},{7,15},{8,0},{9,1},... | collective-permute-start | bytes 393224 | tf_op jit(solution)/shard_map/ppermute | solution.py:62
  63.9 8.3 %collective-permute-start.22 = (bf16[128,896]{1,0:T(8,128)(2,1)S(1)}, bf16[128,896]{1,0:T(8,128)(2,1)S(1)}, u32[]{:S(2)}, u32[]{:S(2)}) collective-permute-start(bf16[128,896]{1,0:T(8,128)(2,1)S(1)} %get-tuple-element.69), channel_id=1, source_target_pairs={{0,2},{1,3},{2,0},{3,1},{4,6},{5,7},{6,4},{7,5},{8,10},{9,11},{10,... | collective-permute-start | bytes 688136 | tf_op jit(solution)/shard_map/ppermute | solution.py:62
  65.5 12.3 %collective-permute-start.21 = (bf16[128,896]{1,0:T(8,128)(2,1)S(1)}, bf16[128,896]{1,0:T(8,128)(2,1)S(1)}, u32[]{:S(2)}, u32[]{:S(2)}) collective-permute-start(bf16[128,896]{1,0:T(8,128)(2,1)S(1)} %add_convert_fusion.1), channel_id=1, source_target_pairs={{0,16},{1,17},{2,18},{3,19},{4,20},{5,21},{6,22},{7,23},{8,24},{9,... | collective-permute-start | bytes 688136 | tf_op jit(solution)/shard_map/ppermute | solution.py:62
  69.3 9.5 %collective-permute-start.19 = (bf16[128,896]{1,0:T(8,128)(2,1)S(1)}, bf16[128,896]{1,0:T(8,128)(2,1)S(1)}, u32[]{:S(2)}, u32[]{:S(2)}) collective-permute-start(bf16[128,896]{1,0:T(8,128)(2,1)S(1)} %get-tuple-element.66), channel_id=1, source_target_pairs={{0,1},{1,0},{2,3},{3,2},{4,5},{5,4},{6,7},{7,6},{8,9},{9,8},{10,11... | collective-permute-start | bytes 688136 | tf_op jit(solution)/shard_map/ppermute | solution.py:62
  70.8 11.3 %collective-permute-start.25 = (bf16[128,896]{1,0:T(8,128)(2,1)S(1)}, bf16[128,896]{1,0:T(8,128)(2,1)S(1)}, u32[]{:S(2)}, u32[]{:S(2)}) collective-permute-start(bf16[128,896]{1,0:T(8,128)(2,1)S(1)} %get-tuple-element.76), channel_id=1, source_target_pairs={{0,2},{1,3},{2,0},{3,1},{4,6},{5,7},{6,4},{7,5},{8,10},{9,11},{10,... | collective-permute-start | bytes 688136 | tf_op jit(solution)/shard_map/ppermute | solution.py:62
  72.3 6.5 %collective-permute-start.24 = (bf16[128,256]{1,0:T(8,128)(2,1)S(1)}, bf16[128,256]{1,0:T(8,128)(2,1)S(1)}, u32[]{:S(2)}, u32[]{:S(2)}) collective-permute-start(bf16[128,256]{1,0:T(8,128)(2,1)S(1)} %add_convert_fusion.3), channel_id=1, source_target_pairs={{0,1},{1,0},{2,3},{3,2},{4,5},{5,4},{6,7},{7,6},{8,9},{9,8},{10,11... | collective-permute-start | bytes 196616 | tf_op jit(solution)/shard_map/ppermute | solution.py:62
  73.6 9.1 %collective-permute-start.26 = (bf16[128,896]{1,0:T(8,128)(2,1)S(1)}, bf16[128,896]{1,0:T(8,128)(2,1)S(1)}, u32[]{:S(2)}, u32[]{:S(2)}) collective-permute-start(bf16[128,896]{1,0:T(8,128)(2,1)S(1)} %add_convert_fusion), channel_id=1, source_target_pairs={{0,8},{1,9},{2,10},{3,11},{4,12},{5,13},{6,14},{7,15},{8,0},{9,1},... | collective-permute-start | bytes 688136 | tf_op jit(solution)/shard_map/ppermute | solution.py:62
  77.9 4.3 %collective-permute-start.27 = (bf16[128,256]{1,0:T(8,128)(2,1)S(1)}, bf16[128,256]{1,0:T(8,128)(2,1)S(1)}, u32[]{:S(2)}, u32[]{:S(2)}) collective-permute-start(bf16[128,256]{1,0:T(8,128)(2,1)S(1)} %add_convert_fusion.2), channel_id=1, source_target_pairs={{0,2},{1,3},{2,0},{3,1},{4,6},{5,7},{6,4},{7,5},{8,10},{9,11},{10,... | collective-permute-start | bytes 196616 | tf_op jit(solution)/shard_map/ppermute | solution.py:62
  (2 other events, 2.0 us)
